TPU v7x, 32 devices: a whole 2x2x4 slice. The times are simulated.
32 devices in a mesh: layer: 8 (over y, x, core), dp: 4 (over z).
Axes of the slice: x: 2, y: 2, z: 4, core: 2. Of those that a mesh axis runs over, the one named last changes fastest.
Arguments:
- inputs: float32 [512, 1024], P('dp'), may hold values from -6 to 6
- guesses: float32 [8, 512, 1024], P('layer', 'dp'), may hold values from -6 to 6
- weights: bfloat16 [32, 1024, 1024], P('layer'), may hold values from -0.1875 to 0.1875
- biases: float32 [32, 1024], P('layer'), may hold values from -3 to 3
- adjoint: bfloat16 [8, 512, 1024], P('layer', 'dp'), may hold values from -6 to 6
Outputs:
- new_states: float32 [8, 512, 1024], P('layer', 'dp')
- coarse_states: float32 [8, 512, 1024], P('layer', 'dp')
- weight_grad: float32 [8, 1024, 1024], P('layer', None, 'dp')
All inputs are finite; a program needn't handle non-finite values.
Results may differ from a plain program's by a relative error of at most 0.007.
Values may be sent and summed in bfloat16 or wider, within the bound.
No kernel may reach another device: no remote copies, remote signals or barrier semaphores. Data moves between devices by JAX's collectives and lax.ppermute only.
A program may use at most 64 MiB of HBM per device.

v0:
```python
import jax
import jax.numpy as jnp
from jax import lax
from jax.sharding import PartitionSpec as P


def passed_along(shard, axis, by):
    devices = lax.axis_size(axis)
    pairs = [(i, i + by) for i in range(devices) if 0 <= i + by < devices]
    return lax.ppermute(shard, axis, pairs)


def advance(layer_state, weight, bias_row, step_size):
    pre_tanh = (
        jnp.dot(layer_state.astype(jnp.bfloat16), weight, preferred_element_type=jnp.float32)
        + bias_row
    )
    return (layer_state + step_size * jnp.tanh(pre_tanh), pre_tanh)


def body(inputs, guesses, weights, biases, adjoint):
    blocks = lax.axis_size("layer")
    step_size = 4.0 / (4 * blocks)
    device_idx = lax.axis_index("layer")
    position = (device_idx + 1) % 4
    is_first = device_idx == 0
    is_early = device_idx < 4

    def fine_block(start):
        current = start
        last_in = start
        pre_tanh = start
        for layer_idx in range(4):
            if layer_idx == 3:
                last_in = current
            current, pre_tanh = advance(current, weights[layer_idx], biases[layer_idx], step_size)
        return (current, last_in, pre_tanh)

    def coarse_step(layer_state, factor):
        return advance(layer_state, weights[0], biases[0], factor * step_size)[0]

    guess_prev = jnp.where(is_first, inputs, passed_along(guesses[0], "layer", 1))
    relaxed = fine_block(guess_prev)[0]
    relaxed_prev = jnp.where(is_first, inputs, passed_along(relaxed, "layer", 1))
    ahead = fine_block(relaxed_prev)[0]
    forcing = ahead - coarse_step(relaxed_prev, 4.0)

    def level_round(current):
        received = passed_along(current, "layer", 1)
        return coarse_step(jnp.where(is_first, inputs, received), 4.0) + forcing

    current = relaxed
    for target in (1, 2, 3, 0, 1, 2, 3):
        current = jnp.where(position == target, level_round(current), current)
    update = level_round(current)
    below = jnp.where(is_early, inputs, passed_along(current, "layer", 4))
    coarse_force = update - coarse_step(below, 16.0)

    def coarse_chain(turn, carried):
        received = passed_along(carried, "layer", 4)
        return coarse_step(jnp.where(is_early, inputs, received), 16.0) + coarse_force

    solved = lax.fori_loop(0, blocks // 4, coarse_chain, current)
    coarse_states = solved - relaxed
    current = jnp.where(position == 0, solved, current)
    for target in (1, 2, 3):
        current = jnp.where(position == target, level_round(current), current)
    final_prev = jnp.where(is_first, inputs, passed_along(current, "layer", 1))
    new_states, last_in, pre_tanh = fine_block(final_prev)
    tanh_val = jnp.tanh(pre_tanh)
    deltas = (adjoint[0].astype(jnp.float32) * step_size * (1.0 - tanh_val * tanh_val)).astype(
        jnp.bfloat16
    )
    left_rows = last_in.astype(jnp.bfloat16)
    all_rows = lax.all_gather(left_rows, "dp", axis=0, tiled=True)
    own_deltas = lax.all_to_all(deltas, "dp", split_axis=1, concat_axis=0, tiled=True)
    weight_grad = jnp.einsum("rd,re->de", all_rows, own_deltas, preferred_element_type=jnp.float32)
    return (new_states[None], coarse_states[None], weight_grad[None])


def solution(mesh):
    return jax.shard_map(
        body,
        mesh=mesh,
        in_specs=(
            P("dp", None),
            P("layer", "dp", None),
            P("layer", None, None),
            P("layer", None),
            P("layer", "dp", None),
        ),
        out_specs=(P("layer", "dp", None), P("layer", "dp", None), P("layer", None, "dp")),
        check_vma=False,
    )
```

profile of v0, /device:TPU:13, one launch (start us, length us, event | category | flops | bytes accessed | tf_op | source)
XLA Modules:
  0.0 281.2 jit_solution(10504057389677241477)
XLA Ops:
  7.2 3.8 %collective-permute-start.1 = (f32[128,1024]{1,0:T(8,128)}, f32[128,1024]{1,0:T(8,128)S(1)}, u32[]{:S(2)}, u32[]{:S(2)}) collective-permute-start(f32[128,1024]{1,0:T(8,128)} %bitcast.344), channel_id=1, source_target_pairs={{0,4},{4,8},{8,12},{12,16},{16,20},{20,24},{24,28},{1,5},{5,9},{9,... | collective-permute-start | bytes 1572872 | tf_op jit(solution)/shard_map/ppermute | solution.py:10
  11.9 5.5 %collective-permute-done.1 = f32[128,1024]{1,0:T(8,128)S(1)} collective-permute-done((f32[128,1024]{1,0:T(8,128)}, f32[128,1024]{1,0:T(8,128)S(1)}, u32[]{:S(2)}, u32[]{:S(2)}) %collective-permute-start.1) | collective-permute-done | bytes 524320 | tf_op jit(solution)/shard_map/ppermute | solution.py:10
  17.5 2.2 fusion.85
  19.6 2.1 fusion.307
  25.8 4.3 %collective-permute-start.2 = (f32[128,1024]{1,0:T(8,128)S(1)}, f32[128,1024]{1,0:T(8,128)S(1)}, u32[]{:S(2)}, u32[]{:S(2)}) collective-permute-start(f32[128,1024]{1,0:T(8,128)S(1)} %fusion.379), channel_id=1, source_target_pairs={{0,4},{4,8},{8,12},{12,16},{16,20},{20,24},{24,28},{1,5},{5,9},{9,... | collective-permute-start | bytes 1572872 | tf_op jit(solution)/shard_map/ppermute | solution.py:10
  30.1 6.1 %collective-permute-done.2 = f32[128,1024]{1,0:T(8,128)S(1)} collective-permute-done((f32[128,1024]{1,0:T(8,128)S(1)}, f32[128,1024]{1,0:T(8,128)S(1)}, u32[]{:S(2)}, u32[]{:S(2)}) %collective-permute-start.2) | collective-permute-done | bytes 524320 | tf_op jit(solution)/shard_map/ppermute | solution.py:10
  38.4 2.1 fusion.319
  40.5 2.1 fusion.355
  42.6 2.2 add_select_fusion
  44.8 4.4 %collective-permute-start.3 = (f32[128,1024]{1,0:T(8,128)S(1)}, f32[128,1024]{1,0:T(8,128)S(1)}, u32[]{:S(2)}, u32[]{:S(2)}) collective-permute-start(f32[128,1024]{1,0:T(8,128)S(1)} %get-tuple-element.63), channel_id=1, source_target_pairs={{0,4},{4,8},{8,12},{12,16},{16,20},{20,24},{24,28},{1,5},{5,9},{9,... | collective-permute-start | bytes 1572872 | tf_op jit(solution)/shard_map/ppermute | solution.py:10
  49.2 6.1 %collective-permute-done.3 = f32[128,1024]{1,0:T(8,128)S(1)} collective-permute-done((f32[128,1024]{1,0:T(8,128)S(1)}, f32[128,1024]{1,0:T(8,128)S(1)}, u32[]{:S(2)}, u32[]{:S(2)}) %collective-permute-start.3) | collective-permute-done | bytes 524320 | tf_op jit(solution)/shard_map/ppermute | solution.py:10
  55.3 2.1 fusion.109
  57.4 4.4 %collective-permute-start.4 = (f32[128,1024]{1,0:T(8,128)S(1)}, f32[128,1024]{1,0:T(8,128)S(1)}, u32[]{:S(2)}, u32[]{:S(2)}) collective-permute-start(f32[128,1024]{1,0:T(8,128)S(1)} %fusion.109), channel_id=1, source_target_pairs={{0,4},{4,8},{8,12},{12,16},{16,20},{20,24},{24,28},{1,5},{5,9},{9,... | collective-permute-start | bytes 1572872 | tf_op jit(solution)/shard_map/ppermute | solution.py:10
  61.8 6.1 %collective-permute-done.4 = f32[128,1024]{1,0:T(8,128)S(1)} collective-permute-done((f32[128,1024]{1,0:T(8,128)S(1)}, f32[128,1024]{1,0:T(8,128)S(1)}, u32[]{:S(2)}, u32[]{:S(2)}) %collective-permute-start.4) | collective-permute-done | bytes 524320 | tf_op jit(solution)/shard_map/ppermute | solution.py:10
  67.9 2.1 fusion.127
  70.0 4.4 %collective-permute-start.5 = (f32[128,1024]{1,0:T(8,128)S(1)}, f32[128,1024]{1,0:T(8,128)S(1)}, u32[]{:S(2)}, u32[]{:S(2)}) collective-permute-start(f32[128,1024]{1,0:T(8,128)S(1)} %fusion.127), channel_id=1, source_target_pairs={{0,4},{4,8},{8,12},{12,16},{16,20},{20,24},{24,28},{1,5},{5,9},{9,... | collective-permute-start | bytes 1572872 | tf_op jit(solution)/shard_map/ppermute | solution.py:10
  74.4 6.1 %collective-permute-done.5 = f32[128,1024]{1,0:T(8,128)S(1)} collective-permute-done((f32[128,1024]{1,0:T(8,128)S(1)}, f32[128,1024]{1,0:T(8,128)S(1)}, u32[]{:S(2)}, u32[]{:S(2)}) %collective-permute-start.5) | collective-permute-done | bytes 524320 | tf_op jit(solution)/shard_map/ppermute | solution.py:10
  80.5 2.1 fusion.145
  82.6 4.4 %collective-permute-start.6 = (f32[128,1024]{1,0:T(8,128)S(1)}, f32[128,1024]{1,0:T(8,128)S(1)}, u32[]{:S(2)}, u32[]{:S(2)}) collective-permute-start(f32[128,1024]{1,0:T(8,128)S(1)} %fusion.145), channel_id=1, source_target_pairs={{0,4},{4,8},{8,12},{12,16},{16,20},{20,24},{24,28},{1,5},{5,9},{9,... | collective-permute-start | bytes 1572872 | tf_op jit(solution)/shard_map/ppermute | solution.py:10
  87.0 6.1 %collective-permute-done.6 = f32[128,1024]{1,0:T(8,128)S(1)} collective-permute-done((f32[128,1024]{1,0:T(8,128)S(1)}, f32[128,1024]{1,0:T(8,128)S(1)}, u32[]{:S(2)}, u32[]{:S(2)}) %collective-permute-start.6) | collective-permute-done | bytes 524320 | tf_op jit(solution)/shard_map/ppermute | solution.py:10
  93.1 2.1 fusion.163
  95.2 4.4 %collective-permute-start.7 = (f32[128,1024]{1,0:T(8,128)S(1)}, f32[128,1024]{1,0:T(8,128)S(1)}, u32[]{:S(2)}, u32[]{:S(2)}) collective-permute-start(f32[128,1024]{1,0:T(8,128)S(1)} %fusion.163), channel_id=1, source_target_pairs={{0,4},{4,8},{8,12},{12,16},{16,20},{20,24},{24,28},{1,5},{5,9},{9,... | collective-permute-start | bytes 1572872 | tf_op jit(solution)/shard_map/ppermute | solution.py:10
  99.6 6.1 %collective-permute-done.7 = f32[128,1024]{1,0:T(8,128)S(1)} collective-permute-done((f32[128,1024]{1,0:T(8,128)S(1)}, f32[128,1024]{1,0:T(8,128)S(1)}, u32[]{:S(2)}, u32[]{:S(2)}) %collective-permute-start.7) | collective-permute-done | bytes 524320 | tf_op jit(solution)/shard_map/ppermute | solution.py:10
  105.7 2.1 fusion.181
  107.9 4.4 %collective-permute-start.8 = (f32[128,1024]{1,0:T(8,128)S(1)}, f32[128,1024]{1,0:T(8,128)S(1)}, u32[]{:S(2)}, u32[]{:S(2)}) collective-permute-start(f32[128,1024]{1,0:T(8,128)S(1)} %fusion.181), channel_id=1, source_target_pairs={{0,4},{4,8},{8,12},{12,16},{16,20},{20,24},{24,28},{1,5},{5,9},{9,... | collective-permute-start | bytes 1572872 | tf_op jit(solution)/shard_map/ppermute | solution.py:10
  112.3 6.6 %collective-permute-done.8 = f32[128,1024]{1,0:T(8,128)S(1)} collective-permute-done((f32[128,1024]{1,0:T(8,128)S(1)}, f32[128,1024]{1,0:T(8,128)S(1)}, u32[]{:S(2)}, u32[]{:S(2)}) %collective-permute-start.8) | collective-permute-done | bytes 524320 | tf_op jit(solution)/shard_map/ppermute | solution.py:10
  118.8 2.1 fusion.199
  122.3 3.9 %collective-permute-start.9 = (f32[128,1024]{1,0:T(8,128)S(1)}, f32[128,1024]{1,0:T(8,128)S(1)}, u32[]{:S(2)}, u32[]{:S(2)}) collective-permute-start(f32[128,1024]{1,0:T(8,128)S(1)} %fusion.199), channel_id=1, source_target_pairs={{0,4},{4,8},{8,12},{12,16},{16,20},{20,24},{24,28},{1,5},{5,9},{9,... | collective-permute-start | bytes 1572872 | tf_op jit(solution)/shard_map/ppermute | solution.py:10
  127.0 4.9 %collective-permute-done.10 = f32[128,1024]{1,0:T(8,128)S(1)} collective-permute-done((f32[128,1024]{1,0:T(8,128)S(1)}, f32[128,1024]{1,0:T(8,128)S(1)}, u32[]{:S(2)}, u32[]{:S(2)}) %collective-permute-start.10) | collective-permute-done | bytes 524320 | tf_op jit(solution)/shard_map/ppermute | solution.py:10
  131.9 2.1 fusion.229
  134.0 2.1 fusion.217
  136.1 35.9 %while.10 = (s32[]{:T(128)}, f32[128,1024]{1,0:T(8,128)}, pred[]{:T(512)}, f32[128,1024]{1,0:T(8,128)S(1)}, bf16[4,1024,1024]{2,1,0:T(8,128)(2,1)}, /*index=5*/f...) while((s32[]{:T(128)}, f32[128,1024]{1,0:T(8,128)}, pred[]{:T(512)}, f32[128,1024]{1,0:T(8,128)S(1)}, ...), condition=%wide.region_1.2_spmd, body=%wide.region_0.1_spmd.sunk | while | flops 269352960 | bytes 7353469 | solution.py:63
  138.1 12.7 %collective-permute-done = f32[128,1024]{1,0:T(8,128)S(1)} collective-permute-done((f32[128,1024]{1,0:T(8,128)}, f32[128,1024]{1,0:T(8,128)S(1)}, u32[]{:S(2)}, u32[]{:S(2)}) %collective-permute-start) | collective-permute-done | bytes 524320 | tf_op jit(solution)/shard_map/while/body/eval_jaxpr/ppermute | solution.py:10
  150.8 2.9 %fusion.480 = f32[128,1024]{1,0:T(8,128)} fusion(f32[128,1024]{1,0:T(8,128)S(1)} %get-tuple-element.132, bf16[4,1024,1024]{2,1,0:T(8,128)(2,1)} %get-tuple-element.130, f32[1024]{0:T(1024)S(1)} %bitcast.333, f32[128,1024]{1,0:T(8,128)S(1)} %get-tuple-element.129, f32[128,1024]{1,0:T(8,128)S(1)} %collective-permute-done, pred[]{:T(512)} %get-tuple-element.128), kind=kOutput, calls=%fused_computation.7.clone.1 | convolution fusion | flops 269352960 | bytes 5248000 | tf_op jit(solution)/shard_map/while/body/eval_jaxpr/dot_general | solution.py:15
  155.7 13.4 %collective-permute-done = f32[128,1024]{1,0:T(8,128)S(1)} collective-permute-done((f32[128,1024]{1,0:T(8,128)}, f32[128,1024]{1,0:T(8,128)S(1)}, u32[]{:S(2)}, u32[]{:S(2)}) %collective-permute-start) | collective-permute-done | bytes 524320 | tf_op jit(solution)/shard_map/while/body/eval_jaxpr/ppermute | solution.py:10
  169.1 2.9 %fusion.480 = f32[128,1024]{1,0:T(8,128)} fusion(f32[128,1024]{1,0:T(8,128)S(1)} %get-tuple-element.132, bf16[4,1024,1024]{2,1,0:T(8,128)(2,1)} %get-tuple-element.130, f32[1024]{0:T(1024)S(1)} %bitcast.333, f32[128,1024]{1,0:T(8,128)S(1)} %get-tuple-element.129, f32[128,1024]{1,0:T(8,128)S(1)} %collective-permute-done, pred[]{:T(512)} %get-tuple-element.128), kind=kOutput, calls=%fused_computation.7.clone.1 | convolution fusion | flops 269352960 | bytes 5248000 | tf_op jit(solution)/shard_map/while/body/eval_jaxpr/dot_general | solution.py:15
  171.9 2.1 subtract_bitcast_fusion
  174.0 8.9 %collective-permute-start.11 = (f32[128,1024]{1,0:T(8,128)S(1)}, f32[128,1024]{1,0:T(8,128)S(1)}, u32[]{:S(2)}, u32[]{:S(2)}) collective-permute-start(f32[128,1024]{1,0:T(8,128)S(1)} %get-tuple-element.58), channel_id=1, source_target_pairs={{0,4},{4,8},{8,12},{12,16},{16,20},{20,24},{24,28},{1,5},{5,9},{9,... | collective-permute-start | bytes 1572872 | tf_op jit(solution)/shard_map/ppermute | solution.py:10
  183.0 9.7 %collective-permute-done.11 = f32[128,1024]{1,0:T(8,128)S(1)} collective-permute-done((f32[128,1024]{1,0:T(8,128)S(1)}, f32[128,1024]{1,0:T(8,128)S(1)}, u32[]{:S(2)}, u32[]{:S(2)}) %collective-permute-start.11) | collective-permute-done | bytes 524320 | tf_op jit(solution)/shard_map/ppermute | solution.py:10
  192.7 2.1 fusion.247
  196.7 9.5 %collective-permute-done.12 = f32[128,1024]{1,0:T(8,128)S(1)} collective-permute-done((f32[128,1024]{1,0:T(8,128)S(1)}, f32[128,1024]{1,0:T(8,128)S(1)}, u32[]{:S(2)}, u32[]{:S(2)}) %collective-permute-start.12) | collective-permute-done | bytes 524320 | tf_op jit(solution)/shard_map/ppermute | solution.py:10
  206.2 2.1 fusion.265
  210.4 9.5 %collective-permute-done.13 = f32[128,1024]{1,0:T(8,128)S(1)} collective-permute-done((f32[128,1024]{1,0:T(8,128)S(1)}, f32[128,1024]{1,0:T(8,128)S(1)}, u32[]{:S(2)}, u32[]{:S(2)}) %collective-permute-start.13) | collective-permute-done | bytes 524320 | tf_op jit(solution)/shard_map/ppermute | solution.py:10
  222.4 9.5 %collective-permute-done.14 = f32[128,1024]{1,0:T(8,128)S(1)} collective-permute-done((f32[128,1024]{1,0:T(8,128)S(1)}, f32[128,1024]{1,0:T(8,128)S(1)}, u32[]{:S(2)}, u32[]{:S(2)}) %collective-permute-start.14) | collective-permute-done | bytes 524320 | tf_op jit(solution)/shard_map/ppermute | solution.py:10
  234.1 3.0 %fusion.403 = (bf16[128,1024]{1,0:T(8,128)(2,1)S(1)}, f32[1,128,1024]{2,1,0:T(8,128)}) fusion(bf16[1,128,1024]{2,1,0:T(8,128)(2,1)S(1)} %copy-done.2, f32[128,1024]{1,0:T(8,128)S(1)} %get-tuple-element.66, f32[1024]{0:T(1024)S(1)} %bitcast.337, bf16[128,1024]{1,0:T(8,128)(2,1)} %get-tuple-element.65, bf16[4,1024,1024]{2,1,0:T(8,128)(2,1)} %get-tuple-element.135), kind=kOutput, calls=%fused_computation.177 | convolution fusion | flops 269615104 | bytes 3936256 | tf_op jit(solution)/shard_map/dot_general | solution.py:15
  237.1 9.9 %all_to_all.19 = bf16[128,4,256]{2,0,1:T(8,128)(2,1)S(1)} all-to-all(bf16[128,4,256]{2,0,1:T(8,128)(2,1)S(1)} %bitcast.318), channel_id=1, replica_groups=mesh['layer'=8,'dp'=4] {'dp'}, dimensions={1} | all-to-all | bytes 524288 | tf_op jit(solution)/shard_map/all_to_all | solution.py:76
  247.0 24.6 %all-gather.2.cloned.1.call-done = bf16[512,1024]{1,0:T(8,128)(2,1)} async-done(((bf16[128,1024]{1,0:T(8,128)(2,1)}), bf16[512,1024]{1,0:T(8,128)(2,1)}) %all-gather.2.cloned.1.call-update) | async-done | bytes 1048592 | tf_op jit(solution)/shard_map/all_gather | solution.py:75
  271.6 2.7 convolution_bitcast_fusion
  (28 shorter events, 22.0 us)
Async XLA Ops:
  7.2 29.1 %copy-start.1 = (f32[128,1024]{1,0:T(8,128)S(1)}, f32[128,1024]{1,0:T(8,128)}, u32[]{:S(2)}) copy-start(f32[128,1024]{1,0:T(8,128)} %param.7) | copy-start | bytes 1572868
  7.2 264.5 %all-gather.2.cloned.1.call-start = ((), (), s32[]{:S(2)}) async-start(), calls=%async_computation.1 | async-start | bytes 1310720 | tf_op jit(solution)/shard_map/all_gather | solution.py:75
  7.2 10.2 %collective-permute-start.1 = (f32[128,1024]{1,0:T(8,128)}, f32[128,1024]{1,0:T(8,128)S(1)}, u32[]{:S(2)}, u32[]{:S(2)}) collective-permute-start(f32[128,1024]{1,0:T(8,128)} %bitcast.344), channel_id=1, source_target_pairs={{0,4},{4,8},{8,12},{12,16},{16,20},{20,24},{24,28},{1,5},{5,9},{9,... | collective-permute-start | bytes 1572872 | tf_op jit(solution)/shard_map/ppermute | solution.py:10
  25.8 10.4 %collective-permute-start.2 = (f32[128,1024]{1,0:T(8,128)S(1)}, f32[128,1024]{1,0:T(8,128)S(1)}, u32[]{:S(2)}, u32[]{:S(2)}) collective-permute-start(f32[128,1024]{1,0:T(8,128)S(1)} %fusion.379), channel_id=1, source_target_pairs={{0,4},{4,8},{8,12},{12,16},{16,20},{20,24},{24,28},{1,5},{5,9},{9,... | collective-permute-start | bytes 1572872 | tf_op jit(solution)/shard_map/ppermute | solution.py:10
  44.8 10.5 %collective-permute-start.3 = (f32[128,1024]{1,0:T(8,128)S(1)}, f32[128,1024]{1,0:T(8,128)S(1)}, u32[]{:S(2)}, u32[]{:S(2)}) collective-permute-start(f32[128,1024]{1,0:T(8,128)S(1)} %get-tuple-element.63), channel_id=1, source_target_pairs={{0,4},{4,8},{8,12},{12,16},{16,20},{20,24},{24,28},{1,5},{5,9},{9,... | collective-permute-start | bytes 1572872 | tf_op jit(solution)/shard_map/ppermute | solution.py:10
  57.4 10.5 %collective-permute-start.4 = (f32[128,1024]{1,0:T(8,128)S(1)}, f32[128,1024]{1,0:T(8,128)S(1)}, u32[]{:S(2)}, u32[]{:S(2)}) collective-permute-start(f32[128,1024]{1,0:T(8,128)S(1)} %fusion.109), channel_id=1, source_target_pairs={{0,4},{4,8},{8,12},{12,16},{16,20},{20,24},{24,28},{1,5},{5,9},{9,... | collective-permute-start | bytes 1572872 | tf_op jit(solution)/shard_map/ppermute | solution.py:10
  70.0 10.5 %collective-permute-start.5 = (f32[128,1024]{1,0:T(8,128)S(1)}, f32[128,1024]{1,0:T(8,128)S(1)}, u32[]{:S(2)}, u32[]{:S(2)}) collective-permute-start(f32[128,1024]{1,0:T(8,128)S(1)} %fusion.127), channel_id=1, source_target_pairs={{0,4},{4,8},{8,12},{12,16},{16,20},{20,24},{24,28},{1,5},{5,9},{9,... | collective-permute-start | bytes 1572872 | tf_op jit(solution)/shard_map/ppermute | solution.py:10
  82.6 10.5 %collective-permute-start.6 = (f32[128,1024]{1,0:T(8,128)S(1)}, f32[128,1024]{1,0:T(8,128)S(1)}, u32[]{:S(2)}, u32[]{:S(2)}) collective-permute-start(f32[128,1024]{1,0:T(8,128)S(1)} %fusion.145), channel_id=1, source_target_pairs={{0,4},{4,8},{8,12},{12,16},{16,20},{20,24},{24,28},{1,5},{5,9},{9,... | collective-permute-start | bytes 1572872 | tf_op jit(solution)/shard_map/ppermute | solution.py:10
  95.2 10.5 %collective-permute-start.7 = (f32[128,1024]{1,0:T(8,128)S(1)}, f32[128,1024]{1,0:T(8,128)S(1)}, u32[]{:S(2)}, u32[]{:S(2)}) collective-permute-start(f32[128,1024]{1,0:T(8,128)S(1)} %fusion.163), channel_id=1, source_target_pairs={{0,4},{4,8},{8,12},{12,16},{16,20},{20,24},{24,28},{1,5},{5,9},{9,... | collective-permute-start | bytes 1572872 | tf_op jit(solution)/shard_map/ppermute | solution.py:10
  107.9 11.0 %collective-permute-start.8 = (f32[128,1024]{1,0:T(8,128)S(1)}, f32[128,1024]{1,0:T(8,128)S(1)}, u32[]{:S(2)}, u32[]{:S(2)}) collective-permute-start(f32[128,1024]{1,0:T(8,128)S(1)} %fusion.181), channel_id=1, source_target_pairs={{0,4},{4,8},{8,12},{12,16},{16,20},{20,24},{24,28},{1,5},{5,9},{9,... | collective-permute-start | bytes 1572872 | tf_op jit(solution)/shard_map/ppermute | solution.py:10
  121.0 10.9 %collective-permute-start.10 = (f32[128,1024]{1,0:T(8,128)S(1)}, f32[128,1024]{1,0:T(8,128)S(1)}, u32[]{:S(2)}, u32[]{:S(2)}) collective-permute-start(f32[128,1024]{1,0:T(8,128)S(1)} %fusion.199), channel_id=1, source_target_pairs={{0,16},{4,20},{8,24},{12,28},{1,17},{5,21},{9,25},{13,29},{2,18},{... | collective-permute-start | bytes 1572872 | tf_op jit(solution)/shard_map/ppermute | solution.py:10
  122.3 11.7 %collective-permute-start.9 = (f32[128,1024]{1,0:T(8,128)S(1)}, f32[128,1024]{1,0:T(8,128)S(1)}, u32[]{:S(2)}, u32[]{:S(2)}) collective-permute-start(f32[128,1024]{1,0:T(8,128)S(1)} %fusion.199), channel_id=1, source_target_pairs={{0,4},{4,8},{8,12},{12,16},{16,20},{20,24},{24,28},{1,5},{5,9},{9,... | collective-permute-start | bytes 1572872 | tf_op jit(solution)/shard_map/ppermute | solution.py:10
  136.1 14.7 %collective-permute-start = (f32[128,1024]{1,0:T(8,128)}, f32[128,1024]{1,0:T(8,128)S(1)}, u32[]{:S(2)}, u32[]{:S(2)}) collective-permute-start(f32[128,1024]{1,0:T(8,128)} %get-tuple-element.119), channel_id=1, source_target_pairs={{0,16},{4,20},{8,24},{12,28},{1,17},{5,21},{9,25},{13,29},{2,18},{... | collective-permute-start | bytes 1572872 | tf_op jit(solution)/shard_map/while/body/eval_jaxpr/ppermute | solution.py:10
  153.7 15.4 %collective-permute-start = (f32[128,1024]{1,0:T(8,128)}, f32[128,1024]{1,0:T(8,128)S(1)}, u32[]{:S(2)}, u32[]{:S(2)}) collective-permute-start(f32[128,1024]{1,0:T(8,128)} %get-tuple-element.119), channel_id=1, source_target_pairs={{0,16},{4,20},{8,24},{12,28},{1,17},{5,21},{9,25},{13,29},{2,18},{... | collective-permute-start | bytes 1572872 | tf_op jit(solution)/shard_map/while/body/eval_jaxpr/ppermute | solution.py:10
  171.9 47.9 %copy-start = (bf16[4,1024,1024]{2,1,0:T(8,128)(2,1)S(1)}, bf16[4,1024,1024]{2,1,0:T(8,128)(2,1)}, u32[]{:S(2)}) copy-start(bf16[4,1024,1024]{2,1,0:T(8,128)(2,1)} %get-tuple-element.135) | copy-start | bytes 25165828
  174.0 18.6 %collective-permute-start.11 = (f32[128,1024]{1,0:T(8,128)S(1)}, f32[128,1024]{1,0:T(8,128)S(1)}, u32[]{:S(2)}, u32[]{:S(2)}) collective-permute-start(f32[128,1024]{1,0:T(8,128)S(1)} %get-tuple-element.58), channel_id=1, source_target_pairs={{0,4},{4,8},{8,12},{12,16},{16,20},{20,24},{24,28},{1,5},{5,9},{9,... | collective-permute-start | bytes 1572872 | tf_op jit(solution)/shard_map/ppermute | solution.py:10
  194.8 11.4 %collective-permute-start.12 = (f32[128,1024]{1,0:T(8,128)S(1)}, f32[128,1024]{1,0:T(8,128)S(1)}, u32[]{:S(2)}, u32[]{:S(2)}) collective-permute-start(f32[128,1024]{1,0:T(8,128)S(1)} %fusion.247), channel_id=1, source_target_pairs={{0,4},{4,8},{8,12},{12,16},{16,20},{20,24},{24,28},{1,5},{5,9},{9,... | collective-permute-start | bytes 1572872 | tf_op jit(solution)/shard_map/ppermute | solution.py:10
  208.3 25.8 %copy-start.2 = (bf16[1,128,1024]{2,1,0:T(8,128)(2,1)S(1)}, bf16[1,128,1024]{2,1,0:T(8,128)(2,1)}, u32[]{:S(2)}) copy-start(bf16[1,128,1024]{2,1,0:T(8,128)(2,1)} %param.11) | copy-start | bytes 786436
  208.4 11.5 %collective-permute-start.13 = (f32[128,1024]{1,0:T(8,128)S(1)}, f32[128,1024]{1,0:T(8,128)S(1)}, u32[]{:S(2)}, u32[]{:S(2)}) collective-permute-start(f32[128,1024]{1,0:T(8,128)S(1)} %fusion.265), channel_id=1, source_target_pairs={{0,4},{4,8},{8,12},{12,16},{16,20},{20,24},{24,28},{1,5},{5,9},{9,... | collective-permute-start | bytes 1572872 | tf_op jit(solution)/shard_map/ppermute | solution.py:10
  220.4 11.4 %collective-permute-start.14 = (f32[128,1024]{1,0:T(8,128)S(1)}, f32[128,1024]{1,0:T(8,128)S(1)}, u32[]{:S(2)}, u32[]{:S(2)}) collective-permute-start(f32[128,1024]{1,0:T(8,128)S(1)} %fusion.283), channel_id=1, source_target_pairs={{0,4},{4,8},{8,12},{12,16},{16,20},{20,24},{24,28},{1,5},{5,9},{9,... | collective-permute-start | bytes 1572872 | tf_op jit(solution)/shard_map/ppermute | solution.py:10
Sparse Core Ops, SparseCore 0:
  234.2 37.3 all-gather.1
where the time goes:
time: 284 us; the launch traced here: 281 us
  waiting for transfers between devices  142 us (50%)
  starting transfers between devices  57 us (20%)
  matrix products  52.1 us (18%)
  between operations  14.4 us (5%)
  blocking collectives  9.91 us (3%)
  local copies, waits for them, and re-layouts  3.16 us (1%)
    ppermute x16, waiting for transfers between devices, passed_along(): return lax.ppermute(shard, axis, pairs)  118 us
    ppermute x16, starting transfers between devices, passed_along(): return lax.ppermute(shard, axis, pairs)  57 us
    dot_general x25, matrix products, advance(): jnp.dot(layer_state.astype(jnp.bfloat16), weight, preferred_element_type=...  49.4 us
    all_gather x1, waiting for transfers between devices, body(): all_rows = lax.all_gather(left_rows, 'dp', axis=0, tiled=True)  24.6 us
    all_to_all x1, blocking collectives, body(): lax.all_to_all(deltas, 'dp', split_axis=1, concat_axis=0, tiled=True)  9.91 us
  transfers between devices with their start and end apart: 17, of which 16 were waited for; matrix products, arithmetic and copies ran while one was open for 3% of the time, Pallas kernels for 0%

commit v1 on v0

v1 whole, which is shorter than its diff:
```python
import functools

import jax
import jax.numpy as jnp
from jax import lax
from jax.experimental import pallas as pl
from jax.experimental.pallas import tpu as pltpu
from jax.sharding import PartitionSpec as P

BF16 = jnp.bfloat16
F32 = jnp.float32
TILE = 256
EXTRA = 16
WHOLE = pl.BlockSpec(memory_space=pltpu.VMEM)
BULK = pl.BlockSpec(memory_space=pltpu.HBM)


def call(kernel, outs, *args, scratch=(), flops=0, specs=None):
    moved = sum(a.size * a.dtype.itemsize for a in args)
    return pl.pallas_call(
        kernel,
        out_shape=outs,
        in_specs=specs or [WHOLE] * len(args),
        out_specs=jax.tree.map(lambda _: WHOLE, outs, is_leaf=lambda leaf: not isinstance(leaf, (tuple, list))),
        scratch_shapes=list(scratch),
        compiler_params=pltpu.CompilerParams(vmem_limit_bytes=24 << 20),
        cost_estimate=pl.CostEstimate(flops=flops, bytes_accessed=moved, transcendentals=0),
    )(*args)


def kept(like, dtype=None):
    return pltpu.VMEM(like.shape, dtype or like.dtype)


def plain(shape, dtype):
    return jax.ShapeDtypeStruct(shape, dtype)


def tiles(width):
    step = min(TILE, width)
    return [slice(at, at + step) for at in range(0, width, step)]


def layer_of(rounded_ref, weight_ref, bias, cols):
    product = jnp.dot(rounded_ref[...], weight_ref[:, cols], preferred_element_type=F32)
    return jnp.tanh(product + bias[:, cols])


def load_kernel(source, target, coarse, sems):
    layers = source.shape[0]
    copies = [pltpu.make_async_copy(source.at[i], target.at[i], sems.at[i]) for i in range(layers)]
    copies.append(pltpu.make_async_copy(source.at[0], coarse, sems.at[layers]))
    for copy in copies:
        copy.start()
    for copy in copies:
        copy.wait()


def run_layers(layers, step_size, weights, biases, state, rounded):
    for layer in layers:
        bias = biases[layer : layer + 1, :]
        now, later = rounded[layer % 2], rounded[(layer + 1) % 2]
        for cols in tiles(state.shape[1]):
            new = state[:, cols] + step_size * layer_of(now, weights.at[layer], bias, cols)
            state[:, cols] = new
            later[:, cols] = new.astype(BF16)


def relax_kernel(step_size, rows, weights, biases, inputs, got, relaxed, sent, even, odd):
    first = lax.axis_index("layer") == 0

    @pl.when(first)
    def _():
        relaxed[...] = inputs[...]

    @pl.when(jnp.logical_not(first))
    def _():
        relaxed[...] = got[...].astype(F32)

    even[...] = relaxed[...].astype(BF16)
    run_layers(range(4), step_size, weights, biases, relaxed, (even, odd))
    sent[:rows, :] = even[...]
    bias = biases[0:1, :]
    high = bias.astype(BF16)
    rest = bias - high.astype(F32)
    middle = rest.astype(BF16)
    low = (rest - middle.astype(F32)).astype(BF16)
    at = lax.broadcasted_iota(jnp.int32, (EXTRA, bias.shape[1]), 0)
    parts = jnp.where(at == 0, high.astype(F32), jnp.where(at == 1, middle.astype(F32), low.astype(F32)))
    sent[rows:, :] = jnp.where(at < 3, parts, 0.0).astype(BF16)


def ahead_kernel(step_size, rows, weights, biases, inputs, got, start, forcing, pair_bias, top, sent_forcing, state, even, odd):
    first = lax.axis_index("layer") == 0

    @pl.when(first)
    def _():
        start[...] = inputs[...]

    @pl.when(jnp.logical_not(first))
    def _():
        start[...] = got[:rows, :].astype(F32)

    even[...] = start[...].astype(BF16)
    bias = biases[0:1, :]
    for cols in tiles(state.shape[1]):
        slope = layer_of(even, weights.at[0], bias, cols)
        new = start[:, cols] + step_size * slope
        state[:, cols] = new
        odd[:, cols] = new.astype(BF16)
        forcing[:, cols] = start[:, cols] + (4.0 * step_size) * slope
    run_layers((1, 2, 3), step_size, weights, biases, state, (even, odd))
    top[...] = even[...]
    difference = state[...] - forcing[...]
    forcing[...] = difference
    sent_forcing[...] = difference.astype(BF16)
    tail = got[rows:, :].astype(F32)
    pair_bias[...] = jnp.broadcast_to(tail[0:1, :] + (tail[1:2, :] + tail[2:3, :]), pair_bias.shape)


def coarse_kernel(chosen, factor, weights, biases, forcing, pair_weight, pair_bias, pair_forcing, got, mid, *rest):
    even, odd = rest[-2:]
    here = lax.axis_index("layer")

    @pl.when(chosen(here % 4, here // 4))
    def _():
        even[...] = got[...]
        for cols in tiles(mid.shape[1]):
            slope = layer_of(even, pair_weight, pair_bias[0:1, :], cols)
            new = got[:, cols].astype(F32) + factor * slope + pair_forcing[:, cols].astype(F32)
            mid[:, cols] = new
            odd[:, cols] = new.astype(BF16)
        bias = biases[0:1, :]
        for top in rest[:-2]:
            for cols in tiles(mid.shape[1]):
                slope = layer_of(odd, weights.at[0], bias, cols)
                top[:, cols] = (mid[:, cols] + factor * slope + forcing[:, cols]).astype(BF16)


def final_kernel(step_size, weights, biases, inputs, one, down, low_mid, first_mid, high_mid, forcing, relaxed, left, state, coarse, even, odd):
    here = lax.axis_index("layer")
    slot, group = here % 4, here // 4

    def start_from(condition, source):
        @pl.when(condition)
        def _():
            state[...] = source[...].astype(F32)

    start_from(here == 0, inputs)
    start_from(here == 1, one)
    start_from((here > 0) & (here % 2 == 0), down)
    start_from((slot == 1) & (group > 0), low_mid)
    start_from((slot == 3) & (group == 0), first_mid)
    start_from((slot == 3) & (group > 0), high_mid)
    even[...] = state[...].astype(BF16)
    bias = biases[0:1, :]
    for cols in tiles(state.shape[1]):
        slope = layer_of(even, weights.at[0], bias, cols)
        old = state[:, cols]
        new = old + step_size * slope
        coarse[:, cols] = old + (4.0 * step_size) * slope + forcing[:, cols] - relaxed[:, cols]
        state[:, cols] = new
        odd[:, cols] = new.astype(BF16)
    run_layers((1, 2), step_size, weights, biases, state, (even, odd))
    left[...] = odd[...]


def last_kernel(step_size, weights, biases, left, state, new_states):
    bias = biases[3:4, :]
    for cols in tiles(state.shape[1]):
        new_states[:, cols] = state[:, cols] + step_size * layer_of(left, weights.at[3], bias, cols)


def grad_kernel(step_size, count, has_total, weights, biases, *refs):
    lefts, adjoints = refs[:count], refs[count : 2 * count]
    total, deltas = refs[-2], refs[-1]
    width = total.shape[1]
    cols = pl.ds(pl.multiple_of(lax.axis_index("dp") * width, width), width)
    weight, bias = weights[3, :, cols], biases[3:4, cols]
    result = refs[2 * count][...] if has_total else None
    for rows, adjoint in zip(lefts, adjoints):
        slope = jnp.tanh(jnp.dot(rows[...], weight, preferred_element_type=F32) + bias)
        deltas[...] = (adjoint[...].astype(F32) * step_size * (1.0 - slope * slope)).astype(BF16)
        part = lax.dot_general(rows[...], deltas[...], (((0,), (0,)), ((), ())), preferred_element_type=F32)
        result = part if result is None else result + part
    total[...] = result


def single_kernel(factor, weights, biases, got, added, out):
    for cols in tiles(out.shape[1]):
        slope = layer_of(got, weights.at[0], biases[0:1, :], cols)
        out[:, cols] = got[:, cols].astype(F32) + factor * slope + added[:, cols]


def pick_kernel(chosen, new, old, out):
    here = lax.axis_index("layer")
    out[...] = jnp.where(chosen(here % 4, here // 4), new[...], old[...])


def body(inputs, guesses, weights, biases, adjoint):
    blocks = lax.axis_size("layer")
    parts = lax.axis_size("dp")
    groups = blocks // 4
    step_size = 4.0 / (4 * blocks)
    part = lax.axis_index("dp")
    rows, depth = inputs.shape
    width = depth // parts
    layer_flops = 2 * rows * depth * depth

    def along(state, pairs):
        return lax.ppermute(state, "layer", pairs)

    def shifted(array, by):
        return lax.ppermute(array, "dp", [(i, (i + by) % parts) for i in range(parts)])

    def adjoint_for(index):
        return lax.dynamic_slice_in_dim(adjoint[0], index * width, width, axis=1)

    up = [(i, i + 1) for i in range(blocks - 1)]
    up_pair = [(i, i + 1) for i in range(0, blocks, 2)]
    down_pair = [(i + 1, i) for i in range(0, blocks, 2)]
    rounded = [pltpu.VMEM((rows, depth), BF16)] * 2

    guess_sent, weights = lax.optimization_barrier((guesses[0].astype(BF16), weights))
    guess_prev = along(guess_sent, up)
    held_weights, coarse_weight = call(
        load_kernel,
        (kept(weights), plain(weights.shape[1:], BF16)),
        pltpu.with_memory_space_constraint(weights, pltpu.HBM),
        scratch=[pltpu.SemaphoreType.DMA((weights.shape[0] + 1,))], specs=[BULK],
    )
    relaxed, relaxed_sent = call(
        functools.partial(relax_kernel, step_size, rows),
        (kept(inputs), plain((rows + EXTRA, depth), BF16)),
        held_weights, biases, inputs, guess_prev,
        scratch=rounded, flops=4 * layer_flops,
    )
    pair_weight = along(coarse_weight, up_pair)
    sent_adjoints = [adjoint_for((part + by) % parts) for by in range(parts)]
    relaxed_sent, *sent_adjoints = lax.optimization_barrier((relaxed_sent, *sent_adjoints))
    relaxed_got = along(relaxed_sent, up)
    adjoints = sent_adjoints[:1] + [shifted(sent_adjoints[by], by) for by in range(1, parts)]
    relaxed_got, *adjoints = lax.optimization_barrier((relaxed_got, *adjoints))
    start, forcing, pair_bias, ahead, forcing_sent = call(
        functools.partial(ahead_kernel, step_size, rows),
        (kept(inputs), kept(inputs), pltpu.VMEM((8, depth), F32), plain((rows, depth), BF16), plain((rows, depth), BF16)),
        held_weights, biases, inputs, relaxed_got,
        scratch=[pltpu.VMEM((rows, depth), F32)] + rounded, flops=4 * layer_flops,
    )
    pair_forcing = along(forcing_sent, up_pair)

    def two_steps(top, pairs, chosen, last=False):
        got = along(top, pairs)
        mid, *new_top = call(
            functools.partial(coarse_kernel, chosen, 4.0 * step_size),
            (kept(inputs),) if last else (kept(inputs), plain((rows, depth), BF16)),
            held_weights, biases, forcing, pair_weight, pair_bias, pair_forcing, got,
            scratch=rounded, flops=2 * layer_flops,
        )
        return got, mid, *new_top

    here = lax.axis_index("layer")
    slot, group = here % 4, here // 4
    last_group = groups - 1

    def single(factor, got, added):
        return call(
            functools.partial(single_kernel, factor), plain((rows, depth), F32),
            held_weights, biases, got, added, flops=layer_flops,
        )

    def finish(gots, mids):
        got_1, got_2, got_3 = gots
        mid_1, mid_2, mid_3 = mids
        held = jnp.where(slot == 1, got_2, jnp.where(group == 0, got_1, got_3))
        down = along(held, down_pair)
        return call(
            functools.partial(final_kernel, step_size),
            (plain((rows, depth), BF16), kept(inputs), plain((rows, depth), F32)),
            held_weights, biases, inputs, start, down, mid_2, mid_1, mid_3, forcing, relaxed,
            scratch=rounded, flops=3 * layer_flops,
        )

    top_0 = ahead
    if groups > 2:
        after = single(4.0 * step_size, along(ahead, up_pair), forcing)
        top_0 = jnp.where((slot == 1) & (group > 0), after.astype(BF16), ahead)
    got_1, mid_1, top_1 = two_steps(
        top_0, [(4 * m + 1, 4 * m + 3) for m in range(groups - 1)], lambda slot, group: (slot == 3) & (group < last_group)
    )
    got_2, mid_2, top_2 = two_steps(
        top_1, [(4 * m - 1, 4 * m + 1) for m in range(1, groups)], lambda slot, group: (slot == 1) & (group > 0)
    )
    got_3, mid_3 = two_steps(
        top_2, [(4 * m + 1, 4 * m + 3) for m in range(1, groups)], lambda slot, group: (slot == 3) & (group > 0), True
    )
    left, state, coarse_states = finish((got_1, got_2, got_3), (mid_1, mid_2, mid_3))
    if groups > 2:
        late = lambda slot, group: group > 1
        relaxed_out = call(functools.partial(pick_kernel, late), plain((rows, depth), F32), relaxed, relaxed)
        solved = coarse_states + relaxed_out
        below = along(top_1, [(4 * m - 1, 4 * m + 3) for m in range(2, groups)])
        base = solved - single(16.0 * step_size, below, jnp.zeros((rows, depth), F32))
        for m in range(2, groups):
            new = single(16.0 * step_size, along(solved.astype(BF16), [(4 * m - 1, 4 * m + 3)]), base)
            solved = jnp.where(here == 4 * m + 3, new, solved)
        new_2, new_mid_2, top_2 = two_steps(
            solved.astype(BF16), [(4 * m - 1, 4 * m + 1) for m in range(2, groups)], lambda slot, group: (slot == 1) & (group > 1)
        )
        new_3, new_mid_3 = two_steps(
            top_2, [(4 * m + 1, 4 * m + 3) for m in range(2, groups)], lambda slot, group: (slot == 3) & (group > 1), True
        )
        mids = [
            call(functools.partial(pick_kernel, late), kept(inputs), new, old)
            for new, old in ((new_mid_2, mid_2), (new_mid_3, mid_3))
        ]
        gots = [jnp.where(group > 1, new, old) for new, old in ((new_2, got_2), (new_3, got_3))]
        left, state, coarse_early = finish((got_1, *gots), (mid_1, *mids))
        coarse_states = jnp.where(slot == 3, solved - relaxed_out, coarse_states)
    lefts = [left] + [shifted(left, by) for by in range(1, parts)]
    new_states = call(
        functools.partial(last_kernel, step_size), plain((rows, depth), F32),
        held_weights, biases, left, state, flops=layer_flops,
    )
    half = parts // 2
    deltas = [pltpu.VMEM((rows, width), BF16)]
    total = call(
        functools.partial(grad_kernel, step_size, half, False), pltpu.VMEM((depth, width), F32),
        held_weights, biases, *lefts[:half], *adjoints[:half], scratch=deltas, flops=layer_flops,
    )
    weight_grad = call(
        functools.partial(grad_kernel, step_size, parts - half, True), plain((depth, width), F32),
        held_weights, biases, *lefts[half:], *adjoints[half:], total, scratch=deltas, flops=layer_flops,
    )
    return (new_states[None], coarse_states[None], weight_grad[None])


def solution(mesh):
    return jax.shard_map(
        body,
        mesh=mesh,
        in_specs=(
            P("dp", None),
            P("layer", "dp", None),
            P("layer", None, None),
            P("layer", None),
            P("layer", "dp", None),
        ),
        out_specs=(P("layer", "dp", None), P("layer", "dp", None), P("layer", None, "dp")),
        check_vma=False,
    )
```

time: 284 us -> 99.7 us (0.35)
  waiting for transfers between devices: 142 us -> 39.4 us
  matrix products: 52.1 us -> 0 us
  starting transfers between devices: 57 us -> 24.2 us
  Pallas kernels: 0 us -> 16.6 us
  between operations: 14.4 us -> 0.91 us
  local copies, waits for them, and re-layouts: 3.16 us -> 15.4 us
  blocking collectives: 9.91 us -> 0 us
    ppermute x16 -> x14, waiting for transfers between devices: 118 us -> 39.4 us  [the longest x6 21.9 us: shifted(): lax.ppermute(array, 'dp', [(i, (i + by) % parts) for i in range(parts)])]
    dot_general x26 -> x0, matrix products: 52.1 us -> none  [the longest x25 49.4 us: advance(): jnp.dot(layer_state.astype(jnp.bfloat16), weight, preferred_element_type=...]
    ppermute x16 -> x14, starting transfers between devices: 57 us -> 24.2 us  [the longest x8 16.5 us: along(): return lax.ppermute(state, 'layer', pairs)]
    all_gather x1 -> x0, waiting for transfers between devices: 24.6 us -> none  [body(): all_rows = lax.all_gather(left_rows, 'dp', axis=0, tiled=True)]
    pallas_call x0 -> x10, Pallas kernels: none -> 16.6 us  [call(): pl.pallas_call(kernel, out_shape=outs, in_specs=specs or [WHOLE] * len(ar...]
    unnamed x7 -> x44, local copies, waits for them, and re-layouts: 0.81 us -> 15.4 us
    all_to_all x1 -> x0, blocking collectives: 9.91 us -> none  [body(): lax.all_to_all(deltas, 'dp', split_axis=1, concat_axis=0, tiled=True)]
  transfers between devices with their start and end apart: 17 -> 14, of which waited for: 16 -> 10; matrix products, arithmetic and copies ran while one was open for 3% -> 0% of each run, Pallas kernels for 0% -> 6%
where the time goes in v1:
time: 99.7 us; the launch traced here: 98.7 us
  waiting for transfers between devices  39.4 us (40%)
  starting transfers between devices  24.2 us (24%)
  Pallas kernels  16.6 us (17%)
  local copies, waits for them, and re-layouts  15.4 us (15%)
  other arithmetic  2.21 us (2%)
    ppermute x6, waiting for transfers between devices, shifted(): lax.ppermute(array, 'dp', [(i, (i + by) % parts) for i in range(parts)])  21.9 us
    ppermute x8, waiting for transfers between devices, along(): return lax.ppermute(state, 'layer', pairs)  17.4 us
    pallas_call x10, Pallas kernels, call(): pl.pallas_call(kernel, out_shape=outs, in_specs=specs or [WHOLE] * len(ar...  16.6 us
    ppermute x8, starting transfers between devices, along(): return lax.ppermute(state, 'layer', pairs)  16.5 us
    unnamed x44, local copies, waits for them, and re-layouts  15.4 us
    ppermute x6, starting transfers between devices, shifted(): lax.ppermute(array, 'dp', [(i, (i + by) % parts) for i in range(parts)])  7.7 us
  transfers between devices with their start and end apart: 14, of which 10 were waited for; matrix products, arithmetic and copies ran while one was open for 0% of the time, Pallas kernels for 6%

profile of v1, /device:TPU:13, one launch (start us, length us, event | category | flops | bytes accessed | tf_op | source)
XLA Modules:
  0.0 98.7 jit_solution(2899044021243234847)
XLA Ops:
  0.7 1.1 %convert_bitcast_fusion = bf16[128,1024]{1,0:T(8,128)(2,1)S(1)} fusion(f32[1,128,1024]{2,1,0:T(8,128)} %param.6), kind=kLoop, calls=%fused_computation.1 | loop fusion | flops 131072 | bytes 786432 | tf_op jit(solution)/shard_map/convert_element_type | solution.py:224
  1.8 5.5 %shard_map.76 = (bf16[4,1024,1024]{2,1,0:T(8,128)(2,1)S(1)}, bf16[1024,1024]{1,0:T(8,128)(2,1)}) custom-call(bf16[4,1024,1024]{2,1,0:T(8,128)(2,1)} %source), custom_call_target="tpu_custom_call" | custom-call | bytes 8388608 | tf_op jit(solution)/shard_map/pallas_call | solution.py:20
  7.3 3.3 %copy-done = bf16[4,1024,1024]{2,1,0:T(8,128)(2,1)} copy-done((bf16[4,1024,1024]{2,1,0:T(8,128)(2,1)}, bf16[4,1024,1024]{2,1,0:T(8,128)(2,1)S(1)}, u32[]{:S(2)}) %copy-start) | copy-done | bytes 8388632
  10.6 1.3 %collective-permute-start.5 = (bf16[1024,1024]{1,0:T(8,128)(2,1)}, bf16[1024,1024]{1,0:T(8,128)(2,1)S(1)}, u32[]{:S(2)}, u32[]{:S(2)}) collective-permute-start(bf16[1024,1024]{1,0:T(8,128)(2,1)} %get-tuple-element.43), channel_id=1, source_target_pairs={{0,4},{8,12},{16,20},{24,28},{1,5},{9,13},{17,21},{25,29},{2,6},{1... | collective-permute-start | bytes 6291464 | tf_op jit(solution)/shard_map/ppermute | solution.py:211
  11.9 4.3 %collective-permute-start = (bf16[128,1024]{1,0:T(8,128)(2,1)S(1)}, bf16[128,1024]{1,0:T(8,128)(2,1)S(1)}, u32[]{:S(2)}, u32[]{:S(2)}) collective-permute-start(bf16[128,1024]{1,0:T(8,128)(2,1)S(1)} %convert_bitcast_fusion), channel_id=1, source_target_pairs={{0,4},{4,8},{8,12},{12,16},{16,20},{20,24},{24,28},{1,5},{5,9},{9,... | collective-permute-start | bytes 786440 | tf_op jit(solution)/shard_map/ppermute | solution.py:211
  16.2 3.2 %collective-permute-done.got = bf16[128,1024]{1,0:T(8,128)(2,1)S(1)} collective-permute-done((bf16[128,1024]{1,0:T(8,128)(2,1)S(1)}, bf16[128,1024]{1,0:T(8,128)(2,1)S(1)}, u32[]{:S(2)}, u32[]{:S(2)}) %collective-permute-start) | collective-permute-done | bytes 262176 | tf_op jit(solution)/shard_map/ppermute | solution.py:211
  19.4 3.4 %copy-done.1 = bf16[4,1024,1024]{2,1,0:T(8,128)(2,1)S(1)} copy-done((bf16[4,1024,1024]{2,1,0:T(8,128)(2,1)S(1)}, bf16[4,1024,1024]{2,1,0:T(8,128)(2,1)}, u32[]{:S(2)}) %copy-start.1) | copy-done | bytes 8388632
  22.8 1.5 %shard_map.77 = (f32[128,1024]{1,0:T(8,128)S(1)}, bf16[144,1024]{1,0:T(8,128)(2,1)S(1)}) custom-call(bf16[4,1024,1024]{2,1,0:T(8,128)(2,1)S(1)} %copy-done.1, f32[4,1024]{1,0:T(4,128)S(1)} %copy-done.4, f32[128,1024]{1,0:T(8,128)S(1)} %copy-done.3, bf16[128,1024]{1,0:T(8,128)(2,1)S(1)} %collective-permute-done.got), custom_call_target="tpu_custom_call" | custom-call | flops 1073741824 | bytes 9191424 | tf_op jit(solution)/shard_map/pallas_call | solution.py:20
  24.4 0.8 copy-done.7
  25.2 4.4 %collective-permute-start.1 = (bf16[144,1024]{1,0:T(8,128)(2,1)S(1)}, bf16[144,1024]{1,0:T(8,128)(2,1)S(1)}, u32[]{:S(2)}, u32[]{:S(2)}) collective-permute-start(bf16[144,1024]{1,0:T(8,128)(2,1)S(1)} %get-tuple-element.35), channel_id=1, source_target_pairs={{0,4},{4,8},{8,12},{12,16},{16,20},{20,24},{24,28},{1,5},{5,9},{9,... | collective-permute-start | bytes 884744 | tf_op jit(solution)/shard_map/ppermute | solution.py:211
  29.5 1.3 %collective-permute-start.2 = (bf16[128,256]{1,0:T(8,128)(2,1)S(1)}, bf16[128,256]{1,0:T(8,128)(2,1)S(1)}, u32[]{:S(2)}, u32[]{:S(2)}) collective-permute-start(bf16[128,256]{1,0:T(8,128)(2,1)S(1)} %get-tuple-element.37), channel_id=1, source_target_pairs={{0,1},{1,2},{2,3},{3,0},{4,5},{5,6},{6,7},{7,4},{8,9},{9,10},{10,1... | collective-permute-start | bytes 196616 | tf_op jit(solution)/shard_map/ppermute | solution.py:214
  30.9 1.1 %collective-permute-start.3 = (bf16[128,256]{1,0:T(8,128)(2,1)S(1)}, bf16[128,256]{1,0:T(8,128)(2,1)S(1)}, u32[]{:S(2)}, u32[]{:S(2)}) collective-permute-start(bf16[128,256]{1,0:T(8,128)(2,1)S(1)} %get-tuple-element.38), channel_id=1, source_target_pairs={{0,2},{1,3},{2,0},{3,1},{4,6},{5,7},{6,4},{7,5},{8,10},{9,11},{10,... | collective-permute-start | bytes 196616 | tf_op jit(solution)/shard_map/ppermute | solution.py:214
  32.0 1.4 %collective-permute-start.4 = (bf16[128,256]{1,0:T(8,128)(2,1)S(1)}, bf16[128,256]{1,0:T(8,128)(2,1)S(1)}, u32[]{:S(2)}, u32[]{:S(2)}) collective-permute-start(bf16[128,256]{1,0:T(8,128)(2,1)S(1)} %get-tuple-element.39), channel_id=1, source_target_pairs={{0,3},{1,0},{2,1},{3,2},{4,7},{5,4},{6,5},{7,6},{8,11},{9,8},{10,9... | collective-permute-start | bytes 196616 | tf_op jit(solution)/shard_map/ppermute | solution.py:214
  33.4 0.1 collective-permute-done.2.refs_3_
  33.4 0.6 copy-done.19
  34.1 1.5 %collective-permute-done.3.refs_2_ = bf16[128,256]{1,0:T(8,128)(2,1)S(1)} collective-permute-done((bf16[128,256]{1,0:T(8,128)(2,1)S(1)}, bf16[128,256]{1,0:T(8,128)(2,1)S(1)}, u32[]{:S(2)}, u32[]{:S(2)}) %collective-permute-start.3) | collective-permute-done | bytes 65568 | tf_op jit(solution)/shard_map/ppermute | solution.py:214
  35.6 0.6 copy-done.15
  36.2 2.5 %collective-permute-done.4.refs_3_ = bf16[128,256]{1,0:T(8,128)(2,1)S(1)} collective-permute-done((bf16[128,256]{1,0:T(8,128)(2,1)S(1)}, bf16[128,256]{1,0:T(8,128)(2,1)S(1)}, u32[]{:S(2)}, u32[]{:S(2)}) %collective-permute-start.4) | collective-permute-done | bytes 65568 | tf_op jit(solution)/shard_map/ppermute | solution.py:214
  38.7 0.6 copy-done.17
  39.4 1.5 %shard_map.78 = (f32[128,1024]{1,0:T(8,128)S(1)}, f32[128,1024]{1,0:T(8,128)S(1)}, f32[8,1024]{1,0:T(8,128)S(1)}, bf16[128,1024]{1,0:T(8,128)(2,1)S(1)}, bf16[128,1024]{1,0:T(8,128)(2,1)S(1)}) custom-call(bf16[4,1024,1024]{2,1,0:T(8,128)(2,1)S(1)} %copy-done.1, f32[4,1024]{1,0:T(4,128)S(1)} %copy-done.4, f32[128,1024]{1,0:T(8,128)S(1)} %copy-done.3, ...), custom_call_target="tpu_custom_call" | custom-call | flops 1073741824 | bytes 9224192 | tf_op jit(solution)/shard_map/pallas_call | solution.py:20
  40.9 0.0 copy-start.9
  40.9 0.8 copy-done.9
  41.7 1.3 %collective-permute-start.6 = (bf16[128,1024]{1,0:T(8,128)(2,1)S(1)}, bf16[128,1024]{1,0:T(8,128)(2,1)S(1)}, u32[]{:S(2)}, u32[]{:S(2)}) collective-permute-start(bf16[128,1024]{1,0:T(8,128)(2,1)S(1)} %get-tuple-element.45), channel_id=1, source_target_pairs={{0,4},{8,12},{16,20},{24,28},{1,5},{9,13},{17,21},{25,29},{2,6},{1... | collective-permute-start | bytes 786440 | tf_op jit(solution)/shard_map/ppermute | solution.py:211
  43.0 0.7 collective-permute-start.7
  43.7 1.4 %collective-permute-done.6.pair_forcing = bf16[128,1024]{1,0:T(8,128)(2,1)S(1)} collective-permute-done((bf16[128,1024]{1,0:T(8,128)(2,1)S(1)}, bf16[128,1024]{1,0:T(8,128)(2,1)S(1)}, u32[]{:S(2)}, u32[]{:S(2)}) %collective-permute-start.6) | collective-permute-done | bytes 262176 | tf_op jit(solution)/shard_map/ppermute | solution.py:211
  45.2 0.8 copy-done.11
  46.0 1.3 %collective-permute-start.8 = (bf16[128,1024]{1,0:T(8,128)(2,1)S(1)}, bf16[128,1024]{1,0:T(8,128)(2,1)S(1)}, u32[]{:S(2)}, u32[]{:S(2)}) collective-permute-start(bf16[128,1024]{1,0:T(8,128)(2,1)S(1)} %get-tuple-element.47), channel_id=1, source_target_pairs={{12,20},{13,21},{14,22},{15,23}} | collective-permute-start | bytes 786440 | tf_op jit(solution)/shard_map/ppermute | solution.py:211
  47.3 9.9 %collective-permute-done.8.got = bf16[128,1024]{1,0:T(8,128)(2,1)S(1)} collective-permute-done((bf16[128,1024]{1,0:T(8,128)(2,1)S(1)}, bf16[128,1024]{1,0:T(8,128)(2,1)S(1)}, u32[]{:S(2)}, u32[]{:S(2)}) %collective-permute-start.8) | collective-permute-done | bytes 262176 | tf_op jit(solution)/shard_map/ppermute | solution.py:211
  57.2 1.6 %shard_map.80 = (f32[128,1024]{1,0:T(8,128)S(1)}, bf16[128,1024]{1,0:T(8,128)(2,1)}) custom-call(bf16[4,1024,1024]{2,1,0:T(8,128)(2,1)S(1)} %copy-done.1, f32[4,1024]{1,0:T(4,128)S(1)} %copy-done.4, f32[128,1024]{1,0:T(8,128)S(1)} %get-tuple-element.42.forcing, bf16[1024,1024]{1,0:T(8,128)(2,1)S(1)} %collective-permute-done.5.pair_weight, ...), custom_call_target="tpu_custom_call" | custom-call | flops 536870912 | bytes 11583488 | tf_op jit(solution)/shard_map/pallas_call | solution.py:20
  58.8 0.8 copy-done.13
  59.6 2.0 %collective-permute-start.9 = (bf16[128,1024]{1,0:T(8,128)(2,1)}, bf16[128,1024]{1,0:T(8,128)(2,1)}, u32[]{:S(2)}, u32[]{:S(2)}) collective-permute-start(bf16[128,1024]{1,0:T(8,128)(2,1)} %get-tuple-element.48), channel_id=1, source_target_pairs={{20,28},{21,29},{22,30},{23,31}} | collective-permute-start | bytes 786440 | tf_op jit(solution)/shard_map/ppermute | solution.py:211
  61.6 2.9 %collective-permute-done.9.got = bf16[128,1024]{1,0:T(8,128)(2,1)} collective-permute-done((bf16[128,1024]{1,0:T(8,128)(2,1)}, bf16[128,1024]{1,0:T(8,128)(2,1)}, u32[]{:S(2)}, u32[]{:S(2)}) %collective-permute-start.9) | collective-permute-done | bytes 262176 | tf_op jit(solution)/shard_map/ppermute | solution.py:211
  64.5 1.1 %select_select_fusion = bf16[128,1024]{1,0:T(8,128)(2,1)S(1)} fusion(bf16[128,1024]{1,0:T(8,128)(2,1)} %copy-done.6, bf16[128,1024]{1,0:T(8,128)(2,1)} %copy-done.5, bf16[128,1024]{1,0:T(8,128)(2,1)} %collective-permute-done.9.got, pred[]{:T(512)S(6)} %eq.13, pred[]{:T(512)S(6)} %eq.12), kind=kLoop, calls=%fused_computation | loop fusion | flops 262144 | bytes 1048578 | tf_op jit(solution)/shard_map/jit(_where)/select_n | solution.py:275
  65.6 1.3 %collective-permute-start.10 = (bf16[128,1024]{1,0:T(8,128)(2,1)S(1)}, bf16[128,1024]{1,0:T(8,128)(2,1)S(1)}, u32[]{:S(2)}, u32[]{:S(2)}) collective-permute-start(bf16[128,1024]{1,0:T(8,128)(2,1)S(1)} %select_select_fusion), channel_id=1, source_target_pairs={{4,0},{12,8},{20,16},{28,24},{5,1},{13,9},{21,17},{29,25},{6,2},{1... | collective-permute-start | bytes 786440 | tf_op jit(solution)/shard_map/ppermute | solution.py:211
  66.9 3.4 %copy-done.2 = bf16[4,1024,1024]{2,1,0:T(8,128)(2,1)S(1)} copy-done((bf16[4,1024,1024]{2,1,0:T(8,128)(2,1)S(1)}, bf16[4,1024,1024]{2,1,0:T(8,128)(2,1)}, u32[]{:S(2)}) %copy-start.2) | copy-done | bytes 8388632
  70.3 1.0 %shard_map.81.high_mid = f32[128,1024]{1,0:T(8,128)S(1)} custom-call(bf16[4,1024,1024]{2,1,0:T(8,128)(2,1)S(1)} %copy-done.2, f32[4,1024]{1,0:T(4,128)S(1)} %copy-done.4, f32[128,1024]{1,0:T(8,128)S(1)} %get-tuple-element.42.forcing, bf16[1024,1024]{1,0:T(8,128)(2,1)S(1)} %collective-permute-done.5.pair_weight, f32[8,1024]{1,0:T(8,128)S(1)} %get-tuple-element.44.pair_bias, ...), custom_call_target="tpu_custom_call" | custom-call | flops 536870912 | bytes 11583488 | tf_op jit(solution)/shard_map/pallas_call | solution.py:20
  71.3 0.1 copy-done.12
  71.4 0.2 copy-done.14
  71.5 1.4 %shard_map.82 = (bf16[128,1024]{1,0:T(8,128)(2,1)S(1)}, f32[128,1024]{1,0:T(8,128)S(1)}, f32[128,1024]{1,0:T(8,128)}) custom-call(bf16[4,1024,1024]{2,1,0:T(8,128)(2,1)S(1)} %copy-done.2, f32[4,1024]{1,0:T(4,128)S(1)} %copy-done.4, f32[128,1024]{1,0:T(8,128)S(1)} %copy-done.3, f32[128,1024]{1,0:T(8,128)S(1)} %copy-done.10, ...), custom_call_target="tpu_custom_call" | custom-call | flops 805306368 | bytes 12337152 | tf_op jit(solution)/shard_map/pallas_call | solution.py:20
  72.9 0.5 collective-permute-start.13
  73.4 2.7 %collective-permute-start.11 = (bf16[128,1024]{1,0:T(8,128)(2,1)S(1)}, bf16[128,1024]{1,0:T(8,128)(2,1)S(1)}, u32[]{:S(2)}, u32[]{:S(2)}) collective-permute-start(bf16[128,1024]{1,0:T(8,128)(2,1)S(1)} %get-tuple-element.52.left.refs_0_), channel_id=1, source_target_pairs={{0,2},{1,3},{2,0},{3,1},{4,6},{5,7},{6,4},{7,5},{8,10},{9,11},{10,... | collective-permute-start | bytes 786440 | tf_op jit(solution)/shard_map/ppermute | solution.py:214
  76.1 0.7 collective-permute-start.12
  76.8 1.3 %shard_map.83 = f32[128,1024]{1,0:T(8,128)} custom-call(bf16[4,1024,1024]{2,1,0:T(8,128)(2,1)S(1)} %copy-done.2, f32[4,1024]{1,0:T(4,128)S(1)} %copy-done.4, bf16[128,1024]{1,0:T(8,128)(2,1)S(1)} %get-tuple-element.52.left.refs_0_, f32[128,1024]{1,0:T(8,128)S(1)} %get-tuple-element.53.state), custom_call_target="tpu_custom_call" | custom-call | flops 268435456 | bytes 9191424 | tf_op jit(solution)/shard_map/pallas_call | solution.py:20
  78.1 12.7 %collective-permute-done.13.refs_1_ = bf16[128,1024]{1,0:T(8,128)(2,1)S(1)} collective-permute-done((bf16[128,1024]{1,0:T(8,128)(2,1)S(1)}, bf16[128,1024]{1,0:T(8,128)(2,1)S(1)}, u32[]{:S(2)}, u32[]{:S(2)}) %collective-permute-start.13) | collective-permute-done | bytes 262176 | tf_op jit(solution)/shard_map/ppermute | solution.py:214
  90.7 0.8 shard_map.84.refs_4_
  91.5 2.3 %collective-permute-done.11.refs_0_ = bf16[128,1024]{1,0:T(8,128)(2,1)S(1)} collective-permute-done((bf16[128,1024]{1,0:T(8,128)(2,1)S(1)}, bf16[128,1024]{1,0:T(8,128)(2,1)S(1)}, u32[]{:S(2)}, u32[]{:S(2)}) %collective-permute-start.11) | collective-permute-done | bytes 262176 | tf_op jit(solution)/shard_map/ppermute | solution.py:214
  93.7 2.9 %collective-permute-done.12.refs_1_ = bf16[128,1024]{1,0:T(8,128)(2,1)S(1)} collective-permute-done((bf16[128,1024]{1,0:T(8,128)(2,1)S(1)}, bf16[128,1024]{1,0:T(8,128)(2,1)S(1)}, u32[]{:S(2)}, u32[]{:S(2)}) %collective-permute-start.12) | collective-permute-done | bytes 262176 | tf_op jit(solution)/shard_map/ppermute | solution.py:214
  96.7 2.1 %shard_map.85 = f32[1024,256]{1,0:T(8,128)} custom-call(bf16[4,1024,1024]{2,1,0:T(8,128)(2,1)S(1)} %copy-done.2, f32[4,1024]{1,0:T(4,128)S(1)} %copy-done.4, bf16[128,1024]{1,0:T(8,128)(2,1)S(1)} %collective-permute-done.11.refs_0_, bf16[128,1024]{1,0:T(8,128)(2,1)S(1)} %collective-permute-done.12.refs_1_, bf16[128,256]{1,0:T(8,128)(2,1)S(1)} %copy-done.16, ...), custom_call_target="tpu_custom_call" | custom-call | flops 268435456 | bytes 10108928 | tf_op jit(solution)/shard_map/pallas_call | solution.py:20
  (37 shorter events, 0.1 us)
Async XLA Ops:
  0.6 15.6 %copy-start.21 = (bf16[1,128,1024]{2,1,0:T(8,128)(2,1)S(1)}, bf16[1,128,1024]{2,1,0:T(8,128)(2,1)}, u32[]{:S(2)}) copy-start(bf16[1,128,1024]{2,1,0:T(8,128)(2,1)} %param.9) | copy-start | bytes 786436
  0.6 18.8 %copy-start.3 = (f32[128,1024]{1,0:T(8,128)S(1)}, f32[128,1024]{1,0:T(8,128)}, u32[]{:S(2)}) copy-start(f32[128,1024]{1,0:T(8,128)} %inputs.5) | copy-start | bytes 1572868
  0.7 18.8 %copy-start.4 = (f32[4,1024]{1,0:T(4,128)S(1)}, f32[4,1024]{1,0:T(4,128)}, u32[]{:S(2)}) copy-start(f32[4,1024]{1,0:T(4,128)} %biases.17) | copy-start | bytes 49156
  7.3 3.3 %copy-start = (bf16[4,1024,1024]{2,1,0:T(8,128)(2,1)}, bf16[4,1024,1024]{2,1,0:T(8,128)(2,1)S(1)}, u32[]{:S(2)}) copy-start(bf16[4,1024,1024]{2,1,0:T(8,128)(2,1)S(1)} %get-tuple-element.32.weights) | copy-start | bytes 25165828
  10.6 34.5 %collective-permute-start.5 = (bf16[1024,1024]{1,0:T(8,128)(2,1)}, bf16[1024,1024]{1,0:T(8,128)(2,1)S(1)}, u32[]{:S(2)}, u32[]{:S(2)}) collective-permute-start(bf16[1024,1024]{1,0:T(8,128)(2,1)} %get-tuple-element.43), channel_id=1, source_target_pairs={{0,4},{8,12},{16,20},{24,28},{1,5},{9,13},{17,21},{25,29},{2,6},{1... | collective-permute-start | bytes 6291464 | tf_op jit(solution)/shard_map/ppermute | solution.py:211
  11.9 7.6 %collective-permute-start = (bf16[128,1024]{1,0:T(8,128)(2,1)S(1)}, bf16[128,1024]{1,0:T(8,128)(2,1)S(1)}, u32[]{:S(2)}, u32[]{:S(2)}) collective-permute-start(bf16[128,1024]{1,0:T(8,128)(2,1)S(1)} %convert_bitcast_fusion), channel_id=1, source_target_pairs={{0,4},{4,8},{8,12},{12,16},{16,20},{20,24},{24,28},{1,5},{5,9},{9,... | collective-permute-start | bytes 786440 | tf_op jit(solution)/shard_map/ppermute | solution.py:211
  19.4 3.4 %copy-start.1 = (bf16[4,1024,1024]{2,1,0:T(8,128)(2,1)S(1)}, bf16[4,1024,1024]{2,1,0:T(8,128)(2,1)}, u32[]{:S(2)}) copy-start(bf16[4,1024,1024]{2,1,0:T(8,128)(2,1)} %copy-done) | copy-start | bytes 25165828
  24.4 0.8 copy-start.7
  25.2 14.2 %collective-permute-start.1 = (bf16[144,1024]{1,0:T(8,128)(2,1)S(1)}, bf16[144,1024]{1,0:T(8,128)(2,1)S(1)}, u32[]{:S(2)}, u32[]{:S(2)}) collective-permute-start(bf16[144,1024]{1,0:T(8,128)(2,1)S(1)} %get-tuple-element.35), channel_id=1, source_target_pairs={{0,4},{4,8},{8,12},{12,16},{16,20},{20,24},{24,28},{1,5},{5,9},{9,... | collective-permute-start | bytes 884744 | tf_op jit(solution)/shard_map/ppermute | solution.py:211
  29.5 3.9 %collective-permute-start.2 = (bf16[128,256]{1,0:T(8,128)(2,1)S(1)}, bf16[128,256]{1,0:T(8,128)(2,1)S(1)}, u32[]{:S(2)}, u32[]{:S(2)}) collective-permute-start(bf16[128,256]{1,0:T(8,128)(2,1)S(1)} %get-tuple-element.37), channel_id=1, source_target_pairs={{0,1},{1,2},{2,3},{3,0},{4,5},{5,6},{6,7},{7,4},{8,9},{9,10},{10,1... | collective-permute-start | bytes 196616 | tf_op jit(solution)/shard_map/ppermute | solution.py:214
  30.9 4.7 %collective-permute-start.3 = (bf16[128,256]{1,0:T(8,128)(2,1)S(1)}, bf16[128,256]{1,0:T(8,128)(2,1)S(1)}, u32[]{:S(2)}, u32[]{:S(2)}) collective-permute-start(bf16[128,256]{1,0:T(8,128)(2,1)S(1)} %get-tuple-element.38), channel_id=1, source_target_pairs={{0,2},{1,3},{2,0},{3,1},{4,6},{5,7},{6,4},{7,5},{8,10},{9,11},{10,... | collective-permute-start | bytes 196616 | tf_op jit(solution)/shard_map/ppermute | solution.py:214
  32.0 6.7 %collective-permute-start.4 = (bf16[128,256]{1,0:T(8,128)(2,1)S(1)}, bf16[128,256]{1,0:T(8,128)(2,1)S(1)}, u32[]{:S(2)}, u32[]{:S(2)}) collective-permute-start(bf16[128,256]{1,0:T(8,128)(2,1)S(1)} %get-tuple-element.39), channel_id=1, source_target_pairs={{0,3},{1,0},{2,1},{3,2},{4,7},{5,4},{6,5},{7,6},{8,11},{9,8},{10,9... | collective-permute-start | bytes 196616 | tf_op jit(solution)/shard_map/ppermute | solution.py:214
  33.4 0.6 copy-start.19
  35.6 0.6 copy-start.15
  38.7 0.6 copy-start.17
  40.9 0.8 copy-start.9
  41.7 3.4 %collective-permute-start.6 = (bf16[128,1024]{1,0:T(8,128)(2,1)S(1)}, bf16[128,1024]{1,0:T(8,128)(2,1)S(1)}, u32[]{:S(2)}, u32[]{:S(2)}) collective-permute-start(bf16[128,1024]{1,0:T(8,128)(2,1)S(1)} %get-tuple-element.45), channel_id=1, source_target_pairs={{0,4},{8,12},{16,20},{24,28},{1,5},{9,13},{17,21},{25,29},{2,6},{1... | collective-permute-start | bytes 786440 | tf_op jit(solution)/shard_map/ppermute | solution.py:211
  43.0 2.1 %collective-permute-start.7 = (bf16[128,1024]{1,0:T(8,128)(2,1)S(1)}, bf16[128,1024]{1,0:T(8,128)(2,1)S(1)}, u32[]{:S(2)}, u32[]{:S(2)}) collective-permute-start(bf16[128,1024]{1,0:T(8,128)(2,1)S(1)} %get-tuple-element.46), channel_id=1, source_target_pairs={{4,12},{5,13},{6,14},{7,15}} | collective-permute-start | bytes 786440 | tf_op jit(solution)/shard_map/ppermute | solution.py:211
  45.1 13.7 %copy-start.5 = (bf16[128,1024]{1,0:T(8,128)(2,1)}, bf16[128,1024]{1,0:T(8,128)(2,1)S(1)}, u32[]{:S(2)}) copy-start(bf16[128,1024]{1,0:T(8,128)(2,1)S(1)} %collective-permute-done.7.got) | copy-start | bytes 786436
  45.1 0.8 copy-start.11
  46.0 11.2 %collective-permute-start.8 = (bf16[128,1024]{1,0:T(8,128)(2,1)S(1)}, bf16[128,1024]{1,0:T(8,128)(2,1)S(1)}, u32[]{:S(2)}, u32[]{:S(2)}) collective-permute-start(bf16[128,1024]{1,0:T(8,128)(2,1)S(1)} %get-tuple-element.47), channel_id=1, source_target_pairs={{12,20},{13,21},{14,22},{15,23}} | collective-permute-start | bytes 786440 | tf_op jit(solution)/shard_map/ppermute | solution.py:211
  57.2 2.4 %copy-start.6 = (bf16[128,1024]{1,0:T(8,128)(2,1)}, bf16[128,1024]{1,0:T(8,128)(2,1)S(1)}, u32[]{:S(2)}) copy-start(bf16[128,1024]{1,0:T(8,128)(2,1)S(1)} %collective-permute-done.8.got) | copy-start | bytes 786436
  58.8 0.8 copy-start.13
  59.6 4.9 %collective-permute-start.9 = (bf16[128,1024]{1,0:T(8,128)(2,1)}, bf16[128,1024]{1,0:T(8,128)(2,1)}, u32[]{:S(2)}, u32[]{:S(2)}) collective-permute-start(bf16[128,1024]{1,0:T(8,128)(2,1)} %get-tuple-element.48), channel_id=1, source_target_pairs={{20,28},{21,29},{22,30},{23,31}} | collective-permute-start | bytes 786440 | tf_op jit(solution)/shard_map/ppermute | solution.py:211
  61.6 9.7 %copy-start.8 = (f32[128,1024]{1,0:T(8,128)S(1)}, f32[128,1024]{1,0:T(8,128)}, u32[]{:S(2)}) copy-start(f32[128,1024]{1,0:T(8,128)} %copy-done.7) | copy-start | bytes 1572868
  61.6 9.7 %copy-start.10 = (f32[128,1024]{1,0:T(8,128)S(1)}, f32[128,1024]{1,0:T(8,128)}, u32[]{:S(2)}) copy-start(f32[128,1024]{1,0:T(8,128)} %copy-done.9) | copy-start | bytes 1572868
  65.6 5.7 %collective-permute-start.10 = (bf16[128,1024]{1,0:T(8,128)(2,1)S(1)}, bf16[128,1024]{1,0:T(8,128)(2,1)S(1)}, u32[]{:S(2)}, u32[]{:S(2)}) collective-permute-start(bf16[128,1024]{1,0:T(8,128)(2,1)S(1)} %select_select_fusion), channel_id=1, source_target_pairs={{4,0},{12,8},{20,16},{28,24},{5,1},{13,9},{21,17},{29,25},{6,2},{1... | collective-permute-start | bytes 786440 | tf_op jit(solution)/shard_map/ppermute | solution.py:211
  66.9 3.4 %copy-start.2 = (bf16[4,1024,1024]{2,1,0:T(8,128)(2,1)S(1)}, bf16[4,1024,1024]{2,1,0:T(8,128)(2,1)}, u32[]{:S(2)}) copy-start(bf16[4,1024,1024]{2,1,0:T(8,128)(2,1)} %copy-done) | copy-start | bytes 25165828
  70.3 1.1 %copy-start.12 = (f32[128,1024]{1,0:T(8,128)S(1)}, f32[128,1024]{1,0:T(8,128)}, u32[]{:S(2)}) copy-start(f32[128,1024]{1,0:T(8,128)} %copy-done.11) | copy-start | bytes 1572868
  70.3 1.3 %copy-start.14 = (f32[128,1024]{1,0:T(8,128)S(1)}, f32[128,1024]{1,0:T(8,128)}, u32[]{:S(2)}) copy-start(f32[128,1024]{1,0:T(8,128)} %copy-done.13) | copy-start | bytes 1572868
  71.5 19.2 %copy-start.20 = (bf16[128,256]{1,0:T(8,128)(2,1)S(1)}, bf16[128,256]{1,0:T(8,128)(2,1)}, u32[]{:S(2)}) copy-start(bf16[128,256]{1,0:T(8,128)(2,1)} %copy-done.19) | copy-start | bytes 196612
  72.9 17.8 %collective-permute-start.13 = (bf16[128,1024]{1,0:T(8,128)(2,1)S(1)}, bf16[128,1024]{1,0:T(8,128)(2,1)S(1)}, u32[]{:S(2)}, u32[]{:S(2)}) collective-permute-start(bf16[128,1024]{1,0:T(8,128)(2,1)S(1)} %get-tuple-element.52.left.refs_0_), channel_id=1, source_target_pairs={{0,1},{1,2},{2,3},{3,0},{4,5},{5,6},{6,7},{7,4},{8,9},{9,10},{10,1... | collective-permute-start | bytes 786440 | tf_op jit(solution)/shard_map/ppermute | solution.py:214
  73.4 20.3 %collective-permute-start.11 = (bf16[128,1024]{1,0:T(8,128)(2,1)S(1)}, bf16[128,1024]{1,0:T(8,128)(2,1)S(1)}, u32[]{:S(2)}, u32[]{:S(2)}) collective-permute-start(bf16[128,1024]{1,0:T(8,128)(2,1)S(1)} %get-tuple-element.52.left.refs_0_), channel_id=1, source_target_pairs={{0,2},{1,3},{2,0},{3,1},{4,6},{5,7},{6,4},{7,5},{8,10},{9,11},{10,... | collective-permute-start | bytes 786440 | tf_op jit(solution)/shard_map/ppermute | solution.py:214
  76.1 20.5 %collective-permute-start.12 = (bf16[128,1024]{1,0:T(8,128)(2,1)S(1)}, bf16[128,1024]{1,0:T(8,128)(2,1)S(1)}, u32[]{:S(2)}, u32[]{:S(2)}) collective-permute-start(bf16[128,1024]{1,0:T(8,128)(2,1)S(1)} %get-tuple-element.52.left.refs_0_), channel_id=1, source_target_pairs={{0,3},{1,0},{2,1},{3,2},{4,7},{5,4},{6,5},{7,6},{8,11},{9,8},{10,9... | collective-permute-start | bytes 786440 | tf_op jit(solution)/shard_map/ppermute | solution.py:214
  76.8 19.9 %copy-start.16 = (bf16[128,256]{1,0:T(8,128)(2,1)S(1)}, bf16[128,256]{1,0:T(8,128)(2,1)}, u32[]{:S(2)}) copy-start(bf16[128,256]{1,0:T(8,128)(2,1)} %copy-done.15) | copy-start | bytes 196612
  76.8 19.9 %copy-start.18 = (bf16[128,256]{1,0:T(8,128)(2,1)S(1)}, bf16[128,256]{1,0:T(8,128)(2,1)}, u32[]{:S(2)}) copy-start(bf16[128,256]{1,0:T(8,128)(2,1)} %copy-done.17) | copy-start | bytes 196612

commit v2 on v1

--- a/solution.py
+++ b/solution.py
@@ -23,7 +23,7 @@
         in_specs=specs or [WHOLE] * len(args),
         out_specs=jax.tree.map(lambda _: WHOLE, outs, is_leaf=lambda leaf: not isinstance(leaf, (tuple, list))),
         scratch_shapes=list(scratch),
-        compiler_params=pltpu.CompilerParams(vmem_limit_bytes=24 << 20),
+        compiler_params=pltpu.CompilerParams(vmem_limit_bytes=8 << 20),
         cost_estimate=pl.CostEstimate(flops=flops, bytes_accessed=moved, transcendentals=0),
     )(*args)
 
@@ -46,14 +46,35 @@
     return jnp.tanh(product + bias[:, cols])
 
 
-def load_kernel(source, target, coarse, sems):
-    layers = source.shape[0]
-    copies = [pltpu.make_async_copy(source.at[i], target.at[i], sems.at[i]) for i in range(layers)]
-    copies.append(pltpu.make_async_copy(source.at[0], coarse, sems.at[layers]))
+def prepare_kernel(parts, guess, adjoint, sent_guess, *columns):
+    sent_guess[...] = guess[...].astype(BF16)
+    width = adjoint.shape[1] // parts
+    for by, target in enumerate(columns):
+        index = lax.rem(lax.axis_index("dp") + by, parts)
+        target[...] = adjoint[:, pl.ds(pl.multiple_of(index * width, width), width)]
+
+
+def load_kernel(source, target, sems):
+    layers, depth = source.shape[:2]
+    pieces = sems.shape[0] // layers
+    step = depth // pieces
+    copies = [
+        pltpu.make_async_copy(
+            source.at[i, pl.ds(at * step, step)], target.at[i, pl.ds(at * step, step)], sems.at[i * pieces + at]
+        )
+        for i in range(layers)
+        for at in range(pieces)
+    ]
     for copy in copies:
         copy.start()
     for copy in copies:
         copy.wait()
+
+
+def coarse_weight_kernel(weights, after, coarse_weight, sem):
+    copy = pltpu.make_async_copy(weights.at[0], coarse_weight, sem)
+    copy.start()
+    copy.wait()
 
 
 def run_layers(layers, step_size, weights, biases, state, rounded):
@@ -135,6 +156,12 @@
             for cols in tiles(mid.shape[1]):
                 slope = layer_of(odd, weights.at[0], bias, cols)
                 top[:, cols] = (mid[:, cols] + factor * slope + forcing[:, cols]).astype(BF16)
+
+
+def held_kernel(got_1, got_2, got_3, held):
+    here = lax.axis_index("layer")
+    low, early = here % 4 < 2, here // 4 == 0
+    held[...] = jnp.where(low, got_2[...], jnp.where(early, got_1[...], got_3[...]))
 
 
 def final_kernel(step_size, weights, biases, inputs, one, down, low_mid, first_mid, high_mid, forcing, relaxed, left, state, coarse, even, odd):
@@ -202,7 +229,6 @@
     parts = lax.axis_size("dp")
     groups = blocks // 4
     step_size = 4.0 / (4 * blocks)
-    part = lax.axis_index("dp")
     rows, depth = inputs.shape
     width = depth // parts
     layer_flops = 2 * rows * depth * depth
@@ -212,22 +238,22 @@
 
     def shifted(array, by):
         return lax.ppermute(array, "dp", [(i, (i + by) % parts) for i in range(parts)])
-
-    def adjoint_for(index):
-        return lax.dynamic_slice_in_dim(adjoint[0], index * width, width, axis=1)
 
     up = [(i, i + 1) for i in range(blocks - 1)]
     up_pair = [(i, i + 1) for i in range(0, blocks, 2)]
     down_pair = [(i + 1, i) for i in range(0, blocks, 2)]
     rounded = [pltpu.VMEM((rows, depth), BF16)] * 2
 
-    guess_sent, weights = lax.optimization_barrier((guesses[0].astype(BF16), weights))
+    guess_sent, *sent_adjoints = call(
+        functools.partial(prepare_kernel, parts),
+        (plain((rows, depth), BF16),) + (plain((rows, width), BF16),) * parts,
+        guesses[0], adjoint[0],
+    )
     guess_prev = along(guess_sent, up)
-    held_weights, coarse_weight = call(
-        load_kernel,
-        (kept(weights), plain(weights.shape[1:], BF16)),
-        pltpu.with_memory_space_constraint(weights, pltpu.HBM),
-        scratch=[pltpu.SemaphoreType.DMA((weights.shape[0] + 1,))], specs=[BULK],
+    guess_sent, weights = lax.optimization_barrier((guess_sent, weights))
+    held_weights = call(
+        load_kernel, kept(weights), pltpu.with_memory_space_constraint(weights, pltpu.HBM),
+        scratch=[pltpu.SemaphoreType.DMA((weights.shape[0] * 4,))], specs=[BULK],
     )
     relaxed, relaxed_sent = call(
         functools.partial(relax_kernel, step_size, rows),
@@ -235,12 +261,12 @@
         held_weights, biases, inputs, guess_prev,
         scratch=rounded, flops=4 * layer_flops,
     )
+    relaxed_got = along(relaxed_sent, up)
+    coarse_weight = call(
+        coarse_weight_kernel, plain((depth, depth), BF16), held_weights, relaxed_sent, scratch=[pltpu.SemaphoreType.DMA]
+    )
     pair_weight = along(coarse_weight, up_pair)
-    sent_adjoints = [adjoint_for((part + by) % parts) for by in range(parts)]
-    relaxed_sent, *sent_adjoints = lax.optimization_barrier((relaxed_sent, *sent_adjoints))
-    relaxed_got = along(relaxed_sent, up)
-    adjoints = sent_adjoints[:1] + [shifted(sent_adjoints[by], by) for by in range(1, parts)]
-    relaxed_got, *adjoints = lax.optimization_barrier((relaxed_got, *adjoints))
+    relaxed_got, pair_weight = lax.optimization_barrier((relaxed_got, pair_weight))
     start, forcing, pair_bias, ahead, forcing_sent = call(
         functools.partial(ahead_kernel, step_size, rows),
         (kept(inputs), kept(inputs), pltpu.VMEM((8, depth), F32), plain((rows, depth), BF16), plain((rows, depth), BF16)),
@@ -249,8 +275,8 @@
     )
     pair_forcing = along(forcing_sent, up_pair)
 
-    def two_steps(top, pairs, chosen, last=False):
-        got = along(top, pairs)
+    def two_steps(top, pairs, chosen, last=False, beside=()):
+        got, *_ = lax.optimization_barrier((along(top, pairs), *beside))
         mid, *new_top = call(
             functools.partial(coarse_kernel, chosen, 4.0 * step_size),
             (kept(inputs),) if last else (kept(inputs), plain((rows, depth), BF16)),
@@ -272,7 +298,7 @@
     def finish(gots, mids):
         got_1, got_2, got_3 = gots
         mid_1, mid_2, mid_3 = mids
-        held = jnp.where(slot == 1, got_2, jnp.where(group == 0, got_1, got_3))
+        held = call(held_kernel, plain((rows, depth), BF16), got_1, got_2, got_3)
         down = along(held, down_pair)
         return call(
             functools.partial(final_kernel, step_size),
@@ -288,8 +314,11 @@
     got_1, mid_1, top_1 = two_steps(
         top_0, [(4 * m + 1, 4 * m + 3) for m in range(groups - 1)], lambda slot, group: (slot == 3) & (group < last_group)
     )
+    top_1, *sent_adjoints = lax.optimization_barrier((top_1, *sent_adjoints))
+    adjoints = sent_adjoints[:1] + [shifted(sent_adjoints[by], by) for by in range(1, parts)]
     got_2, mid_2, top_2 = two_steps(
-        top_1, [(4 * m - 1, 4 * m + 1) for m in range(1, groups)], lambda slot, group: (slot == 1) & (group > 0)
+        top_1, [(4 * m - 1, 4 * m + 1) for m in range(1, groups)], lambda slot, group: (slot == 1) & (group > 0),
+        beside=adjoints,
     )
     got_3, mid_3 = two_steps(
         top_2, [(4 * m + 1, 4 * m + 3) for m in range(1, groups)], lambda slot, group: (slot == 3) & (group > 0), True

time: 99.7 us -> 77.1 us (0.77)
  local copies, waits for them, and re-layouts: 15.4 us -> 2 us
  Pallas kernels: 16.6 us -> 13.2 us
  starting transfers between devices: 24.2 us -> 21.9 us
  other arithmetic: 2.21 us -> 0 us
  waiting for transfers between devices: 39.4 us -> 38.2 us
    unnamed x44 -> x8, local copies, waits for them, and re-layouts: 15.4 us -> 2 us
    ppermute x8, waiting for transfers between devices: 17.4 us -> 12.2 us  [along(): return lax.ppermute(state, 'layer', pairs)]
    ppermute x6, waiting for transfers between devices: 21.9 us -> 26 us  [shifted(): lax.ppermute(array, 'dp', [(i, (i + by) % parts) for i in range(parts)])]
    pallas_call x10 -> x13, Pallas kernels: 16.6 us -> 13.2 us  [call(): pl.pallas_call(kernel, out_shape=outs, in_specs=specs or [WHOLE] * len(ar...]
    ppermute x8, starting transfers between devices: 16.5 us -> 15.2 us  [along(): return lax.ppermute(state, 'layer', pairs)]
    convert_element_type x1 -> x0, other arithmetic: 1.14 us -> none  [body(): guesses[0].astype(BF16)]
    select_n x1 -> x0, other arithmetic: 1.07 us -> none  [finish(): held = jnp.where(slot == 1, got_2, jnp.where(group == 0, got_1, got_3))]
    ppermute x6, starting transfers between devices: 7.7 us -> 6.66 us  [shifted(): lax.ppermute(array, 'dp', [(i, (i + by) % parts) for i in range(parts)])]
  transfers between devices with their start and end apart: 14 -> 14, of which waited for: 10 -> 10; matrix products, arithmetic and copies ran while one was open for 0% -> 0% of each run, Pallas kernels for 6% -> 7%
where the time goes in v2:
time: 77.1 us; the launch traced here: 76.1 us
  waiting for transfers between devices  38.2 us (50%)
  starting transfers between devices  21.9 us (28%)
  Pallas kernels  13.2 us (17%)
  local copies, waits for them, and re-layouts  2 us (3%)
  between operations  0.83 us (1%)
    ppermute x6, waiting for transfers between devices, shifted(): lax.ppermute(array, 'dp', [(i, (i + by) % parts) for i in range(parts)])  26 us
    ppermute x8, starting transfers between devices, along(): return lax.ppermute(state, 'layer', pairs)  15.2 us
    pallas_call x13, Pallas kernels, call(): pl.pallas_call(kernel, out_shape=outs, in_specs=specs or [WHOLE] * len(ar...  13.2 us
    ppermute x8, waiting for transfers between devices, along(): return lax.ppermute(state, 'layer', pairs)  12.2 us
    ppermute x6, starting transfers between devices, shifted(): lax.ppermute(array, 'dp', [(i, (i + by) % parts) for i in range(parts)])  6.66 us
    unnamed x8, local copies, waits for them, and re-layouts  2 us
  transfers between devices with their start and end apart: 14, of which 10 were waited for; matrix products, arithmetic and copies ran while one was open for 0% of the time, Pallas kernels for 7%

profile of v2, /device:TPU:13, one launch (start us, length us, event | category | flops | bytes accessed | tf_op | source)
XLA Modules:
  0.0 76.1 jit_solution(11756676674299661584)
XLA Ops:
  0.6 0.0 copy-start.2
  0.6 1.0 %copy-done.2 = f32[1,128,1024]{2,1,0:T(8,128)S(1)} copy-done((f32[1,128,1024]{2,1,0:T(8,128)S(1)}, f32[1,128,1024]{2,1,0:T(8,128)}, u32[]{:S(2)}) %copy-start.2) | copy-done | bytes 524312
  1.7 0.0 copy-start.3
  1.7 0.9 %copy-done.3 = bf16[1,128,1024]{2,1,0:T(8,128)(2,1)S(1)} copy-done((bf16[1,128,1024]{2,1,0:T(8,128)(2,1)S(1)}, bf16[1,128,1024]{2,1,0:T(8,128)(2,1)}, u32[]{:S(2)}) %copy-start.3) | copy-done | bytes 262168
  2.6 0.1 shard_map.76
  2.7 0.0 copy-start
  2.7 0.0 copy-start.1
  2.7 3.8 %collective-permute-start = (bf16[128,1024]{1,0:T(8,128)(2,1)S(1)}, bf16[128,1024]{1,0:T(8,128)(2,1)S(1)}, u32[]{:S(2)}, u32[]{:S(2)}) collective-permute-start(bf16[128,1024]{1,0:T(8,128)(2,1)S(1)} %get-tuple-element.31), channel_id=1, source_target_pairs={{0,4},{4,8},{8,12},{12,16},{16,20},{20,24},{24,28},{1,5},{5,9},{9,... | collective-permute-start | bytes 786440 | tf_op jit(solution)/shard_map/ppermute | solution.py:237
  6.5 3.5 %shard_map.77.weights = bf16[4,1024,1024]{2,1,0:T(8,128)(2,1)S(1)} custom-call(bf16[4,1024,1024]{2,1,0:T(8,128)(2,1)} %source), custom_call_target="tpu_custom_call" | custom-call | bytes 8388608 | tf_op jit(solution)/shard_map/pallas_call | solution.py:20
  10.1 0.0 collective-permute-done.got
  10.1 0.0 copy-done
  10.1 0.0 copy-done.1
  10.1 1.5 %shard_map.78 = (f32[128,1024]{1,0:T(8,128)S(1)}, bf16[144,1024]{1,0:T(8,128)(2,1)S(1)}) custom-call(bf16[4,1024,1024]{2,1,0:T(8,128)(2,1)S(1)} %shard_map.77.weights, f32[4,1024]{1,0:T(4,128)S(1)} %copy-done.1, f32[128,1024]{1,0:T(8,128)S(1)} %copy-done, bf16[128,1024]{1,0:T(8,128)(2,1)S(1)} %collective-permute-done.got), custom_call_target="tpu_custom_call" | custom-call | flops 1073741824 | bytes 9191424 | tf_op jit(solution)/shard_map/pallas_call | solution.py:20
  11.6 0.2 shard_map.79
  11.8 1.3 %collective-permute-start.2 = (bf16[1024,1024]{1,0:T(8,128)(2,1)S(1)}, bf16[1024,1024]{1,0:T(8,128)(2,1)S(1)}, u32[]{:S(2)}, u32[]{:S(2)}) collective-permute-start(bf16[1024,1024]{1,0:T(8,128)(2,1)S(1)} %shard_map.79), channel_id=1, source_target_pairs={{0,4},{8,12},{16,20},{24,28},{1,5},{9,13},{17,21},{25,29},{2,6},{1... | collective-permute-start | bytes 6291464 | tf_op jit(solution)/shard_map/ppermute | solution.py:237
  13.1 4.3 %collective-permute-start.1 = (bf16[144,1024]{1,0:T(8,128)(2,1)S(1)}, bf16[144,1024]{1,0:T(8,128)(2,1)S(1)}, u32[]{:S(2)}, u32[]{:S(2)}) collective-permute-start(bf16[144,1024]{1,0:T(8,128)(2,1)S(1)} %get-tuple-element.33.after), channel_id=1, source_target_pairs={{0,4},{4,8},{8,12},{12,16},{16,20},{20,24},{24,28},{1,5},{5,9},{9,... | collective-permute-start | bytes 884744 | tf_op jit(solution)/shard_map/ppermute | solution.py:237
  17.4 3.6 %collective-permute-done.1.got = bf16[144,1024]{1,0:T(8,128)(2,1)S(1)} collective-permute-done((bf16[144,1024]{1,0:T(8,128)(2,1)S(1)}, bf16[144,1024]{1,0:T(8,128)(2,1)S(1)}, u32[]{:S(2)}, u32[]{:S(2)}) %collective-permute-start.1) | collective-permute-done | bytes 294944 | tf_op jit(solution)/shard_map/ppermute | solution.py:237
  21.0 0.0 collective-permute-done.2.pair_weight
  21.0 1.5 %shard_map.80 = (f32[128,1024]{1,0:T(8,128)S(1)}, f32[128,1024]{1,0:T(8,128)S(1)}, f32[8,1024]{1,0:T(8,128)S(1)}, bf16[128,1024]{1,0:T(8,128)(2,1)S(1)}, bf16[128,1024]{1,0:T(8,128)(2,1)S(1)}) custom-call(bf16[4,1024,1024]{2,1,0:T(8,128)(2,1)S(1)} %shard_map.77.weights, f32[4,1024]{1,0:T(4,128)S(1)} %copy-done.1, f32[128,1024]{1,0:T(8,128)S(1)} %copy-done, ...), custom_call_target="tpu_custom_call" | custom-call | flops 1073741824 | bytes 9224192 | tf_op jit(solution)/shard_map/pallas_call | solution.py:20
  22.5 0.7 collective-permute-start.3
  23.2 1.3 %collective-permute-start.4 = (bf16[128,1024]{1,0:T(8,128)(2,1)S(1)}, bf16[128,1024]{1,0:T(8,128)(2,1)S(1)}, u32[]{:S(2)}, u32[]{:S(2)}) collective-permute-start(bf16[128,1024]{1,0:T(8,128)(2,1)S(1)} %get-tuple-element.40), channel_id=1, source_target_pairs={{0,4},{8,12},{16,20},{24,28},{1,5},{9,13},{17,21},{25,29},{2,6},{1... | collective-permute-start | bytes 786440 | tf_op jit(solution)/shard_map/ppermute | solution.py:237
  24.5 0.0 collective-permute-done.3.got.got_1
  24.5 4.2 %collective-permute-done.4.pair_forcing = bf16[128,1024]{1,0:T(8,128)(2,1)S(1)} collective-permute-done((bf16[128,1024]{1,0:T(8,128)(2,1)S(1)}, bf16[128,1024]{1,0:T(8,128)(2,1)S(1)}, u32[]{:S(2)}, u32[]{:S(2)}) %collective-permute-start.4) | collective-permute-done | bytes 262176 | tf_op jit(solution)/shard_map/ppermute | solution.py:237
  28.7 1.3 %collective-permute-start.5 = (bf16[128,1024]{1,0:T(8,128)(2,1)S(1)}, bf16[128,1024]{1,0:T(8,128)(2,1)S(1)}, u32[]{:S(2)}, u32[]{:S(2)}) collective-permute-start(bf16[128,1024]{1,0:T(8,128)(2,1)S(1)} %get-tuple-element.46), channel_id=1, source_target_pairs={{12,20},{13,21},{14,22},{15,23}} | collective-permute-start | bytes 786440 | tf_op jit(solution)/shard_map/ppermute | solution.py:237
  30.0 1.4 %collective-permute-start.6 = (bf16[128,256]{1,0:T(8,128)(2,1)S(1)}, bf16[128,256]{1,0:T(8,128)(2,1)S(1)}, u32[]{:S(2)}, u32[]{:S(2)}) collective-permute-start(bf16[128,256]{1,0:T(8,128)(2,1)S(1)} %get-tuple-element.48), channel_id=1, source_target_pairs={{0,1},{1,2},{2,3},{3,0},{4,5},{5,6},{6,7},{7,4},{8,9},{9,10},{10,1... | collective-permute-start | bytes 196616 | tf_op jit(solution)/shard_map/ppermute | solution.py:240
  31.4 1.1 %collective-permute-start.7 = (bf16[128,256]{1,0:T(8,128)(2,1)S(1)}, bf16[128,256]{1,0:T(8,128)(2,1)S(1)}, u32[]{:S(2)}, u32[]{:S(2)}) collective-permute-start(bf16[128,256]{1,0:T(8,128)(2,1)S(1)} %get-tuple-element.49), channel_id=1, source_target_pairs={{0,2},{1,3},{2,0},{3,1},{4,6},{5,7},{6,4},{7,5},{8,10},{9,11},{10,... | collective-permute-start | bytes 196616 | tf_op jit(solution)/shard_map/ppermute | solution.py:240
  32.4 1.4 %collective-permute-start.8 = (bf16[128,256]{1,0:T(8,128)(2,1)S(1)}, bf16[128,256]{1,0:T(8,128)(2,1)S(1)}, u32[]{:S(2)}, u32[]{:S(2)}) collective-permute-start(bf16[128,256]{1,0:T(8,128)(2,1)S(1)} %get-tuple-element.50), channel_id=1, source_target_pairs={{0,3},{1,0},{2,1},{3,2},{4,7},{5,4},{6,5},{7,6},{8,11},{9,8},{10,9... | collective-permute-start | bytes 196616 | tf_op jit(solution)/shard_map/ppermute | solution.py:240
  33.8 0.3 collective-permute-done.6.refs_3_
  34.1 3.2 %collective-permute-done.7.refs_2_ = bf16[128,256]{1,0:T(8,128)(2,1)S(1)} collective-permute-done((bf16[128,256]{1,0:T(8,128)(2,1)S(1)}, bf16[128,256]{1,0:T(8,128)(2,1)S(1)}, u32[]{:S(2)}, u32[]{:S(2)}) %collective-permute-start.7) | collective-permute-done | bytes 65568 | tf_op jit(solution)/shard_map/ppermute | solution.py:240
  37.3 1.8 %collective-permute-done.8.refs_3_ = bf16[128,256]{1,0:T(8,128)(2,1)S(1)} collective-permute-done((bf16[128,256]{1,0:T(8,128)(2,1)S(1)}, bf16[128,256]{1,0:T(8,128)(2,1)S(1)}, u32[]{:S(2)}, u32[]{:S(2)}) %collective-permute-start.8) | collective-permute-done | bytes 65568 | tf_op jit(solution)/shard_map/ppermute | solution.py:240
  39.2 0.0 collective-permute-done.5.got.got_2
  39.2 0.9 %shard_map.82 = (f32[128,1024]{1,0:T(8,128)S(1)}, bf16[128,1024]{1,0:T(8,128)(2,1)S(1)}) custom-call(bf16[4,1024,1024]{2,1,0:T(8,128)(2,1)S(1)} %shard_map.77.weights, f32[4,1024]{1,0:T(4,128)S(1)} %copy-done.1, f32[128,1024]{1,0:T(8,128)S(1)} %get-tuple-element.37.forcing, bf16[1024,1024]{1,0:T(8,128)(2,1)S(1)} %collective-permute-done.2.pair_weight, ...), custom_call_target="tpu_custom_call" | custom-call | flops 536870912 | bytes 11583488 | tf_op jit(solution)/shard_map/pallas_call | solution.py:20
  40.1 1.3 %collective-permute-start.9 = (bf16[128,1024]{1,0:T(8,128)(2,1)S(1)}, bf16[128,1024]{1,0:T(8,128)(2,1)S(1)}, u32[]{:S(2)}, u32[]{:S(2)}) collective-permute-start(bf16[128,1024]{1,0:T(8,128)(2,1)S(1)} %get-tuple-element.52), channel_id=1, source_target_pairs={{20,28},{21,29},{22,30},{23,31}} | collective-permute-start | bytes 786440 | tf_op jit(solution)/shard_map/ppermute | solution.py:237
  41.4 3.3 %collective-permute-done.9.got_3.got = bf16[128,1024]{1,0:T(8,128)(2,1)S(1)} collective-permute-done((bf16[128,1024]{1,0:T(8,128)(2,1)S(1)}, bf16[128,1024]{1,0:T(8,128)(2,1)S(1)}, u32[]{:S(2)}, u32[]{:S(2)}) %collective-permute-start.9) | collective-permute-done | bytes 262176 | tf_op jit(solution)/shard_map/ppermute | solution.py:237
  44.7 1.3 %collective-permute-start.10 = (bf16[128,1024]{1,0:T(8,128)(2,1)S(1)}, bf16[128,1024]{1,0:T(8,128)(2,1)S(1)}, u32[]{:S(2)}, u32[]{:S(2)}) collective-permute-start(bf16[128,1024]{1,0:T(8,128)(2,1)S(1)} %shard_map.83), channel_id=1, source_target_pairs={{4,0},{12,8},{20,16},{28,24},{5,1},{13,9},{21,17},{29,25},{6,2},{1... | collective-permute-start | bytes 786440 | tf_op jit(solution)/shard_map/ppermute | solution.py:237
  46.1 1.1 %collective-permute-done.10.down = bf16[128,1024]{1,0:T(8,128)(2,1)S(1)} collective-permute-done((bf16[128,1024]{1,0:T(8,128)(2,1)S(1)}, bf16[128,1024]{1,0:T(8,128)(2,1)S(1)}, u32[]{:S(2)}, u32[]{:S(2)}) %collective-permute-start.10) | collective-permute-done | bytes 262176 | tf_op jit(solution)/shard_map/ppermute | solution.py:237
  47.2 1.4 %shard_map.85 = (bf16[128,1024]{1,0:T(8,128)(2,1)S(1)}, f32[128,1024]{1,0:T(8,128)S(1)}, f32[128,1024]{1,0:T(8,128)}) custom-call(bf16[4,1024,1024]{2,1,0:T(8,128)(2,1)S(1)} %shard_map.77.weights, f32[4,1024]{1,0:T(4,128)S(1)} %copy-done.1, f32[128,1024]{1,0:T(8,128)S(1)} %copy-done, f32[128,1024]{1,0:T(8,128)S(1)} %get-tuple-element.35.one, ...), custom_call_target="tpu_custom_call" | custom-call | flops 805306368 | bytes 12337152 | tf_op jit(solution)/shard_map/pallas_call | solution.py:20
  48.6 0.0 collective-permute-start.13
  48.6 1.9 %collective-permute-start.11 = (bf16[128,1024]{1,0:T(8,128)(2,1)S(1)}, bf16[128,1024]{1,0:T(8,128)(2,1)S(1)}, u32[]{:S(2)}, u32[]{:S(2)}) collective-permute-start(bf16[128,1024]{1,0:T(8,128)(2,1)S(1)} %get-tuple-element.56.left.refs_0_), channel_id=1, source_target_pairs={{0,2},{1,3},{2,0},{3,1},{4,6},{5,7},{6,4},{7,5},{8,10},{9,11},{10,... | collective-permute-start | bytes 786440 | tf_op jit(solution)/shard_map/ppermute | solution.py:240
  50.4 1.0 %collective-permute-start.12 = (bf16[128,1024]{1,0:T(8,128)(2,1)S(1)}, bf16[128,1024]{1,0:T(8,128)(2,1)S(1)}, u32[]{:S(2)}, u32[]{:S(2)}) collective-permute-start(bf16[128,1024]{1,0:T(8,128)(2,1)S(1)} %get-tuple-element.56.left.refs_0_), channel_id=1, source_target_pairs={{0,3},{1,0},{2,1},{3,2},{4,7},{5,4},{6,5},{7,6},{8,11},{9,8},{10,9... | collective-permute-start | bytes 786440 | tf_op jit(solution)/shard_map/ppermute | solution.py:240
  51.4 1.3 %shard_map.86 = f32[128,1024]{1,0:T(8,128)} custom-call(bf16[4,1024,1024]{2,1,0:T(8,128)(2,1)S(1)} %shard_map.77.weights, f32[4,1024]{1,0:T(4,128)S(1)} %copy-done.1, bf16[128,1024]{1,0:T(8,128)(2,1)S(1)} %get-tuple-element.56.left.refs_0_, f32[128,1024]{1,0:T(8,128)S(1)} %get-tuple-element.57.state), custom_call_target="tpu_custom_call" | custom-call | flops 268435456 | bytes 9191424 | tf_op jit(solution)/shard_map/pallas_call | solution.py:20
  52.6 3.4 %collective-permute-done.13.refs_1_ = bf16[128,1024]{1,0:T(8,128)(2,1)S(1)} collective-permute-done((bf16[128,1024]{1,0:T(8,128)(2,1)S(1)}, bf16[128,1024]{1,0:T(8,128)(2,1)S(1)}, u32[]{:S(2)}, u32[]{:S(2)}) %collective-permute-start.13) | collective-permute-done | bytes 262176 | tf_op jit(solution)/shard_map/ppermute | solution.py:240
  56.1 0.8 shard_map.87.refs_4_
  56.8 14.2 %collective-permute-done.11.refs_0_ = bf16[128,1024]{1,0:T(8,128)(2,1)S(1)} collective-permute-done((bf16[128,1024]{1,0:T(8,128)(2,1)S(1)}, bf16[128,1024]{1,0:T(8,128)(2,1)S(1)}, u32[]{:S(2)}, u32[]{:S(2)}) %collective-permute-start.11) | collective-permute-done | bytes 262176 | tf_op jit(solution)/shard_map/ppermute | solution.py:240
  71.0 3.1 %collective-permute-done.12.refs_1_ = bf16[128,1024]{1,0:T(8,128)(2,1)S(1)} collective-permute-done((bf16[128,1024]{1,0:T(8,128)(2,1)S(1)}, bf16[128,1024]{1,0:T(8,128)(2,1)S(1)}, u32[]{:S(2)}, u32[]{:S(2)}) %collective-permute-start.12) | collective-permute-done | bytes 262176 | tf_op jit(solution)/shard_map/ppermute | solution.py:240
  74.1 2.1 %shard_map.88 = f32[1024,256]{1,0:T(8,128)} custom-call(bf16[4,1024,1024]{2,1,0:T(8,128)(2,1)S(1)} %shard_map.77.weights, f32[4,1024]{1,0:T(4,128)S(1)} %copy-done.1, bf16[128,1024]{1,0:T(8,128)(2,1)S(1)} %collective-permute-done.11.refs_0_, bf16[128,1024]{1,0:T(8,128)(2,1)S(1)} %collective-permute-done.12.refs_1_, ...), custom_call_target="tpu_custom_call" | custom-call | flops 268435456 | bytes 10108928 | tf_op jit(solution)/shard_map/pallas_call | solution.py:20
  (3 shorter events, 0.1 us)
Async XLA Ops:
  0.6 1.0 %copy-start.2 = (f32[1,128,1024]{2,1,0:T(8,128)S(1)}, f32[1,128,1024]{2,1,0:T(8,128)}, u32[]{:S(2)}) copy-start(f32[1,128,1024]{2,1,0:T(8,128)} %param.6) | copy-start | bytes 1572868
  1.7 0.9 %copy-start.3 = (bf16[1,128,1024]{2,1,0:T(8,128)(2,1)S(1)}, bf16[1,128,1024]{2,1,0:T(8,128)(2,1)}, u32[]{:S(2)}) copy-start(bf16[1,128,1024]{2,1,0:T(8,128)(2,1)} %param.9) | copy-start | bytes 786436
  2.7 7.4 %copy-start = (f32[128,1024]{1,0:T(8,128)S(1)}, f32[128,1024]{1,0:T(8,128)}, u32[]{:S(2)}) copy-start(f32[128,1024]{1,0:T(8,128)} %inputs.5) | copy-start | bytes 1572868
  2.7 7.4 %copy-start.1 = (f32[4,1024]{1,0:T(4,128)S(1)}, f32[4,1024]{1,0:T(4,128)}, u32[]{:S(2)}) copy-start(f32[4,1024]{1,0:T(4,128)} %biases.17) | copy-start | bytes 49156
  2.7 7.3 %collective-permute-start = (bf16[128,1024]{1,0:T(8,128)(2,1)S(1)}, bf16[128,1024]{1,0:T(8,128)(2,1)S(1)}, u32[]{:S(2)}, u32[]{:S(2)}) collective-permute-start(bf16[128,1024]{1,0:T(8,128)(2,1)S(1)} %get-tuple-element.31), channel_id=1, source_target_pairs={{0,4},{4,8},{8,12},{12,16},{16,20},{20,24},{24,28},{1,5},{5,9},{9,... | collective-permute-start | bytes 786440 | tf_op jit(solution)/shard_map/ppermute | solution.py:237
  11.8 9.2 %collective-permute-start.2 = (bf16[1024,1024]{1,0:T(8,128)(2,1)S(1)}, bf16[1024,1024]{1,0:T(8,128)(2,1)S(1)}, u32[]{:S(2)}, u32[]{:S(2)}) collective-permute-start(bf16[1024,1024]{1,0:T(8,128)(2,1)S(1)} %shard_map.79), channel_id=1, source_target_pairs={{0,4},{8,12},{16,20},{24,28},{1,5},{9,13},{17,21},{25,29},{2,6},{1... | collective-permute-start | bytes 6291464 | tf_op jit(solution)/shard_map/ppermute | solution.py:237
  13.1 7.9 %collective-permute-start.1 = (bf16[144,1024]{1,0:T(8,128)(2,1)S(1)}, bf16[144,1024]{1,0:T(8,128)(2,1)S(1)}, u32[]{:S(2)}, u32[]{:S(2)}) collective-permute-start(bf16[144,1024]{1,0:T(8,128)(2,1)S(1)} %get-tuple-element.33.after), channel_id=1, source_target_pairs={{0,4},{4,8},{8,12},{12,16},{16,20},{20,24},{24,28},{1,5},{5,9},{9,... | collective-permute-start | bytes 884744 | tf_op jit(solution)/shard_map/ppermute | solution.py:237
  22.5 2.0 %collective-permute-start.3 = (bf16[128,1024]{1,0:T(8,128)(2,1)S(1)}, bf16[128,1024]{1,0:T(8,128)(2,1)S(1)}, u32[]{:S(2)}, u32[]{:S(2)}) collective-permute-start(bf16[128,1024]{1,0:T(8,128)(2,1)S(1)} %get-tuple-element.36), channel_id=1, source_target_pairs={{4,12},{5,13},{6,14},{7,15}} | collective-permute-start | bytes 786440 | tf_op jit(solution)/shard_map/ppermute | solution.py:237
  23.2 5.5 %collective-permute-start.4 = (bf16[128,1024]{1,0:T(8,128)(2,1)S(1)}, bf16[128,1024]{1,0:T(8,128)(2,1)S(1)}, u32[]{:S(2)}, u32[]{:S(2)}) collective-permute-start(bf16[128,1024]{1,0:T(8,128)(2,1)S(1)} %get-tuple-element.40), channel_id=1, source_target_pairs={{0,4},{8,12},{16,20},{24,28},{1,5},{9,13},{17,21},{25,29},{2,6},{1... | collective-permute-start | bytes 786440 | tf_op jit(solution)/shard_map/ppermute | solution.py:237
  28.7 10.5 %collective-permute-start.5 = (bf16[128,1024]{1,0:T(8,128)(2,1)S(1)}, bf16[128,1024]{1,0:T(8,128)(2,1)S(1)}, u32[]{:S(2)}, u32[]{:S(2)}) collective-permute-start(bf16[128,1024]{1,0:T(8,128)(2,1)S(1)} %get-tuple-element.46), channel_id=1, source_target_pairs={{12,20},{13,21},{14,22},{15,23}} | collective-permute-start | bytes 786440 | tf_op jit(solution)/shard_map/ppermute | solution.py:237
  30.0 4.1 %collective-permute-start.6 = (bf16[128,256]{1,0:T(8,128)(2,1)S(1)}, bf16[128,256]{1,0:T(8,128)(2,1)S(1)}, u32[]{:S(2)}, u32[]{:S(2)}) collective-permute-start(bf16[128,256]{1,0:T(8,128)(2,1)S(1)} %get-tuple-element.48), channel_id=1, source_target_pairs={{0,1},{1,2},{2,3},{3,0},{4,5},{5,6},{6,7},{7,4},{8,9},{9,10},{10,1... | collective-permute-start | bytes 196616 | tf_op jit(solution)/shard_map/ppermute | solution.py:240
  31.4 6.0 %collective-permute-start.7 = (bf16[128,256]{1,0:T(8,128)(2,1)S(1)}, bf16[128,256]{1,0:T(8,128)(2,1)S(1)}, u32[]{:S(2)}, u32[]{:S(2)}) collective-permute-start(bf16[128,256]{1,0:T(8,128)(2,1)S(1)} %get-tuple-element.49), channel_id=1, source_target_pairs={{0,2},{1,3},{2,0},{3,1},{4,6},{5,7},{6,4},{7,5},{8,10},{9,11},{10,... | collective-permute-start | bytes 196616 | tf_op jit(solution)/shard_map/ppermute | solution.py:240
  32.4 6.7 %collective-permute-start.8 = (bf16[128,256]{1,0:T(8,128)(2,1)S(1)}, bf16[128,256]{1,0:T(8,128)(2,1)S(1)}, u32[]{:S(2)}, u32[]{:S(2)}) collective-permute-start(bf16[128,256]{1,0:T(8,128)(2,1)S(1)} %get-tuple-element.50), channel_id=1, source_target_pairs={{0,3},{1,0},{2,1},{3,2},{4,7},{5,4},{6,5},{7,6},{8,11},{9,8},{10,9... | collective-permute-start | bytes 196616 | tf_op jit(solution)/shard_map/ppermute | solution.py:240
  40.1 4.6 %collective-permute-start.9 = (bf16[128,1024]{1,0:T(8,128)(2,1)S(1)}, bf16[128,1024]{1,0:T(8,128)(2,1)S(1)}, u32[]{:S(2)}, u32[]{:S(2)}) collective-permute-start(bf16[128,1024]{1,0:T(8,128)(2,1)S(1)} %get-tuple-element.52), channel_id=1, source_target_pairs={{20,28},{21,29},{22,30},{23,31}} | collective-permute-start | bytes 786440 | tf_op jit(solution)/shard_map/ppermute | solution.py:237
  44.7 2.4 %collective-permute-start.10 = (bf16[128,1024]{1,0:T(8,128)(2,1)S(1)}, bf16[128,1024]{1,0:T(8,128)(2,1)S(1)}, u32[]{:S(2)}, u32[]{:S(2)}) collective-permute-start(bf16[128,1024]{1,0:T(8,128)(2,1)S(1)} %shard_map.83), channel_id=1, source_target_pairs={{4,0},{12,8},{20,16},{28,24},{5,1},{13,9},{21,17},{29,25},{6,2},{1... | collective-permute-start | bytes 786440 | tf_op jit(solution)/shard_map/ppermute | solution.py:237
  48.6 7.5 %collective-permute-start.13 = (bf16[128,1024]{1,0:T(8,128)(2,1)S(1)}, bf16[128,1024]{1,0:T(8,128)(2,1)S(1)}, u32[]{:S(2)}, u32[]{:S(2)}) collective-permute-start(bf16[128,1024]{1,0:T(8,128)(2,1)S(1)} %get-tuple-element.56.left.refs_0_), channel_id=1, source_target_pairs={{0,1},{1,2},{2,3},{3,0},{4,5},{5,6},{6,7},{7,4},{8,9},{9,10},{10,1... | collective-permute-start | bytes 786440 | tf_op jit(solution)/shard_map/ppermute | solution.py:240
  48.6 22.4 %collective-permute-start.11 = (bf16[128,1024]{1,0:T(8,128)(2,1)S(1)}, bf16[128,1024]{1,0:T(8,128)(2,1)S(1)}, u32[]{:S(2)}, u32[]{:S(2)}) collective-permute-start(bf16[128,1024]{1,0:T(8,128)(2,1)S(1)} %get-tuple-element.56.left.refs_0_), channel_id=1, source_target_pairs={{0,2},{1,3},{2,0},{3,1},{4,6},{5,7},{6,4},{7,5},{8,10},{9,11},{10,... | collective-permute-start | bytes 786440 | tf_op jit(solution)/shard_map/ppermute | solution.py:240
  50.4 23.7 %collective-permute-start.12 = (bf16[128,1024]{1,0:T(8,128)(2,1)S(1)}, bf16[128,1024]{1,0:T(8,128)(2,1)S(1)}, u32[]{:S(2)}, u32[]{:S(2)}) collective-permute-start(bf16[128,1024]{1,0:T(8,128)(2,1)S(1)} %get-tuple-element.56.left.refs_0_), channel_id=1, source_target_pairs={{0,3},{1,0},{2,1},{3,2},{4,7},{5,4},{6,5},{7,6},{8,11},{9,8},{10,9... | collective-permute-start | bytes 786440 | tf_op jit(solution)/shard_map/ppermute | solution.py:240

commit v3 on v2

--- a/solution.py
+++ b/solution.py
@@ -46,17 +46,20 @@
     return jnp.tanh(product + bias[:, cols])
 
 
-def prepare_kernel(parts, guess, adjoint, sent_guess, *columns):
+def round_kernel(guess, sent_guess):
     sent_guess[...] = guess[...].astype(BF16)
+
+
+def columns_kernel(parts, adjoint, *columns):
     width = adjoint.shape[1] // parts
     for by, target in enumerate(columns):
         index = lax.rem(lax.axis_index("dp") + by, parts)
         target[...] = adjoint[:, pl.ds(pl.multiple_of(index * width, width), width)]
 
 
-def load_kernel(source, target, sems):
+def load_kernel(source, target, coarse_weight, sems):
     layers, depth = source.shape[:2]
-    pieces = sems.shape[0] // layers
+    pieces = (sems.shape[0] - 1) // layers
     step = depth // pieces
     copies = [
         pltpu.make_async_copy(
@@ -67,14 +70,13 @@
     ]
     for copy in copies:
         copy.start()
-    for copy in copies:
+    for copy in copies[:pieces]:
         copy.wait()
-
-
-def coarse_weight_kernel(weights, after, coarse_weight, sem):
-    copy = pltpu.make_async_copy(weights.at[0], coarse_weight, sem)
-    copy.start()
-    copy.wait()
+    again = pltpu.make_async_copy(target.at[0], coarse_weight, sems.at[layers * pieces])
+    again.start()
+    for copy in copies[pieces:]:
+        copy.wait()
+    again.wait()
 
 
 def run_layers(layers, step_size, weights, biases, state, rounded):
@@ -131,7 +133,7 @@
         odd[:, cols] = new.astype(BF16)
         forcing[:, cols] = start[:, cols] + (4.0 * step_size) * slope
     run_layers((1, 2, 3), step_size, weights, biases, state, (even, odd))
-    top[...] = even[...]
+    top[...] = jnp.where(first, inputs[...].astype(BF16), even[...])
     difference = state[...] - forcing[...]
     forcing[...] = difference
     sent_forcing[...] = difference.astype(BF16)
@@ -139,11 +141,18 @@
     pair_bias[...] = jnp.broadcast_to(tail[0:1, :] + (tail[1:2, :] + tail[2:3, :]), pair_bias.shape)
 
 
-def coarse_kernel(chosen, factor, weights, biases, forcing, pair_weight, pair_bias, pair_forcing, got, mid, *rest):
+def coarse_kernel(chosen, factor, weights, biases, forcing, pair_weight, pair_bias, pair_forcing, got, before, mid, *rest):
     even, odd = rest[-2:]
     here = lax.axis_index("layer")
 
-    @pl.when(chosen(here % 4, here // 4))
+    taken = chosen(here % 4, here // 4)
+
+    @pl.when(jnp.logical_not(taken))
+    def _():
+        for top in rest[:-2]:
+            top[...] = before[...]
+
+    @pl.when(taken)
     def _():
         even[...] = got[...]
         for cols in tiles(mid.shape[1]):
@@ -198,19 +207,44 @@
         new_states[:, cols] = state[:, cols] + step_size * layer_of(left, weights.at[3], bias, cols)
 
 
-def grad_kernel(step_size, count, has_total, weights, biases, *refs):
-    lefts, adjoints = refs[:count], refs[count : 2 * count]
-    total, deltas = refs[-2], refs[-1]
-    width = total.shape[1]
+def gradient(step_size, weights, biases, left, adjoint, deltas, width):
     cols = pl.ds(pl.multiple_of(lax.axis_index("dp") * width, width), width)
-    weight, bias = weights[3, :, cols], biases[3:4, cols]
-    result = refs[2 * count][...] if has_total else None
-    for rows, adjoint in zip(lefts, adjoints):
-        slope = jnp.tanh(jnp.dot(rows[...], weight, preferred_element_type=F32) + bias)
-        deltas[...] = (adjoint[...].astype(F32) * step_size * (1.0 - slope * slope)).astype(BF16)
-        part = lax.dot_general(rows[...], deltas[...], (((0,), (0,)), ((), ())), preferred_element_type=F32)
-        result = part if result is None else result + part
-    total[...] = result
+    slope = jnp.tanh(jnp.dot(left[...], weights[3, :, cols], preferred_element_type=F32) + biases[3:4, cols])
+    deltas[...] = (adjoint[...].astype(F32) * step_size * (1.0 - slope * slope)).astype(BF16)
+    return lax.dot_general(left[...], deltas[...], (((0,), (0,)), ((), ())), preferred_element_type=F32)
+
+
+def own_gradient_kernel(step_size, weights, biases, left, adjoint, total, deltas):
+    total[...] = gradient(step_size, weights, biases, left, adjoint, deltas, total.shape[1])
+
+
+def far_kernel(step_size, rows, count, weights, biases, pair_weight, pair_bias, total, *refs):
+    far, down, forcings, adjoints = (refs[i * count : (i + 1) * count] for i in range(4))
+    result, state, even, odd, adjoint, deltas = refs[4 * count :]
+    is_odd = lax.axis_index("layer") % 2 == 1
+    places = [slice(i * rows, (i + 1) * rows) for i in range(count)]
+
+    @pl.when(is_odd)
+    def _():
+        for place, source in zip(places, far):
+            odd[place, :] = source[...]
+        for cols in tiles(state.shape[1]):
+            slope = layer_of(odd, pair_weight, pair_bias[0:1, :], cols)
+            for place, added in zip(places, forcings):
+                new = odd[place, cols].astype(F32) + (4.0 * step_size) * slope[place, :] + added[:, cols].astype(F32)
+                state[place, cols] = new
+                even[place, cols] = new.astype(BF16)
+
+    @pl.when(jnp.logical_not(is_odd))
+    def _():
+        for place, source in zip(places, down):
+            state[place, :] = source[...].astype(F32)
+            even[place, :] = source[...]
+
+    for place, source in zip(places, adjoints):
+        adjoint[place, :] = source[...]
+    run_layers((0, 1, 2), step_size, weights, biases, state, (even, odd))
+    result[...] = total[...] + gradient(step_size, weights, biases, odd, adjoint, deltas, result.shape[1])
 
 
 def single_kernel(factor, weights, biases, got, added, out):
@@ -236,6 +270,10 @@
     def along(state, pairs):
         return lax.ppermute(state, "layer", pairs)
 
+    def across(state, pairs, by):
+        flat = [(i * parts + z, j * parts + (z + by) % parts) for i, j in pairs for z in range(parts)]
+        return lax.ppermute(state, ("layer", "dp"), flat)
+
     def shifted(array, by):
         return lax.ppermute(array, "dp", [(i, (i + by) % parts) for i in range(parts)])
 
@@ -244,16 +282,17 @@
     down_pair = [(i + 1, i) for i in range(0, blocks, 2)]
     rounded = [pltpu.VMEM((rows, depth), BF16)] * 2
 
-    guess_sent, *sent_adjoints = call(
-        functools.partial(prepare_kernel, parts),
-        (plain((rows, depth), BF16),) + (plain((rows, width), BF16),) * parts,
-        guesses[0], adjoint[0],
-    )
+    guess_sent = call(round_kernel, plain((rows, depth), BF16), guesses[0])
     guess_prev = along(guess_sent, up)
     guess_sent, weights = lax.optimization_barrier((guess_sent, weights))
-    held_weights = call(
-        load_kernel, kept(weights), pltpu.with_memory_space_constraint(weights, pltpu.HBM),
-        scratch=[pltpu.SemaphoreType.DMA((weights.shape[0] * 4,))], specs=[BULK],
+    held_weights, coarse_weight = call(
+        load_kernel, (kept(weights), plain((depth, depth), BF16)), pltpu.with_memory_space_constraint(weights, pltpu.HBM),
+        scratch=[pltpu.SemaphoreType.DMA((weights.shape[0] * 4 + 1,))], specs=[BULK],
+    )
+    guess_prev, coarse_weight = lax.optimization_barrier((guess_prev, coarse_weight))
+    pair_weight = along(coarse_weight, up_pair)
+    sent_adjoints = call(
+        functools.partial(columns_kernel, parts), (plain((rows, width), BF16),) * parts, adjoint[0]
     )
     relaxed, relaxed_sent = call(
         functools.partial(relax_kernel, step_size, rows),
@@ -262,11 +301,6 @@
         scratch=rounded, flops=4 * layer_flops,
     )
     relaxed_got = along(relaxed_sent, up)
-    coarse_weight = call(
-        coarse_weight_kernel, plain((depth, depth), BF16), held_weights, relaxed_sent, scratch=[pltpu.SemaphoreType.DMA]
-    )
-    pair_weight = along(coarse_weight, up_pair)
-    relaxed_got, pair_weight = lax.optimization_barrier((relaxed_got, pair_weight))
     start, forcing, pair_bias, ahead, forcing_sent = call(
         functools.partial(ahead_kernel, step_size, rows),
         (kept(inputs), kept(inputs), pltpu.VMEM((8, depth), F32), plain((rows, depth), BF16), plain((rows, depth), BF16)),
@@ -274,13 +308,14 @@
         scratch=[pltpu.VMEM((rows, depth), F32)] + rounded, flops=4 * layer_flops,
     )
     pair_forcing = along(forcing_sent, up_pair)
+    far_forcings = [across(forcing_sent, up_pair, by) for by in range(1, parts)]
 
     def two_steps(top, pairs, chosen, last=False, beside=()):
         got, *_ = lax.optimization_barrier((along(top, pairs), *beside))
         mid, *new_top = call(
             functools.partial(coarse_kernel, chosen, 4.0 * step_size),
             (kept(inputs),) if last else (kept(inputs), plain((rows, depth), BF16)),
-            held_weights, biases, forcing, pair_weight, pair_bias, pair_forcing, got,
+            held_weights, biases, forcing, pair_weight, pair_bias, pair_forcing, got, top,
             scratch=rounded, flops=2 * layer_flops,
         )
         return got, mid, *new_top
@@ -320,6 +355,7 @@
         top_1, [(4 * m - 1, 4 * m + 1) for m in range(1, groups)], lambda slot, group: (slot == 1) & (group > 0),
         beside=adjoints,
     )
+    top_2, *far_forcings = lax.optimization_barrier((top_2, *far_forcings))
     got_3, mid_3 = two_steps(
         top_2, [(4 * m + 1, 4 * m + 3) for m in range(1, groups)], lambda slot, group: (slot == 3) & (group > 0), True
     )
@@ -334,7 +370,7 @@
             new = single(16.0 * step_size, along(solved.astype(BF16), [(4 * m - 1, 4 * m + 3)]), base)
             solved = jnp.where(here == 4 * m + 3, new, solved)
         new_2, new_mid_2, top_2 = two_steps(
-            solved.astype(BF16), [(4 * m - 1, 4 * m + 1) for m in range(2, groups)], lambda slot, group: (slot == 1) & (group > 1)
+            jnp.where(slot == 3, solved.astype(BF16), top_2), [(4 * m - 1, 4 * m + 1) for m in range(2, groups)], lambda slot, group: (slot == 1) & (group > 1)
         )
         new_3, new_mid_3 = two_steps(
             top_2, [(4 * m + 1, 4 * m + 3) for m in range(2, groups)], lambda slot, group: (slot == 3) & (group > 1), True
@@ -346,20 +382,25 @@
         gots = [jnp.where(group > 1, new, old) for new, old in ((new_2, got_2), (new_3, got_3))]
         left, state, coarse_early = finish((got_1, *gots), (mid_1, *mids))
         coarse_states = jnp.where(slot == 3, solved - relaxed_out, coarse_states)
-    lefts = [left] + [shifted(left, by) for by in range(1, parts)]
+    leaps = [(0, 1)] + [(i, i + 2) for i in range(1, blocks - 2, 2)]
+    far = [across(top_2, leaps, by) for by in range(1, parts)]
+    left, *far = lax.optimization_barrier((left, *far))
+    far_down = [along(state_far, down_pair) for state_far in far]
     new_states = call(
         functools.partial(last_kernel, step_size), plain((rows, depth), F32),
         held_weights, biases, left, state, flops=layer_flops,
     )
-    half = parts // 2
-    deltas = [pltpu.VMEM((rows, width), BF16)]
     total = call(
-        functools.partial(grad_kernel, step_size, half, False), pltpu.VMEM((depth, width), F32),
-        held_weights, biases, *lefts[:half], *adjoints[:half], scratch=deltas, flops=layer_flops,
-    )
+        functools.partial(own_gradient_kernel, step_size), pltpu.VMEM((depth, width), F32),
+        held_weights, biases, left, adjoints[0], scratch=[pltpu.VMEM((rows, width), BF16)], flops=layer_flops,
+    )
+    others = (parts - 1) * rows
     weight_grad = call(
-        functools.partial(grad_kernel, step_size, parts - half, True), plain((depth, width), F32),
-        held_weights, biases, *lefts[half:], *adjoints[half:], total, scratch=deltas, flops=layer_flops,
+        functools.partial(far_kernel, step_size, rows, parts - 1), plain((depth, width), F32),
+        held_weights, biases, pair_weight, pair_bias, total, *far, *far_down, *far_forcings, *adjoints[1:],
+        scratch=[pltpu.VMEM((others, depth), F32)] + [pltpu.VMEM((others, depth), BF16)] * 2
+        + [pltpu.VMEM((others, width), BF16)] * 2,
+        flops=6 * (parts - 1) * layer_flops,
     )
     return (new_states[None], coarse_states[None], weight_grad[None])
 

time: 77.1 us -> 103 us (1.34)
  the two profiles are of different devices: /device:TPU:13 before, /device:TPU:9 now
where the time goes in v3:
time: 103 us
  starting transfers between devices  49.2 us (48%)
  waiting for transfers between devices  35.3 us (34%)
  Pallas kernels  16.2 us (16%)
  local copies, waits for them, and re-layouts  1.1 us (1%)
    ppermute x11, starting transfers between devices, along(): return lax.ppermute(state, 'layer', pairs)  30.9 us
    ppermute x6, waiting for transfers between devices, across(): return lax.ppermute(state, ('layer', 'dp'), flat)  17 us
    pallas_call x13, Pallas kernels, call(): pl.pallas_call(kernel, out_shape=outs, in_specs=specs or [WHOLE] * len(ar...  16.2 us
    ppermute x6, starting transfers between devices, across(): return lax.ppermute(state, ('layer', 'dp'), flat)  14.3 us
    ppermute x3, waiting for transfers between devices, shifted(): lax.ppermute(array, 'dp', [(i, (i + by) % parts) for i in range(parts)])  12.5 us
    ppermute x11, waiting for transfers between devices, along(): return lax.ppermute(state, 'layer', pairs)  5.73 us
    ppermute x3, starting transfers between devices, shifted(): lax.ppermute(array, 'dp', [(i, (i + by) % parts) for i in range(parts)])  3.99 us
  transfers between devices with their start and end apart: 20, of which 9 were waited for; matrix products, arithmetic and copies ran while one was open for 0% of the time, Pallas kernels for 10%

profile of v3, /device:TPU:9, one launch (start us, length us, event | category | flops | bytes accessed | tf_op | source)
XLA Modules:
  0.0 102.7 jit_solution(2157745559352232896)
XLA Ops:
  0.7 1.1 %copy-done.2 = f32[1,128,1024]{2,1,0:T(8,128)S(1)} copy-done((f32[1,128,1024]{2,1,0:T(8,128)S(1)}, f32[1,128,1024]{2,1,0:T(8,128)}, u32[]{:S(2)}) %copy-start.2) | copy-done | bytes 524312
  1.8 3.7 %collective-permute-start = (bf16[128,1024]{1,0:T(8,128)(2,1)S(1)}, bf16[128,1024]{1,0:T(8,128)(2,1)S(1)}, u32[]{:S(2)}, u32[]{:S(2)}) collective-permute-start(bf16[128,1024]{1,0:T(8,128)(2,1)S(1)} %shard_map.76), channel_id=1, source_target_pairs={{0,4},{4,8},{8,12},{12,16},{16,20},{20,24},{24,28},{1,5},{5,9},{9,... | collective-permute-start | bytes 786440 | tf_op jit(solution)/shard_map/ppermute | solution.py:271
  5.5 3.5 %shard_map.77 = (bf16[4,1024,1024]{2,1,0:T(8,128)(2,1)S(1)}, bf16[1024,1024]{1,0:T(8,128)(2,1)S(1)}) custom-call(bf16[4,1024,1024]{2,1,0:T(8,128)(2,1)} %source), custom_call_target="tpu_custom_call" | custom-call | bytes 8388608 | tf_op jit(solution)/shard_map/pallas_call | solution.py:20
  9.0 0.0 collective-permute-done.got
  9.0 1.3 %collective-permute-start.3 = (bf16[1024,1024]{1,0:T(8,128)(2,1)S(1)}, bf16[1024,1024]{1,0:T(8,128)(2,1)S(1)}, u32[]{:S(2)}, u32[]{:S(2)}) collective-permute-start(bf16[1024,1024]{1,0:T(8,128)(2,1)S(1)} %get-tuple-element.48), channel_id=1, source_target_pairs={{0,4},{8,12},{16,20},{24,28},{1,5},{9,13},{17,21},{25,29},{2,6},{1... | collective-permute-start | bytes 6291464 | tf_op jit(solution)/shard_map/ppermute | solution.py:271
  10.3 0.0 copy-start.3
  10.3 1.5 %shard_map.78 = (f32[128,1024]{1,0:T(8,128)S(1)}, bf16[144,1024]{1,0:T(8,128)(2,1)S(1)}) custom-call(bf16[4,1024,1024]{2,1,0:T(8,128)(2,1)S(1)} %get-tuple-element.41.weights, f32[4,1024]{1,0:T(4,128)S(1)} %copy-done.1, f32[128,1024]{1,0:T(8,128)S(1)} %copy-done, bf16[128,1024]{1,0:T(8,128)(2,1)S(1)} %collective-permute-done.got), custom_call_target="tpu_custom_call" | custom-call | flops 1073741824 | bytes 9191424 | tf_op jit(solution)/shard_map/pallas_call | solution.py:20
  11.9 4.3 %collective-permute-start.1 = (bf16[144,1024]{1,0:T(8,128)(2,1)S(1)}, bf16[144,1024]{1,0:T(8,128)(2,1)S(1)}, u32[]{:S(2)}, u32[]{:S(2)}) collective-permute-start(bf16[144,1024]{1,0:T(8,128)(2,1)S(1)} %get-tuple-element.44), channel_id=1, source_target_pairs={{0,4},{4,8},{8,12},{12,16},{16,20},{20,24},{24,28},{1,5},{5,9},{9,... | collective-permute-start | bytes 884744 | tf_op jit(solution)/shard_map/ppermute | solution.py:271
  16.2 3.6 %collective-permute-done.1.got = bf16[144,1024]{1,0:T(8,128)(2,1)S(1)} collective-permute-done((bf16[144,1024]{1,0:T(8,128)(2,1)S(1)}, bf16[144,1024]{1,0:T(8,128)(2,1)S(1)}, u32[]{:S(2)}, u32[]{:S(2)}) %collective-permute-start.1) | collective-permute-done | bytes 294944 | tf_op jit(solution)/shard_map/ppermute | solution.py:271
  19.8 1.5 %shard_map.79 = (f32[128,1024]{1,0:T(8,128)S(1)}, f32[128,1024]{1,0:T(8,128)S(1)}, f32[8,1024]{1,0:T(8,128)S(1)}, bf16[128,1024]{1,0:T(8,128)(2,1)S(1)}, bf16[128,1024]{1,0:T(8,128)(2,1)S(1)}) custom-call(bf16[4,1024,1024]{2,1,0:T(8,128)(2,1)S(1)} %get-tuple-element.41.weights, f32[4,1024]{1,0:T(4,128)S(1)} %copy-done.1, f32[128,1024]{1,0:T(8,128)S(1)} %copy-done, ...), custom_call_target="tpu_custom_call" | custom-call | flops 1073741824 | bytes 9224192 | tf_op jit(solution)/shard_map/pallas_call | solution.py:20
  21.4 4.0 %collective-permute-start.2 = (bf16[128,1024]{1,0:T(8,128)(2,1)S(1)}, bf16[128,1024]{1,0:T(8,128)(2,1)S(1)}, u32[]{:S(2)}, u32[]{:S(2)}) collective-permute-start(bf16[128,1024]{1,0:T(8,128)(2,1)S(1)} %get-tuple-element.46.before), channel_id=1, source_target_pairs={{4,12},{5,13},{6,14},{7,15}} | collective-permute-start | bytes 786440 | tf_op jit(solution)/shard_map/ppermute | solution.py:271
  25.4 1.3 %collective-permute-start.4 = (bf16[128,1024]{1,0:T(8,128)(2,1)S(1)}, bf16[128,1024]{1,0:T(8,128)(2,1)S(1)}, u32[]{:S(2)}, u32[]{:S(2)}) collective-permute-start(bf16[128,1024]{1,0:T(8,128)(2,1)S(1)} %get-tuple-element.50), channel_id=1, source_target_pairs={{0,4},{8,12},{16,20},{24,28},{1,5},{9,13},{17,21},{25,29},{2,6},{1... | collective-permute-start | bytes 786440 | tf_op jit(solution)/shard_map/ppermute | solution.py:271
  26.8 1.9 %collective-permute-done.2.got.got_1 = bf16[128,1024]{1,0:T(8,128)(2,1)S(1)} collective-permute-done((bf16[128,1024]{1,0:T(8,128)(2,1)S(1)}, bf16[128,1024]{1,0:T(8,128)(2,1)S(1)}, u32[]{:S(2)}, u32[]{:S(2)}) %collective-permute-start.2) | collective-permute-done | bytes 262176 | tf_op jit(solution)/shard_map/ppermute | solution.py:271
  28.7 0.1 collective-permute-done.4.pair_forcing
  28.8 0.0 collective-permute-done.3.pair_weight
  28.9 0.7 collective-permute-start.5
  29.5 1.3 %collective-permute-start.10 = (bf16[128,1024]{1,0:T(8,128)(2,1)S(1)}, bf16[128,1024]{1,0:T(8,128)(2,1)S(1)}, u32[]{:S(2)}, u32[]{:S(2)}) collective-permute-start(bf16[128,1024]{1,0:T(8,128)(2,1)S(1)} %get-tuple-element.50), channel_id=1, source_target_pairs={{0,6},{1,7},{2,4},{3,5},{8,14},{9,15},{10,12},{11,13},{16,22},{17,... | collective-permute-start | bytes 786440 | tf_op jit(solution)/shard_map/ppermute | solution.py:275
  30.8 1.3 %collective-permute-start.11 = (bf16[128,1024]{1,0:T(8,128)(2,1)S(1)}, bf16[128,1024]{1,0:T(8,128)(2,1)S(1)}, u32[]{:S(2)}, u32[]{:S(2)}) collective-permute-start(bf16[128,1024]{1,0:T(8,128)(2,1)S(1)} %get-tuple-element.50), channel_id=1, source_target_pairs={{0,7},{1,4},{2,5},{3,6},{8,15},{9,12},{10,13},{11,14},{16,23},{17,... | collective-permute-start | bytes 786440 | tf_op jit(solution)/shard_map/ppermute | solution.py:275
  32.1 1.3 %collective-permute-start.9 = (bf16[128,1024]{1,0:T(8,128)(2,1)S(1)}, bf16[128,1024]{1,0:T(8,128)(2,1)S(1)}, u32[]{:S(2)}, u32[]{:S(2)}) collective-permute-start(bf16[128,1024]{1,0:T(8,128)(2,1)S(1)} %get-tuple-element.50), channel_id=1, source_target_pairs={{0,5},{1,6},{2,7},{3,4},{8,13},{9,14},{10,15},{11,12},{16,21},{17,... | collective-permute-start | bytes 786440 | tf_op jit(solution)/shard_map/ppermute | solution.py:275
  33.4 1.3 %collective-permute-start.6 = (bf16[128,256]{1,0:T(8,128)(2,1)S(1)}, bf16[128,256]{1,0:T(8,128)(2,1)S(1)}, u32[]{:S(2)}, u32[]{:S(2)}) collective-permute-start(bf16[128,256]{1,0:T(8,128)(2,1)S(1)} %get-tuple-element.58), channel_id=1, source_target_pairs={{0,1},{1,2},{2,3},{3,0},{4,5},{5,6},{6,7},{7,4},{8,9},{9,10},{10,1... | collective-permute-start | bytes 196616 | tf_op jit(solution)/shard_map/ppermute | solution.py:278
  34.8 6.9 %collective-permute-done.6.refs_9_ = bf16[128,256]{1,0:T(8,128)(2,1)S(1)} collective-permute-done((bf16[128,256]{1,0:T(8,128)(2,1)S(1)}, bf16[128,256]{1,0:T(8,128)(2,1)S(1)}, u32[]{:S(2)}, u32[]{:S(2)}) %collective-permute-start.6) | collective-permute-done | bytes 65568 | tf_op jit(solution)/shard_map/ppermute | solution.py:278
  41.7 0.0 collective-permute-start.7
  41.7 4.3 %collective-permute-done.7.refs_10_ = bf16[128,256]{1,0:T(8,128)(2,1)S(1)} collective-permute-done((bf16[128,256]{1,0:T(8,128)(2,1)S(1)}, bf16[128,256]{1,0:T(8,128)(2,1)S(1)}, u32[]{:S(2)}, u32[]{:S(2)}) %collective-permute-start.7) | collective-permute-done | bytes 65568 | tf_op jit(solution)/shard_map/ppermute | solution.py:278
  46.0 2.6 %collective-permute-start.8 = (bf16[128,256]{1,0:T(8,128)(2,1)S(1)}, bf16[128,256]{1,0:T(8,128)(2,1)S(1)}, u32[]{:S(2)}, u32[]{:S(2)}) collective-permute-start(bf16[128,256]{1,0:T(8,128)(2,1)S(1)} %get-tuple-element.60), channel_id=1, source_target_pairs={{0,3},{1,0},{2,1},{3,2},{4,7},{5,4},{6,5},{7,6},{8,11},{9,8},{10,9... | collective-permute-start | bytes 196616 | tf_op jit(solution)/shard_map/ppermute | solution.py:278
  48.6 1.3 %collective-permute-done.8.refs_11_ = bf16[128,256]{1,0:T(8,128)(2,1)S(1)} collective-permute-done((bf16[128,256]{1,0:T(8,128)(2,1)S(1)}, bf16[128,256]{1,0:T(8,128)(2,1)S(1)}, u32[]{:S(2)}, u32[]{:S(2)}) %collective-permute-start.8) | collective-permute-done | bytes 65568 | tf_op jit(solution)/shard_map/ppermute | solution.py:278
  50.0 0.0 collective-permute-done.5.got.got_2
  50.0 0.0 collective-permute-done.10.refs_7_
  50.0 0.0 collective-permute-done.11.refs_8_
  50.0 0.0 collective-permute-done.9.refs_6_
  50.0 0.7 collective-permute-start.12
  50.7 0.0 collective-permute-done.12.got_3.got
  50.8 11.0 %collective-permute-start.13 = (bf16[128,1024]{1,0:T(8,128)(2,1)S(1)}, bf16[128,1024]{1,0:T(8,128)(2,1)S(1)}, u32[]{:S(2)}, u32[]{:S(2)}) collective-permute-start(bf16[128,1024]{1,0:T(8,128)(2,1)S(1)} %shard_map.83), channel_id=1, source_target_pairs={{4,0},{12,8},{20,16},{28,24},{5,1},{13,9},{21,17},{29,25},{6,2},{1... | collective-permute-start | bytes 786440 | tf_op jit(solution)/shard_map/ppermute | solution.py:271
  61.8 6.6 %collective-permute-start.14 = (bf16[128,1024]{1,0:T(8,128)(2,1)S(1)}, bf16[128,1024]{1,0:T(8,128)(2,1)S(1)}, u32[]{:S(2)}, u32[]{:S(2)}) collective-permute-start(bf16[128,1024]{1,0:T(8,128)(2,1)S(1)} %get-tuple-element.63.before), channel_id=1, source_target_pairs={{0,5},{1,6},{2,7},{3,4},{4,13},{5,14},{6,15},{7,12},{12,21},{13,22... | collective-permute-start | bytes 786440 | tf_op jit(solution)/shard_map/ppermute | solution.py:275
  68.4 1.9 %collective-permute-start.15 = (bf16[128,1024]{1,0:T(8,128)(2,1)S(1)}, bf16[128,1024]{1,0:T(8,128)(2,1)S(1)}, u32[]{:S(2)}, u32[]{:S(2)}) collective-permute-start(bf16[128,1024]{1,0:T(8,128)(2,1)S(1)} %get-tuple-element.63.before), channel_id=1, source_target_pairs={{0,6},{1,7},{2,4},{3,5},{4,14},{5,15},{6,12},{7,13},{12,22},{13,23... | collective-permute-start | bytes 786440 | tf_op jit(solution)/shard_map/ppermute | solution.py:275
  70.4 1.9 %collective-permute-start.16 = (bf16[128,1024]{1,0:T(8,128)(2,1)S(1)}, bf16[128,1024]{1,0:T(8,128)(2,1)S(1)}, u32[]{:S(2)}, u32[]{:S(2)}) collective-permute-start(bf16[128,1024]{1,0:T(8,128)(2,1)S(1)} %get-tuple-element.63.before), channel_id=1, source_target_pairs={{0,7},{1,4},{2,5},{3,6},{4,15},{5,12},{6,13},{7,14},{12,23},{13,20... | collective-permute-start | bytes 786440 | tf_op jit(solution)/shard_map/ppermute | solution.py:275
  72.3 0.0 collective-permute-done.13.down
  72.3 1.4 %shard_map.85 = (bf16[128,1024]{1,0:T(8,128)(2,1)S(1)}, f32[128,1024]{1,0:T(8,128)S(1)}, f32[128,1024]{1,0:T(8,128)}) custom-call(bf16[4,1024,1024]{2,1,0:T(8,128)(2,1)S(1)} %get-tuple-element.41.weights, f32[4,1024]{1,0:T(4,128)S(1)} %copy-done.1, f32[128,1024]{1,0:T(8,128)S(1)} %copy-done, f32[128,1024]{1,0:T(8,128)S(1)} %get-tuple-element.45.one, ...), custom_call_target="tpu_custom_call" | custom-call | flops 805306368 | bytes 12337152 | tf_op jit(solution)/shard_map/pallas_call | solution.py:20
  73.8 9.7 %collective-permute-done.14.refs_0_ = bf16[128,1024]{1,0:T(8,128)(2,1)S(1)} collective-permute-done((bf16[128,1024]{1,0:T(8,128)(2,1)S(1)}, bf16[128,1024]{1,0:T(8,128)(2,1)S(1)}, u32[]{:S(2)}, u32[]{:S(2)}) %collective-permute-start.14) | collective-permute-done | bytes 262176 | tf_op jit(solution)/shard_map/ppermute | solution.py:275
  83.5 5.5 %collective-permute-done.15.refs_1_ = bf16[128,1024]{1,0:T(8,128)(2,1)S(1)} collective-permute-done((bf16[128,1024]{1,0:T(8,128)(2,1)S(1)}, bf16[128,1024]{1,0:T(8,128)(2,1)S(1)}, u32[]{:S(2)}, u32[]{:S(2)}) %collective-permute-start.15) | collective-permute-done | bytes 262176 | tf_op jit(solution)/shard_map/ppermute | solution.py:275
  89.0 1.8 %collective-permute-done.16.refs_2_ = bf16[128,1024]{1,0:T(8,128)(2,1)S(1)} collective-permute-done((bf16[128,1024]{1,0:T(8,128)(2,1)S(1)}, bf16[128,1024]{1,0:T(8,128)(2,1)S(1)}, u32[]{:S(2)}, u32[]{:S(2)}) %collective-permute-start.16) | collective-permute-done | bytes 262176 | tf_op jit(solution)/shard_map/ppermute | solution.py:275
  90.8 1.3 %collective-permute-start.17 = (bf16[128,1024]{1,0:T(8,128)(2,1)S(1)}, bf16[128,1024]{1,0:T(8,128)(2,1)S(1)}, u32[]{:S(2)}, u32[]{:S(2)}) collective-permute-start(bf16[128,1024]{1,0:T(8,128)(2,1)S(1)} %collective-permute-done.14.refs_0_), channel_id=1, source_target_pairs={{4,0},{12,8},{20,16},{28,24},{5,1},{13,9},{21,17},{29,25},{6,2},{1... | collective-permute-start | bytes 786440 | tf_op jit(solution)/shard_map/ppermute | solution.py:271
  92.1 1.3 %collective-permute-start.18 = (bf16[128,1024]{1,0:T(8,128)(2,1)S(1)}, bf16[128,1024]{1,0:T(8,128)(2,1)S(1)}, u32[]{:S(2)}, u32[]{:S(2)}) collective-permute-start(bf16[128,1024]{1,0:T(8,128)(2,1)S(1)} %collective-permute-done.15.refs_1_), channel_id=1, source_target_pairs={{4,0},{12,8},{20,16},{28,24},{5,1},{13,9},{21,17},{29,25},{6,2},{1... | collective-permute-start | bytes 786440 | tf_op jit(solution)/shard_map/ppermute | solution.py:271
  93.4 1.3 %collective-permute-start.19 = (bf16[128,1024]{1,0:T(8,128)(2,1)S(1)}, bf16[128,1024]{1,0:T(8,128)(2,1)S(1)}, u32[]{:S(2)}, u32[]{:S(2)}) collective-permute-start(bf16[128,1024]{1,0:T(8,128)(2,1)S(1)} %collective-permute-done.16.refs_2_), channel_id=1, source_target_pairs={{4,0},{12,8},{20,16},{28,24},{5,1},{13,9},{21,17},{29,25},{6,2},{1... | collective-permute-start | bytes 786440 | tf_op jit(solution)/shard_map/ppermute | solution.py:271
  94.7 0.6 shard_map.87.total
  95.3 1.3 %shard_map.86 = f32[128,1024]{1,0:T(8,128)} custom-call(bf16[4,1024,1024]{2,1,0:T(8,128)(2,1)S(1)} %get-tuple-element.41.weights, f32[4,1024]{1,0:T(4,128)S(1)} %copy-done.1, bf16[128,1024]{1,0:T(8,128)(2,1)S(1)} %get-tuple-element.68.left, f32[128,1024]{1,0:T(8,128)S(1)} %get-tuple-element.69.state), custom_call_target="tpu_custom_call" | custom-call | flops 268435456 | bytes 9191424 | tf_op jit(solution)/shard_map/pallas_call | solution.py:20
  96.6 0.0 collective-permute-done.18.refs_4_
  96.6 0.0 collective-permute-done.19.refs_5_
  96.6 6.1 %shard_map.88 = f32[1024,256]{1,0:T(8,128)} custom-call(bf16[4,1024,1024]{2,1,0:T(8,128)(2,1)S(1)} %get-tuple-element.41.weights, f32[4,1024]{1,0:T(4,128)S(1)} %copy-done.1, bf16[1024,1024]{1,0:T(8,128)(2,1)S(1)} %collective-permute-done.3.pair_weight, f32[8,1024]{1,0:T(8,128)S(1)} %get-tuple-element.49.pair_bias, f32[1024,256]{1,0:T(8,128)S(1)} %shard_map.87.total, ...), custom_call_target="tpu_custom_call" | custom-call | flops 4831838208 | bytes 14139392 | tf_op jit(solution)/shard_map/pallas_call | solution.py:20
  (13 shorter events, 0.2 us)
Async XLA Ops:
  0.6 9.7 %copy-start = (f32[128,1024]{1,0:T(8,128)S(1)}, f32[128,1024]{1,0:T(8,128)}, u32[]{:S(2)}) copy-start(f32[128,1024]{1,0:T(8,128)} %inputs.5) | copy-start | bytes 1572868
  0.6 9.7 %copy-start.1 = (f32[4,1024]{1,0:T(4,128)S(1)}, f32[4,1024]{1,0:T(4,128)}, u32[]{:S(2)}) copy-start(f32[4,1024]{1,0:T(4,128)} %biases.17) | copy-start | bytes 49156
  0.7 1.1 %copy-start.2 = (f32[1,128,1024]{2,1,0:T(8,128)S(1)}, f32[1,128,1024]{2,1,0:T(8,128)}, u32[]{:S(2)}) copy-start(f32[1,128,1024]{2,1,0:T(8,128)} %param.6) | copy-start | bytes 1572868
  1.8 7.2 %collective-permute-start = (bf16[128,1024]{1,0:T(8,128)(2,1)S(1)}, bf16[128,1024]{1,0:T(8,128)(2,1)S(1)}, u32[]{:S(2)}, u32[]{:S(2)}) collective-permute-start(bf16[128,1024]{1,0:T(8,128)(2,1)S(1)} %shard_map.76), channel_id=1, source_target_pairs={{0,4},{4,8},{8,12},{12,16},{16,20},{20,24},{24,28},{1,5},{5,9},{9,... | collective-permute-start | bytes 786440 | tf_op jit(solution)/shard_map/ppermute | solution.py:271
  9.0 19.8 %collective-permute-start.3 = (bf16[1024,1024]{1,0:T(8,128)(2,1)S(1)}, bf16[1024,1024]{1,0:T(8,128)(2,1)S(1)}, u32[]{:S(2)}, u32[]{:S(2)}) collective-permute-start(bf16[1024,1024]{1,0:T(8,128)(2,1)S(1)} %get-tuple-element.48), channel_id=1, source_target_pairs={{0,4},{8,12},{16,20},{24,28},{1,5},{9,13},{17,21},{25,29},{2,6},{1... | collective-permute-start | bytes 6291464 | tf_op jit(solution)/shard_map/ppermute | solution.py:271
  10.3 16.4 %copy-start.3 = (bf16[1,128,1024]{2,1,0:T(8,128)(2,1)S(1)}, bf16[1,128,1024]{2,1,0:T(8,128)(2,1)}, u32[]{:S(2)}) copy-start(bf16[1,128,1024]{2,1,0:T(8,128)(2,1)} %param.9) | copy-start | bytes 786436
  11.9 7.9 %collective-permute-start.1 = (bf16[144,1024]{1,0:T(8,128)(2,1)S(1)}, bf16[144,1024]{1,0:T(8,128)(2,1)S(1)}, u32[]{:S(2)}, u32[]{:S(2)}) collective-permute-start(bf16[144,1024]{1,0:T(8,128)(2,1)S(1)} %get-tuple-element.44), channel_id=1, source_target_pairs={{0,4},{4,8},{8,12},{12,16},{16,20},{20,24},{24,28},{1,5},{5,9},{9,... | collective-permute-start | bytes 884744 | tf_op jit(solution)/shard_map/ppermute | solution.py:271
  21.4 7.3 %collective-permute-start.2 = (bf16[128,1024]{1,0:T(8,128)(2,1)S(1)}, bf16[128,1024]{1,0:T(8,128)(2,1)S(1)}, u32[]{:S(2)}, u32[]{:S(2)}) collective-permute-start(bf16[128,1024]{1,0:T(8,128)(2,1)S(1)} %get-tuple-element.46.before), channel_id=1, source_target_pairs={{4,12},{5,13},{6,14},{7,15}} | collective-permute-start | bytes 786440 | tf_op jit(solution)/shard_map/ppermute | solution.py:271
  25.4 3.4 %collective-permute-start.4 = (bf16[128,1024]{1,0:T(8,128)(2,1)S(1)}, bf16[128,1024]{1,0:T(8,128)(2,1)S(1)}, u32[]{:S(2)}, u32[]{:S(2)}) collective-permute-start(bf16[128,1024]{1,0:T(8,128)(2,1)S(1)} %get-tuple-element.50), channel_id=1, source_target_pairs={{0,4},{8,12},{16,20},{24,28},{1,5},{9,13},{17,21},{25,29},{2,6},{1... | collective-permute-start | bytes 786440 | tf_op jit(solution)/shard_map/ppermute | solution.py:271
  28.9 21.1 %collective-permute-start.5 = (bf16[128,1024]{1,0:T(8,128)(2,1)S(1)}, bf16[128,1024]{1,0:T(8,128)(2,1)S(1)}, u32[]{:S(2)}, u32[]{:S(2)}) collective-permute-start(bf16[128,1024]{1,0:T(8,128)(2,1)S(1)} %get-tuple-element.56.before), channel_id=1, source_target_pairs={{12,20},{13,21},{14,22},{15,23}} | collective-permute-start | bytes 786440 | tf_op jit(solution)/shard_map/ppermute | solution.py:271
  29.5 20.5 %collective-permute-start.10 = (bf16[128,1024]{1,0:T(8,128)(2,1)S(1)}, bf16[128,1024]{1,0:T(8,128)(2,1)S(1)}, u32[]{:S(2)}, u32[]{:S(2)}) collective-permute-start(bf16[128,1024]{1,0:T(8,128)(2,1)S(1)} %get-tuple-element.50), channel_id=1, source_target_pairs={{0,6},{1,7},{2,4},{3,5},{8,14},{9,15},{10,12},{11,13},{16,22},{17,... | collective-permute-start | bytes 786440 | tf_op jit(solution)/shard_map/ppermute | solution.py:275
  30.8 19.2 %collective-permute-start.11 = (bf16[128,1024]{1,0:T(8,128)(2,1)S(1)}, bf16[128,1024]{1,0:T(8,128)(2,1)S(1)}, u32[]{:S(2)}, u32[]{:S(2)}) collective-permute-start(bf16[128,1024]{1,0:T(8,128)(2,1)S(1)} %get-tuple-element.50), channel_id=1, source_target_pairs={{0,7},{1,4},{2,5},{3,6},{8,15},{9,12},{10,13},{11,14},{16,23},{17,... | collective-permute-start | bytes 786440 | tf_op jit(solution)/shard_map/ppermute | solution.py:275
  32.1 17.9 %collective-permute-start.9 = (bf16[128,1024]{1,0:T(8,128)(2,1)S(1)}, bf16[128,1024]{1,0:T(8,128)(2,1)S(1)}, u32[]{:S(2)}, u32[]{:S(2)}) collective-permute-start(bf16[128,1024]{1,0:T(8,128)(2,1)S(1)} %get-tuple-element.50), channel_id=1, source_target_pairs={{0,5},{1,6},{2,7},{3,4},{8,13},{9,14},{10,15},{11,12},{16,21},{17,... | collective-permute-start | bytes 786440 | tf_op jit(solution)/shard_map/ppermute | solution.py:275
  33.4 8.3 %collective-permute-start.6 = (bf16[128,256]{1,0:T(8,128)(2,1)S(1)}, bf16[128,256]{1,0:T(8,128)(2,1)S(1)}, u32[]{:S(2)}, u32[]{:S(2)}) collective-permute-start(bf16[128,256]{1,0:T(8,128)(2,1)S(1)} %get-tuple-element.58), channel_id=1, source_target_pairs={{0,1},{1,2},{2,3},{3,0},{4,5},{5,6},{6,7},{7,4},{8,9},{9,10},{10,1... | collective-permute-start | bytes 196616 | tf_op jit(solution)/shard_map/ppermute | solution.py:278
  41.7 4.3 %collective-permute-start.7 = (bf16[128,256]{1,0:T(8,128)(2,1)S(1)}, bf16[128,256]{1,0:T(8,128)(2,1)S(1)}, u32[]{:S(2)}, u32[]{:S(2)}) collective-permute-start(bf16[128,256]{1,0:T(8,128)(2,1)S(1)} %get-tuple-element.59), channel_id=1, source_target_pairs={{0,2},{1,3},{2,0},{3,1},{4,6},{5,7},{6,4},{7,5},{8,10},{9,11},{10,... | collective-permute-start | bytes 196616 | tf_op jit(solution)/shard_map/ppermute | solution.py:278
  46.0 4.0 %collective-permute-start.8 = (bf16[128,256]{1,0:T(8,128)(2,1)S(1)}, bf16[128,256]{1,0:T(8,128)(2,1)S(1)}, u32[]{:S(2)}, u32[]{:S(2)}) collective-permute-start(bf16[128,256]{1,0:T(8,128)(2,1)S(1)} %get-tuple-element.60), channel_id=1, source_target_pairs={{0,3},{1,0},{2,1},{3,2},{4,7},{5,4},{6,5},{7,6},{8,11},{9,8},{10,9... | collective-permute-start | bytes 196616 | tf_op jit(solution)/shard_map/ppermute | solution.py:278
  50.0 0.7 collective-permute-start.12
  50.8 21.5 %collective-permute-start.13 = (bf16[128,1024]{1,0:T(8,128)(2,1)S(1)}, bf16[128,1024]{1,0:T(8,128)(2,1)S(1)}, u32[]{:S(2)}, u32[]{:S(2)}) collective-permute-start(bf16[128,1024]{1,0:T(8,128)(2,1)S(1)} %shard_map.83), channel_id=1, source_target_pairs={{4,0},{12,8},{20,16},{28,24},{5,1},{13,9},{21,17},{29,25},{6,2},{1... | collective-permute-start | bytes 786440 | tf_op jit(solution)/shard_map/ppermute | solution.py:271
  61.8 21.7 %collective-permute-start.14 = (bf16[128,1024]{1,0:T(8,128)(2,1)S(1)}, bf16[128,1024]{1,0:T(8,128)(2,1)S(1)}, u32[]{:S(2)}, u32[]{:S(2)}) collective-permute-start(bf16[128,1024]{1,0:T(8,128)(2,1)S(1)} %get-tuple-element.63.before), channel_id=1, source_target_pairs={{0,5},{1,6},{2,7},{3,4},{4,13},{5,14},{6,15},{7,12},{12,21},{13,22... | collective-permute-start | bytes 786440 | tf_op jit(solution)/shard_map/ppermute | solution.py:275
  68.4 20.6 %collective-permute-start.15 = (bf16[128,1024]{1,0:T(8,128)(2,1)S(1)}, bf16[128,1024]{1,0:T(8,128)(2,1)S(1)}, u32[]{:S(2)}, u32[]{:S(2)}) collective-permute-start(bf16[128,1024]{1,0:T(8,128)(2,1)S(1)} %get-tuple-element.63.before), channel_id=1, source_target_pairs={{0,6},{1,7},{2,4},{3,5},{4,14},{5,15},{6,12},{7,13},{12,22},{13,23... | collective-permute-start | bytes 786440 | tf_op jit(solution)/shard_map/ppermute | solution.py:275
  70.4 20.4 %collective-permute-start.16 = (bf16[128,1024]{1,0:T(8,128)(2,1)S(1)}, bf16[128,1024]{1,0:T(8,128)(2,1)S(1)}, u32[]{:S(2)}, u32[]{:S(2)}) collective-permute-start(bf16[128,1024]{1,0:T(8,128)(2,1)S(1)} %get-tuple-element.63.before), channel_id=1, source_target_pairs={{0,7},{1,4},{2,5},{3,6},{4,15},{5,12},{6,13},{7,14},{12,23},{13,20... | collective-permute-start | bytes 786440 | tf_op jit(solution)/shard_map/ppermute | solution.py:275
  90.8 5.8 %collective-permute-start.17 = (bf16[128,1024]{1,0:T(8,128)(2,1)S(1)}, bf16[128,1024]{1,0:T(8,128)(2,1)S(1)}, u32[]{:S(2)}, u32[]{:S(2)}) collective-permute-start(bf16[128,1024]{1,0:T(8,128)(2,1)S(1)} %collective-permute-done.14.refs_0_), channel_id=1, source_target_pairs={{4,0},{12,8},{20,16},{28,24},{5,1},{13,9},{21,17},{29,25},{6,2},{1... | collective-permute-start | bytes 786440 | tf_op jit(solution)/shard_map/ppermute | solution.py:271
  92.1 4.5 %collective-permute-start.18 = (bf16[128,1024]{1,0:T(8,128)(2,1)S(1)}, bf16[128,1024]{1,0:T(8,128)(2,1)S(1)}, u32[]{:S(2)}, u32[]{:S(2)}) collective-permute-start(bf16[128,1024]{1,0:T(8,128)(2,1)S(1)} %collective-permute-done.15.refs_1_), channel_id=1, source_target_pairs={{4,0},{12,8},{20,16},{28,24},{5,1},{13,9},{21,17},{29,25},{6,2},{1... | collective-permute-start | bytes 786440 | tf_op jit(solution)/shard_map/ppermute | solution.py:271
  93.4 3.2 %collective-permute-start.19 = (bf16[128,1024]{1,0:T(8,128)(2,1)S(1)}, bf16[128,1024]{1,0:T(8,128)(2,1)S(1)}, u32[]{:S(2)}, u32[]{:S(2)}) collective-permute-start(bf16[128,1024]{1,0:T(8,128)(2,1)S(1)} %collective-permute-done.16.refs_2_), channel_id=1, source_target_pairs={{4,0},{12,8},{20,16},{28,24},{5,1},{13,9},{21,17},{29,25},{6,2},{1... | collective-permute-start | bytes 786440 | tf_op jit(solution)/shard_map/ppermute | solution.py:271

commit v4 on v3

--- a/solution.py
+++ b/solution.py
@@ -133,7 +133,7 @@
         odd[:, cols] = new.astype(BF16)
         forcing[:, cols] = start[:, cols] + (4.0 * step_size) * slope
     run_layers((1, 2, 3), step_size, weights, biases, state, (even, odd))
-    top[...] = jnp.where(first, inputs[...].astype(BF16), even[...])
+    top[...] = even[...]
     difference = state[...] - forcing[...]
     forcing[...] = difference
     sent_forcing[...] = difference.astype(BF16)
@@ -141,18 +141,12 @@
     pair_bias[...] = jnp.broadcast_to(tail[0:1, :] + (tail[1:2, :] + tail[2:3, :]), pair_bias.shape)
 
 
-def coarse_kernel(chosen, factor, weights, biases, forcing, pair_weight, pair_bias, pair_forcing, got, before, mid, *rest):
+def coarse_kernel(chosen, factor, weights, biases, forcing, pair_weight, pair_bias, pair_forcing, got, mid, *rest):
     even, odd = rest[-2:]
     here = lax.axis_index("layer")
 
-    taken = chosen(here % 4, here // 4)
-
-    @pl.when(jnp.logical_not(taken))
-    def _():
-        for top in rest[:-2]:
-            top[...] = before[...]
-
-    @pl.when(taken)
+
+    @pl.when(chosen(here % 4, here // 4))
     def _():
         even[...] = got[...]
         for cols in tiles(mid.shape[1]):
@@ -214,37 +208,20 @@
     return lax.dot_general(left[...], deltas[...], (((0,), (0,)), ((), ())), preferred_element_type=F32)
 
 
-def own_gradient_kernel(step_size, weights, biases, left, adjoint, total, deltas):
-    total[...] = gradient(step_size, weights, biases, left, adjoint, deltas, total.shape[1])
-
-
-def far_kernel(step_size, rows, count, weights, biases, pair_weight, pair_bias, total, *refs):
-    far, down, forcings, adjoints = (refs[i * count : (i + 1) * count] for i in range(4))
-    result, state, even, odd, adjoint, deltas = refs[4 * count :]
-    is_odd = lax.axis_index("layer") % 2 == 1
-    places = [slice(i * rows, (i + 1) * rows) for i in range(count)]
-
-    @pl.when(is_odd)
-    def _():
-        for place, source in zip(places, far):
-            odd[place, :] = source[...]
-        for cols in tiles(state.shape[1]):
-            slope = layer_of(odd, pair_weight, pair_bias[0:1, :], cols)
-            for place, added in zip(places, forcings):
-                new = odd[place, cols].astype(F32) + (4.0 * step_size) * slope[place, :] + added[:, cols].astype(F32)
-                state[place, cols] = new
-                even[place, cols] = new.astype(BF16)
-
-    @pl.when(jnp.logical_not(is_odd))
-    def _():
-        for place, source in zip(places, down):
-            state[place, :] = source[...].astype(F32)
-            even[place, :] = source[...]
-
-    for place, source in zip(places, adjoints):
-        adjoint[place, :] = source[...]
-    run_layers((0, 1, 2), step_size, weights, biases, state, (even, odd))
-    result[...] = total[...] + gradient(step_size, weights, biases, odd, adjoint, deltas, result.shape[1])
+def gradient_kernel(step_size, conditions, has_total, weights, biases, *refs):
+    count = len(conditions)
+    lefts, adjoints, (total, deltas) = refs[:count], refs[count : 2 * count], refs[-2:]
+    place = lax.axis_index("dp")
+    if has_total:
+        total[...] = refs[2 * count][...]
+    for i, (left, adjoint, condition) in enumerate(zip(lefts, adjoints, conditions)):
+        if i == 0 and not has_total:
+            total[...] = gradient(step_size, weights, biases, left, adjoint, deltas, total.shape[1])
+        else:
+
+            @pl.when(condition(place))
+            def _(left=left, adjoint=adjoint):
+                total[...] += gradient(step_size, weights, biases, left, adjoint, deltas, total.shape[1])
 
 
 def single_kernel(factor, weights, biases, got, added, out):
@@ -270,10 +247,6 @@
     def along(state, pairs):
         return lax.ppermute(state, "layer", pairs)
 
-    def across(state, pairs, by):
-        flat = [(i * parts + z, j * parts + (z + by) % parts) for i, j in pairs for z in range(parts)]
-        return lax.ppermute(state, ("layer", "dp"), flat)
-
     def shifted(array, by):
         return lax.ppermute(array, "dp", [(i, (i + by) % parts) for i in range(parts)])
 
@@ -308,14 +281,13 @@
         scratch=[pltpu.VMEM((rows, depth), F32)] + rounded, flops=4 * layer_flops,
     )
     pair_forcing = along(forcing_sent, up_pair)
-    far_forcings = [across(forcing_sent, up_pair, by) for by in range(1, parts)]
 
     def two_steps(top, pairs, chosen, last=False, beside=()):
         got, *_ = lax.optimization_barrier((along(top, pairs), *beside))
         mid, *new_top = call(
             functools.partial(coarse_kernel, chosen, 4.0 * step_size),
             (kept(inputs),) if last else (kept(inputs), plain((rows, depth), BF16)),
-            held_weights, biases, forcing, pair_weight, pair_bias, pair_forcing, got, top,
+            held_weights, biases, forcing, pair_weight, pair_bias, pair_forcing, got,
             scratch=rounded, flops=2 * layer_flops,
         )
         return got, mid, *new_top
@@ -355,7 +327,6 @@
         top_1, [(4 * m - 1, 4 * m + 1) for m in range(1, groups)], lambda slot, group: (slot == 1) & (group > 0),
         beside=adjoints,
     )
-    top_2, *far_forcings = lax.optimization_barrier((top_2, *far_forcings))
     got_3, mid_3 = two_steps(
         top_2, [(4 * m + 1, 4 * m + 3) for m in range(1, groups)], lambda slot, group: (slot == 3) & (group > 0), True
     )
@@ -370,7 +341,7 @@
             new = single(16.0 * step_size, along(solved.astype(BF16), [(4 * m - 1, 4 * m + 3)]), base)
             solved = jnp.where(here == 4 * m + 3, new, solved)
         new_2, new_mid_2, top_2 = two_steps(
-            jnp.where(slot == 3, solved.astype(BF16), top_2), [(4 * m - 1, 4 * m + 1) for m in range(2, groups)], lambda slot, group: (slot == 1) & (group > 1)
+            solved.astype(BF16), [(4 * m - 1, 4 * m + 1) for m in range(2, groups)], lambda slot, group: (slot == 1) & (group > 1)
         )
         new_3, new_mid_3 = two_steps(
             top_2, [(4 * m + 1, 4 * m + 3) for m in range(2, groups)], lambda slot, group: (slot == 3) & (group > 1), True
@@ -382,26 +353,43 @@
         gots = [jnp.where(group > 1, new, old) for new, old in ((new_2, got_2), (new_3, got_3))]
         left, state, coarse_early = finish((got_1, *gots), (mid_1, *mids))
         coarse_states = jnp.where(slot == 3, solved - relaxed_out, coarse_states)
-    leaps = [(0, 1)] + [(i, i + 2) for i in range(1, blocks - 2, 2)]
-    far = [across(top_2, leaps, by) for by in range(1, parts)]
-    left, *far = lax.optimization_barrier((left, *far))
-    far_down = [along(state_far, down_pair) for state_far in far]
+    def along_dp(array, pairs):
+        return lax.ppermute(array, "dp", pairs)
+
+    right = [(i, i + 1) for i in range(parts - 1)]
+    back = [(i + 1, i) for i in range(parts - 1)]
+    from_left, from_right = along_dp(left, right), along_dp(left, back)
+    beyond = []
+    for by in range(3, parts):
+        onward, home = [(i, i + by) for i in range(parts - by)], [(i + by, i) for i in range(parts - by)]
+        if 2 * by >= parts:
+            ahead_rows = behind_rows = along_dp(left, onward + home)
+        else:
+            ahead_rows, behind_rows = along_dp(left, onward), along_dp(left, home)
+        beyond.append((ahead_rows, adjoints[by], lambda place, by=by: place >= by))
+        beyond.append((behind_rows, adjoints[parts - by], lambda place, by=by: place < parts - by))
+    beyond.append((along_dp(from_left, right[1:]), adjoints[2 % parts], lambda place: place >= 2))
+    beyond.append((along_dp(from_right, back[:-1]), adjoints[-2], lambda place: place < parts - 2))
     new_states = call(
         functools.partial(last_kernel, step_size), plain((rows, depth), F32),
         held_weights, biases, left, state, flops=layer_flops,
     )
-    total = call(
-        functools.partial(own_gradient_kernel, step_size), pltpu.VMEM((depth, width), F32),
-        held_weights, biases, left, adjoints[0], scratch=[pltpu.VMEM((rows, width), BF16)], flops=layer_flops,
-    )
-    others = (parts - 1) * rows
-    weight_grad = call(
-        functools.partial(far_kernel, step_size, rows, parts - 1), plain((depth, width), F32),
-        held_weights, biases, pair_weight, pair_bias, total, *far, *far_down, *far_forcings, *adjoints[1:],
-        scratch=[pltpu.VMEM((others, depth), F32)] + [pltpu.VMEM((others, depth), BF16)] * 2
-        + [pltpu.VMEM((others, width), BF16)] * 2,
-        flops=6 * (parts - 1) * layer_flops,
-    )
+
+    def add_up(out, blocks_of_rows, total=()):
+        datas, columns, conditions = zip(*blocks_of_rows)
+        return call(
+            functools.partial(gradient_kernel, step_size, conditions, bool(total)), out,
+            held_weights, biases, *datas, *columns, *total,
+            scratch=[pltpu.VMEM((rows, width), BF16)], flops=len(datas) * layer_flops // 2,
+        )
+
+    near = [
+        (left, adjoints[0], None),
+        (from_left, adjoints[1], lambda place: place >= 1),
+        (from_right, adjoints[-1], lambda place: place < parts - 1),
+    ]
+    total = add_up(pltpu.VMEM((depth, width), F32), near)
+    weight_grad = add_up(plain((depth, width), F32), beyond, (total,))
     return (new_states[None], coarse_states[None], weight_grad[None])
 
 

time: 103 us -> 76.3 us (0.74)
  the two profiles are of different devices: /device:TPU:9 before, /device:TPU:7 now
where the time goes in v4:
time: 76.3 us; the launch traced here: 76 us
  waiting for transfers between devices  34.8 us (46%)
  starting transfers between devices  25.7 us (34%)
  Pallas kernels  13.5 us (18%)
  local copies, waits for them, and re-layouts  1.11 us (1%)
  between operations  0.88 us (1%)
    ppermute x8, waiting for transfers between devices, along(): return lax.ppermute(state, 'layer', pairs)  19.3 us
    pallas_call x13, Pallas kernels, call(): pl.pallas_call(kernel, out_shape=outs, in_specs=specs or [WHOLE] * len(ar...  13.5 us
    ppermute x5, starting transfers between devices, along_dp(): return lax.ppermute(array, 'dp', pairs)  11.9 us
    ppermute x5, waiting for transfers between devices, along_dp(): return lax.ppermute(array, 'dp', pairs)  11.5 us
    ppermute x8, starting transfers between devices, along(): return lax.ppermute(state, 'layer', pairs)  9.11 us
    ppermute x3, starting transfers between devices, shifted(): lax.ppermute(array, 'dp', [(i, (i + by) % parts) for i in range(parts)])  4.71 us
    ppermute x3, waiting for transfers between devices, shifted(): lax.ppermute(array, 'dp', [(i, (i + by) % parts) for i in range(parts)])  4.02 us
  transfers between devices with their start and end apart: 16, of which 9 were waited for; matrix products, arithmetic and copies ran while one was open for 0% of the time, Pallas kernels for 13%

profile of v4, /device:TPU:7, one launch (start us, length us, event | category | flops | bytes accessed | tf_op | source)
XLA Modules:
  0.0 76.0 jit_solution(15857695106944453496)
XLA Ops:
  0.6 0.0 copy-start.1
  0.6 0.0 copy-start
  0.7 0.0 copy-start.2
  0.7 1.1 %copy-done.2 = f32[1,128,1024]{2,1,0:T(8,128)S(1)} copy-done((f32[1,128,1024]{2,1,0:T(8,128)S(1)}, f32[1,128,1024]{2,1,0:T(8,128)}, u32[]{:S(2)}) %copy-start.2) | copy-done | bytes 524312
  1.8 1.3 %collective-permute-start = (bf16[128,1024]{1,0:T(8,128)(2,1)S(1)}, bf16[128,1024]{1,0:T(8,128)(2,1)S(1)}, u32[]{:S(2)}, u32[]{:S(2)}) collective-permute-start(bf16[128,1024]{1,0:T(8,128)(2,1)S(1)} %shard_map.76), channel_id=1, source_target_pairs={{0,4},{4,8},{8,12},{12,16},{16,20},{20,24},{24,28},{1,5},{5,9},{9,... | collective-permute-start | bytes 786440 | tf_op jit(solution)/shard_map/ppermute | solution.py:248
  3.1 3.5 %shard_map.77 = (bf16[4,1024,1024]{2,1,0:T(8,128)(2,1)S(1)}, bf16[1024,1024]{1,0:T(8,128)(2,1)S(1)}) custom-call(bf16[4,1024,1024]{2,1,0:T(8,128)(2,1)} %source), custom_call_target="tpu_custom_call" | custom-call | bytes 8388608 | tf_op jit(solution)/shard_map/pallas_call | solution.py:20
  6.6 0.0 collective-permute-done.got
  6.6 1.3 %collective-permute-start.3 = (bf16[1024,1024]{1,0:T(8,128)(2,1)S(1)}, bf16[1024,1024]{1,0:T(8,128)(2,1)S(1)}, u32[]{:S(2)}, u32[]{:S(2)}) collective-permute-start(bf16[1024,1024]{1,0:T(8,128)(2,1)S(1)} %get-tuple-element.40), channel_id=1, source_target_pairs={{0,4},{8,12},{16,20},{24,28},{1,5},{9,13},{17,21},{25,29},{2,6},{1... | collective-permute-start | bytes 6291464 | tf_op jit(solution)/shard_map/ppermute | solution.py:248
  7.9 0.0 copy-done.1
  7.9 0.0 copy-done
  7.9 0.0 copy-start.3
  8.0 1.5 %shard_map.78 = (f32[128,1024]{1,0:T(8,128)S(1)}, bf16[144,1024]{1,0:T(8,128)(2,1)S(1)}) custom-call(bf16[4,1024,1024]{2,1,0:T(8,128)(2,1)S(1)} %get-tuple-element.33.weights, f32[4,1024]{1,0:T(4,128)S(1)} %copy-done.1, f32[128,1024]{1,0:T(8,128)S(1)} %copy-done, bf16[128,1024]{1,0:T(8,128)(2,1)S(1)} %collective-permute-done.got), custom_call_target="tpu_custom_call" | custom-call | flops 1073741824 | bytes 9191424 | tf_op jit(solution)/shard_map/pallas_call | solution.py:20
  9.5 1.3 %collective-permute-start.1 = (bf16[144,1024]{1,0:T(8,128)(2,1)S(1)}, bf16[144,1024]{1,0:T(8,128)(2,1)S(1)}, u32[]{:S(2)}, u32[]{:S(2)}) collective-permute-start(bf16[144,1024]{1,0:T(8,128)(2,1)S(1)} %get-tuple-element.36), channel_id=1, source_target_pairs={{0,4},{4,8},{8,12},{12,16},{16,20},{20,24},{24,28},{1,5},{5,9},{9,... | collective-permute-start | bytes 884744 | tf_op jit(solution)/shard_map/ppermute | solution.py:248
  10.8 5.3 %collective-permute-done.1.got = bf16[144,1024]{1,0:T(8,128)(2,1)S(1)} collective-permute-done((bf16[144,1024]{1,0:T(8,128)(2,1)S(1)}, bf16[144,1024]{1,0:T(8,128)(2,1)S(1)}, u32[]{:S(2)}, u32[]{:S(2)}) %collective-permute-start.1) | collective-permute-done | bytes 294944 | tf_op jit(solution)/shard_map/ppermute | solution.py:248
  16.1 1.5 %shard_map.79 = (f32[128,1024]{1,0:T(8,128)S(1)}, f32[128,1024]{1,0:T(8,128)S(1)}, f32[8,1024]{1,0:T(8,128)S(1)}, bf16[128,1024]{1,0:T(8,128)(2,1)S(1)}, bf16[128,1024]{1,0:T(8,128)(2,1)S(1)}) custom-call(bf16[4,1024,1024]{2,1,0:T(8,128)(2,1)S(1)} %get-tuple-element.33.weights, f32[4,1024]{1,0:T(4,128)S(1)} %copy-done.1, f32[128,1024]{1,0:T(8,128)S(1)} %copy-done, ...), custom_call_target="tpu_custom_call" | custom-call | flops 1073741824 | bytes 9224192 | tf_op jit(solution)/shard_map/pallas_call | solution.py:20
  17.7 0.7 collective-permute-start.2
  18.4 1.3 %collective-permute-start.4 = (bf16[128,1024]{1,0:T(8,128)(2,1)S(1)}, bf16[128,1024]{1,0:T(8,128)(2,1)S(1)}, u32[]{:S(2)}, u32[]{:S(2)}) collective-permute-start(bf16[128,1024]{1,0:T(8,128)(2,1)S(1)} %get-tuple-element.42), channel_id=1, source_target_pairs={{0,4},{8,12},{16,20},{24,28},{1,5},{9,13},{17,21},{25,29},{2,6},{1... | collective-permute-start | bytes 786440 | tf_op jit(solution)/shard_map/ppermute | solution.py:248
  19.7 0.0 copy-done.3
  19.7 0.0 collective-permute-done.2.got.got_1
  19.7 6.0 %collective-permute-done.4.pair_forcing = bf16[128,1024]{1,0:T(8,128)(2,1)S(1)} collective-permute-done((bf16[128,1024]{1,0:T(8,128)(2,1)S(1)}, bf16[128,1024]{1,0:T(8,128)(2,1)S(1)}, u32[]{:S(2)}, u32[]{:S(2)}) %collective-permute-start.4) | collective-permute-done | bytes 262176 | tf_op jit(solution)/shard_map/ppermute | solution.py:248
  25.7 0.0 collective-permute-done.3.pair_weight
  25.7 0.7 collective-permute-start.5
  26.4 1.4 %collective-permute-start.6 = (bf16[128,256]{1,0:T(8,128)(2,1)S(1)}, bf16[128,256]{1,0:T(8,128)(2,1)S(1)}, u32[]{:S(2)}, u32[]{:S(2)}) collective-permute-start(bf16[128,256]{1,0:T(8,128)(2,1)S(1)} %get-tuple-element.50), channel_id=1, source_target_pairs={{0,1},{1,2},{2,3},{3,0},{4,5},{5,6},{6,7},{7,4},{8,9},{9,10},{10,1... | collective-permute-start | bytes 196616 | tf_op jit(solution)/shard_map/ppermute | solution.py:251
  27.8 2.3 %collective-permute-start.7 = (bf16[128,256]{1,0:T(8,128)(2,1)S(1)}, bf16[128,256]{1,0:T(8,128)(2,1)S(1)}, u32[]{:S(2)}, u32[]{:S(2)}) collective-permute-start(bf16[128,256]{1,0:T(8,128)(2,1)S(1)} %get-tuple-element.51), channel_id=1, source_target_pairs={{0,2},{1,3},{2,0},{3,1},{4,6},{5,7},{6,4},{7,5},{8,10},{9,11},{10,... | collective-permute-start | bytes 196616 | tf_op jit(solution)/shard_map/ppermute | solution.py:251
  30.1 1.1 %collective-permute-start.8 = (bf16[128,256]{1,0:T(8,128)(2,1)S(1)}, bf16[128,256]{1,0:T(8,128)(2,1)S(1)}, u32[]{:S(2)}, u32[]{:S(2)}) collective-permute-start(bf16[128,256]{1,0:T(8,128)(2,1)S(1)} %get-tuple-element.52), channel_id=1, source_target_pairs={{0,3},{1,0},{2,1},{3,2},{4,7},{5,4},{6,5},{7,6},{8,11},{9,8},{10,9... | collective-permute-start | bytes 196616 | tf_op jit(solution)/shard_map/ppermute | solution.py:251
  31.1 0.8 %collective-permute-done.6.refs_4_.refs_5_ = bf16[128,256]{1,0:T(8,128)(2,1)S(1)} collective-permute-done((bf16[128,256]{1,0:T(8,128)(2,1)S(1)}, bf16[128,256]{1,0:T(8,128)(2,1)S(1)}, u32[]{:S(2)}, u32[]{:S(2)}) %collective-permute-start.6) | collective-permute-done | bytes 65568 | tf_op jit(solution)/shard_map/ppermute | solution.py:251
  31.9 3.2 %collective-permute-done.7.refs_6_.refs_7_ = bf16[128,256]{1,0:T(8,128)(2,1)S(1)} collective-permute-done((bf16[128,256]{1,0:T(8,128)(2,1)S(1)}, bf16[128,256]{1,0:T(8,128)(2,1)S(1)}, u32[]{:S(2)}, u32[]{:S(2)}) %collective-permute-start.7) | collective-permute-done | bytes 65568 | tf_op jit(solution)/shard_map/ppermute | solution.py:251
  35.1 0.0 collective-permute-done.8.refs_5_.refs_4_
  35.1 0.0 collective-permute-done.5.got.got_2
  35.2 1.3 %collective-permute-start.9 = (bf16[128,1024]{1,0:T(8,128)(2,1)S(1)}, bf16[128,1024]{1,0:T(8,128)(2,1)S(1)}, u32[]{:S(2)}, u32[]{:S(2)}) collective-permute-start(bf16[128,1024]{1,0:T(8,128)(2,1)S(1)} %get-tuple-element.54), channel_id=1, source_target_pairs={{20,28},{21,29},{22,30},{23,31}} | collective-permute-start | bytes 786440 | tf_op jit(solution)/shard_map/ppermute | solution.py:248
  36.4 7.3 %collective-permute-done.9.got_3.got = bf16[128,1024]{1,0:T(8,128)(2,1)S(1)} collective-permute-done((bf16[128,1024]{1,0:T(8,128)(2,1)S(1)}, bf16[128,1024]{1,0:T(8,128)(2,1)S(1)}, u32[]{:S(2)}, u32[]{:S(2)}) %collective-permute-start.9) | collective-permute-done | bytes 262176 | tf_op jit(solution)/shard_map/ppermute | solution.py:248
  43.8 1.3 %collective-permute-start.10 = (bf16[128,1024]{1,0:T(8,128)(2,1)S(1)}, bf16[128,1024]{1,0:T(8,128)(2,1)S(1)}, u32[]{:S(2)}, u32[]{:S(2)}) collective-permute-start(bf16[128,1024]{1,0:T(8,128)(2,1)S(1)} %shard_map.83), channel_id=1, source_target_pairs={{4,0},{12,8},{20,16},{28,24},{5,1},{13,9},{21,17},{29,25},{6,2},{1... | collective-permute-start | bytes 786440 | tf_op jit(solution)/shard_map/ppermute | solution.py:248
  45.2 0.5 shard_map.84.high_mid
  45.7 0.6 collective-permute-done.10.down
  46.3 1.4 %shard_map.85 = (bf16[128,1024]{1,0:T(8,128)(2,1)S(1)}, f32[128,1024]{1,0:T(8,128)S(1)}, f32[128,1024]{1,0:T(8,128)}) custom-call(bf16[4,1024,1024]{2,1,0:T(8,128)(2,1)S(1)} %get-tuple-element.33.weights, f32[4,1024]{1,0:T(4,128)S(1)} %copy-done.1, f32[128,1024]{1,0:T(8,128)S(1)} %copy-done, f32[128,1024]{1,0:T(8,128)S(1)} %get-tuple-element.37.one, ...), custom_call_target="tpu_custom_call" | custom-call | flops 805306368 | bytes 12337152 | tf_op jit(solution)/shard_map/pallas_call | solution.py:20
  47.7 3.6 %collective-permute-start.12 = (bf16[128,1024]{1,0:T(8,128)(2,1)S(1)}, bf16[128,1024]{1,0:T(8,128)(2,1)S(1)}, u32[]{:S(2)}, u32[]{:S(2)}) collective-permute-start(bf16[128,1024]{1,0:T(8,128)(2,1)S(1)} %get-tuple-element.58.left.refs_0_), channel_id=1, source_target_pairs={{0,1},{1,2},{2,3},{4,5},{5,6},{6,7},{8,9},{9,10},{10,11},{12,13},{... | collective-permute-start | bytes 786440 | tf_op jit(solution)/shard_map/ppermute | solution.py:357
  51.3 1.3 %collective-permute-start.14 = (bf16[128,1024]{1,0:T(8,128)(2,1)S(1)}, bf16[128,1024]{1,0:T(8,128)(2,1)S(1)}, u32[]{:S(2)}, u32[]{:S(2)}) collective-permute-start(bf16[128,1024]{1,0:T(8,128)(2,1)S(1)} %get-tuple-element.58.left.refs_0_), channel_id=1, source_target_pairs={{1,0},{2,1},{3,2},{5,4},{6,5},{7,6},{9,8},{10,9},{11,10},{13,12},{... | collective-permute-start | bytes 786440 | tf_op jit(solution)/shard_map/ppermute | solution.py:357
  52.6 5.1 %collective-permute-start.11 = (bf16[128,1024]{1,0:T(8,128)(2,1)S(1)}, bf16[128,1024]{1,0:T(8,128)(2,1)S(1)}, u32[]{:S(2)}, u32[]{:S(2)}) collective-permute-start(bf16[128,1024]{1,0:T(8,128)(2,1)S(1)} %get-tuple-element.58.left.refs_0_), channel_id=1, source_target_pairs={{0,3},{3,0},{4,7},{7,4},{8,11},{11,8},{12,15},{15,12},{16,19},{19,... | collective-permute-start | bytes 786440 | tf_op jit(solution)/shard_map/ppermute | solution.py:357
  57.6 0.0 collective-permute-done.12.refs_1_
  57.7 0.7 collective-permute-start.13
  58.3 2.0 %collective-permute-done.14.refs_2_ = bf16[128,1024]{1,0:T(8,128)(2,1)S(1)} collective-permute-done((bf16[128,1024]{1,0:T(8,128)(2,1)S(1)}, bf16[128,1024]{1,0:T(8,128)(2,1)S(1)}, u32[]{:S(2)}, u32[]{:S(2)}) %collective-permute-start.14) | collective-permute-done | bytes 262176 | tf_op jit(solution)/shard_map/ppermute | solution.py:357
  60.4 1.3 %collective-permute-start.15 = (bf16[128,1024]{1,0:T(8,128)(2,1)S(1)}, bf16[128,1024]{1,0:T(8,128)(2,1)S(1)}, u32[]{:S(2)}, u32[]{:S(2)}) collective-permute-start(bf16[128,1024]{1,0:T(8,128)(2,1)S(1)} %collective-permute-done.14.refs_2_), channel_id=1, source_target_pairs={{1,0},{2,1},{5,4},{6,5},{9,8},{10,9},{13,12},{14,13},{17,16},{18,1... | collective-permute-start | bytes 786440 | tf_op jit(solution)/shard_map/ppermute | solution.py:357
  61.6 1.3 %shard_map.86 = f32[128,1024]{1,0:T(8,128)} custom-call(bf16[4,1024,1024]{2,1,0:T(8,128)(2,1)S(1)} %get-tuple-element.33.weights, f32[4,1024]{1,0:T(4,128)S(1)} %copy-done.1, bf16[128,1024]{1,0:T(8,128)(2,1)S(1)} %get-tuple-element.58.left.refs_0_, f32[128,1024]{1,0:T(8,128)S(1)} %get-tuple-element.59.state), custom_call_target="tpu_custom_call" | custom-call | flops 268435456 | bytes 9191424 | tf_op jit(solution)/shard_map/pallas_call | solution.py:20
  62.9 1.3 %shard_map.87.refs_8_ = f32[1024,256]{1,0:T(8,128)S(1)} custom-call(bf16[4,1024,1024]{2,1,0:T(8,128)(2,1)S(1)} %get-tuple-element.33.weights, f32[4,1024]{1,0:T(4,128)S(1)} %copy-done.1, bf16[128,1024]{1,0:T(8,128)(2,1)S(1)} %get-tuple-element.58.left.refs_0_, bf16[128,1024]{1,0:T(8,128)(2,1)S(1)} %collective-permute-done.12.refs_1_, ...), custom_call_target="tpu_custom_call" | custom-call | flops 402653184 | bytes 9388032 | tf_op jit(solution)/shard_map/pallas_call | solution.py:20
  64.2 2.9 %collective-permute-done.11.refs_0_.refs_1_ = bf16[128,1024]{1,0:T(8,128)(2,1)S(1)} collective-permute-done((bf16[128,1024]{1,0:T(8,128)(2,1)S(1)}, bf16[128,1024]{1,0:T(8,128)(2,1)S(1)}, u32[]{:S(2)}, u32[]{:S(2)}) %collective-permute-start.11) | collective-permute-done | bytes 262176 | tf_op jit(solution)/shard_map/ppermute | solution.py:357
  67.1 0.0 collective-permute-done.13.refs_2_
  67.1 6.6 %collective-permute-done.15.refs_3_ = bf16[128,1024]{1,0:T(8,128)(2,1)S(1)} collective-permute-done((bf16[128,1024]{1,0:T(8,128)(2,1)S(1)}, bf16[128,1024]{1,0:T(8,128)(2,1)S(1)}, u32[]{:S(2)}, u32[]{:S(2)}) %collective-permute-start.15) | collective-permute-done | bytes 262176 | tf_op jit(solution)/shard_map/ppermute | solution.py:357
  73.6 2.3 %shard_map.88 = f32[1024,256]{1,0:T(8,128)} custom-call(bf16[4,1024,1024]{2,1,0:T(8,128)(2,1)S(1)} %get-tuple-element.33.weights, f32[4,1024]{1,0:T(4,128)S(1)} %copy-done.1, bf16[128,1024]{1,0:T(8,128)(2,1)S(1)} %collective-permute-done.11.refs_0_.refs_1_, bf16[128,1024]{1,0:T(8,128)(2,1)S(1)} %collective-permute-done.11.refs_0_.refs_1_, ...), custom_call_target="tpu_custom_call" | custom-call | flops 536870912 | bytes 10764288 | tf_op jit(solution)/shard_map/pallas_call | solution.py:20
  (5 shorter events, 0.1 us)
Async XLA Ops:
  0.6 7.3 %copy-start.1 = (f32[4,1024]{1,0:T(4,128)S(1)}, f32[4,1024]{1,0:T(4,128)}, u32[]{:S(2)}) copy-start(f32[4,1024]{1,0:T(4,128)} %biases.17) | copy-start | bytes 49156
  0.6 7.3 %copy-start = (f32[128,1024]{1,0:T(8,128)S(1)}, f32[128,1024]{1,0:T(8,128)}, u32[]{:S(2)}) copy-start(f32[128,1024]{1,0:T(8,128)} %inputs.5) | copy-start | bytes 1572868
  0.7 1.1 %copy-start.2 = (f32[1,128,1024]{2,1,0:T(8,128)S(1)}, f32[1,128,1024]{2,1,0:T(8,128)}, u32[]{:S(2)}) copy-start(f32[1,128,1024]{2,1,0:T(8,128)} %param.6) | copy-start | bytes 1572868
  1.8 4.8 %collective-permute-start = (bf16[128,1024]{1,0:T(8,128)(2,1)S(1)}, bf16[128,1024]{1,0:T(8,128)(2,1)S(1)}, u32[]{:S(2)}, u32[]{:S(2)}) collective-permute-start(bf16[128,1024]{1,0:T(8,128)(2,1)S(1)} %shard_map.76), channel_id=1, source_target_pairs={{0,4},{4,8},{8,12},{12,16},{16,20},{20,24},{24,28},{1,5},{5,9},{9,... | collective-permute-start | bytes 786440 | tf_op jit(solution)/shard_map/ppermute | solution.py:248
  6.6 19.1 %collective-permute-start.3 = (bf16[1024,1024]{1,0:T(8,128)(2,1)S(1)}, bf16[1024,1024]{1,0:T(8,128)(2,1)S(1)}, u32[]{:S(2)}, u32[]{:S(2)}) collective-permute-start(bf16[1024,1024]{1,0:T(8,128)(2,1)S(1)} %get-tuple-element.40), channel_id=1, source_target_pairs={{0,4},{8,12},{16,20},{24,28},{1,5},{9,13},{17,21},{25,29},{2,6},{1... | collective-permute-start | bytes 6291464 | tf_op jit(solution)/shard_map/ppermute | solution.py:248
  7.9 11.7 %copy-start.3 = (bf16[1,128,1024]{2,1,0:T(8,128)(2,1)S(1)}, bf16[1,128,1024]{2,1,0:T(8,128)(2,1)}, u32[]{:S(2)}) copy-start(bf16[1,128,1024]{2,1,0:T(8,128)(2,1)} %param.9) | copy-start | bytes 786436
  9.5 6.6 %collective-permute-start.1 = (bf16[144,1024]{1,0:T(8,128)(2,1)S(1)}, bf16[144,1024]{1,0:T(8,128)(2,1)S(1)}, u32[]{:S(2)}, u32[]{:S(2)}) collective-permute-start(bf16[144,1024]{1,0:T(8,128)(2,1)S(1)} %get-tuple-element.36), channel_id=1, source_target_pairs={{0,4},{4,8},{8,12},{12,16},{16,20},{20,24},{24,28},{1,5},{5,9},{9,... | collective-permute-start | bytes 884744 | tf_op jit(solution)/shard_map/ppermute | solution.py:248
  17.7 2.1 %collective-permute-start.2 = (bf16[128,1024]{1,0:T(8,128)(2,1)S(1)}, bf16[128,1024]{1,0:T(8,128)(2,1)S(1)}, u32[]{:S(2)}, u32[]{:S(2)}) collective-permute-start(bf16[128,1024]{1,0:T(8,128)(2,1)S(1)} %get-tuple-element.38), channel_id=1, source_target_pairs={{4,12},{5,13},{6,14},{7,15}} | collective-permute-start | bytes 786440 | tf_op jit(solution)/shard_map/ppermute | solution.py:248
  18.4 7.4 %collective-permute-start.4 = (bf16[128,1024]{1,0:T(8,128)(2,1)S(1)}, bf16[128,1024]{1,0:T(8,128)(2,1)S(1)}, u32[]{:S(2)}, u32[]{:S(2)}) collective-permute-start(bf16[128,1024]{1,0:T(8,128)(2,1)S(1)} %get-tuple-element.42), channel_id=1, source_target_pairs={{0,4},{8,12},{16,20},{24,28},{1,5},{9,13},{17,21},{25,29},{2,6},{1... | collective-permute-start | bytes 786440 | tf_op jit(solution)/shard_map/ppermute | solution.py:248
  25.7 9.4 %collective-permute-start.5 = (bf16[128,1024]{1,0:T(8,128)(2,1)S(1)}, bf16[128,1024]{1,0:T(8,128)(2,1)S(1)}, u32[]{:S(2)}, u32[]{:S(2)}) collective-permute-start(bf16[128,1024]{1,0:T(8,128)(2,1)S(1)} %get-tuple-element.48), channel_id=1, source_target_pairs={{12,20},{13,21},{14,22},{15,23}} | collective-permute-start | bytes 786440 | tf_op jit(solution)/shard_map/ppermute | solution.py:248
  26.4 5.5 %collective-permute-start.6 = (bf16[128,256]{1,0:T(8,128)(2,1)S(1)}, bf16[128,256]{1,0:T(8,128)(2,1)S(1)}, u32[]{:S(2)}, u32[]{:S(2)}) collective-permute-start(bf16[128,256]{1,0:T(8,128)(2,1)S(1)} %get-tuple-element.50), channel_id=1, source_target_pairs={{0,1},{1,2},{2,3},{3,0},{4,5},{5,6},{6,7},{7,4},{8,9},{9,10},{10,1... | collective-permute-start | bytes 196616 | tf_op jit(solution)/shard_map/ppermute | solution.py:251
  27.8 7.4 %collective-permute-start.7 = (bf16[128,256]{1,0:T(8,128)(2,1)S(1)}, bf16[128,256]{1,0:T(8,128)(2,1)S(1)}, u32[]{:S(2)}, u32[]{:S(2)}) collective-permute-start(bf16[128,256]{1,0:T(8,128)(2,1)S(1)} %get-tuple-element.51), channel_id=1, source_target_pairs={{0,2},{1,3},{2,0},{3,1},{4,6},{5,7},{6,4},{7,5},{8,10},{9,11},{10,... | collective-permute-start | bytes 196616 | tf_op jit(solution)/shard_map/ppermute | solution.py:251
  30.1 5.1 %collective-permute-start.8 = (bf16[128,256]{1,0:T(8,128)(2,1)S(1)}, bf16[128,256]{1,0:T(8,128)(2,1)S(1)}, u32[]{:S(2)}, u32[]{:S(2)}) collective-permute-start(bf16[128,256]{1,0:T(8,128)(2,1)S(1)} %get-tuple-element.52), channel_id=1, source_target_pairs={{0,3},{1,0},{2,1},{3,2},{4,7},{5,4},{6,5},{7,6},{8,11},{9,8},{10,9... | collective-permute-start | bytes 196616 | tf_op jit(solution)/shard_map/ppermute | solution.py:251
  35.2 8.6 %collective-permute-start.9 = (bf16[128,1024]{1,0:T(8,128)(2,1)S(1)}, bf16[128,1024]{1,0:T(8,128)(2,1)S(1)}, u32[]{:S(2)}, u32[]{:S(2)}) collective-permute-start(bf16[128,1024]{1,0:T(8,128)(2,1)S(1)} %get-tuple-element.54), channel_id=1, source_target_pairs={{20,28},{21,29},{22,30},{23,31}} | collective-permute-start | bytes 786440 | tf_op jit(solution)/shard_map/ppermute | solution.py:248
  43.8 2.4 %collective-permute-start.10 = (bf16[128,1024]{1,0:T(8,128)(2,1)S(1)}, bf16[128,1024]{1,0:T(8,128)(2,1)S(1)}, u32[]{:S(2)}, u32[]{:S(2)}) collective-permute-start(bf16[128,1024]{1,0:T(8,128)(2,1)S(1)} %shard_map.83), channel_id=1, source_target_pairs={{4,0},{12,8},{20,16},{28,24},{5,1},{13,9},{21,17},{29,25},{6,2},{1... | collective-permute-start | bytes 786440 | tf_op jit(solution)/shard_map/ppermute | solution.py:248
  47.7 10.0 %collective-permute-start.12 = (bf16[128,1024]{1,0:T(8,128)(2,1)S(1)}, bf16[128,1024]{1,0:T(8,128)(2,1)S(1)}, u32[]{:S(2)}, u32[]{:S(2)}) collective-permute-start(bf16[128,1024]{1,0:T(8,128)(2,1)S(1)} %get-tuple-element.58.left.refs_0_), channel_id=1, source_target_pairs={{0,1},{1,2},{2,3},{4,5},{5,6},{6,7},{8,9},{9,10},{10,11},{12,13},{... | collective-permute-start | bytes 786440 | tf_op jit(solution)/shard_map/ppermute | solution.py:357
  51.3 9.1 %collective-permute-start.14 = (bf16[128,1024]{1,0:T(8,128)(2,1)S(1)}, bf16[128,1024]{1,0:T(8,128)(2,1)S(1)}, u32[]{:S(2)}, u32[]{:S(2)}) collective-permute-start(bf16[128,1024]{1,0:T(8,128)(2,1)S(1)} %get-tuple-element.58.left.refs_0_), channel_id=1, source_target_pairs={{1,0},{2,1},{3,2},{5,4},{6,5},{7,6},{9,8},{10,9},{11,10},{13,12},{... | collective-permute-start | bytes 786440 | tf_op jit(solution)/shard_map/ppermute | solution.py:357
  52.6 14.5 %collective-permute-start.11 = (bf16[128,1024]{1,0:T(8,128)(2,1)S(1)}, bf16[128,1024]{1,0:T(8,128)(2,1)S(1)}, u32[]{:S(2)}, u32[]{:S(2)}) collective-permute-start(bf16[128,1024]{1,0:T(8,128)(2,1)S(1)} %get-tuple-element.58.left.refs_0_), channel_id=1, source_target_pairs={{0,3},{3,0},{4,7},{7,4},{8,11},{11,8},{12,15},{15,12},{16,19},{19,... | collective-permute-start | bytes 786440 | tf_op jit(solution)/shard_map/ppermute | solution.py:357
  57.7 9.4 %collective-permute-start.13 = (bf16[128,1024]{1,0:T(8,128)(2,1)S(1)}, bf16[128,1024]{1,0:T(8,128)(2,1)S(1)}, u32[]{:S(2)}, u32[]{:S(2)}) collective-permute-start(bf16[128,1024]{1,0:T(8,128)(2,1)S(1)} %collective-permute-done.12.refs_1_), channel_id=1, source_target_pairs={{1,2},{2,3},{5,6},{6,7},{9,10},{10,11},{13,14},{14,15},{17,18},{18... | collective-permute-start | bytes 786440 | tf_op jit(solution)/shard_map/ppermute | solution.py:357
  60.4 13.3 %collective-permute-start.15 = (bf16[128,1024]{1,0:T(8,128)(2,1)S(1)}, bf16[128,1024]{1,0:T(8,128)(2,1)S(1)}, u32[]{:S(2)}, u32[]{:S(2)}) collective-permute-start(bf16[128,1024]{1,0:T(8,128)(2,1)S(1)} %collective-permute-done.14.refs_2_), channel_id=1, source_target_pairs={{1,0},{2,1},{5,4},{6,5},{9,8},{10,9},{13,12},{14,13},{17,16},{18,1... | collective-permute-start | bytes 786440 | tf_op jit(solution)/shard_map/ppermute | solution.py:357

commit v5 on v3

--- a/solution.py
+++ b/solution.py
@@ -218,33 +218,35 @@
     total[...] = gradient(step_size, weights, biases, left, adjoint, deltas, total.shape[1])
 
 
-def far_kernel(step_size, rows, count, weights, biases, pair_weight, pair_bias, total, *refs):
-    far, down, forcings, adjoints = (refs[i * count : (i + 1) * count] for i in range(4))
-    result, state, even, odd, adjoint, deltas = refs[4 * count :]
-    is_odd = lax.axis_index("layer") % 2 == 1
-    places = [slice(i * rows, (i + 1) * rows) for i in range(count)]
-
-    @pl.when(is_odd)
-    def _():
-        for place, source in zip(places, far):
-            odd[place, :] = source[...]
-        for cols in tiles(state.shape[1]):
-            slope = layer_of(odd, pair_weight, pair_bias[0:1, :], cols)
-            for place, added in zip(places, forcings):
-                new = odd[place, cols].astype(F32) + (4.0 * step_size) * slope[place, :] + added[:, cols].astype(F32)
-                state[place, cols] = new
-                even[place, cols] = new.astype(BF16)
-
-    @pl.when(jnp.logical_not(is_odd))
-    def _():
-        for place, source in zip(places, down):
+def even_kernel(step_size, rows, count, weights, biases, total, *refs):
+    starts, adjoints = refs[:count], refs[count : 2 * count]
+    result, state, even, odd, adjoint, deltas = refs[2 * count :]
+    is_even = lax.axis_index("layer") % 2 == 0
+
+    @pl.when(jnp.logical_not(is_even))
+    def _():
+        result[...] = total[...]
+
+    @pl.when(is_even)
+    def _():
+        for i, (source, columns) in enumerate(zip(starts, adjoints)):
+            place = slice(i * rows, (i + 1) * rows)
             state[place, :] = source[...].astype(F32)
             even[place, :] = source[...]
-
-    for place, source in zip(places, adjoints):
-        adjoint[place, :] = source[...]
-    run_layers((0, 1, 2), step_size, weights, biases, state, (even, odd))
-    result[...] = total[...] + gradient(step_size, weights, biases, odd, adjoint, deltas, result.shape[1])
+            adjoint[place, :] = columns[...]
+        run_layers((0, 1, 2), step_size, weights, biases, state, (even, odd))
+        result[...] = total[...] + gradient(step_size, weights, biases, odd, adjoint, deltas, result.shape[1])
+
+
+def odd_kernel(step_size, count, weights, biases, total, *refs):
+    lefts, adjoints = refs[:count], refs[count : 2 * count]
+    result, deltas = refs[2 * count :]
+    result[...] = total[...]
+
+    @pl.when(lax.axis_index("layer") % 2 == 1)
+    def _():
+        for left, adjoint in zip(lefts, adjoints):
+            result[...] += gradient(step_size, weights, biases, left, adjoint, deltas, result.shape[1])
 
 
 def single_kernel(factor, weights, biases, got, added, out):
@@ -308,7 +310,6 @@
         scratch=[pltpu.VMEM((rows, depth), F32)] + rounded, flops=4 * layer_flops,
     )
     pair_forcing = along(forcing_sent, up_pair)
-    far_forcings = [across(forcing_sent, up_pair, by) for by in range(1, parts)]
 
     def two_steps(top, pairs, chosen, last=False, beside=()):
         got, *_ = lax.optimization_barrier((along(top, pairs), *beside))
@@ -355,10 +356,10 @@
         top_1, [(4 * m - 1, 4 * m + 1) for m in range(1, groups)], lambda slot, group: (slot == 1) & (group > 0),
         beside=adjoints,
     )
-    top_2, *far_forcings = lax.optimization_barrier((top_2, *far_forcings))
     got_3, mid_3 = two_steps(
         top_2, [(4 * m + 1, 4 * m + 3) for m in range(1, groups)], lambda slot, group: (slot == 3) & (group > 0), True
     )
+    top_last = top_2
     left, state, coarse_states = finish((got_1, got_2, got_3), (mid_1, mid_2, mid_3))
     if groups > 2:
         late = lambda slot, group: group > 1
@@ -369,11 +370,11 @@
         for m in range(2, groups):
             new = single(16.0 * step_size, along(solved.astype(BF16), [(4 * m - 1, 4 * m + 3)]), base)
             solved = jnp.where(here == 4 * m + 3, new, solved)
-        new_2, new_mid_2, top_2 = two_steps(
+        new_2, new_mid_2, top_last = two_steps(
             jnp.where(slot == 3, solved.astype(BF16), top_2), [(4 * m - 1, 4 * m + 1) for m in range(2, groups)], lambda slot, group: (slot == 1) & (group > 1)
         )
         new_3, new_mid_3 = two_steps(
-            top_2, [(4 * m + 1, 4 * m + 3) for m in range(2, groups)], lambda slot, group: (slot == 3) & (group > 1), True
+            top_last, [(4 * m + 1, 4 * m + 3) for m in range(2, groups)], lambda slot, group: (slot == 3) & (group > 1), True
         )
         mids = [
             call(functools.partial(pick_kernel, late), kept(inputs), new, old)
@@ -382,25 +383,28 @@
         gots = [jnp.where(group > 1, new, old) for new, old in ((new_2, got_2), (new_3, got_3))]
         left, state, coarse_early = finish((got_1, *gots), (mid_1, *mids))
         coarse_states = jnp.where(slot == 3, solved - relaxed_out, coarse_states)
-    leaps = [(0, 1)] + [(i, i + 2) for i in range(1, blocks - 2, 2)]
-    far = [across(top_2, leaps, by) for by in range(1, parts)]
-    left, *far = lax.optimization_barrier((left, *far))
-    far_down = [along(state_far, down_pair) for state_far in far]
+    far = [across(top_last, [(0, 0)] + [(i, i + 1) for i in range(1, blocks - 1, 2)], by) for by in range(1, parts)]
+    odd_lefts = [across(left, [(i, i) for i in range(1, blocks, 2)], by) for by in range(1, parts)]
     new_states = call(
         functools.partial(last_kernel, step_size), plain((rows, depth), F32),
         held_weights, biases, left, state, flops=layer_flops,
     )
+    deltas = pltpu.VMEM((rows, width), BF16)
     total = call(
         functools.partial(own_gradient_kernel, step_size), pltpu.VMEM((depth, width), F32),
-        held_weights, biases, left, adjoints[0], scratch=[pltpu.VMEM((rows, width), BF16)], flops=layer_flops,
+        held_weights, biases, left, adjoints[0], scratch=[deltas], flops=layer_flops // 2,
     )
     others = (parts - 1) * rows
-    weight_grad = call(
-        functools.partial(far_kernel, step_size, rows, parts - 1), plain((depth, width), F32),
-        held_weights, biases, pair_weight, pair_bias, total, *far, *far_down, *far_forcings, *adjoints[1:],
+    total = call(
+        functools.partial(even_kernel, step_size, rows, parts - 1), pltpu.VMEM((depth, width), F32),
+        held_weights, biases, total, *far, *adjoints[1:],
         scratch=[pltpu.VMEM((others, depth), F32)] + [pltpu.VMEM((others, depth), BF16)] * 2
         + [pltpu.VMEM((others, width), BF16)] * 2,
-        flops=6 * (parts - 1) * layer_flops,
+        flops=4 * (parts - 1) * layer_flops,
+    )
+    weight_grad = call(
+        functools.partial(odd_kernel, step_size, parts - 1), plain((depth, width), F32),
+        held_weights, biases, total, *odd_lefts, *adjoints[1:], scratch=[deltas], flops=2 * layer_flops,
     )
     return (new_states[None], coarse_states[None], weight_grad[None])
 

time: 103 us -> 82.1 us (0.80)
  starting transfers between devices: 49.2 us -> 35 us
  waiting for transfers between devices: 35.3 us -> 31.8 us
  Pallas kernels: 16.2 us -> 12.9 us
    ppermute x11 -> x8, starting transfers between devices: 30.9 us -> 18.3 us  [along(): return lax.ppermute(state, 'layer', pairs)]
    ppermute x3, waiting for transfers between devices: 12.5 us -> 5.31 us  [shifted(): lax.ppermute(array, 'dp', [(i, (i + by) % parts) for i in range(parts)])]
    ppermute x6, waiting for transfers between devices: 17 us -> 20.8 us  [across(): return lax.ppermute(state, ('layer', 'dp'), flat)]
    pallas_call x13 -> x14, Pallas kernels: 16.2 us -> 12.9 us  [call(): pl.pallas_call(kernel, out_shape=outs, in_specs=specs or [WHOLE] * len(ar...]
    ppermute x6, starting transfers between devices: 14.3 us -> 12.8 us  [across(): return lax.ppermute(state, ('layer', 'dp'), flat)]
    ppermute x11 -> x8, waiting for transfers between devices: 5.73 us -> 5.72 us  [along(): return lax.ppermute(state, 'layer', pairs)]
  transfers between devices with their start and end apart: 20 -> 17, of which waited for: 9 -> 9; matrix products, arithmetic and copies ran while one was open for 0% -> 0% of each run, Pallas kernels for 10% -> 13%
where the time goes in v5:
time: 82.1 us; the launch traced here: 81.7 us
  starting transfers between devices  35 us (43%)
  waiting for transfers between devices  31.8 us (39%)
  Pallas kernels  12.9 us (16%)
  local copies, waits for them, and re-layouts  1.11 us (1%)
  between operations  0.9 us (1%)
    ppermute x6, waiting for transfers between devices, across(): return lax.ppermute(state, ('layer', 'dp'), flat)  20.8 us
    ppermute x8, starting transfers between devices, along(): return lax.ppermute(state, 'layer', pairs)  18.3 us
    pallas_call x14, Pallas kernels, call(): pl.pallas_call(kernel, out_shape=outs, in_specs=specs or [WHOLE] * len(ar...  12.9 us
    ppermute x6, starting transfers between devices, across(): return lax.ppermute(state, ('layer', 'dp'), flat)  12.8 us
    ppermute x8, waiting for transfers between devices, along(): return lax.ppermute(state, 'layer', pairs)  5.72 us
    ppermute x3, waiting for transfers between devices, shifted(): lax.ppermute(array, 'dp', [(i, (i + by) % parts) for i in range(parts)])  5.31 us
    ppermute x3, starting transfers between devices, shifted(): lax.ppermute(array, 'dp', [(i, (i + by) % parts) for i in range(parts)])  3.83 us
  transfers between devices with their start and end apart: 17, of which 9 were waited for; matrix products, arithmetic and copies ran while one was open for 0% of the time, Pallas kernels for 13%

profile of v5, /device:TPU:9, one launch (start us, length us, event | category | flops | bytes accessed | tf_op | source)
XLA Modules:
  0.0 81.7 jit_solution(100676156912560269)
XLA Ops:
  0.6 0.0 copy-start.1
  0.6 0.0 copy-start
  0.7 0.0 copy-start.2
  0.7 1.1 %copy-done.2 = f32[1,128,1024]{2,1,0:T(8,128)S(1)} copy-done((f32[1,128,1024]{2,1,0:T(8,128)S(1)}, f32[1,128,1024]{2,1,0:T(8,128)}, u32[]{:S(2)}) %copy-start.2) | copy-done | bytes 524312
  1.8 3.7 %collective-permute-start = (bf16[128,1024]{1,0:T(8,128)(2,1)S(1)}, bf16[128,1024]{1,0:T(8,128)(2,1)S(1)}, u32[]{:S(2)}, u32[]{:S(2)}) collective-permute-start(bf16[128,1024]{1,0:T(8,128)(2,1)S(1)} %shard_map.76), channel_id=1, source_target_pairs={{0,4},{4,8},{8,12},{12,16},{16,20},{20,24},{24,28},{1,5},{5,9},{9,... | collective-permute-start | bytes 786440 | tf_op jit(solution)/shard_map/ppermute | solution.py:273
  5.5 3.5 %shard_map.77 = (bf16[4,1024,1024]{2,1,0:T(8,128)(2,1)S(1)}, bf16[1024,1024]{1,0:T(8,128)(2,1)S(1)}) custom-call(bf16[4,1024,1024]{2,1,0:T(8,128)(2,1)} %source), custom_call_target="tpu_custom_call" | custom-call | bytes 8388608 | tf_op jit(solution)/shard_map/pallas_call | solution.py:20
  9.0 0.0 collective-permute-done.got
  9.0 1.3 %collective-permute-start.3 = (bf16[1024,1024]{1,0:T(8,128)(2,1)S(1)}, bf16[1024,1024]{1,0:T(8,128)(2,1)S(1)}, u32[]{:S(2)}, u32[]{:S(2)}) collective-permute-start(bf16[1024,1024]{1,0:T(8,128)(2,1)S(1)} %get-tuple-element.40), channel_id=1, source_target_pairs={{0,4},{8,12},{16,20},{24,28},{1,5},{9,13},{17,21},{25,29},{2,6},{1... | collective-permute-start | bytes 6291464 | tf_op jit(solution)/shard_map/ppermute | solution.py:273
  10.3 0.0 copy-done.1
  10.3 0.0 copy-start.3
  10.3 1.6 %shard_map.78 = (f32[128,1024]{1,0:T(8,128)S(1)}, bf16[144,1024]{1,0:T(8,128)(2,1)S(1)}) custom-call(bf16[4,1024,1024]{2,1,0:T(8,128)(2,1)S(1)} %get-tuple-element.33.weights, f32[4,1024]{1,0:T(4,128)S(1)} %copy-done.1, f32[128,1024]{1,0:T(8,128)S(1)} %copy-done, bf16[128,1024]{1,0:T(8,128)(2,1)S(1)} %collective-permute-done.got), custom_call_target="tpu_custom_call" | custom-call | flops 1073741824 | bytes 9191424 | tf_op jit(solution)/shard_map/pallas_call | solution.py:20
  11.9 4.3 %collective-permute-start.1 = (bf16[144,1024]{1,0:T(8,128)(2,1)S(1)}, bf16[144,1024]{1,0:T(8,128)(2,1)S(1)}, u32[]{:S(2)}, u32[]{:S(2)}) collective-permute-start(bf16[144,1024]{1,0:T(8,128)(2,1)S(1)} %get-tuple-element.36), channel_id=1, source_target_pairs={{0,4},{4,8},{8,12},{12,16},{16,20},{20,24},{24,28},{1,5},{5,9},{9,... | collective-permute-start | bytes 884744 | tf_op jit(solution)/shard_map/ppermute | solution.py:273
  16.2 3.6 %collective-permute-done.1.got = bf16[144,1024]{1,0:T(8,128)(2,1)S(1)} collective-permute-done((bf16[144,1024]{1,0:T(8,128)(2,1)S(1)}, bf16[144,1024]{1,0:T(8,128)(2,1)S(1)}, u32[]{:S(2)}, u32[]{:S(2)}) %collective-permute-start.1) | collective-permute-done | bytes 294944 | tf_op jit(solution)/shard_map/ppermute | solution.py:273
  19.8 1.5 %shard_map.79 = (f32[128,1024]{1,0:T(8,128)S(1)}, f32[128,1024]{1,0:T(8,128)S(1)}, f32[8,1024]{1,0:T(8,128)S(1)}, bf16[128,1024]{1,0:T(8,128)(2,1)S(1)}, bf16[128,1024]{1,0:T(8,128)(2,1)S(1)}) custom-call(bf16[4,1024,1024]{2,1,0:T(8,128)(2,1)S(1)} %get-tuple-element.33.weights, f32[4,1024]{1,0:T(4,128)S(1)} %copy-done.1, f32[128,1024]{1,0:T(8,128)S(1)} %copy-done, ...), custom_call_target="tpu_custom_call" | custom-call | flops 1073741824 | bytes 9224192 | tf_op jit(solution)/shard_map/pallas_call | solution.py:20
  21.4 4.0 %collective-permute-start.2 = (bf16[128,1024]{1,0:T(8,128)(2,1)S(1)}, bf16[128,1024]{1,0:T(8,128)(2,1)S(1)}, u32[]{:S(2)}, u32[]{:S(2)}) collective-permute-start(bf16[128,1024]{1,0:T(8,128)(2,1)S(1)} %get-tuple-element.38.before), channel_id=1, source_target_pairs={{4,12},{5,13},{6,14},{7,15}} | collective-permute-start | bytes 786440 | tf_op jit(solution)/shard_map/ppermute | solution.py:273
  25.4 1.3 %collective-permute-start.4 = (bf16[128,1024]{1,0:T(8,128)(2,1)S(1)}, bf16[128,1024]{1,0:T(8,128)(2,1)S(1)}, u32[]{:S(2)}, u32[]{:S(2)}) collective-permute-start(bf16[128,1024]{1,0:T(8,128)(2,1)S(1)} %get-tuple-element.42), channel_id=1, source_target_pairs={{0,4},{8,12},{16,20},{24,28},{1,5},{9,13},{17,21},{25,29},{2,6},{1... | collective-permute-start | bytes 786440 | tf_op jit(solution)/shard_map/ppermute | solution.py:273
  26.8 1.9 %collective-permute-done.2.got.got_1 = bf16[128,1024]{1,0:T(8,128)(2,1)S(1)} collective-permute-done((bf16[128,1024]{1,0:T(8,128)(2,1)S(1)}, bf16[128,1024]{1,0:T(8,128)(2,1)S(1)}, u32[]{:S(2)}, u32[]{:S(2)}) %collective-permute-start.2) | collective-permute-done | bytes 262176 | tf_op jit(solution)/shard_map/ppermute | solution.py:273
  28.7 0.1 collective-permute-done.4.pair_forcing
  28.8 0.0 collective-permute-done.3.pair_weight
  28.8 0.7 collective-permute-start.5
  29.5 1.4 %collective-permute-start.6 = (bf16[128,256]{1,0:T(8,128)(2,1)S(1)}, bf16[128,256]{1,0:T(8,128)(2,1)S(1)}, u32[]{:S(2)}, u32[]{:S(2)}) collective-permute-start(bf16[128,256]{1,0:T(8,128)(2,1)S(1)} %get-tuple-element.50), channel_id=1, source_target_pairs={{0,1},{1,2},{2,3},{3,0},{4,5},{5,6},{6,7},{7,4},{8,9},{9,10},{10,1... | collective-permute-start | bytes 196616 | tf_op jit(solution)/shard_map/ppermute | solution.py:280
  30.9 1.1 %collective-permute-start.7 = (bf16[128,256]{1,0:T(8,128)(2,1)S(1)}, bf16[128,256]{1,0:T(8,128)(2,1)S(1)}, u32[]{:S(2)}, u32[]{:S(2)}) collective-permute-start(bf16[128,256]{1,0:T(8,128)(2,1)S(1)} %get-tuple-element.51), channel_id=1, source_target_pairs={{0,2},{1,3},{2,0},{3,1},{4,6},{5,7},{6,4},{7,5},{8,10},{9,11},{10,... | collective-permute-start | bytes 196616 | tf_op jit(solution)/shard_map/ppermute | solution.py:280
  32.0 1.4 %collective-permute-start.8 = (bf16[128,256]{1,0:T(8,128)(2,1)S(1)}, bf16[128,256]{1,0:T(8,128)(2,1)S(1)}, u32[]{:S(2)}, u32[]{:S(2)}) collective-permute-start(bf16[128,256]{1,0:T(8,128)(2,1)S(1)} %get-tuple-element.52), channel_id=1, source_target_pairs={{0,3},{1,0},{2,1},{3,2},{4,7},{5,4},{6,5},{7,6},{8,11},{9,8},{10,9... | collective-permute-start | bytes 196616 | tf_op jit(solution)/shard_map/ppermute | solution.py:280
  33.4 0.0 collective-permute-done.6.refs_3_
  33.4 1.7 %collective-permute-done.7.refs_4_ = bf16[128,256]{1,0:T(8,128)(2,1)S(1)} collective-permute-done((bf16[128,256]{1,0:T(8,128)(2,1)S(1)}, bf16[128,256]{1,0:T(8,128)(2,1)S(1)}, u32[]{:S(2)}, u32[]{:S(2)}) %collective-permute-start.7) | collective-permute-done | bytes 65568 | tf_op jit(solution)/shard_map/ppermute | solution.py:280
  35.1 3.6 %collective-permute-done.8.refs_5_ = bf16[128,256]{1,0:T(8,128)(2,1)S(1)} collective-permute-done((bf16[128,256]{1,0:T(8,128)(2,1)S(1)}, bf16[128,256]{1,0:T(8,128)(2,1)S(1)}, u32[]{:S(2)}, u32[]{:S(2)}) %collective-permute-start.8) | collective-permute-done | bytes 65568 | tf_op jit(solution)/shard_map/ppermute | solution.py:280
  38.7 0.0 collective-permute-done.5.got.got_2
  38.7 0.7 collective-permute-start.9
  39.4 0.0 collective-permute-done.9.got_3.got
  39.5 2.4 %collective-permute-start.10 = (bf16[128,1024]{1,0:T(8,128)(2,1)S(1)}, bf16[128,1024]{1,0:T(8,128)(2,1)S(1)}, u32[]{:S(2)}, u32[]{:S(2)}) collective-permute-start(bf16[128,1024]{1,0:T(8,128)(2,1)S(1)} %shard_map.83), channel_id=1, source_target_pairs={{4,0},{12,8},{20,16},{28,24},{5,1},{13,9},{21,17},{29,25},{6,2},{1... | collective-permute-start | bytes 786440 | tf_op jit(solution)/shard_map/ppermute | solution.py:273
  41.9 1.3 %collective-permute-start.11 = (bf16[128,1024]{1,0:T(8,128)(2,1)S(1)}, bf16[128,1024]{1,0:T(8,128)(2,1)S(1)}, u32[]{:S(2)}, u32[]{:S(2)}) collective-permute-start(bf16[128,1024]{1,0:T(8,128)(2,1)S(1)} %get-tuple-element.54.before), channel_id=1, source_target_pairs={{0,1},{1,2},{2,3},{3,0},{4,9},{5,10},{6,11},{7,8},{12,17},{13,18},... | collective-permute-start | bytes 786440 | tf_op jit(solution)/shard_map/ppermute | solution.py:277
  43.2 1.3 %collective-permute-start.12 = (bf16[128,1024]{1,0:T(8,128)(2,1)S(1)}, bf16[128,1024]{1,0:T(8,128)(2,1)S(1)}, u32[]{:S(2)}, u32[]{:S(2)}) collective-permute-start(bf16[128,1024]{1,0:T(8,128)(2,1)S(1)} %get-tuple-element.54.before), channel_id=1, source_target_pairs={{0,2},{1,3},{2,0},{3,1},{4,10},{5,11},{6,8},{7,9},{12,18},{13,19},... | collective-permute-start | bytes 786440 | tf_op jit(solution)/shard_map/ppermute | solution.py:277
  44.5 1.3 %collective-permute-start.13 = (bf16[128,1024]{1,0:T(8,128)(2,1)S(1)}, bf16[128,1024]{1,0:T(8,128)(2,1)S(1)}, u32[]{:S(2)}, u32[]{:S(2)}) collective-permute-start(bf16[128,1024]{1,0:T(8,128)(2,1)S(1)} %get-tuple-element.54.before), channel_id=1, source_target_pairs={{0,3},{1,0},{2,1},{3,2},{4,11},{5,8},{6,9},{7,10},{12,19},{13,16},... | collective-permute-start | bytes 786440 | tf_op jit(solution)/shard_map/ppermute | solution.py:277
  45.8 0.0 collective-permute-done.10.down
  45.9 1.4 %shard_map.85 = (bf16[128,1024]{1,0:T(8,128)(2,1)S(1)}, f32[128,1024]{1,0:T(8,128)S(1)}, f32[128,1024]{1,0:T(8,128)}) custom-call(bf16[4,1024,1024]{2,1,0:T(8,128)(2,1)S(1)} %get-tuple-element.33.weights, f32[4,1024]{1,0:T(4,128)S(1)} %copy-done.1, f32[128,1024]{1,0:T(8,128)S(1)} %copy-done, f32[128,1024]{1,0:T(8,128)S(1)} %get-tuple-element.37.one, ...), custom_call_target="tpu_custom_call" | custom-call | flops 805306368 | bytes 12337152 | tf_op jit(solution)/shard_map/pallas_call | solution.py:20
  47.3 2.2 %collective-permute-start.14 = (bf16[128,1024]{1,0:T(8,128)(2,1)S(1)}, bf16[128,1024]{1,0:T(8,128)(2,1)S(1)}, u32[]{:S(2)}, u32[]{:S(2)}) collective-permute-start(bf16[128,1024]{1,0:T(8,128)(2,1)S(1)} %get-tuple-element.58.left), channel_id=1, source_target_pairs={{4,5},{5,6},{6,7},{7,4},{12,13},{13,14},{14,15},{15,12},{20,21},{2... | collective-permute-start | bytes 786440 | tf_op jit(solution)/shard_map/ppermute | solution.py:277
  49.5 4.9 %collective-permute-start.15 = (bf16[128,1024]{1,0:T(8,128)(2,1)S(1)}, bf16[128,1024]{1,0:T(8,128)(2,1)S(1)}, u32[]{:S(2)}, u32[]{:S(2)}) collective-permute-start(bf16[128,1024]{1,0:T(8,128)(2,1)S(1)} %get-tuple-element.58.left), channel_id=1, source_target_pairs={{4,6},{5,7},{6,4},{7,5},{12,14},{13,15},{14,12},{15,13},{20,22},{2... | collective-permute-start | bytes 786440 | tf_op jit(solution)/shard_map/ppermute | solution.py:277
  54.3 0.7 shard_map.87.total
  55.0 1.3 %shard_map.86 = f32[128,1024]{1,0:T(8,128)} custom-call(bf16[4,1024,1024]{2,1,0:T(8,128)(2,1)S(1)} %get-tuple-element.33.weights, f32[4,1024]{1,0:T(4,128)S(1)} %copy-done.1, bf16[128,1024]{1,0:T(8,128)(2,1)S(1)} %get-tuple-element.58.left, f32[128,1024]{1,0:T(8,128)S(1)} %get-tuple-element.59.state), custom_call_target="tpu_custom_call" | custom-call | flops 268435456 | bytes 9191424 | tf_op jit(solution)/shard_map/pallas_call | solution.py:20
  56.3 0.0 collective-permute-done.11.refs_0_
  56.3 1.9 %collective-permute-start.16 = (bf16[128,1024]{1,0:T(8,128)(2,1)S(1)}, bf16[128,1024]{1,0:T(8,128)(2,1)S(1)}, u32[]{:S(2)}, u32[]{:S(2)}) collective-permute-start(bf16[128,1024]{1,0:T(8,128)(2,1)S(1)} %get-tuple-element.58.left), channel_id=1, source_target_pairs={{4,7},{5,4},{6,5},{7,6},{12,15},{13,12},{14,13},{15,14},{20,23},{2... | collective-permute-start | bytes 786440 | tf_op jit(solution)/shard_map/ppermute | solution.py:277
  58.2 13.4 %collective-permute-done.12.refs_1_ = bf16[128,1024]{1,0:T(8,128)(2,1)S(1)} collective-permute-done((bf16[128,1024]{1,0:T(8,128)(2,1)S(1)}, bf16[128,1024]{1,0:T(8,128)(2,1)S(1)}, u32[]{:S(2)}, u32[]{:S(2)}) %collective-permute-start.12) | collective-permute-done | bytes 262176 | tf_op jit(solution)/shard_map/ppermute | solution.py:277
  71.6 0.0 collective-permute-done.13.refs_2_
  71.6 0.2 shard_map.88.total
  71.8 2.7 %collective-permute-done.14.refs_0_ = bf16[128,1024]{1,0:T(8,128)(2,1)S(1)} collective-permute-done((bf16[128,1024]{1,0:T(8,128)(2,1)S(1)}, bf16[128,1024]{1,0:T(8,128)(2,1)S(1)}, u32[]{:S(2)}, u32[]{:S(2)}) %collective-permute-start.14) | collective-permute-done | bytes 262176 | tf_op jit(solution)/shard_map/ppermute | solution.py:277
  74.6 2.8 %collective-permute-done.15.refs_1_ = bf16[128,1024]{1,0:T(8,128)(2,1)S(1)} collective-permute-done((bf16[128,1024]{1,0:T(8,128)(2,1)S(1)}, bf16[128,1024]{1,0:T(8,128)(2,1)S(1)}, u32[]{:S(2)}, u32[]{:S(2)}) %collective-permute-start.15) | collective-permute-done | bytes 262176 | tf_op jit(solution)/shard_map/ppermute | solution.py:277
  77.4 1.9 %collective-permute-done.16.refs_2_ = bf16[128,1024]{1,0:T(8,128)(2,1)S(1)} collective-permute-done((bf16[128,1024]{1,0:T(8,128)(2,1)S(1)}, bf16[128,1024]{1,0:T(8,128)(2,1)S(1)}, u32[]{:S(2)}, u32[]{:S(2)}) %collective-permute-start.16) | collective-permute-done | bytes 262176 | tf_op jit(solution)/shard_map/ppermute | solution.py:277
  79.2 2.5 %shard_map.89 = f32[1024,256]{1,0:T(8,128)} custom-call(bf16[4,1024,1024]{2,1,0:T(8,128)(2,1)S(1)} %get-tuple-element.33.weights, f32[4,1024]{1,0:T(4,128)S(1)} %copy-done.1, f32[1024,256]{1,0:T(8,128)S(1)} %shard_map.88.total, bf16[128,1024]{1,0:T(8,128)(2,1)S(1)} %collective-permute-done.14.refs_0_, bf16[128,1024]{1,0:T(8,128)(2,1)S(1)} %collective-permute-done.15.refs_1_, ...), custom_call_target="tpu_custom_call" | custom-call | flops 536870912 | bytes 10436608 | tf_op jit(solution)/shard_map/pallas_call | solution.py:20
  (8 shorter events, 0.2 us)
Async XLA Ops:
  0.6 9.7 %copy-start.1 = (f32[4,1024]{1,0:T(4,128)S(1)}, f32[4,1024]{1,0:T(4,128)}, u32[]{:S(2)}) copy-start(f32[4,1024]{1,0:T(4,128)} %biases.19) | copy-start | bytes 49156
  0.6 9.7 %copy-start = (f32[128,1024]{1,0:T(8,128)S(1)}, f32[128,1024]{1,0:T(8,128)}, u32[]{:S(2)}) copy-start(f32[128,1024]{1,0:T(8,128)} %inputs.5) | copy-start | bytes 1572868
  0.7 1.1 %copy-start.2 = (f32[1,128,1024]{2,1,0:T(8,128)S(1)}, f32[1,128,1024]{2,1,0:T(8,128)}, u32[]{:S(2)}) copy-start(f32[1,128,1024]{2,1,0:T(8,128)} %param.6) | copy-start | bytes 1572868
  1.8 7.2 %collective-permute-start = (bf16[128,1024]{1,0:T(8,128)(2,1)S(1)}, bf16[128,1024]{1,0:T(8,128)(2,1)S(1)}, u32[]{:S(2)}, u32[]{:S(2)}) collective-permute-start(bf16[128,1024]{1,0:T(8,128)(2,1)S(1)} %shard_map.76), channel_id=1, source_target_pairs={{0,4},{4,8},{8,12},{12,16},{16,20},{20,24},{24,28},{1,5},{5,9},{9,... | collective-permute-start | bytes 786440 | tf_op jit(solution)/shard_map/ppermute | solution.py:273
  9.0 19.8 %collective-permute-start.3 = (bf16[1024,1024]{1,0:T(8,128)(2,1)S(1)}, bf16[1024,1024]{1,0:T(8,128)(2,1)S(1)}, u32[]{:S(2)}, u32[]{:S(2)}) collective-permute-start(bf16[1024,1024]{1,0:T(8,128)(2,1)S(1)} %get-tuple-element.40), channel_id=1, source_target_pairs={{0,4},{8,12},{16,20},{24,28},{1,5},{9,13},{17,21},{25,29},{2,6},{1... | collective-permute-start | bytes 6291464 | tf_op jit(solution)/shard_map/ppermute | solution.py:273
  10.3 16.4 %copy-start.3 = (bf16[1,128,1024]{2,1,0:T(8,128)(2,1)S(1)}, bf16[1,128,1024]{2,1,0:T(8,128)(2,1)}, u32[]{:S(2)}) copy-start(bf16[1,128,1024]{2,1,0:T(8,128)(2,1)} %param.9) | copy-start | bytes 786436
  11.9 7.9 %collective-permute-start.1 = (bf16[144,1024]{1,0:T(8,128)(2,1)S(1)}, bf16[144,1024]{1,0:T(8,128)(2,1)S(1)}, u32[]{:S(2)}, u32[]{:S(2)}) collective-permute-start(bf16[144,1024]{1,0:T(8,128)(2,1)S(1)} %get-tuple-element.36), channel_id=1, source_target_pairs={{0,4},{4,8},{8,12},{12,16},{16,20},{20,24},{24,28},{1,5},{5,9},{9,... | collective-permute-start | bytes 884744 | tf_op jit(solution)/shard_map/ppermute | solution.py:273
  21.4 7.3 %collective-permute-start.2 = (bf16[128,1024]{1,0:T(8,128)(2,1)S(1)}, bf16[128,1024]{1,0:T(8,128)(2,1)S(1)}, u32[]{:S(2)}, u32[]{:S(2)}) collective-permute-start(bf16[128,1024]{1,0:T(8,128)(2,1)S(1)} %get-tuple-element.38.before), channel_id=1, source_target_pairs={{4,12},{5,13},{6,14},{7,15}} | collective-permute-start | bytes 786440 | tf_op jit(solution)/shard_map/ppermute | solution.py:273
  25.4 3.4 %collective-permute-start.4 = (bf16[128,1024]{1,0:T(8,128)(2,1)S(1)}, bf16[128,1024]{1,0:T(8,128)(2,1)S(1)}, u32[]{:S(2)}, u32[]{:S(2)}) collective-permute-start(bf16[128,1024]{1,0:T(8,128)(2,1)S(1)} %get-tuple-element.42), channel_id=1, source_target_pairs={{0,4},{8,12},{16,20},{24,28},{1,5},{9,13},{17,21},{25,29},{2,6},{1... | collective-permute-start | bytes 786440 | tf_op jit(solution)/shard_map/ppermute | solution.py:273
  28.8 9.8 %collective-permute-start.5 = (bf16[128,1024]{1,0:T(8,128)(2,1)S(1)}, bf16[128,1024]{1,0:T(8,128)(2,1)S(1)}, u32[]{:S(2)}, u32[]{:S(2)}) collective-permute-start(bf16[128,1024]{1,0:T(8,128)(2,1)S(1)} %get-tuple-element.48.before), channel_id=1, source_target_pairs={{12,20},{13,21},{14,22},{15,23}} | collective-permute-start | bytes 786440 | tf_op jit(solution)/shard_map/ppermute | solution.py:273
  29.5 3.8 %collective-permute-start.6 = (bf16[128,256]{1,0:T(8,128)(2,1)S(1)}, bf16[128,256]{1,0:T(8,128)(2,1)S(1)}, u32[]{:S(2)}, u32[]{:S(2)}) collective-permute-start(bf16[128,256]{1,0:T(8,128)(2,1)S(1)} %get-tuple-element.50), channel_id=1, source_target_pairs={{0,1},{1,2},{2,3},{3,0},{4,5},{5,6},{6,7},{7,4},{8,9},{9,10},{10,1... | collective-permute-start | bytes 196616 | tf_op jit(solution)/shard_map/ppermute | solution.py:280
  30.9 4.2 %collective-permute-start.7 = (bf16[128,256]{1,0:T(8,128)(2,1)S(1)}, bf16[128,256]{1,0:T(8,128)(2,1)S(1)}, u32[]{:S(2)}, u32[]{:S(2)}) collective-permute-start(bf16[128,256]{1,0:T(8,128)(2,1)S(1)} %get-tuple-element.51), channel_id=1, source_target_pairs={{0,2},{1,3},{2,0},{3,1},{4,6},{5,7},{6,4},{7,5},{8,10},{9,11},{10,... | collective-permute-start | bytes 196616 | tf_op jit(solution)/shard_map/ppermute | solution.py:280
  32.0 6.7 %collective-permute-start.8 = (bf16[128,256]{1,0:T(8,128)(2,1)S(1)}, bf16[128,256]{1,0:T(8,128)(2,1)S(1)}, u32[]{:S(2)}, u32[]{:S(2)}) collective-permute-start(bf16[128,256]{1,0:T(8,128)(2,1)S(1)} %get-tuple-element.52), channel_id=1, source_target_pairs={{0,3},{1,0},{2,1},{3,2},{4,7},{5,4},{6,5},{7,6},{8,11},{9,8},{10,9... | collective-permute-start | bytes 196616 | tf_op jit(solution)/shard_map/ppermute | solution.py:280
  38.7 0.7 collective-permute-start.9
  39.5 6.4 %collective-permute-start.10 = (bf16[128,1024]{1,0:T(8,128)(2,1)S(1)}, bf16[128,1024]{1,0:T(8,128)(2,1)S(1)}, u32[]{:S(2)}, u32[]{:S(2)}) collective-permute-start(bf16[128,1024]{1,0:T(8,128)(2,1)S(1)} %shard_map.83), channel_id=1, source_target_pairs={{4,0},{12,8},{20,16},{28,24},{5,1},{13,9},{21,17},{29,25},{6,2},{1... | collective-permute-start | bytes 786440 | tf_op jit(solution)/shard_map/ppermute | solution.py:273
  41.9 14.4 %collective-permute-start.11 = (bf16[128,1024]{1,0:T(8,128)(2,1)S(1)}, bf16[128,1024]{1,0:T(8,128)(2,1)S(1)}, u32[]{:S(2)}, u32[]{:S(2)}) collective-permute-start(bf16[128,1024]{1,0:T(8,128)(2,1)S(1)} %get-tuple-element.54.before), channel_id=1, source_target_pairs={{0,1},{1,2},{2,3},{3,0},{4,9},{5,10},{6,11},{7,8},{12,17},{13,18},... | collective-permute-start | bytes 786440 | tf_op jit(solution)/shard_map/ppermute | solution.py:277
  43.2 28.4 %collective-permute-start.12 = (bf16[128,1024]{1,0:T(8,128)(2,1)S(1)}, bf16[128,1024]{1,0:T(8,128)(2,1)S(1)}, u32[]{:S(2)}, u32[]{:S(2)}) collective-permute-start(bf16[128,1024]{1,0:T(8,128)(2,1)S(1)} %get-tuple-element.54.before), channel_id=1, source_target_pairs={{0,2},{1,3},{2,0},{3,1},{4,10},{5,11},{6,8},{7,9},{12,18},{13,19},... | collective-permute-start | bytes 786440 | tf_op jit(solution)/shard_map/ppermute | solution.py:277
  44.5 27.1 %collective-permute-start.13 = (bf16[128,1024]{1,0:T(8,128)(2,1)S(1)}, bf16[128,1024]{1,0:T(8,128)(2,1)S(1)}, u32[]{:S(2)}, u32[]{:S(2)}) collective-permute-start(bf16[128,1024]{1,0:T(8,128)(2,1)S(1)} %get-tuple-element.54.before), channel_id=1, source_target_pairs={{0,3},{1,0},{2,1},{3,2},{4,11},{5,8},{6,9},{7,10},{12,19},{13,16},... | collective-permute-start | bytes 786440 | tf_op jit(solution)/shard_map/ppermute | solution.py:277
  47.3 27.3 %collective-permute-start.14 = (bf16[128,1024]{1,0:T(8,128)(2,1)S(1)}, bf16[128,1024]{1,0:T(8,128)(2,1)S(1)}, u32[]{:S(2)}, u32[]{:S(2)}) collective-permute-start(bf16[128,1024]{1,0:T(8,128)(2,1)S(1)} %get-tuple-element.58.left), channel_id=1, source_target_pairs={{4,5},{5,6},{6,7},{7,4},{12,13},{13,14},{14,15},{15,12},{20,21},{2... | collective-permute-start | bytes 786440 | tf_op jit(solution)/shard_map/ppermute | solution.py:277
  49.5 27.9 %collective-permute-start.15 = (bf16[128,1024]{1,0:T(8,128)(2,1)S(1)}, bf16[128,1024]{1,0:T(8,128)(2,1)S(1)}, u32[]{:S(2)}, u32[]{:S(2)}) collective-permute-start(bf16[128,1024]{1,0:T(8,128)(2,1)S(1)} %get-tuple-element.58.left), channel_id=1, source_target_pairs={{4,6},{5,7},{6,4},{7,5},{12,14},{13,15},{14,12},{15,13},{20,22},{2... | collective-permute-start | bytes 786440 | tf_op jit(solution)/shard_map/ppermute | solution.py:277
  56.3 23.0 %collective-permute-start.16 = (bf16[128,1024]{1,0:T(8,128)(2,1)S(1)}, bf16[128,1024]{1,0:T(8,128)(2,1)S(1)}, u32[]{:S(2)}, u32[]{:S(2)}) collective-permute-start(bf16[128,1024]{1,0:T(8,128)(2,1)S(1)} %get-tuple-element.58.left), channel_id=1, source_target_pairs={{4,7},{5,4},{6,5},{7,6},{12,15},{13,12},{14,13},{15,14},{20,23},{2... | collective-permute-start | bytes 786440 | tf_op jit(solution)/shard_map/ppermute | solution.py:277

commit v6 on v5

--- a/solution.py
+++ b/solution.py
@@ -167,13 +167,7 @@
                 top[:, cols] = (mid[:, cols] + factor * slope + forcing[:, cols]).astype(BF16)
 
 
-def held_kernel(got_1, got_2, got_3, held):
-    here = lax.axis_index("layer")
-    low, early = here % 4 < 2, here // 4 == 0
-    held[...] = jnp.where(low, got_2[...], jnp.where(early, got_1[...], got_3[...]))
-
-
-def final_kernel(step_size, weights, biases, inputs, one, down, low_mid, first_mid, high_mid, forcing, relaxed, left, state, coarse, even, odd):
+def final_kernel(step_size, weights, biases, inputs, one, got_first, got_low, got_high, low_mid, first_mid, high_mid, forcing, relaxed, left, state, coarse, even, odd):
     here = lax.axis_index("layer")
     slot, group = here % 4, here // 4
 
@@ -184,7 +178,9 @@
 
     start_from(here == 0, inputs)
     start_from(here == 1, one)
-    start_from((here > 0) & (here % 2 == 0), down)
+    start_from((slot == 2) & (group == 0), got_first)
+    start_from((slot == 0) & (group > 0), got_low)
+    start_from((slot == 2) & (group > 0), got_high)
     start_from((slot == 1) & (group > 0), low_mid)
     start_from((slot == 3) & (group == 0), first_mid)
     start_from((slot == 3) & (group > 0), high_mid)
@@ -219,9 +215,21 @@
 
 
 def even_kernel(step_size, rows, count, weights, biases, total, *refs):
-    starts, adjoints = refs[:count], refs[count : 2 * count]
-    result, state, even, odd, adjoint, deltas = refs[2 * count :]
-    is_even = lax.axis_index("layer") % 2 == 0
+    first, low, high, adjoints = (refs[i * count : (i + 1) * count] for i in range(4))
+    result, state, even, odd, adjoint, deltas = refs[4 * count :]
+    here = lax.axis_index("layer")
+    slot, group = here % 4, here // 4
+    is_even = here % 2 == 0
+
+    def start_from(condition, sources):
+        @pl.when(condition)
+        def _():
+            for i, source in enumerate(sources):
+                even[i * rows : (i + 1) * rows, :] = source[...]
+
+    start_from((here == 0) | ((slot == 2) & (group == 0)), first)
+    start_from((slot == 0) & (group > 0), low)
+    start_from((slot == 2) & (group > 0), high)
 
     @pl.when(jnp.logical_not(is_even))
     def _():
@@ -229,11 +237,9 @@
 
     @pl.when(is_even)
     def _():
-        for i, (source, columns) in enumerate(zip(starts, adjoints)):
-            place = slice(i * rows, (i + 1) * rows)
-            state[place, :] = source[...].astype(F32)
-            even[place, :] = source[...]
-            adjoint[place, :] = columns[...]
+        state[...] = even[...].astype(F32)
+        for i, columns in enumerate(adjoints):
+            adjoint[i * rows : (i + 1) * rows, :] = columns[...]
         run_layers((0, 1, 2), step_size, weights, biases, state, (even, odd))
         result[...] = total[...] + gradient(step_size, weights, biases, odd, adjoint, deltas, result.shape[1])
 
@@ -273,7 +279,7 @@
         return lax.ppermute(state, "layer", pairs)
 
     def across(state, pairs, by):
-        flat = [(i * parts + z, j * parts + (z + by) % parts) for i, j in pairs for z in range(parts)]
+        flat = [(i * parts + z, j * parts + (z + by) % parts) for i, j in pairs for z in range(parts) if by or i != j]
         return lax.ppermute(state, ("layer", "dp"), flat)
 
     def shifted(array, by):
@@ -281,7 +287,6 @@
 
     up = [(i, i + 1) for i in range(blocks - 1)]
     up_pair = [(i, i + 1) for i in range(0, blocks, 2)]
-    down_pair = [(i + 1, i) for i in range(0, blocks, 2)]
     rounded = [pltpu.VMEM((rows, depth), BF16)] * 2
 
     guess_sent = call(round_kernel, plain((rows, depth), BF16), guesses[0])
@@ -331,36 +336,39 @@
             held_weights, biases, got, added, flops=layer_flops,
         )
 
-    def finish(gots, mids):
-        got_1, got_2, got_3 = gots
+    def finish(even_starts, mids):
         mid_1, mid_2, mid_3 = mids
-        held = call(held_kernel, plain((rows, depth), BF16), got_1, got_2, got_3)
-        down = along(held, down_pair)
         return call(
             functools.partial(final_kernel, step_size),
             (plain((rows, depth), BF16), kept(inputs), plain((rows, depth), F32)),
-            held_weights, biases, inputs, start, down, mid_2, mid_1, mid_3, forcing, relaxed,
+            held_weights, biases, inputs, start, *even_starts, mid_2, mid_1, mid_3, forcing, relaxed,
             scratch=rounded, flops=3 * layer_flops,
         )
+
+    def to_planes(state, pairs):
+        return [across(state, pairs, by) for by in range(parts)]
 
     top_0 = ahead
     if groups > 2:
         after = single(4.0 * step_size, along(ahead, up_pair), forcing)
         top_0 = jnp.where((slot == 1) & (group > 0), after.astype(BF16), ahead)
-    got_1, mid_1, top_1 = two_steps(
+    _, mid_1, top_1 = two_steps(
         top_0, [(4 * m + 1, 4 * m + 3) for m in range(groups - 1)], lambda slot, group: (slot == 3) & (group < last_group)
     )
+    far_1 = to_planes(top_0, [(0, 0)] + [(4 * m + 1, 4 * m + 2) for m in range(1)])
     top_1, *sent_adjoints = lax.optimization_barrier((top_1, *sent_adjoints))
     adjoints = sent_adjoints[:1] + [shifted(sent_adjoints[by], by) for by in range(1, parts)]
-    got_2, mid_2, top_2 = two_steps(
+    _, mid_2, top_2 = two_steps(
         top_1, [(4 * m - 1, 4 * m + 1) for m in range(1, groups)], lambda slot, group: (slot == 1) & (group > 0),
-        beside=adjoints,
-    )
-    got_3, mid_3 = two_steps(
-        top_2, [(4 * m + 1, 4 * m + 3) for m in range(1, groups)], lambda slot, group: (slot == 3) & (group > 0), True
-    )
-    top_last = top_2
-    left, state, coarse_states = finish((got_1, got_2, got_3), (mid_1, mid_2, mid_3))
+        beside=(*adjoints, *far_1),
+    )
+    far_2 = to_planes(top_1, [(4 * m - 1, 4 * m) for m in range(1, groups)])
+    _, mid_3 = two_steps(
+        top_2, [(4 * m + 1, 4 * m + 3) for m in range(1, groups)], lambda slot, group: (slot == 3) & (group > 0), True,
+        beside=far_2,
+    )
+    far_3 = to_planes(top_2, [(4 * m + 1, 4 * m + 2) for m in range(1, groups)])
+    left, state, coarse_states = finish((far_1[0], far_2[0], far_3[0]), (mid_1, mid_2, mid_3))
     if groups > 2:
         late = lambda slot, group: group > 1
         relaxed_out = call(functools.partial(pick_kernel, late), plain((rows, depth), F32), relaxed, relaxed)
@@ -370,20 +378,22 @@
         for m in range(2, groups):
             new = single(16.0 * step_size, along(solved.astype(BF16), [(4 * m - 1, 4 * m + 3)]), base)
             solved = jnp.where(here == 4 * m + 3, new, solved)
-        new_2, new_mid_2, top_last = two_steps(
-            jnp.where(slot == 3, solved.astype(BF16), top_2), [(4 * m - 1, 4 * m + 1) for m in range(2, groups)], lambda slot, group: (slot == 1) & (group > 1)
-        )
-        new_3, new_mid_3 = two_steps(
-            top_last, [(4 * m + 1, 4 * m + 3) for m in range(2, groups)], lambda slot, group: (slot == 3) & (group > 1), True
-        )
-        mids = [
-            call(functools.partial(pick_kernel, late), kept(inputs), new, old)
-            for new, old in ((new_mid_2, mid_2), (new_mid_3, mid_3))
-        ]
-        gots = [jnp.where(group > 1, new, old) for new, old in ((new_2, got_2), (new_3, got_3))]
-        left, state, coarse_early = finish((got_1, *gots), (mid_1, *mids))
+        _, new_mid_2, top_2 = two_steps(
+            solved.astype(BF16), [(4 * m - 1, 4 * m + 1) for m in range(2, groups)], lambda slot, group: (slot == 1) & (group > 1)
+        )
+        _, new_mid_3 = two_steps(
+            top_2, [(4 * m + 1, 4 * m + 3) for m in range(2, groups)], lambda slot, group: (slot == 3) & (group > 1), True
+        )
+        new_far_2 = to_planes(solved.astype(BF16), [(4 * m - 1, 4 * m) for m in range(2, groups)])
+        new_far_3 = to_planes(top_2, [(4 * m + 1, 4 * m + 2) for m in range(2, groups)])
+        picked = functools.partial(pick_kernel, late)
+        mids = [call(picked, kept(inputs), new, old) for new, old in ((new_mid_2, mid_2), (new_mid_3, mid_3))]
+        far_2, far_3 = (
+            [call(picked, plain((rows, depth), BF16), new, old) for new, old in zip(*pair)]
+            for pair in ((new_far_2, far_2), (new_far_3, far_3))
+        )
+        left, state, _ = finish((far_1[0], far_2[0], far_3[0]), (mid_1, *mids))
         coarse_states = jnp.where(slot == 3, solved - relaxed_out, coarse_states)
-    far = [across(top_last, [(0, 0)] + [(i, i + 1) for i in range(1, blocks - 1, 2)], by) for by in range(1, parts)]
     odd_lefts = [across(left, [(i, i) for i in range(1, blocks, 2)], by) for by in range(1, parts)]
     new_states = call(
         functools.partial(last_kernel, step_size), plain((rows, depth), F32),
@@ -397,7 +407,7 @@
     others = (parts - 1) * rows
     total = call(
         functools.partial(even_kernel, step_size, rows, parts - 1), pltpu.VMEM((depth, width), F32),
-        held_weights, biases, total, *far, *adjoints[1:],
+        held_weights, biases, total, *far_1[1:], *far_2[1:], *far_3[1:], *adjoints[1:],
         scratch=[pltpu.VMEM((others, depth), F32)] + [pltpu.VMEM((others, depth), BF16)] * 2
         + [pltpu.VMEM((others, width), BF16)] * 2,
         flops=4 * (parts - 1) * layer_flops,

time: 82.1 us -> 84.9 us (1.034)
  the two profiles are of different devices: /device:TPU:9 before, /device:TPU:1 now
where the time goes in v6:
time: 84.9 us; the launch traced here: 84.4 us
  starting transfers between devices  53.4 us (63%)
  waiting for transfers between devices  16 us (19%)
  Pallas kernels  12.9 us (15%)
  local copies, waits for them, and re-layouts  1.1 us (1%)
  between operations  1.06 us (1%)
    ppermute x15, starting transfers between devices, across(): return lax.ppermute(state, ('layer', 'dp'), flat)  25 us
    ppermute x7, starting transfers between devices, along(): return lax.ppermute(state, 'layer', pairs)  16.7 us
    pallas_call x13, Pallas kernels, call(): pl.pallas_call(kernel, out_shape=outs, in_specs=specs or [WHOLE] * len(ar...  12.9 us
    ppermute x3, starting transfers between devices, shifted(): lax.ppermute(array, 'dp', [(i, (i + by) % parts) for i in range(parts)])  11.7 us
    ppermute x15, waiting for transfers between devices, across(): return lax.ppermute(state, ('layer', 'dp'), flat)  11.6 us
    ppermute x7, waiting for transfers between devices, along(): return lax.ppermute(state, 'layer', pairs)  3.66 us
  transfers between devices with their start and end apart: 25, of which 6 were waited for; matrix products, arithmetic and copies ran while one was open for 0% of the time, Pallas kernels for 12%

profile of v6, /device:TPU:1, one launch (start us, length us, event | category | flops | bytes accessed | tf_op | source)
XLA Modules:
  0.0 84.4 jit_solution(4767101864966170540)
XLA Ops:
  0.7 1.1 %copy-done.2 = f32[1,128,1024]{2,1,0:T(8,128)S(1)} copy-done((f32[1,128,1024]{2,1,0:T(8,128)S(1)}, f32[1,128,1024]{2,1,0:T(8,128)}, u32[]{:S(2)}) %copy-start.2) | copy-done | bytes 524312
  1.8 4.5 %collective-permute-start = (bf16[128,1024]{1,0:T(8,128)(2,1)S(1)}, bf16[128,1024]{1,0:T(8,128)(2,1)S(1)}, u32[]{:S(2)}, u32[]{:S(2)}) collective-permute-start(bf16[128,1024]{1,0:T(8,128)(2,1)S(1)} %shard_map.76), channel_id=1, source_target_pairs={{0,4},{4,8},{8,12},{12,16},{16,20},{20,24},{24,28},{1,5},{5,9},{9,... | collective-permute-start | bytes 786440 | tf_op jit(solution)/shard_map/ppermute | solution.py:279
  6.3 3.5 %shard_map.77 = (bf16[4,1024,1024]{2,1,0:T(8,128)(2,1)S(1)}, bf16[1024,1024]{1,0:T(8,128)(2,1)S(1)}) custom-call(bf16[4,1024,1024]{2,1,0:T(8,128)(2,1)} %source), custom_call_target="tpu_custom_call" | custom-call | bytes 8388608 | tf_op jit(solution)/shard_map/pallas_call | solution.py:20
  9.8 1.3 %collective-permute-start.3 = (bf16[1024,1024]{1,0:T(8,128)(2,1)S(1)}, bf16[1024,1024]{1,0:T(8,128)(2,1)S(1)}, u32[]{:S(2)}, u32[]{:S(2)}) collective-permute-start(bf16[1024,1024]{1,0:T(8,128)(2,1)S(1)} %get-tuple-element.41), channel_id=1, source_target_pairs={{0,4},{8,12},{16,20},{24,28},{1,5},{9,13},{17,21},{25,29},{2,6},{1... | collective-permute-start | bytes 6291464 | tf_op jit(solution)/shard_map/ppermute | solution.py:279
  11.2 0.0 copy-start.3
  11.2 1.6 %shard_map.78 = (f32[128,1024]{1,0:T(8,128)S(1)}, bf16[144,1024]{1,0:T(8,128)(2,1)S(1)}) custom-call(bf16[4,1024,1024]{2,1,0:T(8,128)(2,1)S(1)} %get-tuple-element.34.weights, f32[4,1024]{1,0:T(4,128)S(1)} %copy-done.1, f32[128,1024]{1,0:T(8,128)S(1)} %copy-done, bf16[128,1024]{1,0:T(8,128)(2,1)S(1)} %collective-permute-done.got), custom_call_target="tpu_custom_call" | custom-call | flops 1073741824 | bytes 9191424 | tf_op jit(solution)/shard_map/pallas_call | solution.py:20
  12.7 4.2 %collective-permute-start.1 = (bf16[144,1024]{1,0:T(8,128)(2,1)S(1)}, bf16[144,1024]{1,0:T(8,128)(2,1)S(1)}, u32[]{:S(2)}, u32[]{:S(2)}) collective-permute-start(bf16[144,1024]{1,0:T(8,128)(2,1)S(1)} %get-tuple-element.37), channel_id=1, source_target_pairs={{0,4},{4,8},{8,12},{12,16},{16,20},{20,24},{24,28},{1,5},{5,9},{9,... | collective-permute-start | bytes 884744 | tf_op jit(solution)/shard_map/ppermute | solution.py:279
  17.0 3.6 %collective-permute-done.1.got = bf16[144,1024]{1,0:T(8,128)(2,1)S(1)} collective-permute-done((bf16[144,1024]{1,0:T(8,128)(2,1)S(1)}, bf16[144,1024]{1,0:T(8,128)(2,1)S(1)}, u32[]{:S(2)}, u32[]{:S(2)}) %collective-permute-start.1) | collective-permute-done | bytes 294944 | tf_op jit(solution)/shard_map/ppermute | solution.py:279
  20.6 1.5 %shard_map.79 = (f32[128,1024]{1,0:T(8,128)S(1)}, f32[128,1024]{1,0:T(8,128)S(1)}, f32[8,1024]{1,0:T(8,128)S(1)}, bf16[128,1024]{1,0:T(8,128)(2,1)S(1)}, bf16[128,1024]{1,0:T(8,128)(2,1)S(1)}) custom-call(bf16[4,1024,1024]{2,1,0:T(8,128)(2,1)S(1)} %get-tuple-element.34.weights, f32[4,1024]{1,0:T(4,128)S(1)} %copy-done.1, f32[128,1024]{1,0:T(8,128)S(1)} %copy-done, ...), custom_call_target="tpu_custom_call" | custom-call | flops 1073741824 | bytes 9224192 | tf_op jit(solution)/shard_map/pallas_call | solution.py:20
  22.2 4.0 %collective-permute-start.5 = (bf16[128,1024]{1,0:T(8,128)(2,1)S(1)}, bf16[128,1024]{1,0:T(8,128)(2,1)S(1)}, u32[]{:S(2)}, u32[]{:S(2)}) collective-permute-start(bf16[128,1024]{1,0:T(8,128)(2,1)S(1)} %get-tuple-element.39.before), channel_id=1, source_target_pairs={{4,12},{5,13},{6,14},{7,15}} | collective-permute-start | bytes 786440 | tf_op jit(solution)/shard_map/ppermute | solution.py:279
  26.2 1.3 %collective-permute-start.4 = (bf16[128,1024]{1,0:T(8,128)(2,1)S(1)}, bf16[128,1024]{1,0:T(8,128)(2,1)S(1)}, u32[]{:S(2)}, u32[]{:S(2)}) collective-permute-start(bf16[128,1024]{1,0:T(8,128)(2,1)S(1)} %get-tuple-element.43), channel_id=1, source_target_pairs={{0,4},{8,12},{16,20},{24,28},{1,5},{9,13},{17,21},{25,29},{2,6},{1... | collective-permute-start | bytes 786440 | tf_op jit(solution)/shard_map/ppermute | solution.py:279
  27.5 3.3 %collective-permute-start.11 = (bf16[128,1024]{1,0:T(8,128)(2,1)S(1)}, bf16[128,1024]{1,0:T(8,128)(2,1)S(1)}, u32[]{:S(2)}, u32[]{:S(2)}) collective-permute-start(bf16[128,1024]{1,0:T(8,128)(2,1)S(1)} %get-tuple-element.39.before), channel_id=1, source_target_pairs={{0,1},{1,2},{2,3},{3,0},{4,9},{5,10},{6,11},{7,8}} | collective-permute-start | bytes 786440 | tf_op jit(solution)/shard_map/ppermute | solution.py:283
  30.9 2.3 %collective-permute-start.12 = (bf16[128,1024]{1,0:T(8,128)(2,1)S(1)}, bf16[128,1024]{1,0:T(8,128)(2,1)S(1)}, u32[]{:S(2)}, u32[]{:S(2)}) collective-permute-start(bf16[128,1024]{1,0:T(8,128)(2,1)S(1)} %get-tuple-element.39.before), channel_id=1, source_target_pairs={{0,2},{1,3},{2,0},{3,1},{4,10},{5,11},{6,8},{7,9}} | collective-permute-start | bytes 786440 | tf_op jit(solution)/shard_map/ppermute | solution.py:283
  33.2 2.3 %collective-permute-start.13 = (bf16[128,1024]{1,0:T(8,128)(2,1)S(1)}, bf16[128,1024]{1,0:T(8,128)(2,1)S(1)}, u32[]{:S(2)}, u32[]{:S(2)}) collective-permute-start(bf16[128,1024]{1,0:T(8,128)(2,1)S(1)} %get-tuple-element.39.before), channel_id=1, source_target_pairs={{0,3},{1,0},{2,1},{3,2},{4,11},{5,8},{6,9},{7,10}} | collective-permute-start | bytes 786440 | tf_op jit(solution)/shard_map/ppermute | solution.py:283
  35.5 0.0 collective-permute-done.4.pair_forcing
  35.5 1.3 %collective-permute-start.2 = (bf16[128,1024]{1,0:T(8,128)(2,1)S(1)}, bf16[128,1024]{1,0:T(8,128)(2,1)S(1)}, u32[]{:S(2)}, u32[]{:S(2)}) collective-permute-start(bf16[128,1024]{1,0:T(8,128)(2,1)S(1)} %get-tuple-element.39.before), channel_id=1, source_target_pairs={{4,8},{5,9},{6,10},{7,11}} | collective-permute-start | bytes 786440 | tf_op jit(solution)/shard_map/ppermute | solution.py:283
  36.9 0.0 collective-permute-done.3.pair_weight
  37.0 0.7 collective-permute-start.7
  37.6 0.7 collective-permute-start.16
  38.3 2.7 %collective-permute-done.12.refs_1_ = bf16[128,1024]{1,0:T(8,128)(2,1)S(1)} collective-permute-done((bf16[128,1024]{1,0:T(8,128)(2,1)S(1)}, bf16[128,1024]{1,0:T(8,128)(2,1)S(1)}, u32[]{:S(2)}, u32[]{:S(2)}) %collective-permute-start.12) | collective-permute-done | bytes 262176 | tf_op jit(solution)/shard_map/ppermute | solution.py:283
  41.1 2.0 %collective-permute-start.10 = (bf16[128,256]{1,0:T(8,128)(2,1)S(1)}, bf16[128,256]{1,0:T(8,128)(2,1)S(1)}, u32[]{:S(2)}, u32[]{:S(2)}) collective-permute-start(bf16[128,256]{1,0:T(8,128)(2,1)S(1)} %get-tuple-element.53), channel_id=1, source_target_pairs={{0,3},{1,0},{2,1},{3,2},{4,7},{5,4},{6,5},{7,6},{8,11},{9,8},{10,9... | collective-permute-start | bytes 196616 | tf_op jit(solution)/shard_map/ppermute | solution.py:286
  43.0 3.7 %collective-permute-done.13.refs_2_ = bf16[128,1024]{1,0:T(8,128)(2,1)S(1)} collective-permute-done((bf16[128,1024]{1,0:T(8,128)(2,1)S(1)}, bf16[128,1024]{1,0:T(8,128)(2,1)S(1)}, u32[]{:S(2)}, u32[]{:S(2)}) %collective-permute-start.13) | collective-permute-done | bytes 262176 | tf_op jit(solution)/shard_map/ppermute | solution.py:283
  46.7 7.6 %collective-permute-start.8 = (bf16[128,256]{1,0:T(8,128)(2,1)S(1)}, bf16[128,256]{1,0:T(8,128)(2,1)S(1)}, u32[]{:S(2)}, u32[]{:S(2)}) collective-permute-start(bf16[128,256]{1,0:T(8,128)(2,1)S(1)} %get-tuple-element.51), channel_id=1, source_target_pairs={{0,1},{1,2},{2,3},{3,0},{4,5},{5,6},{6,7},{7,4},{8,9},{9,10},{10,1... | collective-permute-start | bytes 196616 | tf_op jit(solution)/shard_map/ppermute | solution.py:286
  54.3 2.1 %collective-permute-start.9 = (bf16[128,256]{1,0:T(8,128)(2,1)S(1)}, bf16[128,256]{1,0:T(8,128)(2,1)S(1)}, u32[]{:S(2)}, u32[]{:S(2)}) collective-permute-start(bf16[128,256]{1,0:T(8,128)(2,1)S(1)} %get-tuple-element.52), channel_id=1, source_target_pairs={{0,2},{1,3},{2,0},{3,1},{4,6},{5,7},{6,4},{7,5},{8,10},{9,11},{10,... | collective-permute-start | bytes 196616 | tf_op jit(solution)/shard_map/ppermute | solution.py:286
  56.4 0.7 collective-permute-start.17
  57.1 0.0 collective-permute-done.8.refs_9_.refs_3_
  57.1 0.7 collective-permute-start.18
  57.8 0.7 collective-permute-done.9.refs_10_.refs_4_
  58.4 0.7 collective-permute-start.6
  59.1 0.0 collective-permute-done.7.got
  59.2 0.7 collective-permute-start.15
  59.9 0.7 collective-permute-start.14
  60.5 0.0 collective-permute-done.17.refs_4_
  60.6 0.7 collective-permute-start.19
  61.2 0.7 collective-permute-start.20
  61.9 0.0 collective-permute-done.6.got_low
  61.9 0.7 collective-permute-start.21
  62.7 1.5 %shard_map.84 = (bf16[128,1024]{1,0:T(8,128)(2,1)S(1)}, f32[128,1024]{1,0:T(8,128)S(1)}, f32[128,1024]{1,0:T(8,128)}) custom-call(bf16[4,1024,1024]{2,1,0:T(8,128)(2,1)S(1)} %get-tuple-element.34.weights, f32[4,1024]{1,0:T(4,128)S(1)} %copy-done.1, f32[128,1024]{1,0:T(8,128)S(1)} %copy-done, f32[128,1024]{1,0:T(8,128)S(1)} %get-tuple-element.38.one, ...), custom_call_target="tpu_custom_call" | custom-call | flops 805306368 | bytes 12861440 | tf_op jit(solution)/shard_map/pallas_call | solution.py:20
  64.1 4.5 %collective-permute-start.22 = (bf16[128,1024]{1,0:T(8,128)(2,1)S(1)}, bf16[128,1024]{1,0:T(8,128)(2,1)S(1)}, u32[]{:S(2)}, u32[]{:S(2)}) collective-permute-start(bf16[128,1024]{1,0:T(8,128)(2,1)S(1)} %get-tuple-element.60.left), channel_id=1, source_target_pairs={{4,5},{5,6},{6,7},{7,4},{12,13},{13,14},{14,15},{15,12},{20,21},{2... | collective-permute-start | bytes 786440 | tf_op jit(solution)/shard_map/ppermute | solution.py:283
  68.6 3.3 %collective-permute-start.23 = (bf16[128,1024]{1,0:T(8,128)(2,1)S(1)}, bf16[128,1024]{1,0:T(8,128)(2,1)S(1)}, u32[]{:S(2)}, u32[]{:S(2)}) collective-permute-start(bf16[128,1024]{1,0:T(8,128)(2,1)S(1)} %get-tuple-element.60.left), channel_id=1, source_target_pairs={{4,6},{5,7},{6,4},{7,5},{12,14},{13,15},{14,12},{15,13},{20,22},{2... | collective-permute-start | bytes 786440 | tf_op jit(solution)/shard_map/ppermute | solution.py:283
  71.9 0.6 shard_map.86.total
  72.5 1.3 %shard_map.85 = f32[128,1024]{1,0:T(8,128)} custom-call(bf16[4,1024,1024]{2,1,0:T(8,128)(2,1)S(1)} %get-tuple-element.34.weights, f32[4,1024]{1,0:T(4,128)S(1)} %copy-done.1, bf16[128,1024]{1,0:T(8,128)(2,1)S(1)} %get-tuple-element.60.left, f32[128,1024]{1,0:T(8,128)S(1)} %get-tuple-element.61.state), custom_call_target="tpu_custom_call" | custom-call | flops 268435456 | bytes 9191424 | tf_op jit(solution)/shard_map/pallas_call | solution.py:20
  73.8 2.6 %collective-permute-start.24 = (bf16[128,1024]{1,0:T(8,128)(2,1)S(1)}, bf16[128,1024]{1,0:T(8,128)(2,1)S(1)}, u32[]{:S(2)}, u32[]{:S(2)}) collective-permute-start(bf16[128,1024]{1,0:T(8,128)(2,1)S(1)} %get-tuple-element.60.left), channel_id=1, source_target_pairs={{4,7},{5,4},{6,5},{7,6},{12,15},{13,12},{14,13},{15,14},{20,23},{2... | collective-permute-start | bytes 786440 | tf_op jit(solution)/shard_map/ppermute | solution.py:283
  76.5 0.0 collective-permute-done.21.refs_8_
  76.5 0.3 shard_map.87.total
  76.8 2.5 %collective-permute-done.23.refs_1_ = bf16[128,1024]{1,0:T(8,128)(2,1)S(1)} collective-permute-done((bf16[128,1024]{1,0:T(8,128)(2,1)S(1)}, bf16[128,1024]{1,0:T(8,128)(2,1)S(1)}, u32[]{:S(2)}, u32[]{:S(2)}) %collective-permute-start.23) | collective-permute-done | bytes 262176 | tf_op jit(solution)/shard_map/ppermute | solution.py:283
  79.3 2.7 %collective-permute-done.24.refs_2_ = bf16[128,1024]{1,0:T(8,128)(2,1)S(1)} collective-permute-done((bf16[128,1024]{1,0:T(8,128)(2,1)S(1)}, bf16[128,1024]{1,0:T(8,128)(2,1)S(1)}, u32[]{:S(2)}, u32[]{:S(2)}) %collective-permute-start.24) | collective-permute-done | bytes 262176 | tf_op jit(solution)/shard_map/ppermute | solution.py:283
  82.0 2.5 %shard_map.88 = f32[1024,256]{1,0:T(8,128)} custom-call(bf16[4,1024,1024]{2,1,0:T(8,128)(2,1)S(1)} %get-tuple-element.34.weights, f32[4,1024]{1,0:T(4,128)S(1)} %copy-done.1, f32[1024,256]{1,0:T(8,128)S(1)} %shard_map.87.total, bf16[128,1024]{1,0:T(8,128)(2,1)S(1)} %collective-permute-done.22.refs_0_, bf16[128,1024]{1,0:T(8,128)(2,1)S(1)} %collective-permute-done.23.refs_1_, ...), custom_call_target="tpu_custom_call" | custom-call | flops 536870912 | bytes 10436608 | tf_op jit(solution)/shard_map/pallas_call | solution.py:20
  (23 shorter events, 0.2 us)
Async XLA Ops:
  0.6 10.5 %copy-start = (f32[128,1024]{1,0:T(8,128)S(1)}, f32[128,1024]{1,0:T(8,128)}, u32[]{:S(2)}) copy-start(f32[128,1024]{1,0:T(8,128)} %inputs.5) | copy-start | bytes 1572868
  0.6 10.5 %copy-start.1 = (f32[4,1024]{1,0:T(4,128)S(1)}, f32[4,1024]{1,0:T(4,128)}, u32[]{:S(2)}) copy-start(f32[4,1024]{1,0:T(4,128)} %biases.19) | copy-start | bytes 49156
  0.7 1.1 %copy-start.2 = (f32[1,128,1024]{2,1,0:T(8,128)S(1)}, f32[1,128,1024]{2,1,0:T(8,128)}, u32[]{:S(2)}) copy-start(f32[1,128,1024]{2,1,0:T(8,128)} %param.6) | copy-start | bytes 1572868
  1.8 8.1 %collective-permute-start = (bf16[128,1024]{1,0:T(8,128)(2,1)S(1)}, bf16[128,1024]{1,0:T(8,128)(2,1)S(1)}, u32[]{:S(2)}, u32[]{:S(2)}) collective-permute-start(bf16[128,1024]{1,0:T(8,128)(2,1)S(1)} %shard_map.76), channel_id=1, source_target_pairs={{0,4},{4,8},{8,12},{12,16},{16,20},{20,24},{24,28},{1,5},{5,9},{9,... | collective-permute-start | bytes 786440 | tf_op jit(solution)/shard_map/ppermute | solution.py:279
  9.8 27.1 %collective-permute-start.3 = (bf16[1024,1024]{1,0:T(8,128)(2,1)S(1)}, bf16[1024,1024]{1,0:T(8,128)(2,1)S(1)}, u32[]{:S(2)}, u32[]{:S(2)}) collective-permute-start(bf16[1024,1024]{1,0:T(8,128)(2,1)S(1)} %get-tuple-element.41), channel_id=1, source_target_pairs={{0,4},{8,12},{16,20},{24,28},{1,5},{9,13},{17,21},{25,29},{2,6},{1... | collective-permute-start | bytes 6291464 | tf_op jit(solution)/shard_map/ppermute | solution.py:279
  11.2 25.7 %copy-start.3 = (bf16[1,128,1024]{2,1,0:T(8,128)(2,1)S(1)}, bf16[1,128,1024]{2,1,0:T(8,128)(2,1)}, u32[]{:S(2)}) copy-start(bf16[1,128,1024]{2,1,0:T(8,128)(2,1)} %param.9) | copy-start | bytes 786436
  12.7 7.9 %collective-permute-start.1 = (bf16[144,1024]{1,0:T(8,128)(2,1)S(1)}, bf16[144,1024]{1,0:T(8,128)(2,1)S(1)}, u32[]{:S(2)}, u32[]{:S(2)}) collective-permute-start(bf16[144,1024]{1,0:T(8,128)(2,1)S(1)} %get-tuple-element.37), channel_id=1, source_target_pairs={{0,4},{4,8},{8,12},{12,16},{16,20},{20,24},{24,28},{1,5},{5,9},{9,... | collective-permute-start | bytes 884744 | tf_op jit(solution)/shard_map/ppermute | solution.py:279
  22.2 11.0 %collective-permute-start.5 = (bf16[128,1024]{1,0:T(8,128)(2,1)S(1)}, bf16[128,1024]{1,0:T(8,128)(2,1)S(1)}, u32[]{:S(2)}, u32[]{:S(2)}) collective-permute-start(bf16[128,1024]{1,0:T(8,128)(2,1)S(1)} %get-tuple-element.39.before), channel_id=1, source_target_pairs={{4,12},{5,13},{6,14},{7,15}} | collective-permute-start | bytes 786440 | tf_op jit(solution)/shard_map/ppermute | solution.py:279
  26.2 9.3 %collective-permute-start.4 = (bf16[128,1024]{1,0:T(8,128)(2,1)S(1)}, bf16[128,1024]{1,0:T(8,128)(2,1)S(1)}, u32[]{:S(2)}, u32[]{:S(2)}) collective-permute-start(bf16[128,1024]{1,0:T(8,128)(2,1)S(1)} %get-tuple-element.43), channel_id=1, source_target_pairs={{0,4},{8,12},{16,20},{24,28},{1,5},{9,13},{17,21},{25,29},{2,6},{1... | collective-permute-start | bytes 786440 | tf_op jit(solution)/shard_map/ppermute | solution.py:279
  27.5 10.1 %collective-permute-start.11 = (bf16[128,1024]{1,0:T(8,128)(2,1)S(1)}, bf16[128,1024]{1,0:T(8,128)(2,1)S(1)}, u32[]{:S(2)}, u32[]{:S(2)}) collective-permute-start(bf16[128,1024]{1,0:T(8,128)(2,1)S(1)} %get-tuple-element.39.before), channel_id=1, source_target_pairs={{0,1},{1,2},{2,3},{3,0},{4,9},{5,10},{6,11},{7,8}} | collective-permute-start | bytes 786440 | tf_op jit(solution)/shard_map/ppermute | solution.py:283
  30.9 10.2 %collective-permute-start.12 = (bf16[128,1024]{1,0:T(8,128)(2,1)S(1)}, bf16[128,1024]{1,0:T(8,128)(2,1)S(1)}, u32[]{:S(2)}, u32[]{:S(2)}) collective-permute-start(bf16[128,1024]{1,0:T(8,128)(2,1)S(1)} %get-tuple-element.39.before), channel_id=1, source_target_pairs={{0,2},{1,3},{2,0},{3,1},{4,10},{5,11},{6,8},{7,9}} | collective-permute-start | bytes 786440 | tf_op jit(solution)/shard_map/ppermute | solution.py:283
  33.2 13.5 %collective-permute-start.13 = (bf16[128,1024]{1,0:T(8,128)(2,1)S(1)}, bf16[128,1024]{1,0:T(8,128)(2,1)S(1)}, u32[]{:S(2)}, u32[]{:S(2)}) collective-permute-start(bf16[128,1024]{1,0:T(8,128)(2,1)S(1)} %get-tuple-element.39.before), channel_id=1, source_target_pairs={{0,3},{1,0},{2,1},{3,2},{4,11},{5,8},{6,9},{7,10}} | collective-permute-start | bytes 786440 | tf_op jit(solution)/shard_map/ppermute | solution.py:283
  35.5 18.7 %collective-permute-start.2 = (bf16[128,1024]{1,0:T(8,128)(2,1)S(1)}, bf16[128,1024]{1,0:T(8,128)(2,1)S(1)}, u32[]{:S(2)}, u32[]{:S(2)}) collective-permute-start(bf16[128,1024]{1,0:T(8,128)(2,1)S(1)} %get-tuple-element.39.before), channel_id=1, source_target_pairs={{4,8},{5,9},{6,10},{7,11}} | collective-permute-start | bytes 786440 | tf_op jit(solution)/shard_map/ppermute | solution.py:283
  37.0 22.2 %collective-permute-start.7 = (bf16[128,1024]{1,0:T(8,128)(2,1)S(1)}, bf16[128,1024]{1,0:T(8,128)(2,1)S(1)}, u32[]{:S(2)}, u32[]{:S(2)}) collective-permute-start(bf16[128,1024]{1,0:T(8,128)(2,1)S(1)} %get-tuple-element.49.before), channel_id=1, source_target_pairs={{12,20},{13,21},{14,22},{15,23}} | collective-permute-start | bytes 786440 | tf_op jit(solution)/shard_map/ppermute | solution.py:279
  37.6 22.2 %collective-permute-start.16 = (bf16[128,1024]{1,0:T(8,128)(2,1)S(1)}, bf16[128,1024]{1,0:T(8,128)(2,1)S(1)}, u32[]{:S(2)}, u32[]{:S(2)}) collective-permute-start(bf16[128,1024]{1,0:T(8,128)(2,1)S(1)} %get-tuple-element.49.before), channel_id=1, source_target_pairs={{12,17},{13,18},{14,19},{15,16}} | collective-permute-start | bytes 786440 | tf_op jit(solution)/shard_map/ppermute | solution.py:283
  41.1 15.3 %collective-permute-start.10 = (bf16[128,256]{1,0:T(8,128)(2,1)S(1)}, bf16[128,256]{1,0:T(8,128)(2,1)S(1)}, u32[]{:S(2)}, u32[]{:S(2)}) collective-permute-start(bf16[128,256]{1,0:T(8,128)(2,1)S(1)} %get-tuple-element.53), channel_id=1, source_target_pairs={{0,3},{1,0},{2,1},{3,2},{4,7},{5,4},{6,5},{7,6},{8,11},{9,8},{10,9... | collective-permute-start | bytes 196616 | tf_op jit(solution)/shard_map/ppermute | solution.py:286
  46.7 10.4 %collective-permute-start.8 = (bf16[128,256]{1,0:T(8,128)(2,1)S(1)}, bf16[128,256]{1,0:T(8,128)(2,1)S(1)}, u32[]{:S(2)}, u32[]{:S(2)}) collective-permute-start(bf16[128,256]{1,0:T(8,128)(2,1)S(1)} %get-tuple-element.51), channel_id=1, source_target_pairs={{0,1},{1,2},{2,3},{3,0},{4,5},{5,6},{6,7},{7,4},{8,9},{9,10},{10,1... | collective-permute-start | bytes 196616 | tf_op jit(solution)/shard_map/ppermute | solution.py:286
  54.3 4.2 %collective-permute-start.9 = (bf16[128,256]{1,0:T(8,128)(2,1)S(1)}, bf16[128,256]{1,0:T(8,128)(2,1)S(1)}, u32[]{:S(2)}, u32[]{:S(2)}) collective-permute-start(bf16[128,256]{1,0:T(8,128)(2,1)S(1)} %get-tuple-element.52), channel_id=1, source_target_pairs={{0,2},{1,3},{2,0},{3,1},{4,6},{5,7},{6,4},{7,5},{8,10},{9,11},{10,... | collective-permute-start | bytes 196616 | tf_op jit(solution)/shard_map/ppermute | solution.py:286
  56.4 4.2 %collective-permute-start.17 = (bf16[128,1024]{1,0:T(8,128)(2,1)S(1)}, bf16[128,1024]{1,0:T(8,128)(2,1)S(1)}, u32[]{:S(2)}, u32[]{:S(2)}) collective-permute-start(bf16[128,1024]{1,0:T(8,128)(2,1)S(1)} %get-tuple-element.49.before), channel_id=1, source_target_pairs={{12,18},{13,19},{14,16},{15,17}} | collective-permute-start | bytes 786440 | tf_op jit(solution)/shard_map/ppermute | solution.py:283
  57.1 4.2 %collective-permute-start.18 = (bf16[128,1024]{1,0:T(8,128)(2,1)S(1)}, bf16[128,1024]{1,0:T(8,128)(2,1)S(1)}, u32[]{:S(2)}, u32[]{:S(2)}) collective-permute-start(bf16[128,1024]{1,0:T(8,128)(2,1)S(1)} %get-tuple-element.49.before), channel_id=1, source_target_pairs={{12,19},{13,16},{14,17},{15,18}} | collective-permute-start | bytes 786440 | tf_op jit(solution)/shard_map/ppermute | solution.py:283
  58.4 3.5 %collective-permute-start.6 = (bf16[128,1024]{1,0:T(8,128)(2,1)S(1)}, bf16[128,1024]{1,0:T(8,128)(2,1)S(1)}, u32[]{:S(2)}, u32[]{:S(2)}) collective-permute-start(bf16[128,1024]{1,0:T(8,128)(2,1)S(1)} %get-tuple-element.49.before), channel_id=1, source_target_pairs={{12,16},{13,17},{14,18},{15,19}} | collective-permute-start | bytes 786440 | tf_op jit(solution)/shard_map/ppermute | solution.py:283
  59.2 3.5 %collective-permute-start.15 = (bf16[128,1024]{1,0:T(8,128)(2,1)S(1)}, bf16[128,1024]{1,0:T(8,128)(2,1)S(1)}, u32[]{:S(2)}, u32[]{:S(2)}) collective-permute-start(bf16[128,1024]{1,0:T(8,128)(2,1)S(1)} %get-tuple-element.55.before), channel_id=1, source_target_pairs={{20,28},{21,29},{22,30},{23,31}} | collective-permute-start | bytes 786440 | tf_op jit(solution)/shard_map/ppermute | solution.py:279
  59.9 2.8 %collective-permute-start.14 = (bf16[128,1024]{1,0:T(8,128)(2,1)S(1)}, bf16[128,1024]{1,0:T(8,128)(2,1)S(1)}, u32[]{:S(2)}, u32[]{:S(2)}) collective-permute-start(bf16[128,1024]{1,0:T(8,128)(2,1)S(1)} %get-tuple-element.55.before), channel_id=1, source_target_pairs={{20,24},{21,25},{22,26},{23,27}} | collective-permute-start | bytes 786440 | tf_op jit(solution)/shard_map/ppermute | solution.py:283
  60.6 13.3 %collective-permute-start.19 = (bf16[128,1024]{1,0:T(8,128)(2,1)S(1)}, bf16[128,1024]{1,0:T(8,128)(2,1)S(1)}, u32[]{:S(2)}, u32[]{:S(2)}) collective-permute-start(bf16[128,1024]{1,0:T(8,128)(2,1)S(1)} %get-tuple-element.55.before), channel_id=1, source_target_pairs={{20,25},{21,26},{22,27},{23,24}} | collective-permute-start | bytes 786440 | tf_op jit(solution)/shard_map/ppermute | solution.py:283
  61.2 15.2 %collective-permute-start.20 = (bf16[128,1024]{1,0:T(8,128)(2,1)S(1)}, bf16[128,1024]{1,0:T(8,128)(2,1)S(1)}, u32[]{:S(2)}, u32[]{:S(2)}) collective-permute-start(bf16[128,1024]{1,0:T(8,128)(2,1)S(1)} %get-tuple-element.55.before), channel_id=1, source_target_pairs={{20,26},{21,27},{22,24},{23,25}} | collective-permute-start | bytes 786440 | tf_op jit(solution)/shard_map/ppermute | solution.py:283
  61.9 14.5 %collective-permute-start.21 = (bf16[128,1024]{1,0:T(8,128)(2,1)S(1)}, bf16[128,1024]{1,0:T(8,128)(2,1)S(1)}, u32[]{:S(2)}, u32[]{:S(2)}) collective-permute-start(bf16[128,1024]{1,0:T(8,128)(2,1)S(1)} %get-tuple-element.55.before), channel_id=1, source_target_pairs={{20,27},{21,24},{22,25},{23,26}} | collective-permute-start | bytes 786440 | tf_op jit(solution)/shard_map/ppermute | solution.py:283
  64.1 12.6 %collective-permute-start.22 = (bf16[128,1024]{1,0:T(8,128)(2,1)S(1)}, bf16[128,1024]{1,0:T(8,128)(2,1)S(1)}, u32[]{:S(2)}, u32[]{:S(2)}) collective-permute-start(bf16[128,1024]{1,0:T(8,128)(2,1)S(1)} %get-tuple-element.60.left), channel_id=1, source_target_pairs={{4,5},{5,6},{6,7},{7,4},{12,13},{13,14},{14,15},{15,12},{20,21},{2... | collective-permute-start | bytes 786440 | tf_op jit(solution)/shard_map/ppermute | solution.py:283
  68.6 10.7 %collective-permute-start.23 = (bf16[128,1024]{1,0:T(8,128)(2,1)S(1)}, bf16[128,1024]{1,0:T(8,128)(2,1)S(1)}, u32[]{:S(2)}, u32[]{:S(2)}) collective-permute-start(bf16[128,1024]{1,0:T(8,128)(2,1)S(1)} %get-tuple-element.60.left), channel_id=1, source_target_pairs={{4,6},{5,7},{6,4},{7,5},{12,14},{13,15},{14,12},{15,13},{20,22},{2... | collective-permute-start | bytes 786440 | tf_op jit(solution)/shard_map/ppermute | solution.py:283
  73.8 8.2 %collective-permute-start.24 = (bf16[128,1024]{1,0:T(8,128)(2,1)S(1)}, bf16[128,1024]{1,0:T(8,128)(2,1)S(1)}, u32[]{:S(2)}, u32[]{:S(2)}) collective-permute-start(bf16[128,1024]{1,0:T(8,128)(2,1)S(1)} %get-tuple-element.60.left), channel_id=1, source_target_pairs={{4,7},{5,4},{6,5},{7,6},{12,15},{13,12},{14,13},{15,14},{20,23},{2... | collective-permute-start | bytes 786440 | tf_op jit(solution)/shard_map/ppermute | solution.py:283

commit v7 on v5

--- a/solution.py
+++ b/solution.py
@@ -46,8 +46,9 @@
     return jnp.tanh(product + bias[:, cols])
 
 
-def round_kernel(guess, sent_guess):
+def round_kernel(guess, inputs, sent_guess, sent_inputs):
     sent_guess[...] = guess[...].astype(BF16)
+    sent_inputs[...] = inputs[...].astype(BF16)
 
 
 def columns_kernel(parts, adjoint, *columns):
@@ -133,7 +134,7 @@
         odd[:, cols] = new.astype(BF16)
         forcing[:, cols] = start[:, cols] + (4.0 * step_size) * slope
     run_layers((1, 2, 3), step_size, weights, biases, state, (even, odd))
-    top[...] = jnp.where(first, inputs[...].astype(BF16), even[...])
+    top[...] = even[...]
     difference = state[...] - forcing[...]
     forcing[...] = difference
     sent_forcing[...] = difference.astype(BF16)
@@ -219,9 +220,19 @@
 
 
 def even_kernel(step_size, rows, count, weights, biases, total, *refs):
-    starts, adjoints = refs[:count], refs[count : 2 * count]
-    result, state, even, odd, adjoint, deltas = refs[2 * count :]
-    is_even = lax.axis_index("layer") % 2 == 0
+    points, starts, adjoints = (refs[i * count : (i + 1) * count] for i in range(3))
+    result, state, even, odd, adjoint, deltas = refs[3 * count :]
+    here = lax.axis_index("layer")
+    is_even = here % 2 == 0
+
+    def start_from(condition, sources):
+        @pl.when(condition)
+        def _():
+            for i, source in enumerate(sources):
+                even[i * rows : (i + 1) * rows, :] = source[...]
+
+    start_from(here == 0, points)
+    start_from((here > 0) & is_even, starts)
 
     @pl.when(jnp.logical_not(is_even))
     def _():
@@ -229,11 +240,9 @@
 
     @pl.when(is_even)
     def _():
-        for i, (source, columns) in enumerate(zip(starts, adjoints)):
-            place = slice(i * rows, (i + 1) * rows)
-            state[place, :] = source[...].astype(F32)
-            even[place, :] = source[...]
-            adjoint[place, :] = columns[...]
+        state[...] = even[...].astype(F32)
+        for i, columns in enumerate(adjoints):
+            adjoint[i * rows : (i + 1) * rows, :] = columns[...]
         run_layers((0, 1, 2), step_size, weights, biases, state, (even, odd))
         result[...] = total[...] + gradient(step_size, weights, biases, odd, adjoint, deltas, result.shape[1])
 
@@ -284,7 +293,7 @@
     down_pair = [(i + 1, i) for i in range(0, blocks, 2)]
     rounded = [pltpu.VMEM((rows, depth), BF16)] * 2
 
-    guess_sent = call(round_kernel, plain((rows, depth), BF16), guesses[0])
+    guess_sent, inputs_sent = call(round_kernel, (plain((rows, depth), BF16),) * 2, guesses[0], inputs)
     guess_prev = along(guess_sent, up)
     guess_sent, weights = lax.optimization_barrier((guess_sent, weights))
     held_weights, coarse_weight = call(
@@ -302,7 +311,10 @@
         held_weights, biases, inputs, guess_prev,
         scratch=rounded, flops=4 * layer_flops,
     )
+    relaxed_sent, inputs_sent = lax.optimization_barrier((relaxed_sent, inputs_sent))
     relaxed_got = along(relaxed_sent, up)
+    far_inputs = [across(inputs_sent, [(0, 0)], by) for by in range(1, parts)]
+    relaxed_got, *far_inputs = lax.optimization_barrier((relaxed_got, *far_inputs))
     start, forcing, pair_bias, ahead, forcing_sent = call(
         functools.partial(ahead_kernel, step_size, rows),
         (kept(inputs), kept(inputs), pltpu.VMEM((8, depth), F32), plain((rows, depth), BF16), plain((rows, depth), BF16)),
@@ -383,7 +395,7 @@
         gots = [jnp.where(group > 1, new, old) for new, old in ((new_2, got_2), (new_3, got_3))]
         left, state, coarse_early = finish((got_1, *gots), (mid_1, *mids))
         coarse_states = jnp.where(slot == 3, solved - relaxed_out, coarse_states)
-    far = [across(top_last, [(0, 0)] + [(i, i + 1) for i in range(1, blocks - 1, 2)], by) for by in range(1, parts)]
+    far = [across(top_last, [(i, i + 1) for i in range(1, blocks - 1, 2)], by) for by in range(1, parts)]
     odd_lefts = [across(left, [(i, i) for i in range(1, blocks, 2)], by) for by in range(1, parts)]
     new_states = call(
         functools.partial(last_kernel, step_size), plain((rows, depth), F32),
@@ -397,7 +409,7 @@
     others = (parts - 1) * rows
     total = call(
         functools.partial(even_kernel, step_size, rows, parts - 1), pltpu.VMEM((depth, width), F32),
-        held_weights, biases, total, *far, *adjoints[1:],
+        held_weights, biases, total, *far_inputs, *far, *adjoints[1:],
         scratch=[pltpu.VMEM((others, depth), F32)] + [pltpu.VMEM((others, depth), BF16)] * 2
         + [pltpu.VMEM((others, width), BF16)] * 2,
         flops=4 * (parts - 1) * layer_flops,

time: 82.1 us -> 79.4 us (0.967)
  waiting for transfers between devices: 31.8 us -> 26.6 us
  starting transfers between devices: 35 us -> 36.3 us
  local copies, waits for them, and re-layouts: 1.11 us -> 2.09 us
    ppermute x6 -> x9, waiting for transfers between devices: 20.8 us -> 9.27 us  [across(): return lax.ppermute(state, ('layer', 'dp'), flat)]
    ppermute x8, waiting for transfers between devices: 5.72 us -> 11.3 us  [along(): return lax.ppermute(state, 'layer', pairs)]
    ppermute x6 -> x9, starting transfers between devices: 12.8 us -> 14.3 us  [across(): return lax.ppermute(state, ('layer', 'dp'), flat)]
    unnamed x8 -> x10, local copies, waits for them, and re-layouts: 1.11 us -> 2.09 us
  transfers between devices with their start and end apart: 17 -> 20, of which waited for: 9 -> 9; matrix products, arithmetic and copies ran while one was open for 0% -> 0% of each run, Pallas kernels for 13% -> 13%
where the time goes in v7:
time: 79.4 us; the launch traced here: 78.8 us
  starting transfers between devices  36.3 us (46%)
  waiting for transfers between devices  26.6 us (34%)
  Pallas kernels  12.9 us (16%)
  local copies, waits for them, and re-layouts  2.09 us (3%)
  between operations  0.97 us (1%)
    ppermute x8, starting transfers between devices, along(): return lax.ppermute(state, 'layer', pairs)  18.7 us
    ppermute x9, starting transfers between devices, across(): return lax.ppermute(state, ('layer', 'dp'), flat)  14.3 us
    pallas_call x14, Pallas kernels, call(): pl.pallas_call(kernel, out_shape=outs, in_specs=specs or [WHOLE] * len(ar...  12.9 us
    ppermute x8, waiting for transfers between devices, along(): return lax.ppermute(state, 'layer', pairs)  11.3 us
    ppermute x9, waiting for transfers between devices, across(): return lax.ppermute(state, ('layer', 'dp'), flat)  9.27 us
    ppermute x3, waiting for transfers between devices, shifted(): lax.ppermute(array, 'dp', [(i, (i + by) % parts) for i in range(parts)])  5.97 us
    ppermute x3, starting transfers between devices, shifted(): lax.ppermute(array, 'dp', [(i, (i + by) % parts) for i in range(parts)])  3.23 us
    unnamed x10, local copies, waits for them, and re-layouts  2.09 us
  transfers between devices with their start and end apart: 20, of which 9 were waited for; matrix products, arithmetic and copies ran while one was open for 0% of the time, Pallas kernels for 13%

profile of v7, /device:TPU:9, one launch (start us, length us, event | category | flops | bytes accessed | tf_op | source)
XLA Modules:
  0.0 78.8 jit_solution(11974028957063993702)
XLA Ops:
  0.6 0.0 copy-start
  0.6 1.0 %copy-done = f32[128,1024]{1,0:T(8,128)S(1)} copy-done((f32[128,1024]{1,0:T(8,128)S(1)}, f32[128,1024]{1,0:T(8,128)}, u32[]{:S(2)}) %copy-start) | copy-done | bytes 524312
  1.7 1.0 %copy-done.3 = f32[1,128,1024]{2,1,0:T(8,128)S(1)} copy-done((f32[1,128,1024]{2,1,0:T(8,128)S(1)}, f32[1,128,1024]{2,1,0:T(8,128)}, u32[]{:S(2)}) %copy-start.3) | copy-done | bytes 524312
  2.7 0.1 shard_map.76
  2.8 3.7 %collective-permute-start = (bf16[128,1024]{1,0:T(8,128)(2,1)S(1)}, bf16[128,1024]{1,0:T(8,128)(2,1)S(1)}, u32[]{:S(2)}, u32[]{:S(2)}) collective-permute-start(bf16[128,1024]{1,0:T(8,128)(2,1)S(1)} %get-tuple-element.40), channel_id=1, source_target_pairs={{0,4},{4,8},{8,12},{12,16},{16,20},{20,24},{24,28},{1,5},{5,9},{9,... | collective-permute-start | bytes 786440 | tf_op jit(solution)/shard_map/ppermute | solution.py:282
  6.5 3.5 %shard_map.77 = (bf16[4,1024,1024]{2,1,0:T(8,128)(2,1)S(1)}, bf16[1024,1024]{1,0:T(8,128)(2,1)S(1)}) custom-call(bf16[4,1024,1024]{2,1,0:T(8,128)(2,1)} %source), custom_call_target="tpu_custom_call" | custom-call | bytes 8388608 | tf_op jit(solution)/shard_map/pallas_call | solution.py:20
  10.0 0.0 collective-permute-done.got
  10.0 1.3 %collective-permute-start.6 = (bf16[1024,1024]{1,0:T(8,128)(2,1)S(1)}, bf16[1024,1024]{1,0:T(8,128)(2,1)S(1)}, u32[]{:S(2)}, u32[]{:S(2)}) collective-permute-start(bf16[1024,1024]{1,0:T(8,128)(2,1)S(1)} %get-tuple-element.53), channel_id=1, source_target_pairs={{0,4},{8,12},{16,20},{24,28},{1,5},{9,13},{17,21},{25,29},{2,6},{1... | collective-permute-start | bytes 6291464 | tf_op jit(solution)/shard_map/ppermute | solution.py:282
  11.3 0.0 copy-start.4
  11.3 1.6 %shard_map.78 = (f32[128,1024]{1,0:T(8,128)S(1)}, bf16[144,1024]{1,0:T(8,128)(2,1)S(1)}) custom-call(bf16[4,1024,1024]{2,1,0:T(8,128)(2,1)S(1)} %get-tuple-element.42.weights, f32[4,1024]{1,0:T(4,128)S(1)} %copy-done.2, f32[128,1024]{1,0:T(8,128)S(1)} %copy-done, bf16[128,1024]{1,0:T(8,128)(2,1)S(1)} %collective-permute-done.got), custom_call_target="tpu_custom_call" | custom-call | flops 1073741824 | bytes 9191424 | tf_op jit(solution)/shard_map/pallas_call | solution.py:20
  12.9 4.3 %collective-permute-start.1 = (bf16[144,1024]{1,0:T(8,128)(2,1)S(1)}, bf16[144,1024]{1,0:T(8,128)(2,1)S(1)}, u32[]{:S(2)}, u32[]{:S(2)}) collective-permute-start(bf16[144,1024]{1,0:T(8,128)(2,1)S(1)} %get-tuple-element.47), channel_id=1, source_target_pairs={{0,4},{4,8},{8,12},{12,16},{16,20},{20,24},{24,28},{1,5},{5,9},{9,... | collective-permute-start | bytes 884744 | tf_op jit(solution)/shard_map/ppermute | solution.py:282
  17.2 0.7 collective-permute-start.2
  17.8 0.7 collective-permute-start.3
  18.5 0.7 collective-permute-start.4
  19.2 0.0 collective-permute-done.2.refs_0_
  19.2 0.0 collective-permute-done.3.refs_1_
  19.2 1.6 %collective-permute-done.1.got = bf16[144,1024]{1,0:T(8,128)(2,1)S(1)} collective-permute-done((bf16[144,1024]{1,0:T(8,128)(2,1)S(1)}, bf16[144,1024]{1,0:T(8,128)(2,1)S(1)}, u32[]{:S(2)}, u32[]{:S(2)}) %collective-permute-start.1) | collective-permute-done | bytes 294944 | tf_op jit(solution)/shard_map/ppermute | solution.py:282
  20.8 1.5 %shard_map.79 = (f32[128,1024]{1,0:T(8,128)S(1)}, f32[128,1024]{1,0:T(8,128)S(1)}, f32[8,1024]{1,0:T(8,128)S(1)}, bf16[128,1024]{1,0:T(8,128)(2,1)S(1)}, bf16[128,1024]{1,0:T(8,128)(2,1)S(1)}) custom-call(bf16[4,1024,1024]{2,1,0:T(8,128)(2,1)S(1)} %get-tuple-element.42.weights, f32[4,1024]{1,0:T(4,128)S(1)} %copy-done.2, f32[128,1024]{1,0:T(8,128)S(1)} %copy-done, ...), custom_call_target="tpu_custom_call" | custom-call | flops 1073741824 | bytes 9224192 | tf_op jit(solution)/shard_map/pallas_call | solution.py:20
  22.3 4.0 %collective-permute-start.5 = (bf16[128,1024]{1,0:T(8,128)(2,1)S(1)}, bf16[128,1024]{1,0:T(8,128)(2,1)S(1)}, u32[]{:S(2)}, u32[]{:S(2)}) collective-permute-start(bf16[128,1024]{1,0:T(8,128)(2,1)S(1)} %get-tuple-element.51.before), channel_id=1, source_target_pairs={{4,12},{5,13},{6,14},{7,15}} | collective-permute-start | bytes 786440 | tf_op jit(solution)/shard_map/ppermute | solution.py:282
  26.4 1.3 %collective-permute-start.7 = (bf16[128,1024]{1,0:T(8,128)(2,1)S(1)}, bf16[128,1024]{1,0:T(8,128)(2,1)S(1)}, u32[]{:S(2)}, u32[]{:S(2)}) collective-permute-start(bf16[128,1024]{1,0:T(8,128)(2,1)S(1)} %get-tuple-element.55), channel_id=1, source_target_pairs={{0,4},{8,12},{16,20},{24,28},{1,5},{9,13},{17,21},{25,29},{2,6},{1... | collective-permute-start | bytes 786440 | tf_op jit(solution)/shard_map/ppermute | solution.py:282
  27.7 1.9 %collective-permute-done.5.got.got_1 = bf16[128,1024]{1,0:T(8,128)(2,1)S(1)} collective-permute-done((bf16[128,1024]{1,0:T(8,128)(2,1)S(1)}, bf16[128,1024]{1,0:T(8,128)(2,1)S(1)}, u32[]{:S(2)}, u32[]{:S(2)}) %collective-permute-start.5) | collective-permute-done | bytes 262176 | tf_op jit(solution)/shard_map/ppermute | solution.py:282
  29.7 7.9 %collective-permute-done.7.pair_forcing = bf16[128,1024]{1,0:T(8,128)(2,1)S(1)} collective-permute-done((bf16[128,1024]{1,0:T(8,128)(2,1)S(1)}, bf16[128,1024]{1,0:T(8,128)(2,1)S(1)}, u32[]{:S(2)}, u32[]{:S(2)}) %collective-permute-start.7) | collective-permute-done | bytes 262176 | tf_op jit(solution)/shard_map/ppermute | solution.py:282
  37.5 0.0 collective-permute-done.6.pair_weight
  37.5 0.7 collective-permute-start.8
  38.2 0.1 collective-permute-start.9
  38.3 2.9 %collective-permute-start.10 = (bf16[128,256]{1,0:T(8,128)(2,1)S(1)}, bf16[128,256]{1,0:T(8,128)(2,1)S(1)}, u32[]{:S(2)}, u32[]{:S(2)}) collective-permute-start(bf16[128,256]{1,0:T(8,128)(2,1)S(1)} %get-tuple-element.64), channel_id=1, source_target_pairs={{0,2},{1,3},{2,0},{3,1},{4,6},{5,7},{6,4},{7,5},{8,10},{9,11},{10,... | collective-permute-start | bytes 196616 | tf_op jit(solution)/shard_map/ppermute | solution.py:289
  41.2 0.3 collective-permute-start.11
  41.5 0.4 collective-permute-done.9.refs_6_.refs_3_
  41.8 3.9 %collective-permute-done.10.refs_7_.refs_4_ = bf16[128,256]{1,0:T(8,128)(2,1)S(1)} collective-permute-done((bf16[128,256]{1,0:T(8,128)(2,1)S(1)}, bf16[128,256]{1,0:T(8,128)(2,1)S(1)}, u32[]{:S(2)}, u32[]{:S(2)}) %collective-permute-start.10) | collective-permute-done | bytes 65568 | tf_op jit(solution)/shard_map/ppermute | solution.py:289
  45.7 1.7 %collective-permute-done.11.refs_8_.refs_5_ = bf16[128,256]{1,0:T(8,128)(2,1)S(1)} collective-permute-done((bf16[128,256]{1,0:T(8,128)(2,1)S(1)}, bf16[128,256]{1,0:T(8,128)(2,1)S(1)}, u32[]{:S(2)}, u32[]{:S(2)}) %collective-permute-start.11) | collective-permute-done | bytes 65568 | tf_op jit(solution)/shard_map/ppermute | solution.py:289
  47.4 0.0 collective-permute-done.8.got.got_2
  47.5 0.0 copy-start.1
  47.5 0.8 %collective-permute-start.12 = (bf16[128,1024]{1,0:T(8,128)(2,1)S(1)}, bf16[128,1024]{1,0:T(8,128)(2,1)S(1)}, u32[]{:S(2)}, u32[]{:S(2)}) collective-permute-start(bf16[128,1024]{1,0:T(8,128)(2,1)S(1)} %get-tuple-element.67.before), channel_id=1, source_target_pairs={{20,28},{21,29},{22,30},{23,31}} | collective-permute-start | bytes 786440 | tf_op jit(solution)/shard_map/ppermute | solution.py:282
  48.4 2.7 %collective-permute-start.13 = (bf16[128,1024]{1,0:T(8,128)(2,1)S(1)}, bf16[128,1024]{1,0:T(8,128)(2,1)S(1)}, u32[]{:S(2)}, u32[]{:S(2)}) collective-permute-start(bf16[128,1024]{1,0:T(8,128)(2,1)S(1)} %shard_map.83), channel_id=1, source_target_pairs={{4,0},{12,8},{20,16},{28,24},{5,1},{13,9},{21,17},{29,25},{6,2},{1... | collective-permute-start | bytes 786440 | tf_op jit(solution)/shard_map/ppermute | solution.py:282
  51.0 1.3 %collective-permute-start.14 = (bf16[128,1024]{1,0:T(8,128)(2,1)S(1)}, bf16[128,1024]{1,0:T(8,128)(2,1)S(1)}, u32[]{:S(2)}, u32[]{:S(2)}) collective-permute-start(bf16[128,1024]{1,0:T(8,128)(2,1)S(1)} %get-tuple-element.67.before), channel_id=1, source_target_pairs={{4,9},{5,10},{6,11},{7,8},{12,17},{13,18},{14,19},{15,16},{20,25},... | collective-permute-start | bytes 786440 | tf_op jit(solution)/shard_map/ppermute | solution.py:286
  52.3 1.3 %collective-permute-start.15 = (bf16[128,1024]{1,0:T(8,128)(2,1)S(1)}, bf16[128,1024]{1,0:T(8,128)(2,1)S(1)}, u32[]{:S(2)}, u32[]{:S(2)}) collective-permute-start(bf16[128,1024]{1,0:T(8,128)(2,1)S(1)} %get-tuple-element.67.before), channel_id=1, source_target_pairs={{4,10},{5,11},{6,8},{7,9},{12,18},{13,19},{14,16},{15,17},{20,26},... | collective-permute-start | bytes 786440 | tf_op jit(solution)/shard_map/ppermute | solution.py:286
  53.7 1.3 %collective-permute-start.16 = (bf16[128,1024]{1,0:T(8,128)(2,1)S(1)}, bf16[128,1024]{1,0:T(8,128)(2,1)S(1)}, u32[]{:S(2)}, u32[]{:S(2)}) collective-permute-start(bf16[128,1024]{1,0:T(8,128)(2,1)S(1)} %get-tuple-element.67.before), channel_id=1, source_target_pairs={{4,11},{5,8},{6,9},{7,10},{12,19},{13,16},{14,17},{15,18},{20,27},... | collective-permute-start | bytes 786440 | tf_op jit(solution)/shard_map/ppermute | solution.py:286
  55.0 1.4 %shard_map.85 = (bf16[128,1024]{1,0:T(8,128)(2,1)S(1)}, f32[128,1024]{1,0:T(8,128)S(1)}, f32[128,1024]{1,0:T(8,128)}) custom-call(bf16[4,1024,1024]{2,1,0:T(8,128)(2,1)S(1)} %get-tuple-element.42.weights, f32[4,1024]{1,0:T(4,128)S(1)} %copy-done.2, f32[128,1024]{1,0:T(8,128)S(1)} %copy-done.1, f32[128,1024]{1,0:T(8,128)S(1)} %get-tuple-element.50.one, ...), custom_call_target="tpu_custom_call" | custom-call | flops 805306368 | bytes 12337152 | tf_op jit(solution)/shard_map/pallas_call | solution.py:20
  56.5 1.9 %collective-permute-start.17 = (bf16[128,1024]{1,0:T(8,128)(2,1)S(1)}, bf16[128,1024]{1,0:T(8,128)(2,1)S(1)}, u32[]{:S(2)}, u32[]{:S(2)}) collective-permute-start(bf16[128,1024]{1,0:T(8,128)(2,1)S(1)} %get-tuple-element.71.left), channel_id=1, source_target_pairs={{4,5},{5,6},{6,7},{7,4},{12,13},{13,14},{14,15},{15,12},{20,21},{2... | collective-permute-start | bytes 786440 | tf_op jit(solution)/shard_map/ppermute | solution.py:286
  58.4 4.1 %collective-permute-start.18 = (bf16[128,1024]{1,0:T(8,128)(2,1)S(1)}, bf16[128,1024]{1,0:T(8,128)(2,1)S(1)}, u32[]{:S(2)}, u32[]{:S(2)}) collective-permute-start(bf16[128,1024]{1,0:T(8,128)(2,1)S(1)} %get-tuple-element.71.left), channel_id=1, source_target_pairs={{4,6},{5,7},{6,4},{7,5},{12,14},{13,15},{14,12},{15,13},{20,22},{2... | collective-permute-start | bytes 786440 | tf_op jit(solution)/shard_map/ppermute | solution.py:286
  62.5 0.7 shard_map.87.total
  63.1 1.3 %shard_map.86 = f32[128,1024]{1,0:T(8,128)} custom-call(bf16[4,1024,1024]{2,1,0:T(8,128)(2,1)S(1)} %get-tuple-element.42.weights, f32[4,1024]{1,0:T(4,128)S(1)} %copy-done.2, bf16[128,1024]{1,0:T(8,128)(2,1)S(1)} %get-tuple-element.71.left, f32[128,1024]{1,0:T(8,128)S(1)} %get-tuple-element.72.state), custom_call_target="tpu_custom_call" | custom-call | flops 268435456 | bytes 9191424 | tf_op jit(solution)/shard_map/pallas_call | solution.py:20
  64.4 2.4 %collective-permute-start.19 = (bf16[128,1024]{1,0:T(8,128)(2,1)S(1)}, bf16[128,1024]{1,0:T(8,128)(2,1)S(1)}, u32[]{:S(2)}, u32[]{:S(2)}) collective-permute-start(bf16[128,1024]{1,0:T(8,128)(2,1)S(1)} %get-tuple-element.71.left), channel_id=1, source_target_pairs={{4,7},{5,4},{6,5},{7,6},{12,15},{13,12},{14,13},{15,14},{20,23},{2... | collective-permute-start | bytes 786440 | tf_op jit(solution)/shard_map/ppermute | solution.py:286
  66.8 0.3 shard_map.88.total
  67.1 5.4 %collective-permute-done.17.refs_0_ = bf16[128,1024]{1,0:T(8,128)(2,1)S(1)} collective-permute-done((bf16[128,1024]{1,0:T(8,128)(2,1)S(1)}, bf16[128,1024]{1,0:T(8,128)(2,1)S(1)}, u32[]{:S(2)}, u32[]{:S(2)}) %collective-permute-start.17) | collective-permute-done | bytes 262176 | tf_op jit(solution)/shard_map/ppermute | solution.py:286
  72.5 2.8 %collective-permute-done.18.refs_1_ = bf16[128,1024]{1,0:T(8,128)(2,1)S(1)} collective-permute-done((bf16[128,1024]{1,0:T(8,128)(2,1)S(1)}, bf16[128,1024]{1,0:T(8,128)(2,1)S(1)}, u32[]{:S(2)}, u32[]{:S(2)}) %collective-permute-start.18) | collective-permute-done | bytes 262176 | tf_op jit(solution)/shard_map/ppermute | solution.py:286
  75.3 1.1 %collective-permute-done.19.refs_2_ = bf16[128,1024]{1,0:T(8,128)(2,1)S(1)} collective-permute-done((bf16[128,1024]{1,0:T(8,128)(2,1)S(1)}, bf16[128,1024]{1,0:T(8,128)(2,1)S(1)}, u32[]{:S(2)}, u32[]{:S(2)}) %collective-permute-start.19) | collective-permute-done | bytes 262176 | tf_op jit(solution)/shard_map/ppermute | solution.py:286
  76.4 2.5 %shard_map.89 = f32[1024,256]{1,0:T(8,128)} custom-call(bf16[4,1024,1024]{2,1,0:T(8,128)(2,1)S(1)} %get-tuple-element.42.weights, f32[4,1024]{1,0:T(4,128)S(1)} %copy-done.2, f32[1024,256]{1,0:T(8,128)S(1)} %shard_map.88.total, bf16[128,1024]{1,0:T(8,128)(2,1)S(1)} %collective-permute-done.17.refs_0_, bf16[128,1024]{1,0:T(8,128)(2,1)S(1)} %collective-permute-done.18.refs_1_, ...), custom_call_target="tpu_custom_call" | custom-call | flops 536870912 | bytes 10436608 | tf_op jit(solution)/shard_map/pallas_call | solution.py:20
  (16 shorter events, 0.2 us)
Async XLA Ops:
  0.6 1.0 %copy-start = (f32[128,1024]{1,0:T(8,128)S(1)}, f32[128,1024]{1,0:T(8,128)}, u32[]{:S(2)}) copy-start(f32[128,1024]{1,0:T(8,128)} %inputs.7) | copy-start | bytes 1572868
  1.7 1.0 %copy-start.3 = (f32[1,128,1024]{2,1,0:T(8,128)S(1)}, f32[1,128,1024]{2,1,0:T(8,128)}, u32[]{:S(2)}) copy-start(f32[1,128,1024]{2,1,0:T(8,128)} %param.6) | copy-start | bytes 1572868
  2.7 8.6 %copy-start.2 = (f32[4,1024]{1,0:T(4,128)S(1)}, f32[4,1024]{1,0:T(4,128)}, u32[]{:S(2)}) copy-start(f32[4,1024]{1,0:T(4,128)} %biases.19) | copy-start | bytes 49156
  2.8 7.2 %collective-permute-start = (bf16[128,1024]{1,0:T(8,128)(2,1)S(1)}, bf16[128,1024]{1,0:T(8,128)(2,1)S(1)}, u32[]{:S(2)}, u32[]{:S(2)}) collective-permute-start(bf16[128,1024]{1,0:T(8,128)(2,1)S(1)} %get-tuple-element.40), channel_id=1, source_target_pairs={{0,4},{4,8},{8,12},{12,16},{16,20},{20,24},{24,28},{1,5},{5,9},{9,... | collective-permute-start | bytes 786440 | tf_op jit(solution)/shard_map/ppermute | solution.py:282
  10.0 27.5 %collective-permute-start.6 = (bf16[1024,1024]{1,0:T(8,128)(2,1)S(1)}, bf16[1024,1024]{1,0:T(8,128)(2,1)S(1)}, u32[]{:S(2)}, u32[]{:S(2)}) collective-permute-start(bf16[1024,1024]{1,0:T(8,128)(2,1)S(1)} %get-tuple-element.53), channel_id=1, source_target_pairs={{0,4},{8,12},{16,20},{24,28},{1,5},{9,13},{17,21},{25,29},{2,6},{1... | collective-permute-start | bytes 6291464 | tf_op jit(solution)/shard_map/ppermute | solution.py:282
  11.3 16.3 %copy-start.4 = (bf16[1,128,1024]{2,1,0:T(8,128)(2,1)S(1)}, bf16[1,128,1024]{2,1,0:T(8,128)(2,1)}, u32[]{:S(2)}) copy-start(bf16[1,128,1024]{2,1,0:T(8,128)(2,1)} %param.9) | copy-start | bytes 786436
  12.9 7.9 %collective-permute-start.1 = (bf16[144,1024]{1,0:T(8,128)(2,1)S(1)}, bf16[144,1024]{1,0:T(8,128)(2,1)S(1)}, u32[]{:S(2)}, u32[]{:S(2)}) collective-permute-start(bf16[144,1024]{1,0:T(8,128)(2,1)S(1)} %get-tuple-element.47), channel_id=1, source_target_pairs={{0,4},{4,8},{8,12},{12,16},{16,20},{20,24},{24,28},{1,5},{5,9},{9,... | collective-permute-start | bytes 884744 | tf_op jit(solution)/shard_map/ppermute | solution.py:282
  17.2 2.1 %collective-permute-start.2 = (bf16[128,1024]{1,0:T(8,128)(2,1)S(1)}, bf16[128,1024]{1,0:T(8,128)(2,1)S(1)}, u32[]{:S(2)}, u32[]{:S(2)}) collective-permute-start(bf16[128,1024]{1,0:T(8,128)(2,1)S(1)} %get-tuple-element.48), channel_id=1, source_target_pairs={{0,1},{1,2},{2,3},{3,0}} | collective-permute-start | bytes 786440 | tf_op jit(solution)/shard_map/ppermute | solution.py:286
  17.8 1.4 %collective-permute-start.3 = (bf16[128,1024]{1,0:T(8,128)(2,1)S(1)}, bf16[128,1024]{1,0:T(8,128)(2,1)S(1)}, u32[]{:S(2)}, u32[]{:S(2)}) collective-permute-start(bf16[128,1024]{1,0:T(8,128)(2,1)S(1)} %get-tuple-element.48), channel_id=1, source_target_pairs={{0,2},{1,3},{2,0},{3,1}} | collective-permute-start | bytes 786440 | tf_op jit(solution)/shard_map/ppermute | solution.py:286
  18.5 0.7 collective-permute-start.4
  22.3 7.3 %collective-permute-start.5 = (bf16[128,1024]{1,0:T(8,128)(2,1)S(1)}, bf16[128,1024]{1,0:T(8,128)(2,1)S(1)}, u32[]{:S(2)}, u32[]{:S(2)}) collective-permute-start(bf16[128,1024]{1,0:T(8,128)(2,1)S(1)} %get-tuple-element.51.before), channel_id=1, source_target_pairs={{4,12},{5,13},{6,14},{7,15}} | collective-permute-start | bytes 786440 | tf_op jit(solution)/shard_map/ppermute | solution.py:282
  26.4 11.1 %collective-permute-start.7 = (bf16[128,1024]{1,0:T(8,128)(2,1)S(1)}, bf16[128,1024]{1,0:T(8,128)(2,1)S(1)}, u32[]{:S(2)}, u32[]{:S(2)}) collective-permute-start(bf16[128,1024]{1,0:T(8,128)(2,1)S(1)} %get-tuple-element.55), channel_id=1, source_target_pairs={{0,4},{8,12},{16,20},{24,28},{1,5},{9,13},{17,21},{25,29},{2,6},{1... | collective-permute-start | bytes 786440 | tf_op jit(solution)/shard_map/ppermute | solution.py:282
  37.5 9.9 %collective-permute-start.8 = (bf16[128,1024]{1,0:T(8,128)(2,1)S(1)}, bf16[128,1024]{1,0:T(8,128)(2,1)S(1)}, u32[]{:S(2)}, u32[]{:S(2)}) collective-permute-start(bf16[128,1024]{1,0:T(8,128)(2,1)S(1)} %get-tuple-element.61.before), channel_id=1, source_target_pairs={{12,20},{13,21},{14,22},{15,23}} | collective-permute-start | bytes 786440 | tf_op jit(solution)/shard_map/ppermute | solution.py:282
  38.2 3.6 %collective-permute-start.9 = (bf16[128,256]{1,0:T(8,128)(2,1)S(1)}, bf16[128,256]{1,0:T(8,128)(2,1)S(1)}, u32[]{:S(2)}, u32[]{:S(2)}) collective-permute-start(bf16[128,256]{1,0:T(8,128)(2,1)S(1)} %get-tuple-element.63), channel_id=1, source_target_pairs={{0,1},{1,2},{2,3},{3,0},{4,5},{5,6},{6,7},{7,4},{8,9},{9,10},{10,1... | collective-permute-start | bytes 196616 | tf_op jit(solution)/shard_map/ppermute | solution.py:289
  38.3 7.4 %collective-permute-start.10 = (bf16[128,256]{1,0:T(8,128)(2,1)S(1)}, bf16[128,256]{1,0:T(8,128)(2,1)S(1)}, u32[]{:S(2)}, u32[]{:S(2)}) collective-permute-start(bf16[128,256]{1,0:T(8,128)(2,1)S(1)} %get-tuple-element.64), channel_id=1, source_target_pairs={{0,2},{1,3},{2,0},{3,1},{4,6},{5,7},{6,4},{7,5},{8,10},{9,11},{10,... | collective-permute-start | bytes 196616 | tf_op jit(solution)/shard_map/ppermute | solution.py:289
  41.2 6.2 %collective-permute-start.11 = (bf16[128,256]{1,0:T(8,128)(2,1)S(1)}, bf16[128,256]{1,0:T(8,128)(2,1)S(1)}, u32[]{:S(2)}, u32[]{:S(2)}) collective-permute-start(bf16[128,256]{1,0:T(8,128)(2,1)S(1)} %get-tuple-element.65), channel_id=1, source_target_pairs={{0,3},{1,0},{2,1},{3,2},{4,7},{5,4},{6,5},{7,6},{8,11},{9,8},{10,9... | collective-permute-start | bytes 196616 | tf_op jit(solution)/shard_map/ppermute | solution.py:289
  47.5 7.6 %copy-start.1 = (f32[128,1024]{1,0:T(8,128)S(1)}, f32[128,1024]{1,0:T(8,128)}, u32[]{:S(2)}) copy-start(f32[128,1024]{1,0:T(8,128)} %inputs.7) | copy-start | bytes 1572868
  47.5 0.8 %collective-permute-start.12 = (bf16[128,1024]{1,0:T(8,128)(2,1)S(1)}, bf16[128,1024]{1,0:T(8,128)(2,1)S(1)}, u32[]{:S(2)}, u32[]{:S(2)}) collective-permute-start(bf16[128,1024]{1,0:T(8,128)(2,1)S(1)} %get-tuple-element.67.before), channel_id=1, source_target_pairs={{20,28},{21,29},{22,30},{23,31}} | collective-permute-start | bytes 786440 | tf_op jit(solution)/shard_map/ppermute | solution.py:282
  48.4 6.7 %collective-permute-start.13 = (bf16[128,1024]{1,0:T(8,128)(2,1)S(1)}, bf16[128,1024]{1,0:T(8,128)(2,1)S(1)}, u32[]{:S(2)}, u32[]{:S(2)}) collective-permute-start(bf16[128,1024]{1,0:T(8,128)(2,1)S(1)} %shard_map.83), channel_id=1, source_target_pairs={{4,0},{12,8},{20,16},{28,24},{5,1},{13,9},{21,17},{29,25},{6,2},{1... | collective-permute-start | bytes 786440 | tf_op jit(solution)/shard_map/ppermute | solution.py:282
  51.0 13.4 %collective-permute-start.14 = (bf16[128,1024]{1,0:T(8,128)(2,1)S(1)}, bf16[128,1024]{1,0:T(8,128)(2,1)S(1)}, u32[]{:S(2)}, u32[]{:S(2)}) collective-permute-start(bf16[128,1024]{1,0:T(8,128)(2,1)S(1)} %get-tuple-element.67.before), channel_id=1, source_target_pairs={{4,9},{5,10},{6,11},{7,8},{12,17},{13,18},{14,19},{15,16},{20,25},... | collective-permute-start | bytes 786440 | tf_op jit(solution)/shard_map/ppermute | solution.py:286
  52.3 14.4 %collective-permute-start.15 = (bf16[128,1024]{1,0:T(8,128)(2,1)S(1)}, bf16[128,1024]{1,0:T(8,128)(2,1)S(1)}, u32[]{:S(2)}, u32[]{:S(2)}) collective-permute-start(bf16[128,1024]{1,0:T(8,128)(2,1)S(1)} %get-tuple-element.67.before), channel_id=1, source_target_pairs={{4,10},{5,11},{6,8},{7,9},{12,18},{13,19},{14,16},{15,17},{20,26},... | collective-permute-start | bytes 786440 | tf_op jit(solution)/shard_map/ppermute | solution.py:286
  53.7 13.1 %collective-permute-start.16 = (bf16[128,1024]{1,0:T(8,128)(2,1)S(1)}, bf16[128,1024]{1,0:T(8,128)(2,1)S(1)}, u32[]{:S(2)}, u32[]{:S(2)}) collective-permute-start(bf16[128,1024]{1,0:T(8,128)(2,1)S(1)} %get-tuple-element.67.before), channel_id=1, source_target_pairs={{4,11},{5,8},{6,9},{7,10},{12,19},{13,16},{14,17},{15,18},{20,27},... | collective-permute-start | bytes 786440 | tf_op jit(solution)/shard_map/ppermute | solution.py:286
  56.5 16.0 %collective-permute-start.17 = (bf16[128,1024]{1,0:T(8,128)(2,1)S(1)}, bf16[128,1024]{1,0:T(8,128)(2,1)S(1)}, u32[]{:S(2)}, u32[]{:S(2)}) collective-permute-start(bf16[128,1024]{1,0:T(8,128)(2,1)S(1)} %get-tuple-element.71.left), channel_id=1, source_target_pairs={{4,5},{5,6},{6,7},{7,4},{12,13},{13,14},{14,15},{15,12},{20,21},{2... | collective-permute-start | bytes 786440 | tf_op jit(solution)/shard_map/ppermute | solution.py:286
  58.4 16.9 %collective-permute-start.18 = (bf16[128,1024]{1,0:T(8,128)(2,1)S(1)}, bf16[128,1024]{1,0:T(8,128)(2,1)S(1)}, u32[]{:S(2)}, u32[]{:S(2)}) collective-permute-start(bf16[128,1024]{1,0:T(8,128)(2,1)S(1)} %get-tuple-element.71.left), channel_id=1, source_target_pairs={{4,6},{5,7},{6,4},{7,5},{12,14},{13,15},{14,12},{15,13},{20,22},{2... | collective-permute-start | bytes 786440 | tf_op jit(solution)/shard_map/ppermute | solution.py:286
  64.4 11.9 %collective-permute-start.19 = (bf16[128,1024]{1,0:T(8,128)(2,1)S(1)}, bf16[128,1024]{1,0:T(8,128)(2,1)S(1)}, u32[]{:S(2)}, u32[]{:S(2)}) collective-permute-start(bf16[128,1024]{1,0:T(8,128)(2,1)S(1)} %get-tuple-element.71.left), channel_id=1, source_target_pairs={{4,7},{5,4},{6,5},{7,6},{12,15},{13,12},{14,13},{15,14},{20,23},{2... | collective-permute-start | bytes 786440 | tf_op jit(solution)/shard_map/ppermute | solution.py:286

commit v8 on v7

--- a/solution.py
+++ b/solution.py
@@ -314,7 +314,6 @@
     relaxed_sent, inputs_sent = lax.optimization_barrier((relaxed_sent, inputs_sent))
     relaxed_got = along(relaxed_sent, up)
     far_inputs = [across(inputs_sent, [(0, 0)], by) for by in range(1, parts)]
-    relaxed_got, *far_inputs = lax.optimization_barrier((relaxed_got, *far_inputs))
     start, forcing, pair_bias, ahead, forcing_sent = call(
         functools.partial(ahead_kernel, step_size, rows),
         (kept(inputs), kept(inputs), pltpu.VMEM((8, depth), F32), plain((rows, depth), BF16), plain((rows, depth), BF16)),
@@ -360,7 +359,8 @@
         after = single(4.0 * step_size, along(ahead, up_pair), forcing)
         top_0 = jnp.where((slot == 1) & (group > 0), after.astype(BF16), ahead)
     got_1, mid_1, top_1 = two_steps(
-        top_0, [(4 * m + 1, 4 * m + 3) for m in range(groups - 1)], lambda slot, group: (slot == 3) & (group < last_group)
+        top_0, [(4 * m + 1, 4 * m + 3) for m in range(groups - 1)], lambda slot, group: (slot == 3) & (group < last_group),
+        beside=far_inputs,
     )
     top_1, *sent_adjoints = lax.optimization_barrier((top_1, *sent_adjoints))
     adjoints = sent_adjoints[:1] + [shifted(sent_adjoints[by], by) for by in range(1, parts)]

time: 79.4 us -> 74.8 us (0.942)
  the two profiles are of different devices: /device:TPU:9 before, /device:TPU:13 now
where the time goes in v8:
time: 74.8 us; the launch traced here: 74.2 us
  starting transfers between devices  33.6 us (45%)
  waiting for transfers between devices  23.8 us (32%)
  Pallas kernels  13.8 us (18%)
  local copies, waits for them, and re-layouts  2.09 us (3%)
  between operations  0.96 us (1%)
    ppermute x8, starting transfers between devices, along(): return lax.ppermute(state, 'layer', pairs)  15.2 us
    ppermute x9, starting transfers between devices, across(): return lax.ppermute(state, ('layer', 'dp'), flat)  14.5 us
    pallas_call x14, Pallas kernels, call(): pl.pallas_call(kernel, out_shape=outs, in_specs=specs or [WHOLE] * len(ar...  13.8 us
    ppermute x9, waiting for transfers between devices, across(): return lax.ppermute(state, ('layer', 'dp'), flat)  9.52 us
    ppermute x8, waiting for transfers between devices, along(): return lax.ppermute(state, 'layer', pairs)  8.97 us
    ppermute x3, waiting for transfers between devices, shifted(): lax.ppermute(array, 'dp', [(i, (i + by) % parts) for i in range(parts)])  5.32 us
    ppermute x3, starting transfers between devices, shifted(): lax.ppermute(array, 'dp', [(i, (i + by) % parts) for i in range(parts)])  3.84 us
    unnamed x10, local copies, waits for them, and re-layouts  2.09 us
  transfers between devices with their start and end apart: 20, of which 9 were waited for; matrix products, arithmetic and copies ran while one was open for 0% of the time, Pallas kernels for 14%

profile of v8, /device:TPU:13, one launch (start us, length us, event | category | flops | bytes accessed | tf_op | source)
XLA Modules:
  0.0 74.2 jit_solution(5827502137227019828)
XLA Ops:
  0.6 0.0 copy-start
  0.6 1.0 %copy-done = f32[128,1024]{1,0:T(8,128)S(1)} copy-done((f32[128,1024]{1,0:T(8,128)S(1)}, f32[128,1024]{1,0:T(8,128)}, u32[]{:S(2)}) %copy-start) | copy-done | bytes 524312
  1.7 1.0 %copy-done.3 = f32[1,128,1024]{2,1,0:T(8,128)S(1)} copy-done((f32[1,128,1024]{2,1,0:T(8,128)S(1)}, f32[1,128,1024]{2,1,0:T(8,128)}, u32[]{:S(2)}) %copy-start.3) | copy-done | bytes 524312
  2.7 0.1 shard_map.76
  2.8 3.7 %collective-permute-start = (bf16[128,1024]{1,0:T(8,128)(2,1)S(1)}, bf16[128,1024]{1,0:T(8,128)(2,1)S(1)}, u32[]{:S(2)}, u32[]{:S(2)}) collective-permute-start(bf16[128,1024]{1,0:T(8,128)(2,1)S(1)} %get-tuple-element.37), channel_id=1, source_target_pairs={{0,4},{4,8},{8,12},{12,16},{16,20},{20,24},{24,28},{1,5},{5,9},{9,... | collective-permute-start | bytes 786440 | tf_op jit(solution)/shard_map/ppermute | solution.py:282
  6.5 3.5 %shard_map.77 = (bf16[4,1024,1024]{2,1,0:T(8,128)(2,1)S(1)}, bf16[1024,1024]{1,0:T(8,128)(2,1)S(1)}) custom-call(bf16[4,1024,1024]{2,1,0:T(8,128)(2,1)} %source), custom_call_target="tpu_custom_call" | custom-call | bytes 8388608 | tf_op jit(solution)/shard_map/pallas_call | solution.py:20
  10.0 0.0 collective-permute-done.got
  10.0 1.3 %collective-permute-start.6 = (bf16[1024,1024]{1,0:T(8,128)(2,1)S(1)}, bf16[1024,1024]{1,0:T(8,128)(2,1)S(1)}, u32[]{:S(2)}, u32[]{:S(2)}) collective-permute-start(bf16[1024,1024]{1,0:T(8,128)(2,1)S(1)} %get-tuple-element.50), channel_id=1, source_target_pairs={{0,4},{8,12},{16,20},{24,28},{1,5},{9,13},{17,21},{25,29},{2,6},{1... | collective-permute-start | bytes 6291464 | tf_op jit(solution)/shard_map/ppermute | solution.py:282
  11.3 0.0 copy-start.4
  11.3 1.6 %shard_map.78 = (f32[128,1024]{1,0:T(8,128)S(1)}, bf16[144,1024]{1,0:T(8,128)(2,1)S(1)}) custom-call(bf16[4,1024,1024]{2,1,0:T(8,128)(2,1)S(1)} %get-tuple-element.39.weights, f32[4,1024]{1,0:T(4,128)S(1)} %copy-done.2, f32[128,1024]{1,0:T(8,128)S(1)} %copy-done, bf16[128,1024]{1,0:T(8,128)(2,1)S(1)} %collective-permute-done.got), custom_call_target="tpu_custom_call" | custom-call | flops 1073741824 | bytes 9191424 | tf_op jit(solution)/shard_map/pallas_call | solution.py:20
  12.9 4.2 %collective-permute-start.1 = (bf16[144,1024]{1,0:T(8,128)(2,1)S(1)}, bf16[144,1024]{1,0:T(8,128)(2,1)S(1)}, u32[]{:S(2)}, u32[]{:S(2)}) collective-permute-start(bf16[144,1024]{1,0:T(8,128)(2,1)S(1)} %get-tuple-element.44), channel_id=1, source_target_pairs={{0,4},{4,8},{8,12},{12,16},{16,20},{20,24},{24,28},{1,5},{5,9},{9,... | collective-permute-start | bytes 884744 | tf_op jit(solution)/shard_map/ppermute | solution.py:282
  17.2 0.7 collective-permute-start.3
  17.8 0.7 collective-permute-start.4
  18.5 0.7 collective-permute-start.5
  19.2 1.6 %collective-permute-done.1.got = bf16[144,1024]{1,0:T(8,128)(2,1)S(1)} collective-permute-done((bf16[144,1024]{1,0:T(8,128)(2,1)S(1)}, bf16[144,1024]{1,0:T(8,128)(2,1)S(1)}, u32[]{:S(2)}, u32[]{:S(2)}) %collective-permute-start.1) | collective-permute-done | bytes 294944 | tf_op jit(solution)/shard_map/ppermute | solution.py:282
  20.8 1.5 %shard_map.79 = (f32[128,1024]{1,0:T(8,128)S(1)}, f32[128,1024]{1,0:T(8,128)S(1)}, f32[8,1024]{1,0:T(8,128)S(1)}, bf16[128,1024]{1,0:T(8,128)(2,1)S(1)}, bf16[128,1024]{1,0:T(8,128)(2,1)S(1)}) custom-call(bf16[4,1024,1024]{2,1,0:T(8,128)(2,1)S(1)} %get-tuple-element.39.weights, f32[4,1024]{1,0:T(4,128)S(1)} %copy-done.2, f32[128,1024]{1,0:T(8,128)S(1)} %copy-done, ...), custom_call_target="tpu_custom_call" | custom-call | flops 1073741824 | bytes 9224192 | tf_op jit(solution)/shard_map/pallas_call | solution.py:20
  22.3 0.7 collective-permute-start.2
  23.0 0.0 collective-permute-done.3.refs_0_
  23.0 1.3 %collective-permute-start.7 = (bf16[128,1024]{1,0:T(8,128)(2,1)S(1)}, bf16[128,1024]{1,0:T(8,128)(2,1)S(1)}, u32[]{:S(2)}, u32[]{:S(2)}) collective-permute-start(bf16[128,1024]{1,0:T(8,128)(2,1)S(1)} %get-tuple-element.52), channel_id=1, source_target_pairs={{0,4},{8,12},{16,20},{24,28},{1,5},{9,13},{17,21},{25,29},{2,6},{1... | collective-permute-start | bytes 786440 | tf_op jit(solution)/shard_map/ppermute | solution.py:282
  24.4 0.0 collective-permute-done.4.refs_1_
  24.4 0.0 collective-permute-done.5.refs_2_
  24.4 4.1 %collective-permute-done.7.pair_forcing = bf16[128,1024]{1,0:T(8,128)(2,1)S(1)} collective-permute-done((bf16[128,1024]{1,0:T(8,128)(2,1)S(1)}, bf16[128,1024]{1,0:T(8,128)(2,1)S(1)}, u32[]{:S(2)}, u32[]{:S(2)}) %collective-permute-start.7) | collective-permute-done | bytes 262176 | tf_op jit(solution)/shard_map/ppermute | solution.py:282
  28.5 1.3 %collective-permute-start.8 = (bf16[128,1024]{1,0:T(8,128)(2,1)S(1)}, bf16[128,1024]{1,0:T(8,128)(2,1)S(1)}, u32[]{:S(2)}, u32[]{:S(2)}) collective-permute-start(bf16[128,1024]{1,0:T(8,128)(2,1)S(1)} %get-tuple-element.58.before), channel_id=1, source_target_pairs={{12,20},{13,21},{14,22},{15,23}} | collective-permute-start | bytes 786440 | tf_op jit(solution)/shard_map/ppermute | solution.py:282
  29.8 1.4 %collective-permute-start.9 = (bf16[128,256]{1,0:T(8,128)(2,1)S(1)}, bf16[128,256]{1,0:T(8,128)(2,1)S(1)}, u32[]{:S(2)}, u32[]{:S(2)}) collective-permute-start(bf16[128,256]{1,0:T(8,128)(2,1)S(1)} %get-tuple-element.60), channel_id=1, source_target_pairs={{0,1},{1,2},{2,3},{3,0},{4,5},{5,6},{6,7},{7,4},{8,9},{9,10},{10,1... | collective-permute-start | bytes 196616 | tf_op jit(solution)/shard_map/ppermute | solution.py:289
  31.2 1.1 %collective-permute-start.10 = (bf16[128,256]{1,0:T(8,128)(2,1)S(1)}, bf16[128,256]{1,0:T(8,128)(2,1)S(1)}, u32[]{:S(2)}, u32[]{:S(2)}) collective-permute-start(bf16[128,256]{1,0:T(8,128)(2,1)S(1)} %get-tuple-element.61), channel_id=1, source_target_pairs={{0,2},{1,3},{2,0},{3,1},{4,6},{5,7},{6,4},{7,5},{8,10},{9,11},{10,... | collective-permute-start | bytes 196616 | tf_op jit(solution)/shard_map/ppermute | solution.py:289
  32.3 1.4 %collective-permute-start.11 = (bf16[128,256]{1,0:T(8,128)(2,1)S(1)}, bf16[128,256]{1,0:T(8,128)(2,1)S(1)}, u32[]{:S(2)}, u32[]{:S(2)}) collective-permute-start(bf16[128,256]{1,0:T(8,128)(2,1)S(1)} %get-tuple-element.62), channel_id=1, source_target_pairs={{0,3},{1,0},{2,1},{3,2},{4,7},{5,4},{6,5},{7,6},{8,11},{9,8},{10,9... | collective-permute-start | bytes 196616 | tf_op jit(solution)/shard_map/ppermute | solution.py:289
  33.7 0.3 collective-permute-done.9.refs_6_.refs_3_
  34.0 3.2 %collective-permute-done.10.refs_7_.refs_4_ = bf16[128,256]{1,0:T(8,128)(2,1)S(1)} collective-permute-done((bf16[128,256]{1,0:T(8,128)(2,1)S(1)}, bf16[128,256]{1,0:T(8,128)(2,1)S(1)}, u32[]{:S(2)}, u32[]{:S(2)}) %collective-permute-start.10) | collective-permute-done | bytes 65568 | tf_op jit(solution)/shard_map/ppermute | solution.py:289
  37.2 1.8 %collective-permute-done.11.refs_8_.refs_5_ = bf16[128,256]{1,0:T(8,128)(2,1)S(1)} collective-permute-done((bf16[128,256]{1,0:T(8,128)(2,1)S(1)}, bf16[128,256]{1,0:T(8,128)(2,1)S(1)}, u32[]{:S(2)}, u32[]{:S(2)}) %collective-permute-start.11) | collective-permute-done | bytes 65568 | tf_op jit(solution)/shard_map/ppermute | solution.py:289
  39.0 0.9 %shard_map.82 = (f32[128,1024]{1,0:T(8,128)S(1)}, bf16[128,1024]{1,0:T(8,128)(2,1)S(1)}) custom-call(bf16[4,1024,1024]{2,1,0:T(8,128)(2,1)S(1)} %get-tuple-element.39.weights, f32[4,1024]{1,0:T(4,128)S(1)} %copy-done.2, f32[128,1024]{1,0:T(8,128)S(1)} %get-tuple-element.49.forcing, bf16[1024,1024]{1,0:T(8,128)(2,1)S(1)} %collective-permute-done.6.pair_weight, ...), custom_call_target="tpu_custom_call" | custom-call | flops 536870912 | bytes 11845632 | tf_op jit(solution)/shard_map/pallas_call | solution.py:20
  39.9 0.0 copy-start.1
  39.9 1.4 %collective-permute-start.12 = (bf16[128,1024]{1,0:T(8,128)(2,1)S(1)}, bf16[128,1024]{1,0:T(8,128)(2,1)S(1)}, u32[]{:S(2)}, u32[]{:S(2)}) collective-permute-start(bf16[128,1024]{1,0:T(8,128)(2,1)S(1)} %get-tuple-element.64.before), channel_id=1, source_target_pairs={{20,28},{21,29},{22,30},{23,31}} | collective-permute-start | bytes 786440 | tf_op jit(solution)/shard_map/ppermute | solution.py:282
  41.4 3.3 %collective-permute-done.12.got_3.got = bf16[128,1024]{1,0:T(8,128)(2,1)S(1)} collective-permute-done((bf16[128,1024]{1,0:T(8,128)(2,1)S(1)}, bf16[128,1024]{1,0:T(8,128)(2,1)S(1)}, u32[]{:S(2)}, u32[]{:S(2)}) %collective-permute-start.12) | collective-permute-done | bytes 262176 | tf_op jit(solution)/shard_map/ppermute | solution.py:282
  44.7 1.3 %collective-permute-start.13 = (bf16[128,1024]{1,0:T(8,128)(2,1)S(1)}, bf16[128,1024]{1,0:T(8,128)(2,1)S(1)}, u32[]{:S(2)}, u32[]{:S(2)}) collective-permute-start(bf16[128,1024]{1,0:T(8,128)(2,1)S(1)} %shard_map.83), channel_id=1, source_target_pairs={{4,0},{12,8},{20,16},{28,24},{5,1},{13,9},{21,17},{29,25},{6,2},{1... | collective-permute-start | bytes 786440 | tf_op jit(solution)/shard_map/ppermute | solution.py:282
  46.0 1.3 %collective-permute-start.14 = (bf16[128,1024]{1,0:T(8,128)(2,1)S(1)}, bf16[128,1024]{1,0:T(8,128)(2,1)S(1)}, u32[]{:S(2)}, u32[]{:S(2)}) collective-permute-start(bf16[128,1024]{1,0:T(8,128)(2,1)S(1)} %get-tuple-element.64.before), channel_id=1, source_target_pairs={{4,9},{5,10},{6,11},{7,8},{12,17},{13,18},{14,19},{15,16},{20,25},... | collective-permute-start | bytes 786440 | tf_op jit(solution)/shard_map/ppermute | solution.py:286
  47.3 1.3 %collective-permute-start.15 = (bf16[128,1024]{1,0:T(8,128)(2,1)S(1)}, bf16[128,1024]{1,0:T(8,128)(2,1)S(1)}, u32[]{:S(2)}, u32[]{:S(2)}) collective-permute-start(bf16[128,1024]{1,0:T(8,128)(2,1)S(1)} %get-tuple-element.64.before), channel_id=1, source_target_pairs={{4,10},{5,11},{6,8},{7,9},{12,18},{13,19},{14,16},{15,17},{20,26},... | collective-permute-start | bytes 786440 | tf_op jit(solution)/shard_map/ppermute | solution.py:286
  48.6 1.3 %collective-permute-start.16 = (bf16[128,1024]{1,0:T(8,128)(2,1)S(1)}, bf16[128,1024]{1,0:T(8,128)(2,1)S(1)}, u32[]{:S(2)}, u32[]{:S(2)}) collective-permute-start(bf16[128,1024]{1,0:T(8,128)(2,1)S(1)} %get-tuple-element.64.before), channel_id=1, source_target_pairs={{4,11},{5,8},{6,9},{7,10},{12,19},{13,16},{14,17},{15,18},{20,27},... | collective-permute-start | bytes 786440 | tf_op jit(solution)/shard_map/ppermute | solution.py:286
  50.0 1.4 %shard_map.85 = (bf16[128,1024]{1,0:T(8,128)(2,1)S(1)}, f32[128,1024]{1,0:T(8,128)S(1)}, f32[128,1024]{1,0:T(8,128)}) custom-call(bf16[4,1024,1024]{2,1,0:T(8,128)(2,1)S(1)} %get-tuple-element.39.weights, f32[4,1024]{1,0:T(4,128)S(1)} %copy-done.2, f32[128,1024]{1,0:T(8,128)S(1)} %copy-done.1, f32[128,1024]{1,0:T(8,128)S(1)} %get-tuple-element.45.one, ...), custom_call_target="tpu_custom_call" | custom-call | flops 805306368 | bytes 12337152 | tf_op jit(solution)/shard_map/pallas_call | solution.py:20
  51.4 1.9 %collective-permute-start.17 = (bf16[128,1024]{1,0:T(8,128)(2,1)S(1)}, bf16[128,1024]{1,0:T(8,128)(2,1)S(1)}, u32[]{:S(2)}, u32[]{:S(2)}) collective-permute-start(bf16[128,1024]{1,0:T(8,128)(2,1)S(1)} %get-tuple-element.68.left), channel_id=1, source_target_pairs={{4,5},{5,6},{6,7},{7,4},{12,13},{13,14},{14,15},{15,12},{20,21},{2... | collective-permute-start | bytes 786440 | tf_op jit(solution)/shard_map/ppermute | solution.py:286
  53.4 3.8 %collective-permute-start.18 = (bf16[128,1024]{1,0:T(8,128)(2,1)S(1)}, bf16[128,1024]{1,0:T(8,128)(2,1)S(1)}, u32[]{:S(2)}, u32[]{:S(2)}) collective-permute-start(bf16[128,1024]{1,0:T(8,128)(2,1)S(1)} %get-tuple-element.68.left), channel_id=1, source_target_pairs={{4,6},{5,7},{6,4},{7,5},{12,14},{13,15},{14,12},{15,13},{20,22},{2... | collective-permute-start | bytes 786440 | tf_op jit(solution)/shard_map/ppermute | solution.py:286
  57.1 0.7 shard_map.87.total
  57.8 1.3 %shard_map.86 = f32[128,1024]{1,0:T(8,128)} custom-call(bf16[4,1024,1024]{2,1,0:T(8,128)(2,1)S(1)} %get-tuple-element.39.weights, f32[4,1024]{1,0:T(4,128)S(1)} %copy-done.2, bf16[128,1024]{1,0:T(8,128)(2,1)S(1)} %get-tuple-element.68.left, f32[128,1024]{1,0:T(8,128)S(1)} %get-tuple-element.69.state), custom_call_target="tpu_custom_call" | custom-call | flops 268435456 | bytes 9191424 | tf_op jit(solution)/shard_map/pallas_call | solution.py:20
  59.0 2.9 %collective-permute-start.19 = (bf16[128,1024]{1,0:T(8,128)(2,1)S(1)}, bf16[128,1024]{1,0:T(8,128)(2,1)S(1)}, u32[]{:S(2)}, u32[]{:S(2)}) collective-permute-start(bf16[128,1024]{1,0:T(8,128)(2,1)S(1)} %get-tuple-element.68.left), channel_id=1, source_target_pairs={{4,7},{5,4},{6,5},{7,6},{12,15},{13,12},{14,13},{15,14},{20,23},{2... | collective-permute-start | bytes 786440 | tf_op jit(solution)/shard_map/ppermute | solution.py:286
  62.0 0.3 shard_map.88.total
  62.2 5.2 %collective-permute-done.17.refs_0_ = bf16[128,1024]{1,0:T(8,128)(2,1)S(1)} collective-permute-done((bf16[128,1024]{1,0:T(8,128)(2,1)S(1)}, bf16[128,1024]{1,0:T(8,128)(2,1)S(1)}, u32[]{:S(2)}, u32[]{:S(2)}) %collective-permute-start.17) | collective-permute-done | bytes 262176 | tf_op jit(solution)/shard_map/ppermute | solution.py:286
  67.5 2.8 %collective-permute-done.18.refs_1_ = bf16[128,1024]{1,0:T(8,128)(2,1)S(1)} collective-permute-done((bf16[128,1024]{1,0:T(8,128)(2,1)S(1)}, bf16[128,1024]{1,0:T(8,128)(2,1)S(1)}, u32[]{:S(2)}, u32[]{:S(2)}) %collective-permute-start.18) | collective-permute-done | bytes 262176 | tf_op jit(solution)/shard_map/ppermute | solution.py:286
  70.3 1.5 %collective-permute-done.19.refs_2_ = bf16[128,1024]{1,0:T(8,128)(2,1)S(1)} collective-permute-done((bf16[128,1024]{1,0:T(8,128)(2,1)S(1)}, bf16[128,1024]{1,0:T(8,128)(2,1)S(1)}, u32[]{:S(2)}, u32[]{:S(2)}) %collective-permute-start.19) | collective-permute-done | bytes 262176 | tf_op jit(solution)/shard_map/ppermute | solution.py:286
  71.8 2.5 %shard_map.89 = f32[1024,256]{1,0:T(8,128)} custom-call(bf16[4,1024,1024]{2,1,0:T(8,128)(2,1)S(1)} %get-tuple-element.39.weights, f32[4,1024]{1,0:T(4,128)S(1)} %copy-done.2, f32[1024,256]{1,0:T(8,128)S(1)} %shard_map.88.total, bf16[128,1024]{1,0:T(8,128)(2,1)S(1)} %collective-permute-done.17.refs_0_, bf16[128,1024]{1,0:T(8,128)(2,1)S(1)} %collective-permute-done.18.refs_1_, ...), custom_call_target="tpu_custom_call" | custom-call | flops 536870912 | bytes 10436608 | tf_op jit(solution)/shard_map/pallas_call | solution.py:20
  (16 shorter events, 0.2 us)
Async XLA Ops:
  0.6 1.0 %copy-start = (f32[128,1024]{1,0:T(8,128)S(1)}, f32[128,1024]{1,0:T(8,128)}, u32[]{:S(2)}) copy-start(f32[128,1024]{1,0:T(8,128)} %inputs.7) | copy-start | bytes 1572868
  1.7 1.0 %copy-start.3 = (f32[1,128,1024]{2,1,0:T(8,128)S(1)}, f32[1,128,1024]{2,1,0:T(8,128)}, u32[]{:S(2)}) copy-start(f32[1,128,1024]{2,1,0:T(8,128)} %param.6) | copy-start | bytes 1572868
  2.7 8.6 %copy-start.2 = (f32[4,1024]{1,0:T(4,128)S(1)}, f32[4,1024]{1,0:T(4,128)}, u32[]{:S(2)}) copy-start(f32[4,1024]{1,0:T(4,128)} %biases.19) | copy-start | bytes 49156
  2.8 7.2 %collective-permute-start = (bf16[128,1024]{1,0:T(8,128)(2,1)S(1)}, bf16[128,1024]{1,0:T(8,128)(2,1)S(1)}, u32[]{:S(2)}, u32[]{:S(2)}) collective-permute-start(bf16[128,1024]{1,0:T(8,128)(2,1)S(1)} %get-tuple-element.37), channel_id=1, source_target_pairs={{0,4},{4,8},{8,12},{12,16},{16,20},{20,24},{24,28},{1,5},{5,9},{9,... | collective-permute-start | bytes 786440 | tf_op jit(solution)/shard_map/ppermute | solution.py:282
  10.0 18.5 %collective-permute-start.6 = (bf16[1024,1024]{1,0:T(8,128)(2,1)S(1)}, bf16[1024,1024]{1,0:T(8,128)(2,1)S(1)}, u32[]{:S(2)}, u32[]{:S(2)}) collective-permute-start(bf16[1024,1024]{1,0:T(8,128)(2,1)S(1)} %get-tuple-element.50), channel_id=1, source_target_pairs={{0,4},{8,12},{16,20},{24,28},{1,5},{9,13},{17,21},{25,29},{2,6},{1... | collective-permute-start | bytes 6291464 | tf_op jit(solution)/shard_map/ppermute | solution.py:282
  11.3 13.0 %copy-start.4 = (bf16[1,128,1024]{2,1,0:T(8,128)(2,1)S(1)}, bf16[1,128,1024]{2,1,0:T(8,128)(2,1)}, u32[]{:S(2)}) copy-start(bf16[1,128,1024]{2,1,0:T(8,128)(2,1)} %param.9) | copy-start | bytes 786436
  12.9 7.9 %collective-permute-start.1 = (bf16[144,1024]{1,0:T(8,128)(2,1)S(1)}, bf16[144,1024]{1,0:T(8,128)(2,1)S(1)}, u32[]{:S(2)}, u32[]{:S(2)}) collective-permute-start(bf16[144,1024]{1,0:T(8,128)(2,1)S(1)} %get-tuple-element.44), channel_id=1, source_target_pairs={{0,4},{4,8},{8,12},{12,16},{16,20},{20,24},{24,28},{1,5},{5,9},{9,... | collective-permute-start | bytes 884744 | tf_op jit(solution)/shard_map/ppermute | solution.py:282
  17.2 5.9 %collective-permute-start.3 = (bf16[128,1024]{1,0:T(8,128)(2,1)S(1)}, bf16[128,1024]{1,0:T(8,128)(2,1)S(1)}, u32[]{:S(2)}, u32[]{:S(2)}) collective-permute-start(bf16[128,1024]{1,0:T(8,128)(2,1)S(1)} %get-tuple-element.47), channel_id=1, source_target_pairs={{0,1},{1,2},{2,3},{3,0}} | collective-permute-start | bytes 786440 | tf_op jit(solution)/shard_map/ppermute | solution.py:286
  17.8 6.6 %collective-permute-start.4 = (bf16[128,1024]{1,0:T(8,128)(2,1)S(1)}, bf16[128,1024]{1,0:T(8,128)(2,1)S(1)}, u32[]{:S(2)}, u32[]{:S(2)}) collective-permute-start(bf16[128,1024]{1,0:T(8,128)(2,1)S(1)} %get-tuple-element.47), channel_id=1, source_target_pairs={{0,2},{1,3},{2,0},{3,1}} | collective-permute-start | bytes 786440 | tf_op jit(solution)/shard_map/ppermute | solution.py:286
  18.5 5.9 %collective-permute-start.5 = (bf16[128,1024]{1,0:T(8,128)(2,1)S(1)}, bf16[128,1024]{1,0:T(8,128)(2,1)S(1)}, u32[]{:S(2)}, u32[]{:S(2)}) collective-permute-start(bf16[128,1024]{1,0:T(8,128)(2,1)S(1)} %get-tuple-element.47), channel_id=1, source_target_pairs={{0,3},{1,0},{2,1},{3,2}} | collective-permute-start | bytes 786440 | tf_op jit(solution)/shard_map/ppermute | solution.py:286
  22.3 2.1 %collective-permute-start.2 = (bf16[128,1024]{1,0:T(8,128)(2,1)S(1)}, bf16[128,1024]{1,0:T(8,128)(2,1)S(1)}, u32[]{:S(2)}, u32[]{:S(2)}) collective-permute-start(bf16[128,1024]{1,0:T(8,128)(2,1)S(1)} %get-tuple-element.46.before), channel_id=1, source_target_pairs={{4,12},{5,13},{6,14},{7,15}} | collective-permute-start | bytes 786440 | tf_op jit(solution)/shard_map/ppermute | solution.py:282
  23.0 5.5 %collective-permute-start.7 = (bf16[128,1024]{1,0:T(8,128)(2,1)S(1)}, bf16[128,1024]{1,0:T(8,128)(2,1)S(1)}, u32[]{:S(2)}, u32[]{:S(2)}) collective-permute-start(bf16[128,1024]{1,0:T(8,128)(2,1)S(1)} %get-tuple-element.52), channel_id=1, source_target_pairs={{0,4},{8,12},{16,20},{24,28},{1,5},{9,13},{17,21},{25,29},{2,6},{1... | collective-permute-start | bytes 786440 | tf_op jit(solution)/shard_map/ppermute | solution.py:282
  28.5 10.5 %collective-permute-start.8 = (bf16[128,1024]{1,0:T(8,128)(2,1)S(1)}, bf16[128,1024]{1,0:T(8,128)(2,1)S(1)}, u32[]{:S(2)}, u32[]{:S(2)}) collective-permute-start(bf16[128,1024]{1,0:T(8,128)(2,1)S(1)} %get-tuple-element.58.before), channel_id=1, source_target_pairs={{12,20},{13,21},{14,22},{15,23}} | collective-permute-start | bytes 786440 | tf_op jit(solution)/shard_map/ppermute | solution.py:282
  29.8 4.1 %collective-permute-start.9 = (bf16[128,256]{1,0:T(8,128)(2,1)S(1)}, bf16[128,256]{1,0:T(8,128)(2,1)S(1)}, u32[]{:S(2)}, u32[]{:S(2)}) collective-permute-start(bf16[128,256]{1,0:T(8,128)(2,1)S(1)} %get-tuple-element.60), channel_id=1, source_target_pairs={{0,1},{1,2},{2,3},{3,0},{4,5},{5,6},{6,7},{7,4},{8,9},{9,10},{10,1... | collective-permute-start | bytes 196616 | tf_op jit(solution)/shard_map/ppermute | solution.py:289
  31.2 6.0 %collective-permute-start.10 = (bf16[128,256]{1,0:T(8,128)(2,1)S(1)}, bf16[128,256]{1,0:T(8,128)(2,1)S(1)}, u32[]{:S(2)}, u32[]{:S(2)}) collective-permute-start(bf16[128,256]{1,0:T(8,128)(2,1)S(1)} %get-tuple-element.61), channel_id=1, source_target_pairs={{0,2},{1,3},{2,0},{3,1},{4,6},{5,7},{6,4},{7,5},{8,10},{9,11},{10,... | collective-permute-start | bytes 196616 | tf_op jit(solution)/shard_map/ppermute | solution.py:289
  32.3 6.7 %collective-permute-start.11 = (bf16[128,256]{1,0:T(8,128)(2,1)S(1)}, bf16[128,256]{1,0:T(8,128)(2,1)S(1)}, u32[]{:S(2)}, u32[]{:S(2)}) collective-permute-start(bf16[128,256]{1,0:T(8,128)(2,1)S(1)} %get-tuple-element.62), channel_id=1, source_target_pairs={{0,3},{1,0},{2,1},{3,2},{4,7},{5,4},{6,5},{7,6},{8,11},{9,8},{10,9... | collective-permute-start | bytes 196616 | tf_op jit(solution)/shard_map/ppermute | solution.py:289
  39.9 10.1 %copy-start.1 = (f32[128,1024]{1,0:T(8,128)S(1)}, f32[128,1024]{1,0:T(8,128)}, u32[]{:S(2)}) copy-start(f32[128,1024]{1,0:T(8,128)} %inputs.7) | copy-start | bytes 1572868
  39.9 4.7 %collective-permute-start.12 = (bf16[128,1024]{1,0:T(8,128)(2,1)S(1)}, bf16[128,1024]{1,0:T(8,128)(2,1)S(1)}, u32[]{:S(2)}, u32[]{:S(2)}) collective-permute-start(bf16[128,1024]{1,0:T(8,128)(2,1)S(1)} %get-tuple-element.64.before), channel_id=1, source_target_pairs={{20,28},{21,29},{22,30},{23,31}} | collective-permute-start | bytes 786440 | tf_op jit(solution)/shard_map/ppermute | solution.py:282
  44.7 5.3 %collective-permute-start.13 = (bf16[128,1024]{1,0:T(8,128)(2,1)S(1)}, bf16[128,1024]{1,0:T(8,128)(2,1)S(1)}, u32[]{:S(2)}, u32[]{:S(2)}) collective-permute-start(bf16[128,1024]{1,0:T(8,128)(2,1)S(1)} %shard_map.83), channel_id=1, source_target_pairs={{4,0},{12,8},{20,16},{28,24},{5,1},{13,9},{21,17},{29,25},{6,2},{1... | collective-permute-start | bytes 786440 | tf_op jit(solution)/shard_map/ppermute | solution.py:282
  46.0 13.0 %collective-permute-start.14 = (bf16[128,1024]{1,0:T(8,128)(2,1)S(1)}, bf16[128,1024]{1,0:T(8,128)(2,1)S(1)}, u32[]{:S(2)}, u32[]{:S(2)}) collective-permute-start(bf16[128,1024]{1,0:T(8,128)(2,1)S(1)} %get-tuple-element.64.before), channel_id=1, source_target_pairs={{4,9},{5,10},{6,11},{7,8},{12,17},{13,18},{14,19},{15,16},{20,25},... | collective-permute-start | bytes 786440 | tf_op jit(solution)/shard_map/ppermute | solution.py:286
  47.3 14.6 %collective-permute-start.15 = (bf16[128,1024]{1,0:T(8,128)(2,1)S(1)}, bf16[128,1024]{1,0:T(8,128)(2,1)S(1)}, u32[]{:S(2)}, u32[]{:S(2)}) collective-permute-start(bf16[128,1024]{1,0:T(8,128)(2,1)S(1)} %get-tuple-element.64.before), channel_id=1, source_target_pairs={{4,10},{5,11},{6,8},{7,9},{12,18},{13,19},{14,16},{15,17},{20,26},... | collective-permute-start | bytes 786440 | tf_op jit(solution)/shard_map/ppermute | solution.py:286
  48.6 13.3 %collective-permute-start.16 = (bf16[128,1024]{1,0:T(8,128)(2,1)S(1)}, bf16[128,1024]{1,0:T(8,128)(2,1)S(1)}, u32[]{:S(2)}, u32[]{:S(2)}) collective-permute-start(bf16[128,1024]{1,0:T(8,128)(2,1)S(1)} %get-tuple-element.64.before), channel_id=1, source_target_pairs={{4,11},{5,8},{6,9},{7,10},{12,19},{13,16},{14,17},{15,18},{20,27},... | collective-permute-start | bytes 786440 | tf_op jit(solution)/shard_map/ppermute | solution.py:286
  51.4 16.0 %collective-permute-start.17 = (bf16[128,1024]{1,0:T(8,128)(2,1)S(1)}, bf16[128,1024]{1,0:T(8,128)(2,1)S(1)}, u32[]{:S(2)}, u32[]{:S(2)}) collective-permute-start(bf16[128,1024]{1,0:T(8,128)(2,1)S(1)} %get-tuple-element.68.left), channel_id=1, source_target_pairs={{4,5},{5,6},{6,7},{7,4},{12,13},{13,14},{14,15},{15,12},{20,21},{2... | collective-permute-start | bytes 786440 | tf_op jit(solution)/shard_map/ppermute | solution.py:286
  53.4 16.9 %collective-permute-start.18 = (bf16[128,1024]{1,0:T(8,128)(2,1)S(1)}, bf16[128,1024]{1,0:T(8,128)(2,1)S(1)}, u32[]{:S(2)}, u32[]{:S(2)}) collective-permute-start(bf16[128,1024]{1,0:T(8,128)(2,1)S(1)} %get-tuple-element.68.left), channel_id=1, source_target_pairs={{4,6},{5,7},{6,4},{7,5},{12,14},{13,15},{14,12},{15,13},{20,22},{2... | collective-permute-start | bytes 786440 | tf_op jit(solution)/shard_map/ppermute | solution.py:286
  59.0 12.7 %collective-permute-start.19 = (bf16[128,1024]{1,0:T(8,128)(2,1)S(1)}, bf16[128,1024]{1,0:T(8,128)(2,1)S(1)}, u32[]{:S(2)}, u32[]{:S(2)}) collective-permute-start(bf16[128,1024]{1,0:T(8,128)(2,1)S(1)} %get-tuple-element.68.left), channel_id=1, source_target_pairs={{4,7},{5,4},{6,5},{7,6},{12,15},{13,12},{14,13},{15,14},{20,23},{2... | collective-permute-start | bytes 786440 | tf_op jit(solution)/shard_map/ppermute | solution.py:286

commit v9 on v8

--- a/solution.py
+++ b/solution.py
@@ -46,9 +46,8 @@
     return jnp.tanh(product + bias[:, cols])
 
 
-def round_kernel(guess, inputs, sent_guess, sent_inputs):
+def round_kernel(guess, sent_guess):
     sent_guess[...] = guess[...].astype(BF16)
-    sent_inputs[...] = inputs[...].astype(BF16)
 
 
 def columns_kernel(parts, adjoint, *columns):
@@ -90,7 +89,8 @@
             later[:, cols] = new.astype(BF16)
 
 
-def relax_kernel(step_size, rows, weights, biases, inputs, got, relaxed, sent, even, odd):
+def relax_kernel(step_size, rows, weights, biases, inputs, got, relaxed, sent, sent_inputs, even, odd):
+    sent_inputs[...] = inputs[...].astype(BF16)
     first = lax.axis_index("layer") == 0
 
     @pl.when(first)
@@ -293,7 +293,7 @@
     down_pair = [(i + 1, i) for i in range(0, blocks, 2)]
     rounded = [pltpu.VMEM((rows, depth), BF16)] * 2
 
-    guess_sent, inputs_sent = call(round_kernel, (plain((rows, depth), BF16),) * 2, guesses[0], inputs)
+    guess_sent = call(round_kernel, plain((rows, depth), BF16), guesses[0])
     guess_prev = along(guess_sent, up)
     guess_sent, weights = lax.optimization_barrier((guess_sent, weights))
     held_weights, coarse_weight = call(
@@ -305,13 +305,12 @@
     sent_adjoints = call(
         functools.partial(columns_kernel, parts), (plain((rows, width), BF16),) * parts, adjoint[0]
     )
-    relaxed, relaxed_sent = call(
+    relaxed, relaxed_sent, inputs_sent = call(
         functools.partial(relax_kernel, step_size, rows),
-        (kept(inputs), plain((rows + EXTRA, depth), BF16)),
+        (kept(inputs), plain((rows + EXTRA, depth), BF16), plain((rows, depth), BF16)),
         held_weights, biases, inputs, guess_prev,
         scratch=rounded, flops=4 * layer_flops,
     )
-    relaxed_sent, inputs_sent = lax.optimization_barrier((relaxed_sent, inputs_sent))
     relaxed_got = along(relaxed_sent, up)
     far_inputs = [across(inputs_sent, [(0, 0)], by) for by in range(1, parts)]
     start, forcing, pair_bias, ahead, forcing_sent = call(

time: 74.8 us -> 73.5 us (0.983)
  local copies, waits for them, and re-layouts: 2.09 us -> 1.11 us
    unnamed x10 -> x8, local copies, waits for them, and re-layouts: 2.09 us -> 1.11 us
where the time goes in v9:
time: 73.5 us; the launch traced here: 73.1 us
  starting transfers between devices  33.4 us (45%)
  waiting for transfers between devices  23.8 us (32%)
  Pallas kernels  13.7 us (19%)
  local copies, waits for them, and re-layouts  1.11 us (2%)
  between operations  0.97 us (1%)
    ppermute x8, starting transfers between devices, along(): return lax.ppermute(state, 'layer', pairs)  15.1 us
    ppermute x9, starting transfers between devices, across(): return lax.ppermute(state, ('layer', 'dp'), flat)  14.5 us
    pallas_call x14, Pallas kernels, call(): pl.pallas_call(kernel, out_shape=outs, in_specs=specs or [WHOLE] * len(ar...  13.7 us
    ppermute x9, waiting for transfers between devices, across(): return lax.ppermute(state, ('layer', 'dp'), flat)  9.54 us
    ppermute x8, waiting for transfers between devices, along(): return lax.ppermute(state, 'layer', pairs)  8.98 us
    ppermute x3, waiting for transfers between devices, shifted(): lax.ppermute(array, 'dp', [(i, (i + by) % parts) for i in range(parts)])  5.32 us
    ppermute x3, starting transfers between devices, shifted(): lax.ppermute(array, 'dp', [(i, (i + by) % parts) for i in range(parts)])  3.84 us
  transfers between devices with their start and end apart: 20, of which 9 were waited for; matrix products, arithmetic and copies ran while one was open for 0% of the time, Pallas kernels for 14%

profile of v9, /device:TPU:13, one launch (start us, length us, event | category | flops | bytes accessed | tf_op | source)
XLA Modules:
  0.0 73.1 jit_solution(2607225845288110692)
XLA Ops:
  0.7 1.1 %copy-done.2 = f32[1,128,1024]{2,1,0:T(8,128)S(1)} copy-done((f32[1,128,1024]{2,1,0:T(8,128)S(1)}, f32[1,128,1024]{2,1,0:T(8,128)}, u32[]{:S(2)}) %copy-start.2) | copy-done | bytes 524312
  1.8 3.7 %collective-permute-start = (bf16[128,1024]{1,0:T(8,128)(2,1)S(1)}, bf16[128,1024]{1,0:T(8,128)(2,1)S(1)}, u32[]{:S(2)}, u32[]{:S(2)}) collective-permute-start(bf16[128,1024]{1,0:T(8,128)(2,1)S(1)} %shard_map.76), channel_id=1, source_target_pairs={{0,4},{4,8},{8,12},{12,16},{16,20},{20,24},{24,28},{1,5},{5,9},{9,... | collective-permute-start | bytes 786440 | tf_op jit(solution)/shard_map/ppermute | solution.py:282
  5.5 3.5 %shard_map.77 = (bf16[4,1024,1024]{2,1,0:T(8,128)(2,1)S(1)}, bf16[1024,1024]{1,0:T(8,128)(2,1)S(1)}) custom-call(bf16[4,1024,1024]{2,1,0:T(8,128)(2,1)} %source), custom_call_target="tpu_custom_call" | custom-call | bytes 8388608 | tf_op jit(solution)/shard_map/pallas_call | solution.py:20
  9.0 0.0 collective-permute-done.got
  9.0 1.3 %collective-permute-start.6 = (bf16[1024,1024]{1,0:T(8,128)(2,1)S(1)}, bf16[1024,1024]{1,0:T(8,128)(2,1)S(1)}, u32[]{:S(2)}, u32[]{:S(2)}) collective-permute-start(bf16[1024,1024]{1,0:T(8,128)(2,1)S(1)} %get-tuple-element.44), channel_id=1, source_target_pairs={{0,4},{8,12},{16,20},{24,28},{1,5},{9,13},{17,21},{25,29},{2,6},{1... | collective-permute-start | bytes 6291464 | tf_op jit(solution)/shard_map/ppermute | solution.py:282
  10.3 0.0 copy-start.3
  10.3 1.6 %shard_map.78 = (f32[128,1024]{1,0:T(8,128)S(1)}, bf16[144,1024]{1,0:T(8,128)(2,1)S(1)}, bf16[128,1024]{1,0:T(8,128)(2,1)S(1)}) custom-call(bf16[4,1024,1024]{2,1,0:T(8,128)(2,1)S(1)} %get-tuple-element.35.weights, f32[4,1024]{1,0:T(4,128)S(1)} %copy-done.1, f32[128,1024]{1,0:T(8,128)S(1)} %copy-done, bf16[128,1024]{1,0:T(8,128)(2,1)S(1)} %collective-permute-done.got), custom_call_target="tpu_custom_call" | custom-call | flops 1073741824 | bytes 9191424 | tf_op jit(solution)/shard_map/pallas_call | solution.py:20
  11.9 4.3 %collective-permute-start.1 = (bf16[144,1024]{1,0:T(8,128)(2,1)S(1)}, bf16[144,1024]{1,0:T(8,128)(2,1)S(1)}, u32[]{:S(2)}, u32[]{:S(2)}) collective-permute-start(bf16[144,1024]{1,0:T(8,128)(2,1)S(1)} %get-tuple-element.38), channel_id=1, source_target_pairs={{0,4},{4,8},{8,12},{12,16},{16,20},{20,24},{24,28},{1,5},{5,9},{9,... | collective-permute-start | bytes 884744 | tf_op jit(solution)/shard_map/ppermute | solution.py:282
  16.2 0.7 collective-permute-start.3
  16.9 0.7 collective-permute-start.4
  17.6 0.7 collective-permute-start.5
  18.2 1.6 %collective-permute-done.1.got = bf16[144,1024]{1,0:T(8,128)(2,1)S(1)} collective-permute-done((bf16[144,1024]{1,0:T(8,128)(2,1)S(1)}, bf16[144,1024]{1,0:T(8,128)(2,1)S(1)}, u32[]{:S(2)}, u32[]{:S(2)}) %collective-permute-start.1) | collective-permute-done | bytes 294944 | tf_op jit(solution)/shard_map/ppermute | solution.py:282
  19.8 1.5 %shard_map.79 = (f32[128,1024]{1,0:T(8,128)S(1)}, f32[128,1024]{1,0:T(8,128)S(1)}, f32[8,1024]{1,0:T(8,128)S(1)}, bf16[128,1024]{1,0:T(8,128)(2,1)S(1)}, bf16[128,1024]{1,0:T(8,128)(2,1)S(1)}) custom-call(bf16[4,1024,1024]{2,1,0:T(8,128)(2,1)S(1)} %get-tuple-element.35.weights, f32[4,1024]{1,0:T(4,128)S(1)} %copy-done.1, f32[128,1024]{1,0:T(8,128)S(1)} %copy-done, ...), custom_call_target="tpu_custom_call" | custom-call | flops 1073741824 | bytes 9224192 | tf_op jit(solution)/shard_map/pallas_call | solution.py:20
  21.4 0.7 collective-permute-start.2
  22.0 0.0 collective-permute-done.3.refs_0_
  22.1 1.3 %collective-permute-start.7 = (bf16[128,1024]{1,0:T(8,128)(2,1)S(1)}, bf16[128,1024]{1,0:T(8,128)(2,1)S(1)}, u32[]{:S(2)}, u32[]{:S(2)}) collective-permute-start(bf16[128,1024]{1,0:T(8,128)(2,1)S(1)} %get-tuple-element.46), channel_id=1, source_target_pairs={{0,4},{8,12},{16,20},{24,28},{1,5},{9,13},{17,21},{25,29},{2,6},{1... | collective-permute-start | bytes 786440 | tf_op jit(solution)/shard_map/ppermute | solution.py:282
  23.4 0.0 collective-permute-done.4.refs_1_
  23.4 0.0 collective-permute-done.5.refs_2_
  23.4 0.0 collective-permute-done.2.got.got_1
  23.5 4.1 %collective-permute-done.7.pair_forcing = bf16[128,1024]{1,0:T(8,128)(2,1)S(1)} collective-permute-done((bf16[128,1024]{1,0:T(8,128)(2,1)S(1)}, bf16[128,1024]{1,0:T(8,128)(2,1)S(1)}, u32[]{:S(2)}, u32[]{:S(2)}) %collective-permute-start.7) | collective-permute-done | bytes 262176 | tf_op jit(solution)/shard_map/ppermute | solution.py:282
  27.6 1.3 %collective-permute-start.8 = (bf16[128,1024]{1,0:T(8,128)(2,1)S(1)}, bf16[128,1024]{1,0:T(8,128)(2,1)S(1)}, u32[]{:S(2)}, u32[]{:S(2)}) collective-permute-start(bf16[128,1024]{1,0:T(8,128)(2,1)S(1)} %get-tuple-element.52.before), channel_id=1, source_target_pairs={{12,20},{13,21},{14,22},{15,23}} | collective-permute-start | bytes 786440 | tf_op jit(solution)/shard_map/ppermute | solution.py:282
  28.9 1.3 %collective-permute-start.9 = (bf16[128,256]{1,0:T(8,128)(2,1)S(1)}, bf16[128,256]{1,0:T(8,128)(2,1)S(1)}, u32[]{:S(2)}, u32[]{:S(2)}) collective-permute-start(bf16[128,256]{1,0:T(8,128)(2,1)S(1)} %get-tuple-element.54), channel_id=1, source_target_pairs={{0,1},{1,2},{2,3},{3,0},{4,5},{5,6},{6,7},{7,4},{8,9},{9,10},{10,1... | collective-permute-start | bytes 196616 | tf_op jit(solution)/shard_map/ppermute | solution.py:289
  30.2 1.1 %collective-permute-start.10 = (bf16[128,256]{1,0:T(8,128)(2,1)S(1)}, bf16[128,256]{1,0:T(8,128)(2,1)S(1)}, u32[]{:S(2)}, u32[]{:S(2)}) collective-permute-start(bf16[128,256]{1,0:T(8,128)(2,1)S(1)} %get-tuple-element.55), channel_id=1, source_target_pairs={{0,2},{1,3},{2,0},{3,1},{4,6},{5,7},{6,4},{7,5},{8,10},{9,11},{10,... | collective-permute-start | bytes 196616 | tf_op jit(solution)/shard_map/ppermute | solution.py:289
  31.3 1.4 %collective-permute-start.11 = (bf16[128,256]{1,0:T(8,128)(2,1)S(1)}, bf16[128,256]{1,0:T(8,128)(2,1)S(1)}, u32[]{:S(2)}, u32[]{:S(2)}) collective-permute-start(bf16[128,256]{1,0:T(8,128)(2,1)S(1)} %get-tuple-element.56), channel_id=1, source_target_pairs={{0,3},{1,0},{2,1},{3,2},{4,7},{5,4},{6,5},{7,6},{8,11},{9,8},{10,9... | collective-permute-start | bytes 196616 | tf_op jit(solution)/shard_map/ppermute | solution.py:289
  32.7 0.3 collective-permute-done.9.refs_6_.refs_3_
  33.0 3.2 %collective-permute-done.10.refs_7_.refs_4_ = bf16[128,256]{1,0:T(8,128)(2,1)S(1)} collective-permute-done((bf16[128,256]{1,0:T(8,128)(2,1)S(1)}, bf16[128,256]{1,0:T(8,128)(2,1)S(1)}, u32[]{:S(2)}, u32[]{:S(2)}) %collective-permute-start.10) | collective-permute-done | bytes 65568 | tf_op jit(solution)/shard_map/ppermute | solution.py:289
  36.2 1.8 %collective-permute-done.11.refs_8_.refs_5_ = bf16[128,256]{1,0:T(8,128)(2,1)S(1)} collective-permute-done((bf16[128,256]{1,0:T(8,128)(2,1)S(1)}, bf16[128,256]{1,0:T(8,128)(2,1)S(1)}, u32[]{:S(2)}, u32[]{:S(2)}) %collective-permute-start.11) | collective-permute-done | bytes 65568 | tf_op jit(solution)/shard_map/ppermute | solution.py:289
  38.0 0.0 collective-permute-done.8.got.got_2
  38.0 0.9 %shard_map.82 = (f32[128,1024]{1,0:T(8,128)S(1)}, bf16[128,1024]{1,0:T(8,128)(2,1)S(1)}) custom-call(bf16[4,1024,1024]{2,1,0:T(8,128)(2,1)S(1)} %get-tuple-element.35.weights, f32[4,1024]{1,0:T(4,128)S(1)} %copy-done.1, f32[128,1024]{1,0:T(8,128)S(1)} %get-tuple-element.43.forcing, bf16[1024,1024]{1,0:T(8,128)(2,1)S(1)} %collective-permute-done.6.pair_weight, ...), custom_call_target="tpu_custom_call" | custom-call | flops 536870912 | bytes 11845632 | tf_op jit(solution)/shard_map/pallas_call | solution.py:20
  38.9 1.3 %collective-permute-start.12 = (bf16[128,1024]{1,0:T(8,128)(2,1)S(1)}, bf16[128,1024]{1,0:T(8,128)(2,1)S(1)}, u32[]{:S(2)}, u32[]{:S(2)}) collective-permute-start(bf16[128,1024]{1,0:T(8,128)(2,1)S(1)} %get-tuple-element.58.before), channel_id=1, source_target_pairs={{20,28},{21,29},{22,30},{23,31}} | collective-permute-start | bytes 786440 | tf_op jit(solution)/shard_map/ppermute | solution.py:282
  40.2 3.3 %collective-permute-done.12.got_3.got = bf16[128,1024]{1,0:T(8,128)(2,1)S(1)} collective-permute-done((bf16[128,1024]{1,0:T(8,128)(2,1)S(1)}, bf16[128,1024]{1,0:T(8,128)(2,1)S(1)}, u32[]{:S(2)}, u32[]{:S(2)}) %collective-permute-start.12) | collective-permute-done | bytes 262176 | tf_op jit(solution)/shard_map/ppermute | solution.py:282
  43.6 1.3 %collective-permute-start.13 = (bf16[128,1024]{1,0:T(8,128)(2,1)S(1)}, bf16[128,1024]{1,0:T(8,128)(2,1)S(1)}, u32[]{:S(2)}, u32[]{:S(2)}) collective-permute-start(bf16[128,1024]{1,0:T(8,128)(2,1)S(1)} %shard_map.83), channel_id=1, source_target_pairs={{4,0},{12,8},{20,16},{28,24},{5,1},{13,9},{21,17},{29,25},{6,2},{1... | collective-permute-start | bytes 786440 | tf_op jit(solution)/shard_map/ppermute | solution.py:282
  44.9 1.3 %collective-permute-start.14 = (bf16[128,1024]{1,0:T(8,128)(2,1)S(1)}, bf16[128,1024]{1,0:T(8,128)(2,1)S(1)}, u32[]{:S(2)}, u32[]{:S(2)}) collective-permute-start(bf16[128,1024]{1,0:T(8,128)(2,1)S(1)} %get-tuple-element.58.before), channel_id=1, source_target_pairs={{4,9},{5,10},{6,11},{7,8},{12,17},{13,18},{14,19},{15,16},{20,25},... | collective-permute-start | bytes 786440 | tf_op jit(solution)/shard_map/ppermute | solution.py:286
  46.2 1.3 %collective-permute-start.15 = (bf16[128,1024]{1,0:T(8,128)(2,1)S(1)}, bf16[128,1024]{1,0:T(8,128)(2,1)S(1)}, u32[]{:S(2)}, u32[]{:S(2)}) collective-permute-start(bf16[128,1024]{1,0:T(8,128)(2,1)S(1)} %get-tuple-element.58.before), channel_id=1, source_target_pairs={{4,10},{5,11},{6,8},{7,9},{12,18},{13,19},{14,16},{15,17},{20,26},... | collective-permute-start | bytes 786440 | tf_op jit(solution)/shard_map/ppermute | solution.py:286
  47.5 1.3 %collective-permute-start.16 = (bf16[128,1024]{1,0:T(8,128)(2,1)S(1)}, bf16[128,1024]{1,0:T(8,128)(2,1)S(1)}, u32[]{:S(2)}, u32[]{:S(2)}) collective-permute-start(bf16[128,1024]{1,0:T(8,128)(2,1)S(1)} %get-tuple-element.58.before), channel_id=1, source_target_pairs={{4,11},{5,8},{6,9},{7,10},{12,19},{13,16},{14,17},{15,18},{20,27},... | collective-permute-start | bytes 786440 | tf_op jit(solution)/shard_map/ppermute | solution.py:286
  48.9 0.0 collective-permute-done.13.down
  48.9 1.4 %shard_map.85 = (bf16[128,1024]{1,0:T(8,128)(2,1)S(1)}, f32[128,1024]{1,0:T(8,128)S(1)}, f32[128,1024]{1,0:T(8,128)}) custom-call(bf16[4,1024,1024]{2,1,0:T(8,128)(2,1)S(1)} %get-tuple-element.35.weights, f32[4,1024]{1,0:T(4,128)S(1)} %copy-done.1, f32[128,1024]{1,0:T(8,128)S(1)} %copy-done, f32[128,1024]{1,0:T(8,128)S(1)} %get-tuple-element.39.one, ...), custom_call_target="tpu_custom_call" | custom-call | flops 805306368 | bytes 12337152 | tf_op jit(solution)/shard_map/pallas_call | solution.py:20
  50.3 1.9 %collective-permute-start.17 = (bf16[128,1024]{1,0:T(8,128)(2,1)S(1)}, bf16[128,1024]{1,0:T(8,128)(2,1)S(1)}, u32[]{:S(2)}, u32[]{:S(2)}) collective-permute-start(bf16[128,1024]{1,0:T(8,128)(2,1)S(1)} %get-tuple-element.62.left), channel_id=1, source_target_pairs={{4,5},{5,6},{6,7},{7,4},{12,13},{13,14},{14,15},{15,12},{20,21},{2... | collective-permute-start | bytes 786440 | tf_op jit(solution)/shard_map/ppermute | solution.py:286
  52.2 3.8 %collective-permute-start.18 = (bf16[128,1024]{1,0:T(8,128)(2,1)S(1)}, bf16[128,1024]{1,0:T(8,128)(2,1)S(1)}, u32[]{:S(2)}, u32[]{:S(2)}) collective-permute-start(bf16[128,1024]{1,0:T(8,128)(2,1)S(1)} %get-tuple-element.62.left), channel_id=1, source_target_pairs={{4,6},{5,7},{6,4},{7,5},{12,14},{13,15},{14,12},{15,13},{20,22},{2... | collective-permute-start | bytes 786440 | tf_op jit(solution)/shard_map/ppermute | solution.py:286
  56.0 0.7 shard_map.87.total
  56.7 1.3 %shard_map.86 = f32[128,1024]{1,0:T(8,128)} custom-call(bf16[4,1024,1024]{2,1,0:T(8,128)(2,1)S(1)} %get-tuple-element.35.weights, f32[4,1024]{1,0:T(4,128)S(1)} %copy-done.1, bf16[128,1024]{1,0:T(8,128)(2,1)S(1)} %get-tuple-element.62.left, f32[128,1024]{1,0:T(8,128)S(1)} %get-tuple-element.63.state), custom_call_target="tpu_custom_call" | custom-call | flops 268435456 | bytes 9191424 | tf_op jit(solution)/shard_map/pallas_call | solution.py:20
  57.9 0.0 collective-permute-done.14.refs_3_
  57.9 2.9 %collective-permute-start.19 = (bf16[128,1024]{1,0:T(8,128)(2,1)S(1)}, bf16[128,1024]{1,0:T(8,128)(2,1)S(1)}, u32[]{:S(2)}, u32[]{:S(2)}) collective-permute-start(bf16[128,1024]{1,0:T(8,128)(2,1)S(1)} %get-tuple-element.62.left), channel_id=1, source_target_pairs={{4,7},{5,4},{6,5},{7,6},{12,15},{13,12},{14,13},{15,14},{20,23},{2... | collective-permute-start | bytes 786440 | tf_op jit(solution)/shard_map/ppermute | solution.py:286
  60.8 0.3 shard_map.88.total
  61.1 5.2 %collective-permute-done.17.refs_0_ = bf16[128,1024]{1,0:T(8,128)(2,1)S(1)} collective-permute-done((bf16[128,1024]{1,0:T(8,128)(2,1)S(1)}, bf16[128,1024]{1,0:T(8,128)(2,1)S(1)}, u32[]{:S(2)}, u32[]{:S(2)}) %collective-permute-start.17) | collective-permute-done | bytes 262176 | tf_op jit(solution)/shard_map/ppermute | solution.py:286
  66.3 2.8 %collective-permute-done.18.refs_1_ = bf16[128,1024]{1,0:T(8,128)(2,1)S(1)} collective-permute-done((bf16[128,1024]{1,0:T(8,128)(2,1)S(1)}, bf16[128,1024]{1,0:T(8,128)(2,1)S(1)}, u32[]{:S(2)}, u32[]{:S(2)}) %collective-permute-start.18) | collective-permute-done | bytes 262176 | tf_op jit(solution)/shard_map/ppermute | solution.py:286
  69.1 1.5 %collective-permute-done.19.refs_2_ = bf16[128,1024]{1,0:T(8,128)(2,1)S(1)} collective-permute-done((bf16[128,1024]{1,0:T(8,128)(2,1)S(1)}, bf16[128,1024]{1,0:T(8,128)(2,1)S(1)}, u32[]{:S(2)}, u32[]{:S(2)}) %collective-permute-start.19) | collective-permute-done | bytes 262176 | tf_op jit(solution)/shard_map/ppermute | solution.py:286
  70.6 2.5 %shard_map.89 = f32[1024,256]{1,0:T(8,128)} custom-call(bf16[4,1024,1024]{2,1,0:T(8,128)(2,1)S(1)} %get-tuple-element.35.weights, f32[4,1024]{1,0:T(4,128)S(1)} %copy-done.1, f32[1024,256]{1,0:T(8,128)S(1)} %shard_map.88.total, bf16[128,1024]{1,0:T(8,128)(2,1)S(1)} %collective-permute-done.17.refs_0_, bf16[128,1024]{1,0:T(8,128)(2,1)S(1)} %collective-permute-done.18.refs_1_, ...), custom_call_target="tpu_custom_call" | custom-call | flops 536870912 | bytes 10436608 | tf_op jit(solution)/shard_map/pallas_call | solution.py:20
  (14 shorter events, 0.2 us)
Async XLA Ops:
  0.6 9.7 %copy-start.1 = (f32[4,1024]{1,0:T(4,128)S(1)}, f32[4,1024]{1,0:T(4,128)}, u32[]{:S(2)}) copy-start(f32[4,1024]{1,0:T(4,128)} %biases.19) | copy-start | bytes 49156
  0.6 9.7 %copy-start = (f32[128,1024]{1,0:T(8,128)S(1)}, f32[128,1024]{1,0:T(8,128)}, u32[]{:S(2)}) copy-start(f32[128,1024]{1,0:T(8,128)} %inputs.5) | copy-start | bytes 1572868
  0.7 1.1 %copy-start.2 = (f32[1,128,1024]{2,1,0:T(8,128)S(1)}, f32[1,128,1024]{2,1,0:T(8,128)}, u32[]{:S(2)}) copy-start(f32[1,128,1024]{2,1,0:T(8,128)} %param.6) | copy-start | bytes 1572868
  1.8 7.2 %collective-permute-start = (bf16[128,1024]{1,0:T(8,128)(2,1)S(1)}, bf16[128,1024]{1,0:T(8,128)(2,1)S(1)}, u32[]{:S(2)}, u32[]{:S(2)}) collective-permute-start(bf16[128,1024]{1,0:T(8,128)(2,1)S(1)} %shard_map.76), channel_id=1, source_target_pairs={{0,4},{4,8},{8,12},{12,16},{16,20},{20,24},{24,28},{1,5},{5,9},{9,... | collective-permute-start | bytes 786440 | tf_op jit(solution)/shard_map/ppermute | solution.py:282
  9.0 18.5 %collective-permute-start.6 = (bf16[1024,1024]{1,0:T(8,128)(2,1)S(1)}, bf16[1024,1024]{1,0:T(8,128)(2,1)S(1)}, u32[]{:S(2)}, u32[]{:S(2)}) collective-permute-start(bf16[1024,1024]{1,0:T(8,128)(2,1)S(1)} %get-tuple-element.44), channel_id=1, source_target_pairs={{0,4},{8,12},{16,20},{24,28},{1,5},{9,13},{17,21},{25,29},{2,6},{1... | collective-permute-start | bytes 6291464 | tf_op jit(solution)/shard_map/ppermute | solution.py:282
  10.3 13.0 %copy-start.3 = (bf16[1,128,1024]{2,1,0:T(8,128)(2,1)S(1)}, bf16[1,128,1024]{2,1,0:T(8,128)(2,1)}, u32[]{:S(2)}) copy-start(bf16[1,128,1024]{2,1,0:T(8,128)(2,1)} %param.9) | copy-start | bytes 786436
  11.9 7.9 %collective-permute-start.1 = (bf16[144,1024]{1,0:T(8,128)(2,1)S(1)}, bf16[144,1024]{1,0:T(8,128)(2,1)S(1)}, u32[]{:S(2)}, u32[]{:S(2)}) collective-permute-start(bf16[144,1024]{1,0:T(8,128)(2,1)S(1)} %get-tuple-element.38), channel_id=1, source_target_pairs={{0,4},{4,8},{8,12},{12,16},{16,20},{20,24},{24,28},{1,5},{5,9},{9,... | collective-permute-start | bytes 884744 | tf_op jit(solution)/shard_map/ppermute | solution.py:282
  16.2 5.9 %collective-permute-start.3 = (bf16[128,1024]{1,0:T(8,128)(2,1)S(1)}, bf16[128,1024]{1,0:T(8,128)(2,1)S(1)}, u32[]{:S(2)}, u32[]{:S(2)}) collective-permute-start(bf16[128,1024]{1,0:T(8,128)(2,1)S(1)} %get-tuple-element.41), channel_id=1, source_target_pairs={{0,1},{1,2},{2,3},{3,0}} | collective-permute-start | bytes 786440 | tf_op jit(solution)/shard_map/ppermute | solution.py:286
  16.9 6.5 %collective-permute-start.4 = (bf16[128,1024]{1,0:T(8,128)(2,1)S(1)}, bf16[128,1024]{1,0:T(8,128)(2,1)S(1)}, u32[]{:S(2)}, u32[]{:S(2)}) collective-permute-start(bf16[128,1024]{1,0:T(8,128)(2,1)S(1)} %get-tuple-element.41), channel_id=1, source_target_pairs={{0,2},{1,3},{2,0},{3,1}} | collective-permute-start | bytes 786440 | tf_op jit(solution)/shard_map/ppermute | solution.py:286
  17.6 5.9 %collective-permute-start.5 = (bf16[128,1024]{1,0:T(8,128)(2,1)S(1)}, bf16[128,1024]{1,0:T(8,128)(2,1)S(1)}, u32[]{:S(2)}, u32[]{:S(2)}) collective-permute-start(bf16[128,1024]{1,0:T(8,128)(2,1)S(1)} %get-tuple-element.41), channel_id=1, source_target_pairs={{0,3},{1,0},{2,1},{3,2}} | collective-permute-start | bytes 786440 | tf_op jit(solution)/shard_map/ppermute | solution.py:286
  21.4 2.1 %collective-permute-start.2 = (bf16[128,1024]{1,0:T(8,128)(2,1)S(1)}, bf16[128,1024]{1,0:T(8,128)(2,1)S(1)}, u32[]{:S(2)}, u32[]{:S(2)}) collective-permute-start(bf16[128,1024]{1,0:T(8,128)(2,1)S(1)} %get-tuple-element.40.before), channel_id=1, source_target_pairs={{4,12},{5,13},{6,14},{7,15}} | collective-permute-start | bytes 786440 | tf_op jit(solution)/shard_map/ppermute | solution.py:282
  22.1 5.5 %collective-permute-start.7 = (bf16[128,1024]{1,0:T(8,128)(2,1)S(1)}, bf16[128,1024]{1,0:T(8,128)(2,1)S(1)}, u32[]{:S(2)}, u32[]{:S(2)}) collective-permute-start(bf16[128,1024]{1,0:T(8,128)(2,1)S(1)} %get-tuple-element.46), channel_id=1, source_target_pairs={{0,4},{8,12},{16,20},{24,28},{1,5},{9,13},{17,21},{25,29},{2,6},{1... | collective-permute-start | bytes 786440 | tf_op jit(solution)/shard_map/ppermute | solution.py:282
  27.6 10.5 %collective-permute-start.8 = (bf16[128,1024]{1,0:T(8,128)(2,1)S(1)}, bf16[128,1024]{1,0:T(8,128)(2,1)S(1)}, u32[]{:S(2)}, u32[]{:S(2)}) collective-permute-start(bf16[128,1024]{1,0:T(8,128)(2,1)S(1)} %get-tuple-element.52.before), channel_id=1, source_target_pairs={{12,20},{13,21},{14,22},{15,23}} | collective-permute-start | bytes 786440 | tf_op jit(solution)/shard_map/ppermute | solution.py:282
  28.9 4.1 %collective-permute-start.9 = (bf16[128,256]{1,0:T(8,128)(2,1)S(1)}, bf16[128,256]{1,0:T(8,128)(2,1)S(1)}, u32[]{:S(2)}, u32[]{:S(2)}) collective-permute-start(bf16[128,256]{1,0:T(8,128)(2,1)S(1)} %get-tuple-element.54), channel_id=1, source_target_pairs={{0,1},{1,2},{2,3},{3,0},{4,5},{5,6},{6,7},{7,4},{8,9},{9,10},{10,1... | collective-permute-start | bytes 196616 | tf_op jit(solution)/shard_map/ppermute | solution.py:289
  30.2 6.0 %collective-permute-start.10 = (bf16[128,256]{1,0:T(8,128)(2,1)S(1)}, bf16[128,256]{1,0:T(8,128)(2,1)S(1)}, u32[]{:S(2)}, u32[]{:S(2)}) collective-permute-start(bf16[128,256]{1,0:T(8,128)(2,1)S(1)} %get-tuple-element.55), channel_id=1, source_target_pairs={{0,2},{1,3},{2,0},{3,1},{4,6},{5,7},{6,4},{7,5},{8,10},{9,11},{10,... | collective-permute-start | bytes 196616 | tf_op jit(solution)/shard_map/ppermute | solution.py:289
  31.3 6.7 %collective-permute-start.11 = (bf16[128,256]{1,0:T(8,128)(2,1)S(1)}, bf16[128,256]{1,0:T(8,128)(2,1)S(1)}, u32[]{:S(2)}, u32[]{:S(2)}) collective-permute-start(bf16[128,256]{1,0:T(8,128)(2,1)S(1)} %get-tuple-element.56), channel_id=1, source_target_pairs={{0,3},{1,0},{2,1},{3,2},{4,7},{5,4},{6,5},{7,6},{8,11},{9,8},{10,9... | collective-permute-start | bytes 196616 | tf_op jit(solution)/shard_map/ppermute | solution.py:289
  38.9 4.6 %collective-permute-start.12 = (bf16[128,1024]{1,0:T(8,128)(2,1)S(1)}, bf16[128,1024]{1,0:T(8,128)(2,1)S(1)}, u32[]{:S(2)}, u32[]{:S(2)}) collective-permute-start(bf16[128,1024]{1,0:T(8,128)(2,1)S(1)} %get-tuple-element.58.before), channel_id=1, source_target_pairs={{20,28},{21,29},{22,30},{23,31}} | collective-permute-start | bytes 786440 | tf_op jit(solution)/shard_map/ppermute | solution.py:282
  43.6 5.3 %collective-permute-start.13 = (bf16[128,1024]{1,0:T(8,128)(2,1)S(1)}, bf16[128,1024]{1,0:T(8,128)(2,1)S(1)}, u32[]{:S(2)}, u32[]{:S(2)}) collective-permute-start(bf16[128,1024]{1,0:T(8,128)(2,1)S(1)} %shard_map.83), channel_id=1, source_target_pairs={{4,0},{12,8},{20,16},{28,24},{5,1},{13,9},{21,17},{29,25},{6,2},{1... | collective-permute-start | bytes 786440 | tf_op jit(solution)/shard_map/ppermute | solution.py:282
  44.9 13.0 %collective-permute-start.14 = (bf16[128,1024]{1,0:T(8,128)(2,1)S(1)}, bf16[128,1024]{1,0:T(8,128)(2,1)S(1)}, u32[]{:S(2)}, u32[]{:S(2)}) collective-permute-start(bf16[128,1024]{1,0:T(8,128)(2,1)S(1)} %get-tuple-element.58.before), channel_id=1, source_target_pairs={{4,9},{5,10},{6,11},{7,8},{12,17},{13,18},{14,19},{15,16},{20,25},... | collective-permute-start | bytes 786440 | tf_op jit(solution)/shard_map/ppermute | solution.py:286
  46.2 14.6 %collective-permute-start.15 = (bf16[128,1024]{1,0:T(8,128)(2,1)S(1)}, bf16[128,1024]{1,0:T(8,128)(2,1)S(1)}, u32[]{:S(2)}, u32[]{:S(2)}) collective-permute-start(bf16[128,1024]{1,0:T(8,128)(2,1)S(1)} %get-tuple-element.58.before), channel_id=1, source_target_pairs={{4,10},{5,11},{6,8},{7,9},{12,18},{13,19},{14,16},{15,17},{20,26},... | collective-permute-start | bytes 786440 | tf_op jit(solution)/shard_map/ppermute | solution.py:286
  47.5 13.3 %collective-permute-start.16 = (bf16[128,1024]{1,0:T(8,128)(2,1)S(1)}, bf16[128,1024]{1,0:T(8,128)(2,1)S(1)}, u32[]{:S(2)}, u32[]{:S(2)}) collective-permute-start(bf16[128,1024]{1,0:T(8,128)(2,1)S(1)} %get-tuple-element.58.before), channel_id=1, source_target_pairs={{4,11},{5,8},{6,9},{7,10},{12,19},{13,16},{14,17},{15,18},{20,27},... | collective-permute-start | bytes 786440 | tf_op jit(solution)/shard_map/ppermute | solution.py:286
  50.3 16.0 %collective-permute-start.17 = (bf16[128,1024]{1,0:T(8,128)(2,1)S(1)}, bf16[128,1024]{1,0:T(8,128)(2,1)S(1)}, u32[]{:S(2)}, u32[]{:S(2)}) collective-permute-start(bf16[128,1024]{1,0:T(8,128)(2,1)S(1)} %get-tuple-element.62.left), channel_id=1, source_target_pairs={{4,5},{5,6},{6,7},{7,4},{12,13},{13,14},{14,15},{15,12},{20,21},{2... | collective-permute-start | bytes 786440 | tf_op jit(solution)/shard_map/ppermute | solution.py:286
  52.2 16.9 %collective-permute-start.18 = (bf16[128,1024]{1,0:T(8,128)(2,1)S(1)}, bf16[128,1024]{1,0:T(8,128)(2,1)S(1)}, u32[]{:S(2)}, u32[]{:S(2)}) collective-permute-start(bf16[128,1024]{1,0:T(8,128)(2,1)S(1)} %get-tuple-element.62.left), channel_id=1, source_target_pairs={{4,6},{5,7},{6,4},{7,5},{12,14},{13,15},{14,12},{15,13},{20,22},{2... | collective-permute-start | bytes 786440 | tf_op jit(solution)/shard_map/ppermute | solution.py:286
  57.9 12.7 %collective-permute-start.19 = (bf16[128,1024]{1,0:T(8,128)(2,1)S(1)}, bf16[128,1024]{1,0:T(8,128)(2,1)S(1)}, u32[]{:S(2)}, u32[]{:S(2)}) collective-permute-start(bf16[128,1024]{1,0:T(8,128)(2,1)S(1)} %get-tuple-element.62.left), channel_id=1, source_target_pairs={{4,7},{5,4},{6,5},{7,6},{12,15},{13,12},{14,13},{15,14},{20,23},{2... | collective-permute-start | bytes 786440 | tf_op jit(solution)/shard_map/ppermute | solution.py:286

commit v10 on v9

--- a/solution.py
+++ b/solution.py
@@ -168,7 +168,7 @@
                 top[:, cols] = (mid[:, cols] + factor * slope + forcing[:, cols]).astype(BF16)
 
 
-def held_kernel(got_1, got_2, got_3, held):
+def held_kernel(got_1, got_2, got_3, after, held):
     here = lax.axis_index("layer")
     low, early = here % 4 < 2, here // 4 == 0
     held[...] = jnp.where(low, got_2[...], jnp.where(early, got_1[...], got_3[...]))
@@ -290,7 +290,7 @@
 
     up = [(i, i + 1) for i in range(blocks - 1)]
     up_pair = [(i, i + 1) for i in range(0, blocks, 2)]
-    down_pair = [(i + 1, i) for i in range(0, blocks, 2)]
+    down_pair = [(i + 1, i) for i in range(2, blocks, 2)]
     rounded = [pltpu.VMEM((rows, depth), BF16)] * 2
 
     guess_sent = call(round_kernel, plain((rows, depth), BF16), guesses[0])
@@ -344,9 +344,9 @@
     def finish(gots, mids):
         got_1, got_2, got_3 = gots
         mid_1, mid_2, mid_3 = mids
-        held = call(held_kernel, plain((rows, depth), BF16), got_1, got_2, got_3)
+        held = call(held_kernel, plain((rows, depth), BF16), got_1, got_2, got_3, mid_3)
         down = along(held, down_pair)
-        return call(
+        return down, *call(
             functools.partial(final_kernel, step_size),
             (plain((rows, depth), BF16), kept(inputs), plain((rows, depth), F32)),
             held_weights, biases, inputs, start, down, mid_2, mid_1, mid_3, forcing, relaxed,
@@ -371,7 +371,7 @@
         top_2, [(4 * m + 1, 4 * m + 3) for m in range(1, groups)], lambda slot, group: (slot == 3) & (group > 0), True
     )
     top_last = top_2
-    left, state, coarse_states = finish((got_1, got_2, got_3), (mid_1, mid_2, mid_3))
+    down, left, state, coarse_states = finish((got_1, got_2, got_3), (mid_1, mid_2, mid_3))
     if groups > 2:
         late = lambda slot, group: group > 1
         relaxed_out = call(functools.partial(pick_kernel, late), plain((rows, depth), F32), relaxed, relaxed)
@@ -392,9 +392,17 @@
             for new, old in ((new_mid_2, mid_2), (new_mid_3, mid_3))
         ]
         gots = [jnp.where(group > 1, new, old) for new, old in ((new_2, got_2), (new_3, got_3))]
-        left, state, coarse_early = finish((got_1, *gots), (mid_1, *mids))
+        down, left, state, coarse_early = finish((got_1, *gots), (mid_1, *mids))
         coarse_states = jnp.where(slot == 3, solved - relaxed_out, coarse_states)
-    far = [across(top_last, [(i, i + 1) for i in range(1, blocks - 1, 2)], by) for by in range(1, parts)]
+    onward = [(i, i + 1) for i in range(1, blocks - 1, 2)]
+    last_even = [(blocks - 2, blocks - 2)]
+    newest = call(
+        functools.partial(pick_kernel, lambda slot, group: slot % 2 == 0), plain((rows, depth), BF16), down, top_last
+    )
+    far = [
+        across(newest, onward[:-1] + last_even, by) if 2 * by == parts else across(top_last, onward, by)
+        for by in range(1, parts)
+    ]
     odd_lefts = [across(left, [(i, i) for i in range(1, blocks, 2)], by) for by in range(1, parts)]
     new_states = call(
         functools.partial(last_kernel, step_size), plain((rows, depth), F32),
@@ -413,10 +421,13 @@
         + [pltpu.VMEM((others, width), BF16)] * 2,
         flops=4 * (parts - 1) * layer_flops,
     )
-    weight_grad = call(
-        functools.partial(odd_kernel, step_size, parts - 1), plain((depth, width), F32),
-        held_weights, biases, total, *odd_lefts, *adjoints[1:], scratch=[deltas], flops=2 * layer_flops,
-    )
+    for at, out in ((slice(0, parts - 2), pltpu.VMEM((depth, width), F32)), (slice(parts - 2, parts), plain((depth, width), F32))):
+        batch = odd_lefts[at]
+        total = call(
+            functools.partial(odd_kernel, step_size, len(batch)), out,
+            held_weights, biases, total, *batch, *adjoints[1:][at], scratch=[deltas], flops=len(batch) * layer_flops // 2,
+        )
+    weight_grad = total
     return (new_states[None], coarse_states[None], weight_grad[None])
 
 

time: 73.5 us -> 72 us (0.980)
  the two profiles are of different devices: /device:TPU:13 before, /device:TPU:3 now
where the time goes in v10:
time: 72 us; the launch traced here: 71.5 us
  starting transfers between devices  41.8 us (58%)
  Pallas kernels  14.2 us (20%)
  waiting for transfers between devices  13.5 us (19%)
  local copies, waits for them, and re-layouts  1.11 us (2%)
  between operations  0.99 us (1%)
    ppermute x9, starting transfers between devices, across(): return lax.ppermute(state, ('layer', 'dp'), flat)  21.1 us
    ppermute x8, starting transfers between devices, along(): return lax.ppermute(state, 'layer', pairs)  16 us
    pallas_call x16, Pallas kernels, call(): pl.pallas_call(kernel, out_shape=outs, in_specs=specs or [WHOLE] * len(ar...  14.2 us
    ppermute x8, waiting for transfers between devices, along(): return lax.ppermute(state, 'layer', pairs)  6.02 us
    ppermute x9, waiting for transfers between devices, across(): return lax.ppermute(state, ('layer', 'dp'), flat)  5.39 us
    ppermute x3, starting transfers between devices, shifted(): lax.ppermute(array, 'dp', [(i, (i + by) % parts) for i in range(parts)])  4.72 us
    ppermute x3, waiting for transfers between devices, shifted(): lax.ppermute(array, 'dp', [(i, (i + by) % parts) for i in range(parts)])  2.06 us
  transfers between devices with their start and end apart: 20, of which 7 were waited for; matrix products, arithmetic and copies ran while one was open for 0% of the time, Pallas kernels for 16%

profile of v10, /device:TPU:3, one launch (start us, length us, event | category | flops | bytes accessed | tf_op | source)
XLA Modules:
  0.0 71.5 jit_solution(6017815434322468081)
XLA Ops:
  0.7 1.1 %copy-done.2 = f32[1,128,1024]{2,1,0:T(8,128)S(1)} copy-done((f32[1,128,1024]{2,1,0:T(8,128)S(1)}, f32[1,128,1024]{2,1,0:T(8,128)}, u32[]{:S(2)}) %copy-start.2) | copy-done | bytes 524312
  1.8 3.7 %collective-permute-start = (bf16[128,1024]{1,0:T(8,128)(2,1)S(1)}, bf16[128,1024]{1,0:T(8,128)(2,1)S(1)}, u32[]{:S(2)}, u32[]{:S(2)}) collective-permute-start(bf16[128,1024]{1,0:T(8,128)(2,1)S(1)} %shard_map.76), channel_id=1, source_target_pairs={{0,4},{4,8},{8,12},{12,16},{16,20},{20,24},{24,28},{1,5},{5,9},{9,... | collective-permute-start | bytes 786440 | tf_op jit(solution)/shard_map/ppermute | solution.py:282
  5.5 3.5 %shard_map.77 = (bf16[4,1024,1024]{2,1,0:T(8,128)(2,1)S(1)}, bf16[1024,1024]{1,0:T(8,128)(2,1)S(1)}) custom-call(bf16[4,1024,1024]{2,1,0:T(8,128)(2,1)} %source), custom_call_target="tpu_custom_call" | custom-call | bytes 8388608 | tf_op jit(solution)/shard_map/pallas_call | solution.py:20
  9.0 1.3 %collective-permute-start.6 = (bf16[1024,1024]{1,0:T(8,128)(2,1)S(1)}, bf16[1024,1024]{1,0:T(8,128)(2,1)S(1)}, u32[]{:S(2)}, u32[]{:S(2)}) collective-permute-start(bf16[1024,1024]{1,0:T(8,128)(2,1)S(1)} %get-tuple-element.44), channel_id=1, source_target_pairs={{0,4},{8,12},{16,20},{24,28},{1,5},{9,13},{17,21},{25,29},{2,6},{1... | collective-permute-start | bytes 6291464 | tf_op jit(solution)/shard_map/ppermute | solution.py:282
  10.3 0.0 copy-start.3
  10.3 1.6 %shard_map.78 = (f32[128,1024]{1,0:T(8,128)S(1)}, bf16[144,1024]{1,0:T(8,128)(2,1)S(1)}, bf16[128,1024]{1,0:T(8,128)(2,1)S(1)}) custom-call(bf16[4,1024,1024]{2,1,0:T(8,128)(2,1)S(1)} %get-tuple-element.35.weights, f32[4,1024]{1,0:T(4,128)S(1)} %copy-done.1, f32[128,1024]{1,0:T(8,128)S(1)} %copy-done, bf16[128,1024]{1,0:T(8,128)(2,1)S(1)} %collective-permute-done.got), custom_call_target="tpu_custom_call" | custom-call | flops 1073741824 | bytes 9191424 | tf_op jit(solution)/shard_map/pallas_call | solution.py:20
  11.9 5.2 %collective-permute-start.1 = (bf16[144,1024]{1,0:T(8,128)(2,1)S(1)}, bf16[144,1024]{1,0:T(8,128)(2,1)S(1)}, u32[]{:S(2)}, u32[]{:S(2)}) collective-permute-start(bf16[144,1024]{1,0:T(8,128)(2,1)S(1)} %get-tuple-element.38), channel_id=1, source_target_pairs={{0,4},{4,8},{8,12},{12,16},{16,20},{20,24},{24,28},{1,5},{5,9},{9,... | collective-permute-start | bytes 884744 | tf_op jit(solution)/shard_map/ppermute | solution.py:282
  17.1 0.7 collective-permute-start.3
  17.8 0.7 collective-permute-start.4
  18.5 0.7 collective-permute-start.5
  19.1 1.6 %collective-permute-done.1.got = bf16[144,1024]{1,0:T(8,128)(2,1)S(1)} collective-permute-done((bf16[144,1024]{1,0:T(8,128)(2,1)S(1)}, bf16[144,1024]{1,0:T(8,128)(2,1)S(1)}, u32[]{:S(2)}, u32[]{:S(2)}) %collective-permute-start.1) | collective-permute-done | bytes 294944 | tf_op jit(solution)/shard_map/ppermute | solution.py:282
  20.7 1.5 %shard_map.79 = (f32[128,1024]{1,0:T(8,128)S(1)}, f32[128,1024]{1,0:T(8,128)S(1)}, f32[8,1024]{1,0:T(8,128)S(1)}, bf16[128,1024]{1,0:T(8,128)(2,1)S(1)}, bf16[128,1024]{1,0:T(8,128)(2,1)S(1)}) custom-call(bf16[4,1024,1024]{2,1,0:T(8,128)(2,1)S(1)} %get-tuple-element.35.weights, f32[4,1024]{1,0:T(4,128)S(1)} %copy-done.1, f32[128,1024]{1,0:T(8,128)S(1)} %copy-done, ...), custom_call_target="tpu_custom_call" | custom-call | flops 1073741824 | bytes 9224192 | tf_op jit(solution)/shard_map/pallas_call | solution.py:20
  22.3 1.3 %collective-permute-start.2 = (bf16[128,1024]{1,0:T(8,128)(2,1)S(1)}, bf16[128,1024]{1,0:T(8,128)(2,1)S(1)}, u32[]{:S(2)}, u32[]{:S(2)}) collective-permute-start(bf16[128,1024]{1,0:T(8,128)(2,1)S(1)} %get-tuple-element.40.before), channel_id=1, source_target_pairs={{4,12},{5,13},{6,14},{7,15}} | collective-permute-start | bytes 786440 | tf_op jit(solution)/shard_map/ppermute | solution.py:282
  23.6 0.0 collective-permute-done.3.refs_0_
  23.6 1.3 %collective-permute-start.7 = (bf16[128,1024]{1,0:T(8,128)(2,1)S(1)}, bf16[128,1024]{1,0:T(8,128)(2,1)S(1)}, u32[]{:S(2)}, u32[]{:S(2)}) collective-permute-start(bf16[128,1024]{1,0:T(8,128)(2,1)S(1)} %get-tuple-element.46), channel_id=1, source_target_pairs={{0,4},{8,12},{16,20},{24,28},{1,5},{9,13},{17,21},{25,29},{2,6},{1... | collective-permute-start | bytes 786440 | tf_op jit(solution)/shard_map/ppermute | solution.py:282
  24.9 0.0 collective-permute-done.4.refs_1_
  24.9 0.0 collective-permute-done.5.refs_2_
  25.0 4.4 %collective-permute-done.2.got.got_1 = bf16[128,1024]{1,0:T(8,128)(2,1)S(1)} collective-permute-done((bf16[128,1024]{1,0:T(8,128)(2,1)S(1)}, bf16[128,1024]{1,0:T(8,128)(2,1)S(1)}, u32[]{:S(2)}, u32[]{:S(2)}) %collective-permute-start.2) | collective-permute-done | bytes 262176 | tf_op jit(solution)/shard_map/ppermute | solution.py:282
  29.4 0.0 collective-permute-done.7.pair_forcing
  29.4 0.0 collective-permute-done.6.pair_weight
  29.4 0.9 %shard_map.80 = (f32[128,1024]{1,0:T(8,128)S(1)}, bf16[128,1024]{1,0:T(8,128)(2,1)S(1)}) custom-call(bf16[4,1024,1024]{2,1,0:T(8,128)(2,1)S(1)} %get-tuple-element.35.weights, f32[4,1024]{1,0:T(4,128)S(1)} %copy-done.1, f32[128,1024]{1,0:T(8,128)S(1)} %get-tuple-element.43.forcing, bf16[1024,1024]{1,0:T(8,128)(2,1)S(1)} %collective-permute-done.6.pair_weight, ...), custom_call_target="tpu_custom_call" | custom-call | flops 536870912 | bytes 11845632 | tf_op jit(solution)/shard_map/pallas_call | solution.py:20
  30.3 1.3 %collective-permute-start.8 = (bf16[128,1024]{1,0:T(8,128)(2,1)S(1)}, bf16[128,1024]{1,0:T(8,128)(2,1)S(1)}, u32[]{:S(2)}, u32[]{:S(2)}) collective-permute-start(bf16[128,1024]{1,0:T(8,128)(2,1)S(1)} %get-tuple-element.52.before), channel_id=1, source_target_pairs={{12,20},{13,21},{14,22},{15,23}} | collective-permute-start | bytes 786440 | tf_op jit(solution)/shard_map/ppermute | solution.py:282
  31.6 1.4 %collective-permute-start.9 = (bf16[128,256]{1,0:T(8,128)(2,1)S(1)}, bf16[128,256]{1,0:T(8,128)(2,1)S(1)}, u32[]{:S(2)}, u32[]{:S(2)}) collective-permute-start(bf16[128,256]{1,0:T(8,128)(2,1)S(1)} %get-tuple-element.54), channel_id=1, source_target_pairs={{0,1},{1,2},{2,3},{3,0},{4,5},{5,6},{6,7},{7,4},{8,9},{9,10},{10,1... | collective-permute-start | bytes 196616 | tf_op jit(solution)/shard_map/ppermute | solution.py:289
  32.9 2.3 %collective-permute-start.10 = (bf16[128,256]{1,0:T(8,128)(2,1)S(1)}, bf16[128,256]{1,0:T(8,128)(2,1)S(1)}, u32[]{:S(2)}, u32[]{:S(2)}) collective-permute-start(bf16[128,256]{1,0:T(8,128)(2,1)S(1)} %get-tuple-element.55), channel_id=1, source_target_pairs={{0,2},{1,3},{2,0},{3,1},{4,6},{5,7},{6,4},{7,5},{8,10},{9,11},{10,... | collective-permute-start | bytes 196616 | tf_op jit(solution)/shard_map/ppermute | solution.py:289
  35.2 1.1 %collective-permute-start.11 = (bf16[128,256]{1,0:T(8,128)(2,1)S(1)}, bf16[128,256]{1,0:T(8,128)(2,1)S(1)}, u32[]{:S(2)}, u32[]{:S(2)}) collective-permute-start(bf16[128,256]{1,0:T(8,128)(2,1)S(1)} %get-tuple-element.56), channel_id=1, source_target_pairs={{0,3},{1,0},{2,1},{3,2},{4,7},{5,4},{6,5},{7,6},{8,11},{9,8},{10,9... | collective-permute-start | bytes 196616 | tf_op jit(solution)/shard_map/ppermute | solution.py:289
  36.3 0.4 collective-permute-done.9.refs_6_.refs_2_
  36.7 0.7 collective-permute-done.10.refs_7_.refs_3_
  37.3 1.0 %collective-permute-done.11.refs_8_.refs_1_ = bf16[128,256]{1,0:T(8,128)(2,1)S(1)} collective-permute-done((bf16[128,256]{1,0:T(8,128)(2,1)S(1)}, bf16[128,256]{1,0:T(8,128)(2,1)S(1)}, u32[]{:S(2)}, u32[]{:S(2)}) %collective-permute-start.11) | collective-permute-done | bytes 65568 | tf_op jit(solution)/shard_map/ppermute | solution.py:289
  38.4 0.0 collective-permute-done.8.got.got_2
  38.4 0.7 collective-permute-start.12
  39.1 0.0 collective-permute-done.12.got.got_3
  39.2 1.3 %collective-permute-start.13 = (bf16[128,1024]{1,0:T(8,128)(2,1)S(1)}, bf16[128,1024]{1,0:T(8,128)(2,1)S(1)}, u32[]{:S(2)}, u32[]{:S(2)}) collective-permute-start(bf16[128,1024]{1,0:T(8,128)(2,1)S(1)} %shard_map.84), channel_id=1, source_target_pairs={{12,8},{20,16},{28,24},{13,9},{21,17},{29,25},{14,10},{22,18},{30,... | collective-permute-start | bytes 786440 | tf_op jit(solution)/shard_map/ppermute | solution.py:282
  40.5 4.1 %collective-permute-start.14 = (bf16[128,1024]{1,0:T(8,128)(2,1)S(1)}, bf16[128,1024]{1,0:T(8,128)(2,1)S(1)}, u32[]{:S(2)}, u32[]{:S(2)}) collective-permute-start(bf16[128,1024]{1,0:T(8,128)(2,1)S(1)} %get-tuple-element.58.before.old), channel_id=1, source_target_pairs={{4,9},{5,10},{6,11},{7,8},{12,17},{13,18},{14,19},{15,16},{20,25},... | collective-permute-start | bytes 786440 | tf_op jit(solution)/shard_map/ppermute | solution.py:286
  44.6 2.4 %collective-permute-start.16 = (bf16[128,1024]{1,0:T(8,128)(2,1)S(1)}, bf16[128,1024]{1,0:T(8,128)(2,1)S(1)}, u32[]{:S(2)}, u32[]{:S(2)}) collective-permute-start(bf16[128,1024]{1,0:T(8,128)(2,1)S(1)} %get-tuple-element.58.before.old), channel_id=1, source_target_pairs={{4,11},{5,8},{6,9},{7,10},{12,19},{13,16},{14,17},{15,18},{20,27},... | collective-permute-start | bytes 786440 | tf_op jit(solution)/shard_map/ppermute | solution.py:286
  47.0 0.0 collective-permute-done.13.down.new
  47.0 2.9 %collective-permute-start.15 = (bf16[128,1024]{1,0:T(8,128)(2,1)S(1)}, bf16[128,1024]{1,0:T(8,128)(2,1)S(1)}, u32[]{:S(2)}, u32[]{:S(2)}) collective-permute-start(bf16[128,1024]{1,0:T(8,128)(2,1)S(1)} %shard_map.88), channel_id=1, source_target_pairs={{4,10},{5,11},{6,8},{7,9},{12,18},{13,19},{14,16},{15,17},{24,26},... | collective-permute-start | bytes 786440 | tf_op jit(solution)/shard_map/ppermute | solution.py:286
  49.9 1.4 %shard_map.85 = (bf16[128,1024]{1,0:T(8,128)(2,1)S(1)}, f32[128,1024]{1,0:T(8,128)S(1)}, f32[128,1024]{1,0:T(8,128)}) custom-call(bf16[4,1024,1024]{2,1,0:T(8,128)(2,1)S(1)} %get-tuple-element.35.weights, f32[4,1024]{1,0:T(4,128)S(1)} %copy-done.1, f32[128,1024]{1,0:T(8,128)S(1)} %copy-done, f32[128,1024]{1,0:T(8,128)S(1)} %get-tuple-element.39.one, ...), custom_call_target="tpu_custom_call" | custom-call | flops 805306368 | bytes 12337152 | tf_op jit(solution)/shard_map/pallas_call | solution.py:20
  51.3 3.8 %collective-permute-start.17 = (bf16[128,1024]{1,0:T(8,128)(2,1)S(1)}, bf16[128,1024]{1,0:T(8,128)(2,1)S(1)}, u32[]{:S(2)}, u32[]{:S(2)}) collective-permute-start(bf16[128,1024]{1,0:T(8,128)(2,1)S(1)} %get-tuple-element.62.left), channel_id=1, source_target_pairs={{4,5},{5,6},{6,7},{7,4},{12,13},{13,14},{14,15},{15,12},{20,21},{2... | collective-permute-start | bytes 786440 | tf_op jit(solution)/shard_map/ppermute | solution.py:286
  55.2 2.9 %collective-permute-start.18 = (bf16[128,1024]{1,0:T(8,128)(2,1)S(1)}, bf16[128,1024]{1,0:T(8,128)(2,1)S(1)}, u32[]{:S(2)}, u32[]{:S(2)}) collective-permute-start(bf16[128,1024]{1,0:T(8,128)(2,1)S(1)} %get-tuple-element.62.left), channel_id=1, source_target_pairs={{4,6},{5,7},{6,4},{7,5},{12,14},{13,15},{14,12},{15,13},{20,22},{2... | collective-permute-start | bytes 786440 | tf_op jit(solution)/shard_map/ppermute | solution.py:286
  58.1 0.6 shard_map.87.total
  58.7 1.3 %shard_map.86 = f32[128,1024]{1,0:T(8,128)} custom-call(bf16[4,1024,1024]{2,1,0:T(8,128)(2,1)S(1)} %get-tuple-element.35.weights, f32[4,1024]{1,0:T(4,128)S(1)} %copy-done.1, bf16[128,1024]{1,0:T(8,128)(2,1)S(1)} %get-tuple-element.62.left, f32[128,1024]{1,0:T(8,128)S(1)} %get-tuple-element.63.state), custom_call_target="tpu_custom_call" | custom-call | flops 268435456 | bytes 9191424 | tf_op jit(solution)/shard_map/pallas_call | solution.py:20
  60.0 0.0 collective-permute-done.14.refs_3_
  60.0 3.0 %collective-permute-start.19 = (bf16[128,1024]{1,0:T(8,128)(2,1)S(1)}, bf16[128,1024]{1,0:T(8,128)(2,1)S(1)}, u32[]{:S(2)}, u32[]{:S(2)}) collective-permute-start(bf16[128,1024]{1,0:T(8,128)(2,1)S(1)} %get-tuple-element.62.left), channel_id=1, source_target_pairs={{4,7},{5,4},{6,5},{7,6},{12,15},{13,12},{14,13},{15,14},{20,23},{2... | collective-permute-start | bytes 786440 | tf_op jit(solution)/shard_map/ppermute | solution.py:286
  63.0 0.3 shard_map.89.total
  63.3 3.8 %collective-permute-done.18.refs_1_ = bf16[128,1024]{1,0:T(8,128)(2,1)S(1)} collective-permute-done((bf16[128,1024]{1,0:T(8,128)(2,1)S(1)}, bf16[128,1024]{1,0:T(8,128)(2,1)S(1)}, u32[]{:S(2)}, u32[]{:S(2)}) %collective-permute-start.18) | collective-permute-done | bytes 262176 | tf_op jit(solution)/shard_map/ppermute | solution.py:286
  67.2 1.1 %shard_map.90.total = f32[1024,256]{1,0:T(8,128)S(1)} custom-call(bf16[4,1024,1024]{2,1,0:T(8,128)(2,1)S(1)} %get-tuple-element.35.weights, f32[4,1024]{1,0:T(4,128)S(1)} %copy-done.1, f32[1024,256]{1,0:T(8,128)S(1)} %shard_map.89.total, bf16[128,1024]{1,0:T(8,128)(2,1)S(1)} %collective-permute-done.17.refs_0_, ...), custom_call_target="tpu_custom_call" | custom-call | flops 268435456 | bytes 10108928 | tf_op jit(solution)/shard_map/pallas_call | solution.py:20
  68.3 1.6 %collective-permute-done.19.refs_0_ = bf16[128,1024]{1,0:T(8,128)(2,1)S(1)} collective-permute-done((bf16[128,1024]{1,0:T(8,128)(2,1)S(1)}, bf16[128,1024]{1,0:T(8,128)(2,1)S(1)}, u32[]{:S(2)}, u32[]{:S(2)}) %collective-permute-start.19) | collective-permute-done | bytes 262176 | tf_op jit(solution)/shard_map/ppermute | solution.py:286
  69.9 1.7 %shard_map.91 = f32[1024,256]{1,0:T(8,128)} custom-call(bf16[4,1024,1024]{2,1,0:T(8,128)(2,1)S(1)} %get-tuple-element.35.weights, f32[4,1024]{1,0:T(4,128)S(1)} %copy-done.1, f32[1024,256]{1,0:T(8,128)S(1)} %shard_map.90.total, bf16[128,1024]{1,0:T(8,128)(2,1)S(1)} %collective-permute-done.19.refs_0_, ...), custom_call_target="tpu_custom_call" | custom-call | flops 134217728 | bytes 9781248 | tf_op jit(solution)/shard_map/pallas_call | solution.py:20
  (16 shorter events, 0.2 us)
Async XLA Ops:
  0.6 9.7 %copy-start.1 = (f32[4,1024]{1,0:T(4,128)S(1)}, f32[4,1024]{1,0:T(4,128)}, u32[]{:S(2)}) copy-start(f32[4,1024]{1,0:T(4,128)} %biases.21) | copy-start | bytes 49156
  0.6 9.7 %copy-start = (f32[128,1024]{1,0:T(8,128)S(1)}, f32[128,1024]{1,0:T(8,128)}, u32[]{:S(2)}) copy-start(f32[128,1024]{1,0:T(8,128)} %inputs.5) | copy-start | bytes 1572868
  0.7 1.1 %copy-start.2 = (f32[1,128,1024]{2,1,0:T(8,128)S(1)}, f32[1,128,1024]{2,1,0:T(8,128)}, u32[]{:S(2)}) copy-start(f32[1,128,1024]{2,1,0:T(8,128)} %param.6) | copy-start | bytes 1572868
  1.8 7.2 %collective-permute-start = (bf16[128,1024]{1,0:T(8,128)(2,1)S(1)}, bf16[128,1024]{1,0:T(8,128)(2,1)S(1)}, u32[]{:S(2)}, u32[]{:S(2)}) collective-permute-start(bf16[128,1024]{1,0:T(8,128)(2,1)S(1)} %shard_map.76), channel_id=1, source_target_pairs={{0,4},{4,8},{8,12},{12,16},{16,20},{20,24},{24,28},{1,5},{5,9},{9,... | collective-permute-start | bytes 786440 | tf_op jit(solution)/shard_map/ppermute | solution.py:282
  9.0 20.4 %collective-permute-start.6 = (bf16[1024,1024]{1,0:T(8,128)(2,1)S(1)}, bf16[1024,1024]{1,0:T(8,128)(2,1)S(1)}, u32[]{:S(2)}, u32[]{:S(2)}) collective-permute-start(bf16[1024,1024]{1,0:T(8,128)(2,1)S(1)} %get-tuple-element.44), channel_id=1, source_target_pairs={{0,4},{8,12},{16,20},{24,28},{1,5},{9,13},{17,21},{25,29},{2,6},{1... | collective-permute-start | bytes 6291464 | tf_op jit(solution)/shard_map/ppermute | solution.py:282
  10.3 14.5 %copy-start.3 = (bf16[1,128,1024]{2,1,0:T(8,128)(2,1)S(1)}, bf16[1,128,1024]{2,1,0:T(8,128)(2,1)}, u32[]{:S(2)}) copy-start(bf16[1,128,1024]{2,1,0:T(8,128)(2,1)} %param.9) | copy-start | bytes 786436
  11.9 8.8 %collective-permute-start.1 = (bf16[144,1024]{1,0:T(8,128)(2,1)S(1)}, bf16[144,1024]{1,0:T(8,128)(2,1)S(1)}, u32[]{:S(2)}, u32[]{:S(2)}) collective-permute-start(bf16[144,1024]{1,0:T(8,128)(2,1)S(1)} %get-tuple-element.38), channel_id=1, source_target_pairs={{0,4},{4,8},{8,12},{12,16},{16,20},{20,24},{24,28},{1,5},{5,9},{9,... | collective-permute-start | bytes 884744 | tf_op jit(solution)/shard_map/ppermute | solution.py:282
  17.1 6.5 %collective-permute-start.3 = (bf16[128,1024]{1,0:T(8,128)(2,1)S(1)}, bf16[128,1024]{1,0:T(8,128)(2,1)S(1)}, u32[]{:S(2)}, u32[]{:S(2)}) collective-permute-start(bf16[128,1024]{1,0:T(8,128)(2,1)S(1)} %get-tuple-element.41), channel_id=1, source_target_pairs={{0,1},{1,2},{2,3},{3,0}} | collective-permute-start | bytes 786440 | tf_op jit(solution)/shard_map/ppermute | solution.py:286
  17.8 7.2 %collective-permute-start.4 = (bf16[128,1024]{1,0:T(8,128)(2,1)S(1)}, bf16[128,1024]{1,0:T(8,128)(2,1)S(1)}, u32[]{:S(2)}, u32[]{:S(2)}) collective-permute-start(bf16[128,1024]{1,0:T(8,128)(2,1)S(1)} %get-tuple-element.41), channel_id=1, source_target_pairs={{0,2},{1,3},{2,0},{3,1}} | collective-permute-start | bytes 786440 | tf_op jit(solution)/shard_map/ppermute | solution.py:286
  18.5 6.5 %collective-permute-start.5 = (bf16[128,1024]{1,0:T(8,128)(2,1)S(1)}, bf16[128,1024]{1,0:T(8,128)(2,1)S(1)}, u32[]{:S(2)}, u32[]{:S(2)}) collective-permute-start(bf16[128,1024]{1,0:T(8,128)(2,1)S(1)} %get-tuple-element.41), channel_id=1, source_target_pairs={{0,3},{1,0},{2,1},{3,2}} | collective-permute-start | bytes 786440 | tf_op jit(solution)/shard_map/ppermute | solution.py:286
  22.3 7.1 %collective-permute-start.2 = (bf16[128,1024]{1,0:T(8,128)(2,1)S(1)}, bf16[128,1024]{1,0:T(8,128)(2,1)S(1)}, u32[]{:S(2)}, u32[]{:S(2)}) collective-permute-start(bf16[128,1024]{1,0:T(8,128)(2,1)S(1)} %get-tuple-element.40.before), channel_id=1, source_target_pairs={{4,12},{5,13},{6,14},{7,15}} | collective-permute-start | bytes 786440 | tf_op jit(solution)/shard_map/ppermute | solution.py:282
  23.6 5.8 %collective-permute-start.7 = (bf16[128,1024]{1,0:T(8,128)(2,1)S(1)}, bf16[128,1024]{1,0:T(8,128)(2,1)S(1)}, u32[]{:S(2)}, u32[]{:S(2)}) collective-permute-start(bf16[128,1024]{1,0:T(8,128)(2,1)S(1)} %get-tuple-element.46), channel_id=1, source_target_pairs={{0,4},{8,12},{16,20},{24,28},{1,5},{9,13},{17,21},{25,29},{2,6},{1... | collective-permute-start | bytes 786440 | tf_op jit(solution)/shard_map/ppermute | solution.py:282
  30.3 8.1 %collective-permute-start.8 = (bf16[128,1024]{1,0:T(8,128)(2,1)S(1)}, bf16[128,1024]{1,0:T(8,128)(2,1)S(1)}, u32[]{:S(2)}, u32[]{:S(2)}) collective-permute-start(bf16[128,1024]{1,0:T(8,128)(2,1)S(1)} %get-tuple-element.52.before), channel_id=1, source_target_pairs={{12,20},{13,21},{14,22},{15,23}} | collective-permute-start | bytes 786440 | tf_op jit(solution)/shard_map/ppermute | solution.py:282
  31.6 5.1 %collective-permute-start.9 = (bf16[128,256]{1,0:T(8,128)(2,1)S(1)}, bf16[128,256]{1,0:T(8,128)(2,1)S(1)}, u32[]{:S(2)}, u32[]{:S(2)}) collective-permute-start(bf16[128,256]{1,0:T(8,128)(2,1)S(1)} %get-tuple-element.54), channel_id=1, source_target_pairs={{0,1},{1,2},{2,3},{3,0},{4,5},{5,6},{6,7},{7,4},{8,9},{9,10},{10,1... | collective-permute-start | bytes 196616 | tf_op jit(solution)/shard_map/ppermute | solution.py:289
  32.9 4.4 %collective-permute-start.10 = (bf16[128,256]{1,0:T(8,128)(2,1)S(1)}, bf16[128,256]{1,0:T(8,128)(2,1)S(1)}, u32[]{:S(2)}, u32[]{:S(2)}) collective-permute-start(bf16[128,256]{1,0:T(8,128)(2,1)S(1)} %get-tuple-element.55), channel_id=1, source_target_pairs={{0,2},{1,3},{2,0},{3,1},{4,6},{5,7},{6,4},{7,5},{8,10},{9,11},{10,... | collective-permute-start | bytes 196616 | tf_op jit(solution)/shard_map/ppermute | solution.py:289
  35.2 3.1 %collective-permute-start.11 = (bf16[128,256]{1,0:T(8,128)(2,1)S(1)}, bf16[128,256]{1,0:T(8,128)(2,1)S(1)}, u32[]{:S(2)}, u32[]{:S(2)}) collective-permute-start(bf16[128,256]{1,0:T(8,128)(2,1)S(1)} %get-tuple-element.56), channel_id=1, source_target_pairs={{0,3},{1,0},{2,1},{3,2},{4,7},{5,4},{6,5},{7,6},{8,11},{9,8},{10,9... | collective-permute-start | bytes 196616 | tf_op jit(solution)/shard_map/ppermute | solution.py:289
  38.4 0.7 collective-permute-start.12
  39.2 7.8 %collective-permute-start.13 = (bf16[128,1024]{1,0:T(8,128)(2,1)S(1)}, bf16[128,1024]{1,0:T(8,128)(2,1)S(1)}, u32[]{:S(2)}, u32[]{:S(2)}) collective-permute-start(bf16[128,1024]{1,0:T(8,128)(2,1)S(1)} %shard_map.84), channel_id=1, source_target_pairs={{12,8},{20,16},{28,24},{13,9},{21,17},{29,25},{14,10},{22,18},{30,... | collective-permute-start | bytes 786440 | tf_op jit(solution)/shard_map/ppermute | solution.py:282
  40.5 19.5 %collective-permute-start.14 = (bf16[128,1024]{1,0:T(8,128)(2,1)S(1)}, bf16[128,1024]{1,0:T(8,128)(2,1)S(1)}, u32[]{:S(2)}, u32[]{:S(2)}) collective-permute-start(bf16[128,1024]{1,0:T(8,128)(2,1)S(1)} %get-tuple-element.58.before.old), channel_id=1, source_target_pairs={{4,9},{5,10},{6,11},{7,8},{12,17},{13,18},{14,19},{15,16},{20,25},... | collective-permute-start | bytes 786440 | tf_op jit(solution)/shard_map/ppermute | solution.py:286
  44.6 18.4 %collective-permute-start.16 = (bf16[128,1024]{1,0:T(8,128)(2,1)S(1)}, bf16[128,1024]{1,0:T(8,128)(2,1)S(1)}, u32[]{:S(2)}, u32[]{:S(2)}) collective-permute-start(bf16[128,1024]{1,0:T(8,128)(2,1)S(1)} %get-tuple-element.58.before.old), channel_id=1, source_target_pairs={{4,11},{5,8},{6,9},{7,10},{12,19},{13,16},{14,17},{15,18},{20,27},... | collective-permute-start | bytes 786440 | tf_op jit(solution)/shard_map/ppermute | solution.py:286
  47.0 16.0 %collective-permute-start.15 = (bf16[128,1024]{1,0:T(8,128)(2,1)S(1)}, bf16[128,1024]{1,0:T(8,128)(2,1)S(1)}, u32[]{:S(2)}, u32[]{:S(2)}) collective-permute-start(bf16[128,1024]{1,0:T(8,128)(2,1)S(1)} %shard_map.88), channel_id=1, source_target_pairs={{4,10},{5,11},{6,8},{7,9},{12,18},{13,19},{14,16},{15,17},{24,26},... | collective-permute-start | bytes 786440 | tf_op jit(solution)/shard_map/ppermute | solution.py:286
  51.3 12.0 %collective-permute-start.17 = (bf16[128,1024]{1,0:T(8,128)(2,1)S(1)}, bf16[128,1024]{1,0:T(8,128)(2,1)S(1)}, u32[]{:S(2)}, u32[]{:S(2)}) collective-permute-start(bf16[128,1024]{1,0:T(8,128)(2,1)S(1)} %get-tuple-element.62.left), channel_id=1, source_target_pairs={{4,5},{5,6},{6,7},{7,4},{12,13},{13,14},{14,15},{15,12},{20,21},{2... | collective-permute-start | bytes 786440 | tf_op jit(solution)/shard_map/ppermute | solution.py:286
  55.2 12.0 %collective-permute-start.18 = (bf16[128,1024]{1,0:T(8,128)(2,1)S(1)}, bf16[128,1024]{1,0:T(8,128)(2,1)S(1)}, u32[]{:S(2)}, u32[]{:S(2)}) collective-permute-start(bf16[128,1024]{1,0:T(8,128)(2,1)S(1)} %get-tuple-element.62.left), channel_id=1, source_target_pairs={{4,6},{5,7},{6,4},{7,5},{12,14},{13,15},{14,12},{15,13},{20,22},{2... | collective-permute-start | bytes 786440 | tf_op jit(solution)/shard_map/ppermute | solution.py:286
  60.0 9.9 %collective-permute-start.19 = (bf16[128,1024]{1,0:T(8,128)(2,1)S(1)}, bf16[128,1024]{1,0:T(8,128)(2,1)S(1)}, u32[]{:S(2)}, u32[]{:S(2)}) collective-permute-start(bf16[128,1024]{1,0:T(8,128)(2,1)S(1)} %get-tuple-element.62.left), channel_id=1, source_target_pairs={{4,7},{5,4},{6,5},{7,6},{12,15},{13,12},{14,13},{15,14},{20,23},{2... | collective-permute-start | bytes 786440 | tf_op jit(solution)/shard_map/ppermute | solution.py:286
